TPU v7x, 32 devices: a whole 2x2x4 slice. The times are simulated.
32 devices in a mesh: groups: 2 (over x), fsdp: 16 (over z, y, core).
Axes of the slice: x: 2, y: 2, z: 4, core: 2. Of those that a mesh axis runs over, the one named last changes fastest.
Arguments:
- obs_feat: bfloat16 [12288, 2048], P(('groups', 'fsdp')), parts along dimension 0, may hold values from -6 to 6
- reward: float32 [512, 24], P(('groups', 'fsdp')), parts along dimension 0, may hold values from -22 to 22
- value_old: float32 [512, 25], P(('groups', 'fsdp')), parts along dimension 0, may hold values from -6 to 6
- done: int32 [512, 24], P(('groups', 'fsdp')), parts along dimension 0, may hold values 0 or 1
- minibatch_perm: int32 [12288], P(('groups', 'fsdp')), parts along dimension 0, may hold values from 0 to 6143, as said below
- old_mean: bfloat16 [12288, 12], P(('groups', 'fsdp')), parts along dimension 0, may hold values from -6 to 6
- noise: bfloat16 [12288, 12], P(('groups', 'fsdp')), parts along dimension 0, may hold values from -6 to 6
- gain_in: float32 [2048], replicated, may hold values from 0.5 to 1.5
- out_weight: bfloat16 [2048, 2048], P('fsdp'), may hold values from -0.125 to 0.125
- head_weight: bfloat16 [2048, 13], replicated, may hold values from -0.125 to 0.125
- log_std: float32 [12], replicated, may hold values from 0.7 to 1.3
Outputs:
- hidden_out: bfloat16 [12288, 2048], P(('groups', 'fsdp')), parts along dimension 0
- grad_weight: float32 [4096, 2048], P(('groups', 'fsdp')), parts along dimension 0
- grad_head: float32 [4096, 13], P('groups'), parts along dimension 0
- grad_std: float32 [24], P('groups'), parts along dimension 0
There are 2 independent parts, one for each index of `groups`. A program takes and returns all parts, laid end to end along the dimension named above; an argument that names none is the same for every part. Nothing has to cross between parts.
Inputs may be any that keep to these rules, and one draw needn't show every extreme that they name: `minibatch_perm`: rows of one index of fsdp go 24 to each index of fsdp; the block of 384 minibatch positions of index j holds at positions j * 384 + s * 24 + c the rows from index s; a permutation of all rows.
All inputs are finite; a program needn't handle non-finite values. No bound on the sum of `done` on one device may be relied on, other than what follows from the above.
Results may differ from a plain program's by a relative error of at most 0.0095.
Values may be sent and summed in bfloat16 or wider, within the bound.
No kernel may reach another device: no remote copies, remote signals or barrier semaphores. Data moves between devices by JAX's collectives and lax.ppermute only.
A program may use at most 128 MiB of HBM per device.

v0:
```python
import jax
import jax.numpy as jnp
from jax import lax
from jax.sharding import PartitionSpec as P

GAMMA = 0.99
LAMBDA_GAE = 0.95
CLIP_EPS = 0.2
NORM_EPS = 1e-05


def advantages(reward, value_old, done):
    keep = 1.0 - done.astype(jnp.float32)
    deltas = reward + GAMMA * value_old[:, 1:] * keep - value_old[:, :-1]

    def walk(carry, inputs):
        dstep, kstep = inputs
        carry = dstep + GAMMA * LAMBDA_GAE * kstep * carry
        return (carry, carry)

    start = jnp.zeros((reward.shape[0],), jnp.float32)
    _, stacked = lax.scan(walk, start, (deltas.T, keep.T), reverse=True)
    gae = stacked.T
    return (gae.reshape(-1), (gae + value_old[:, :-1]).reshape(-1))


def compute_rows(
    rows_x, old_mean, noise, adv_b, ret_b, gain_in, out_weight, head_weight, log_std, scale
):
    xf = rows_x.astype(jnp.float32)
    normed = (xf * lax.rsqrt(jnp.mean(xf * xf, -1, keepdims=True) + NORM_EPS) * gain_in).astype(
        jnp.bfloat16
    )
    columns = normed
    hidden = xf + jnp.dot(
        columns,
        lax.all_gather(out_weight, "fsdp", axis=0, tiled=True),
        preferred_element_type=jnp.float32,
    )
    rinv = lax.rsqrt(jnp.mean(hidden * hidden, -1, keepdims=True) + NORM_EPS)
    hnorm = hidden * rinv
    hnorm_b = hnorm.astype(jnp.bfloat16)
    heads = jnp.dot(hnorm_b, head_weight, preferred_element_type=jnp.float32)
    nact = log_std.shape[0]
    mean_act = heads[:, :nact]
    value = heads[:, nact]
    std_dev = jnp.exp(log_std)
    offset = old_mean.astype(jnp.float32) - mean_act
    sample = noise.astype(jnp.float32)
    logr = jnp.sum(-sample * offset / std_dev - offset * offset / (2.0 * std_dev * std_dev), -1)
    ratio = jnp.exp(logr)
    advant = adv_b.astype(jnp.float32)
    clipped = jnp.clip(ratio, 1.0 - CLIP_EPS, 1.0 + CLIP_EPS)
    active = ratio * advant <= clipped * advant
    gratio = jnp.where(active, -scale * advant, 0.0)
    glogr = gratio * ratio
    gmean = glogr[:, None] * (sample / std_dev + offset / (std_dev * std_dev))
    gvalue = scale * (value - ret_b.astype(jnp.float32))
    std_local = jnp.sum(
        glogr[:, None] * (sample * offset / std_dev + offset * offset / (std_dev * std_dev)), 0
    )
    ghead = jnp.concatenate([gmean, gvalue[:, None]], 1)
    head_local = jnp.dot(hnorm_b.astype(jnp.float32).T, ghead, precision=lax.Precision.HIGHEST)
    ghn = jnp.dot(ghead, head_weight.astype(jnp.float32).T, precision=lax.Precision.HIGHEST)
    ghid = rinv * (ghn - hnorm * jnp.mean(ghn * hnorm, -1, keepdims=True))
    ghid_b = ghid.astype(jnp.bfloat16)
    columns = normed
    grad_weight = lax.psum_scatter(
        lax.dot_general(
            columns, ghid_b, (((0,), (0,)), ((), ())), preferred_element_type=jnp.float32
        ),
        "fsdp",
        scatter_dimension=0,
        tiled=True,
    )
    grad_head, grad_std = lax.psum((head_local, std_local), "fsdp")
    return (hidden.astype(jnp.bfloat16), grad_weight, grad_head, grad_std)


def local(
    obs_feat,
    reward,
    value_old,
    done,
    minibatch_perm,
    old_mean,
    noise,
    gain_in,
    out_weight,
    head_weight,
    log_std,
):
    gae, returns = advantages(reward, value_old, done)
    local_rows = obs_feat.shape[0]
    devices = lax.axis_size("fsdp")
    total_rows = local_rows * devices
    sums, squares = lax.psum((jnp.sum(gae), jnp.sum(gae * gae)), "fsdp")
    mean_adv = sums / total_rows
    var_adv = squares / total_rows - mean_adv * mean_adv
    adv_b = ((gae - mean_adv) * lax.rsqrt(var_adv + NORM_EPS)).astype(jnp.bfloat16)
    ret_b = returns.astype(jnp.bfloat16)
    scale = 1.0 / jnp.sqrt(jnp.float32(total_rows))
    per_peer = local_rows // devices
    send_slot = minibatch_perm // local_rows * per_peer + minibatch_perm % per_peer
    hidden_local, grad_weight, grad_head, grad_std = compute_rows(
        obs_feat, old_mean, noise, adv_b, ret_b, gain_in, out_weight, head_weight, log_std, scale
    )
    send_hidden = jnp.zeros_like(hidden_local).at[send_slot].set(hidden_local)
    hidden_out = lax.all_to_all(send_hidden, "fsdp", split_axis=0, concat_axis=0, tiled=True)
    return (hidden_out, grad_weight, grad_head, grad_std)


def solution(mesh):
    return jax.shard_map(
        local,
        mesh=mesh,
        in_specs=(
            P(("groups", "fsdp"), None),
            P(("groups", "fsdp"), None),
            P(("groups", "fsdp"), None),
            P(("groups", "fsdp"), None),
            P(("groups", "fsdp")),
            P(("groups", "fsdp"), None),
            P(("groups", "fsdp"), None),
            P(),
            P("fsdp", None),
            P(),
            P(),
        ),
        out_specs=(
            P(("groups", "fsdp"), None),
            P(("groups", "fsdp"), None),
            P("groups", None),
            P("groups"),
        ),
        check_vma=False,
    )
```

profile of v0, /device:TPU:0, one launch (start us, length us, event | category | flops | bytes accessed | tf_op | source)
XLA Modules:
  0.0 391.2 jit_solution(8685224248298809231)
XLA Ops:
  7.2 0.7 all-gather.2.cloned.1.call-update
  8.0 0.9 fusion.31
  8.8 0.1 copy.26
  8.9 0.1 copy.27
  9.0 1.8 while.17
  10.8 0.1 copy.28
  10.8 0.6 fusion.29
  11.5 0.6 reduce_sum.66
  12.1 36.1 %all-reduce = (f32[]{:T(128)}, f32[]{:T(128)}) all-reduce(f32[]{:T(128)} %fusion.29, f32[]{:T(128)} %reduce_sum.66), channel_id=1, replica_groups=mesh['groups'=2,'fsdp'=16] {'fsdp'}, use_global_device_ids=true, to_apply=%region_9.10 | all-reduce | flops 2 | bytes 16 | tf_op jit(solution)/shard_map/psum | solution.py:97
  50.8 0.7 fusion.33
  51.5 0.1 reshape.79
  51.6 0.1 reshape.80
  51.7 1.8 fusion.2
  53.5 0.7 fusion.39
  54.2 33.8 %all-gather.2.cloned.1.call-done = bf16[2048,2048]{1,0:T(8,128)(2,1)} async-done(((bf16[128,2048]{1,0:T(8,128)(2,1)}), bf16[2048,2048]{1,0:T(8,128)(2,1)}) %all-gather.2.cloned.1.call-update) | async-done | bytes 8388624 | tf_op jit(solution)/shard_map/all_gather | solution.py:37
  88.1 7.9 %multiply_reduce_fusion.1 = (f32[384]{0:T(512)S(1)}, f32[384,2048]{1,0:T(8,128)S(1)}) fusion(bf16[2048,2048]{1,0:T(8,128)(2,1)} %all-gather.2.cloned.1.call-done, bf16[384,2048]{1,0:T(8,128)(2,1)} %param.13, f32[2048]{0:T(1024)} %param.20, f32[384]{0:T(512)S(1)} %add_rsqrt_fusion.1), kind=kOutput, calls=%fused_computation.12 | convolution fusion | flops 3227516416 | bytes 13118464 | tf_op jit(solution)/shard_map/dot_general | solution.py:35
  95.9 0.2 multiply_convert_fusion.1
  96.2 0.5 fusion.40
  96.7 0.1 fusion.23
  96.9 0.2 fusion.24
  97.1 3.4 multiply_reduce_fusion
  100.4 1.4 fusion.25
  101.8 0.2 reduce-scatter.2.cloned.1.call-start
  102.1 12.9 %fusion.5 = f32[2048,2048]{1,0:T(8,128)} fusion(f32[384,2048]{1,0:T(8,128)} %get-tuple-element.155, f32[384,2048]{1,0:T(8,128)S(1)} %get-tuple-element.153, f32[384]{0:T(512)S(1)} %broadcast_multiply_fusion, f32[384]{0:T(512)S(1)} %add_rsqrt_fusion, bf16[384,2048]{1,0:T(8,128)(2,1)} %param.13, f32[2048]{0:T(1024)S(1)} %copy-done.4, f32[384]{0:T(512)S(1)} %add_rsqrt_fusion.1), kind=kOutput, calls=%fused_computation.14 | convolution fusion | flops 3228303360 | bytes 24654336 | tf_op jit(solution)/shard_map/dot_general | solution.py:69
  115.0 0.7 copy-done.5
  115.6 4.1 %scatter_custom_fusion = bf16[384,2048]{1,0:T(8,128)(2,1)} fusion(s32[384]{0:T(512)S(1)} %compare_select_fusion, f32[384,2048]{1,0:T(8,128)S(1)} %get-tuple-element.153, bf16[]{:T(256)} %constant.88.clone.1), kind=kCustom, calls=%fused_computation.17 | custom fusion | flops 786432 | bytes 4718594 | tf_op jit(solution)/shard_map/scatter | solution.py:108
  119.8 3.7 all-to-all-start
  123.5 54.6 %psum.31 = f32[12]{0:T(128)} all-reduce(f32[12]{0:T(128)S(1)} %get-tuple-element.143), channel_id=1, replica_groups=mesh['groups'=2,'fsdp'=16] {'fsdp'}, use_global_device_ids=true, to_apply=%region_14.15 | all-reduce | flops 12 | bytes 96 | tf_op jit(solution)/shard_map/psum | solution.py:76
  178.1 19.9 %all-reduce.3.cloned.1.call-done = f32[2048,13]{0,1:T(8,128)} async-done(((f32[2048,13]{0,1:T(8,128)}), f32[2048,13]{0,1:T(8,128)}) %all-reduce.3.cloned.1.call-update) | async-done | bytes 106512 | tf_op jit(solution)/shard_map/psum | solution.py:76
  198.0 184.9 %reduce-scatter.2.cloned.1.call-done = f32[128,2048]{1,0:T(8,128)} async-done(((f32[2048,2048]{1,0:T(8,128)}), f32[128,2048]{1,0:T(8,128)}) %reduce-scatter.2.cloned.1.call-update) | async-done | bytes 1048592 | tf_op jit(solution)/shard_map/reduce_scatter | solution.py:68
  382.9 1.1 copy.41
  384.0 0.7 copy.42
  (72 shorter events, 1.6 us)
Async XLA Ops:
  7.2 89.0 %copy-start = (bf16[2048,13]{0,1:T(8,128)(2,1)S(1)}, bf16[2048,13]{0,1:T(8,128)(2,1)}, u32[]{:S(2)}) copy-start(bf16[2048,13]{0,1:T(8,128)(2,1)} %param.22) | copy-start | bytes 159748
  7.2 80.9 %all-gather.2.cloned.1.call-start = ((), (), s32[]{:S(2)}) async-start(), calls=%async_computation.2 | async-start | bytes 8912896 | tf_op jit(solution)/shard_map/all_gather | solution.py:37
  7.9 190.1 %all-reduce.3.cloned.1.call-start = ((), (), s32[]{:S(2)}) async-start(), calls=%async_computation.4 | async-start | bytes 262144 | tf_op jit(solution)/shard_map/psum | solution.py:76
  95.9 0.8 copy-start.2
  95.9 0.8 copy-start.3
  97.1 5.0 %copy-start.4 = (f32[2048]{0:T(1024)S(1)}, f32[2048]{0:T(1024)}, u32[]{:S(2)}) copy-start(f32[2048]{0:T(1024)} %param.20) | copy-start | bytes 24580
  101.8 281.0 %reduce-scatter.2.cloned.1.call-start = ((), (), s32[]{:S(2)}) async-start(), calls=%async_computation.3 | async-start | bytes 17825792 | tf_op jit(solution)/shard_map/reduce_scatter | solution.py:68
  115.0 0.7 copy-start.5
  119.8 58.4 %all-to-all-start = ((bf16[16,24,2048]{2,1,0:T(8,128)(2,1)}), bf16[16,24,2048]{2,1,0:T(8,128)(2,1)S(1)}, u32[]{:S(2)}, u32[]{:S(2)}) async-start(bf16[16,24,2048]{2,1,0:T(8,128)(2,1)} %bitcast.39), calls=%async_computation | async-start | bytes 3145728 | tf_op jit(solution)/shard_map/all_to_all | solution.py:109
  198.0 186.1 %copy-start.1 = (f32[2048,13]{0,1:T(8,128)S(1)}, f32[2048,13]{0,1:T(8,128)}, u32[]{:S(2)}) copy-start(f32[2048,13]{0,1:T(8,128)} %all-reduce.3.cloned.1.call-done) | copy-start | bytes 319492
Sparse Core Ops, SparseCore 0:
  10.2 77.8 all-gather.1
  102.0 95.9 all-reduce.2
  202.7 180.1 reduce-scatter.1
where the time goes:
time: 392 us; the launch traced here: 391 us
  waiting for transfers between devices  239 us (61%)
  blocking collectives  90.8 us (23%)
  matrix products  26 us (7%)
  between operations  16.5 us (4%)
  other arithmetic  10.4 us (3%)
  starting transfers between devices  4.01 us (1%)
    reduce_scatter x1, waiting for transfers between devices, compute_rows(): lax.psum_scatter(lax.dot_general(columns, ghid_b, (((0,), (0,)), ((), ())...  185 us
    psum x1, blocking collectives, compute_rows(): grad_head, grad_std = lax.psum((head_local, std_local), 'fsdp')  54.6 us
    psum x1, blocking collectives, local(): sums, squares = lax.psum((jnp.sum(gae), jnp.sum(gae * gae)), 'fsdp')  36.1 us
    all_gather x1, waiting for transfers between devices, compute_rows(): lax.all_gather(out_weight, 'fsdp', axis=0, tiled=True)  33.8 us
    psum x1, waiting for transfers between devices, compute_rows(): grad_head, grad_std = lax.psum((head_local, std_local), 'fsdp')  19.9 us
    dot_general x1, matrix products, compute_rows(): lax.dot_general(columns, ghid_b, (((0,), (0,)), ((), ())), preferred_elem...  12.9 us
    dot_general x1, matrix products, compute_rows(): jnp.dot(columns, lax.all_gather(out_weight, 'fsdp', axis=0, tiled=True),...  7.85 us
  transfers between devices with their start and end apart: 4, of which 3 were waited for; matrix products, arithmetic and copies ran while one was open for 6% of the time, Pallas kernels for 0%

commit v1 on v0

v1 whole, which is shorter than its diff:
```python
import functools

import jax
import jax.numpy as jnp
from jax import lax
from jax.experimental import pallas as pl
from jax.experimental.pallas import tpu as pltpu
from jax.sharding import PartitionSpec as P

GAMMA = 0.99
LAMBDA_GAE = 0.95
CLIP_EPS = 0.2
NORM_EPS = 1e-05
F32 = jnp.float32
BF16 = jnp.bfloat16
LANES = 128
HALF = 16
VMEM_BYTES = 56 * 1024 * 1024
CHEAP = pl.CostEstimate(flops=1, bytes_accessed=1, transcendentals=0)


def params():
    return pltpu.CompilerParams(
        vmem_limit_bytes=VMEM_BYTES, dimension_semantics=("arbitrary",)
    )


def split(x):
    high = x.astype(BF16)
    return high, (x - high.astype(F32)).astype(BF16)


def dot(a, b):
    return jnp.dot(a, b, preferred_element_type=F32)


def dot_t(a, b):
    return lax.dot_general(a, b, (((1,), (1,)), ((), ())), preferred_element_type=F32)


def shifted(x, by):
    return pltpu.roll(x, LANES - by, 1)


def small_kernel(
    nact, per_peer, reward_ref, value_ref, done_ref, old_ref, noise_ref, perm_ref, small_ref, pair_ref, pad_ref, tall_ref
):
    envs, steps = reward_ref.shape
    rows = perm_ref.shape[1]

    def wide(x):
        pad_ref[...] = jnp.zeros_like(pad_ref)
        pad_ref[:, : x.shape[1]] = x
        return pad_ref[...]

    inside = lax.broadcasted_iota(jnp.int32, (envs, LANES), 1) < steps
    value = wide(value_ref[...])
    keep = 1.0 - wide(done_ref[...].astype(F32))
    delta = wide(reward_ref[...]) + GAMMA * shifted(value, 1) * keep - value
    gae = jnp.where(inside, delta, 0.0)
    factor = jnp.where(inside, GAMMA * LAMBDA_GAE * keep, 0.0)
    reach = 1
    while reach < steps:
        gae = gae + factor * shifted(gae, reach)
        factor = factor * shifted(factor, reach)
        reach *= 2
    ret = gae + value
    high, low = split(gae)
    mid, low = split(gae - high.astype(F32))
    lane = lax.broadcasted_iota(jnp.int32, (LANES, rows), 1)
    pick = jnp.where(
        lax.rem(lane, steps) == lax.broadcasted_iota(jnp.int32, (LANES, rows), 0), 1.0, 0.0
    ).astype(BF16)
    lane = lax.broadcasted_iota(jnp.int32, (envs, rows), 1)
    mine = lane // steps == lax.broadcasted_iota(jnp.int32, (envs, rows), 0)

    def flat(x):
        return jnp.sum(jnp.where(mine, dot(x, pick), 0.0), 0, keepdims=True)

    perm = perm_ref[...]
    slot = perm // rows * per_peer + lax.rem(perm, per_peer)
    row = lax.broadcasted_iota(jnp.int32, (HALF, rows), 0)

    def put(block, index, values):
        return jnp.where(row == index, values, block)

    def tall(x):
        tall_ref[...] = jnp.zeros_like(tall_ref)
        tall_ref[:nact, :] = x.astype(F32)
        return tall_ref[...]

    top = tall(old_ref[...])
    for index, values in enumerate((high, mid, low, ret.astype(BF16))):
        top = put(top, nact + index, flat(values))
    bottom = tall(noise_ref[...])
    bottom = put(bottom, nact, (slot // 256).astype(F32))
    bottom = put(bottom, nact + 1, lax.rem(slot, 256).astype(F32))
    small = jnp.concatenate([top, bottom], 0).astype(BF16)
    small_ref[...] = small
    gae = gae_of(small[:HALF], nact)
    lane = lax.broadcasted_iota(jnp.int32, pair_ref.shape, 1)
    pair = jnp.zeros(pair_ref.shape, F32)
    for first, value in ((0, gae), (3, gae * gae)):
        value = jnp.sum(value, 1, keepdims=True)
        for i in range(3):
            rounded = value.astype(BF16).astype(F32)
            pair = jnp.where(lane == first + i, rounded, pair)
            value = value - rounded
    pair_ref[...] = pair.astype(BF16)


def gae_of(small, nact):
    block = small.astype(F32)
    return block[nact : nact + 1] + block[nact + 1 : nact + 2] + block[nact + 2 : nact + 3]


def join_kernel(where_ref, *refs):
    pieces, pair_ref, block_ref = refs[:-2], refs[-2], refs[-1]
    kr = pieces[0].shape[0]
    for r, piece in enumerate(pieces):
        here = pl.ds(pl.multiple_of((where_ref[0] ^ r) * kr, kr), kr)
        block_ref[here, :] = piece[...]
    block_ref[kr * len(pieces) :, :] = pair_ref[...]


def norm_kernel(count, where_ref, *refs):
    x_refs, xq_refs, gain_ref = refs[:count], refs[count : 2 * count], refs[2 * count]
    normed_ref, turned_ref, xq_ref = refs[-3:]
    if count == 1:
        x, xq = x_refs[0][...], xq_refs[0][...]
    else:
        first = pl.program_id(0) == 0
        x = jnp.where(first, x_refs[0][...], x_refs[1][...])
        xq = jnp.where(first, xq_refs[0][...], xq_refs[1][...])
    xf = x.astype(F32)
    rms = lax.rsqrt(jnp.mean(xf * xf, -1, keepdims=True) + NORM_EPS)
    normed = xf * rms * gain_ref[...]
    normed_ref[...] = normed.astype(BF16)
    turned_ref[...] = normed.T.astype(BF16)
    xq_ref[...] = xq


def norm_piece(where, xs, gain, start, apart, total, part, buffers):
    rows, width = xs[0].shape
    step = LANES
    base = start // step
    far = apart // step
    if len(xs) == 1:
        grid, source, target = rows // step, (lambda i: i), (lambda i: base + i)
    else:
        grid, source, target = len(xs), (lambda i: 0), (lambda i: base + i * far)
    shapes = (
        jax.ShapeDtypeStruct((total, width), BF16),
        jax.ShapeDtypeStruct((width, total), BF16),
        jax.ShapeDtypeStruct((total, part), BF16),
    )
    buffers = () if buffers is None else buffers
    return pl.pallas_call(
        functools.partial(norm_kernel, len(xs)),
        out_shape=shapes,
        grid_spec=pltpu.PrefetchScalarGridSpec(
            num_scalar_prefetch=1,
            grid=(grid,),
            in_specs=[pl.BlockSpec((step, width), lambda i, w: (source(i), 0))] * len(xs)
            + [pl.BlockSpec((step, part), lambda i, w: (source(i), w[0]))] * len(xs)
            + [pl.BlockSpec((1, width), lambda i, w: (0, 0))]
            + [pl.BlockSpec(memory_space=pl.ANY)] * len(buffers),
            out_specs=[
                pl.BlockSpec((step, width), lambda i, w: (target(i), 0)),
                pl.BlockSpec((width, step), lambda i, w: (0, target(i))),
                pl.BlockSpec((step, part), lambda i, w: (target(i), 0)),
            ],
        ),
        input_output_aliases={2 * len(xs) + 2 + i: i for i in range(len(buffers))},
        compiler_params=params(),
        cost_estimate=CHEAP,
        name="norm",
    )(where, *xs, *xs, gain, *buffers)


def hidden_kernel(line, nact, packed, given, where_ref, *refs):
    count = 1 if given else 2 * line - 2
    weights, refs = refs[:count], refs[count:]
    normed_ref, xq_ref, row_ref, hw_ref, high_ref, sums_ref, send_ref = refs[:7]
    w_ref = weights[0] if given else refs[7]
    step = pl.program_id(0)
    z = where_ref[1]
    rows = normed_ref.shape[0]
    slab = w_ref.shape[0] // line

    def pick():
        own, direct = weights[0], weights[-1]
        fwd, bwd = weights[1 : line - 1] + (direct,), weights[line - 1 : -1] + (direct,)
        w_ref[pl.ds(pl.multiple_of(z * slab, slab), slab), :] = own[:slab, :]
        for j in range(1, line):
            place = pl.multiple_of(lax.rem(z - j + line, line) * slab, slab)
            w_ref[pl.ds(place, slab), :] = jnp.where(
                z >= j, fwd[j - 1][:slab, :], bwd[line - j - 1][:slab, :]
            )

    if not given:
        pl.when(step == 0)(pick)

    hidden = xq_ref[...].astype(F32) + dot(normed_ref[...], w_ref[...])
    high, low = split(hidden)
    high_ref[...] = high
    heads = dot(high, hw_ref[...]) + dot(low, hw_ref[...])
    lane = lax.broadcasted_iota(jnp.int32, heads.shape, 1)
    square = jnp.sum(hidden * hidden, 1, keepdims=True)
    sums = jnp.where(lane == nact + 1, square, heads).T[:HALF]
    if not given:
        pair = jnp.zeros((HALF, LANES), F32)
        for ref in weights:
            pair = pair + ref[slab:, :LANES].astype(F32)
        pair = jnp.concatenate([pair[:1], jnp.zeros((1, rows - LANES), F32)], 1)
        row = lax.broadcasted_iota(jnp.int32, sums.shape, 0)
        sums = jnp.where(row == nact + 2, pair, sums)
    sums_ref[...] = sums
    slot = row_ref[HALF + nact : HALF + nact + 1, :].astype(F32) * 256.0
    slot = (slot + row_ref[HALF + nact + 1 : HALF + nact + 2, :].astype(F32)).astype(jnp.int32)
    order = jnp.where(lax.broadcasted_iota(jnp.int32, (rows, rows), 0) == slot, 1.0, 0.0).astype(BF16)
    ranked = dot(order, high)
    if not packed:
        send_ref[...] = ranked.astype(BF16)
        return
    sorted_ref = refs[-1]
    sorted_ref[pl.ds(pl.multiple_of(step * rows, rows), rows), :] = ranked

    @pl.when(step == sorted_ref.shape[0] // rows - 1)
    def _():
        n, size, _ = send_ref.shape
        members = sorted_ref.shape[0] // rows
        peer = size // members
        for j in range(n):
            send_ref[j] = jnp.concatenate(
                [sorted_ref[r * rows + j * peer : r * rows + (j + 1) * peer, :] for r in range(members)],
                0,
            ).astype(BF16)


def rest_kernel(line, team, nact, width, total_rows, where_ref, *refs):
    sums, refs = refs[:team], refs[team:]
    row_ref, isd_ref, *high_refs = refs[:4]
    hw_ref, turned_ref = refs[4:6]
    grads = refs[6 : 6 + line]
    firsts, (direct_ref, head_ref, ghid_ref) = refs[6 + line : -3], refs[-3:]
    z = where_ref[1]
    step = pl.program_id(0)
    scale = total_rows**-0.5
    slab, part = grads[0].shape

    @pl.when(step == 0)
    def _():
        half = team // 2
        rows = high_refs[0].shape[0] // half
        row = lax.broadcasted_iota(jnp.int32, (HALF, rows), 0)
        isd = isd_ref[:, :1]
        pair = sums[0][nact + 2 : nact + 3, :LANES]
        for other in sums[1:]:
            pair = pair + other[nact + 2 : nact + 3, :LANES]
        lane = lax.broadcasted_iota(jnp.int32, (1, LANES), 1)
        mean = jnp.sum(jnp.where(lane < 3, pair, 0.0), 1, keepdims=True) / total_rows
        square = jnp.sum(jnp.where((lane >= 3) & (lane < 6), pair, 0.0), 1, keepdims=True) / total_rows
        spread = lax.rsqrt(square - mean * mean + NORM_EPS)
        std = jnp.zeros((HALF, rows), F32)
        head = jnp.zeros((HALF, part), F32)
        for r in range(team):
            here = slice(r * rows, (r + 1) * rows)
            total = sums[0][:, here]
            for s in range(1, team):
                total = total + sums[s][:, (r ^ s) * rows : ((r ^ s) + 1) * rows]
            rinv = lax.rsqrt(total[nact + 1 : nact + 2] / width + NORM_EPS)
            heads = total * rinv
            top = row_ref[:HALF, here].astype(F32)
            offset = jnp.where(row < nact, top - heads, 0.0)
            sample = row_ref[HALF:, here].astype(F32)
            advant = ((gae_of(row_ref[:HALF, here], nact) - mean) * spread).astype(BF16).astype(F32)
            ret = top[nact + 3 : nact + 4]
            logr = jnp.sum(
                -sample * offset * isd - 0.5 * offset * offset * isd * isd, 0, keepdims=True
            )
            ratio = jnp.exp(logr)
            clipped = jnp.clip(ratio, 1.0 - CLIP_EPS, 1.0 + CLIP_EPS)
            active = ratio * advant <= clipped * advant
            glogr = jnp.where(active, -scale * advant, 0.0) * ratio
            slope = sample * isd + offset * isd * isd
            ghead = jnp.where(
                row < nact, glogr * slope, jnp.where(row == nact, scale * (heads - ret), 0.0)
            )
            std = std + jnp.where(row < nact, glogr * slope * offset, 0.0)
            mean_gh = jnp.sum(ghead * heads, 0, keepdims=True) / width
            scaled = ghead * rinv
            high = high_refs[r // half][(r % half) * rows : (r % half + 1) * rows, :]
            both = dot(jnp.concatenate(split(scaled), 0), high)
            head = head + both[:HALF] + both[HALF:]
            turned = jnp.concatenate(
                [
                    scaled,
                    jnp.broadcast_to(rinv * rinv * mean_gh, (HALF, rows)),
                    jnp.zeros((LANES - 2 * HALF, rows), F32),
                ],
                0,
            ).T
            ghn = dot(jnp.concatenate(split(turned), 1), hw_ref[...])
            ghid_ref[here, :] = (
                ghn - high.astype(F32) * turned[:, HALF : HALF + 1]
            ).astype(BF16)
        row = lax.broadcasted_iota(jnp.int32, (HALF, part), 0)
        lane = lax.broadcasted_iota(jnp.int32, (HALF, part), 1)
        std = jnp.where(row == lane, jnp.sum(std, 1, keepdims=True), 0.0)
        std = jnp.sum(std, 0, keepdims=True)
        head = jnp.where(row == nact + 1, std, head)
        head_ref[...] = head
        for ref in (*firsts, direct_ref):
            ref[slab:, :] = jnp.concatenate(split(head), 0)

    grad = dot(turned_ref[...], ghid_ref[...])
    for k in range(line):

        @pl.when(step == k)
        def _(k=k):
            grads[k][...] = grad
            for ref, index in zip(firsts, first_blocks(line)):
                if k == index:
                    ref[:slab, :] = grad.astype(BF16)

    @pl.when(step == jnp.where(z == 0, line - 1, 1))
    def _():
        direct_ref[:slab, :] = grad.astype(BF16)


def first_blocks(line):
    return sorted({line - 2, 2})


def hop_kernel(head_ref, *refs):
    head = head_ref[...]
    for mine, got, send in zip(refs[:2], refs[2:4], refs[4:]):
        slab = mine.shape[0]
        send[:slab, :] = (mine[...] + got[:slab, :].astype(F32)).astype(BF16)
        send[slab:, :] = jnp.concatenate(split(head + joined(got, slab)), 0)


def joined(ref, slab):
    return ref[slab : slab + HALF, :].astype(F32) + ref[slab + HALF :, :].astype(F32)


def final_kernel(where_ref, mine_ref, head_ref, *refs):
    got, pieces = refs[:3], refs[3:]
    q = where_ref[0]
    slab = mine_ref.shape[0]
    kr = slab // len(pieces)
    head = head_ref[...]
    for ref in got:
        head = head + joined(ref, slab)
    for r, piece in enumerate(pieces):
        here = pl.ds(pl.multiple_of((q ^ r) * kr, kr), kr)
        total = mine_ref[here, :]
        for ref in got:
            total = total + ref[here, :].astype(F32)
        if r == 0:
            piece[:kr, :] = total
            piece[kr:, :] = head
        else:
            piece[:kr, :] = total.astype(BF16)
            piece[kr:, :] = jnp.concatenate(split(head), 0)


def assemble_kernel(where_ref, *refs):
    pieces, (grad_ref, head_ref, std_ref) = refs[:-3], refs[-3:]
    heads_n = head_ref.shape[0]
    q = where_ref[0]
    kr, part = grad_ref.shape[0], pieces[0].shape[1]
    for r, piece in enumerate(pieces):
        here = pl.ds(pl.multiple_of((q ^ r) * part, part), part)
        grad_ref[:, here] = piece[:kr, :].astype(F32)
        head = piece[kr:, :] if r == 0 else joined(piece, kr)
        head_ref[:, here] = head[:heads_n]
        if r == 0:
            std_ref[...] = head[heads_n : heads_n + 1, :LANES]


def plain(shape):
    return pl.BlockSpec(shape, lambda i: (0,) * len(shape))


def whole(shape):
    return pl.BlockSpec(shape, lambda i, w: (0,) * len(shape))


def local(
    obs_feat,
    reward,
    value_old,
    done,
    minibatch_perm,
    old_mean,
    noise,
    gain_in,
    out_weight,
    head_weight,
    log_std,
):
    n = lax.axis_size("fsdp")
    me = lax.axis_index("fsdp")
    team = 4
    line = n // team
    q = me % team
    z = me // team
    rows, width = obs_feat.shape
    part = width // team
    kr = out_weight.shape[0]
    slab = kr * team
    nact = log_std.shape[0]
    heads_n = nact + 1
    per_peer = rows // n
    total_rows = rows * n
    team_rows = team * rows
    where = jnp.stack([q, z]).astype(jnp.int32)

    def mate(x, r):
        return lax.ppermute(x, "fsdp", [(i, i ^ r) for i in range(n)]) if r else x

    def up(x, low, high):
        return lax.ppermute(
            x, "fsdp", [(a * team + b, (a + 1) * team + b) for a in range(low, high) for b in range(team)]
        )

    def down(x, low, high):
        return lax.ppermute(
            x, "fsdp", [(a * team + b, (a - 1) * team + b) for a in range(low, high) for b in range(team)]
        )

    def ends(x):
        far = n - team
        pairs = [(b, far + b) for b in range(team)] + [(far + b, b) for b in range(team)]
        return lax.ppermute(x, "fsdp", pairs)

    pieces = [
        mate(lax.dynamic_slice(out_weight, (0, (q ^ r) * part), (kr, part)), r) for r in range(team)
    ]
    x_core = mate(obs_feat, 1)
    small, pair = pl.pallas_call(
        functools.partial(small_kernel, nact, per_peer),
        out_shape=(
            jax.ShapeDtypeStruct((2 * HALF, rows), BF16),
            jax.ShapeDtypeStruct((HALF, part), BF16),
        ),
        grid=(1,),
        in_specs=[
            plain(reward.shape),
            plain(value_old.shape),
            plain(done.shape),
            plain((nact, rows)),
            plain((nact, rows)),
            plain((1, rows)),
        ],
        out_specs=[plain((2 * HALF, rows)), plain((HALF, part))],
        scratch_shapes=[pltpu.VMEM((reward.shape[0], LANES), F32), pltpu.VMEM((HALF, rows), F32)],
        compiler_params=params(),
        cost_estimate=CHEAP,
        name="small",
    )(reward, value_old, done, old_mean.T, noise.T, minibatch_perm[None, :])
    obs_late, x_core, small, pair, pieces = lax.optimization_barrier(
        (obs_feat, x_core, small, pair, pieces)
    )

    gain = gain_in[None, :]
    cut = rows // 3 * 2 if rows % 3 == 0 and rows // 3 % LANES == 0 else rows
    block = pl.pallas_call(
        join_kernel,
        out_shape=jax.ShapeDtypeStruct((slab + HALF, part), BF16),
        grid_spec=pltpu.PrefetchScalarGridSpec(
            num_scalar_prefetch=1,
            grid=(1,),
            in_specs=[whole((kr, part))] * team + [whole((HALF, part))],
            out_specs=whole((slab + HALF, part)),
        ),
        compiler_params=params(),
        cost_estimate=CHEAP,
        name="join",
    )(where, *pieces, pair)

    def norm(xs, start, apart=0):
        return norm_piece(where, xs, gain, start, apart, team_rows, part, buffers)

    direct = ends(block)
    fs, bs = [up(block, 0, line - 1)], [down(block, 1, line)]
    far = mate(obs_late[:cut], 2)
    small_core = mate(small, 1)
    buffers = None
    buffers = norm([obs_late], 0)
    buffers = norm([x_core], rows)
    direct, fs, bs, far, small, small_core, buffers, obs_late = lax.optimization_barrier(
        (direct, fs, bs, far, small, small_core, buffers, obs_late)
    )
    small = jnp.concatenate([small, small_core], 1)
    small_far = mate(small, 2)
    for j in range(2, line - 1):
        fs.append(up(fs[-1], j - 1, line - 1))
        bs.append(down(bs[-1], 1, line - j + 1))
    diag = mate(far, 1)
    late = mate(obs_late[cut:], 2) if cut < rows else far
    buffers = norm([far], 2 * rows)
    buffers = norm([diag], 3 * rows)
    fs, bs, late, small, small_far, buffers = lax.optimization_barrier(
        (fs, bs, late, small, small_far, buffers)
    )
    weights = [block] + fs + bs + [direct]

    hw = lax.dynamic_slice(head_weight, (q * part, 0), (part, heads_n)).T
    hw_twice = jnp.pad(hw, ((0, LANES - heads_n), (0, 0)))
    hw_wide = hw_twice.T
    hw_twice = jnp.concatenate([hw_twice, hw_twice], 0)
    isd = jnp.pad(jnp.exp(-log_std), (0, HALF - nact))
    isd = jnp.broadcast_to(isd[:, None], (HALF, LANES))

    packed = per_peer % 8 == 0 and team // 2 * per_peer % 16 == 0
    some = team // 2
    some_rows = some * rows

    def hidden(weights, first, rowdata):
        given = len(weights) == 1
        send_shape = (n, some * per_peer, part) if packed else (some_rows, part)
        out = pl.pallas_call(
            functools.partial(hidden_kernel, line, nact, packed, given),
            out_shape=[
                jax.ShapeDtypeStruct((some_rows, part), BF16),
                jax.ShapeDtypeStruct((HALF, some_rows), F32),
                jax.ShapeDtypeStruct(send_shape, BF16),
            ]
            + ([] if given else [jax.ShapeDtypeStruct((width, part), BF16)]),
            grid_spec=pltpu.PrefetchScalarGridSpec(
                num_scalar_prefetch=1,
                grid=(some,),
                in_specs=[whole(weight.shape) for weight in weights]
                + [
                    pl.BlockSpec((rows, width), lambda i, w: (first + i, 0)),
                    pl.BlockSpec((rows, part), lambda i, w: (first + i, 0)),
                    pl.BlockSpec((2 * HALF, rows), lambda i, w: (0, i)),
                    whole((part, LANES)),
                ],
                out_specs=[
                    pl.BlockSpec((rows, part), lambda i, w: (i, 0)),
                    pl.BlockSpec((HALF, rows), lambda i, w: (0, i)),
                    whole(send_shape) if packed else pl.BlockSpec((rows, part), lambda i, w: (i, 0)),
                ]
                + ([] if given else [whole((width, part))]),
                scratch_shapes=[pltpu.VMEM((some_rows, part), F32)] if packed else [],
            ),
            compiler_params=params(),
            cost_estimate=CHEAP,
            name="hidden",
        )(where, *weights, normed, xq, rowdata, hw_wide)
        if not packed:
            high, sums, send, *weight = out
            send = send.reshape(some, n, per_peer, part).transpose(1, 0, 2, 3)
            return high, sums, send.reshape(n, some * per_peer, part), *weight
        return out

    def scatter(send):
        return lax.all_to_all(send, "fsdp", split_axis=0, concat_axis=0, tiled=True)

    normed, turned, xq = buffers
    high_near, sums_near, send, weight = hidden(weights, 0, small)
    recv_near = scatter(send)
    if cut < rows:
        last = mate(late, 1)
        late, last, sums_near, buffers = lax.optimization_barrier((late, last, sums_near, buffers))
        buffers = norm([late, last], 2 * rows + cut, rows)
        normed, turned, xq = buffers
    high_far, sums_far, send, *_ = hidden([weight], some, small_far)
    sums = jnp.concatenate([sums_near, sums_far], 1)
    sums = [mate(sums, r) for r in range(team)]
    send, recv_near, *sums = lax.optimization_barrier((send, recv_near, *sums))
    recv_far = scatter(send)
    small = jnp.concatenate([small, small_far], 1)

    nfirst = len(first_blocks(line))
    outs = pl.pallas_call(
        functools.partial(rest_kernel, line, team, nact, width, total_rows),
        out_shape=[jax.ShapeDtypeStruct((slab, part), F32)] * line
        + [jax.ShapeDtypeStruct((slab + 2 * HALF, part), BF16)] * (nfirst + 1)
        + [jax.ShapeDtypeStruct((HALF, part), F32)],
        grid_spec=pltpu.PrefetchScalarGridSpec(
            num_scalar_prefetch=1,
            grid=(line,),
            in_specs=[whole((HALF, team_rows))] * team
            + [
                whole((2 * HALF, team_rows)),
                whole((HALF, LANES)),
                whole((some_rows, part)),
                whole((some_rows, part)),
                whole((2 * LANES, part)),
                pl.BlockSpec((slab, team_rows), lambda i, w: (lax.rem(w[1] + i, line), 0)),
            ],
            out_specs=[whole((slab, part))] * line
            + [whole((slab + 2 * HALF, part))] * (nfirst + 1)
            + [whole((HALF, part))],
            scratch_shapes=[pltpu.VMEM((team_rows, part), BF16)],
        ),
        compiler_params=params(),
        cost_estimate=CHEAP,
        name="rest",
    )(where, *sums, small, isd, high_near, high_far, hw_twice, turned)
    grads, firsts, direct, head = outs[:line], outs[line:-2], outs[-2], outs[-1]

    def hop(*operands):
        return pl.pallas_call(
            hop_kernel,
            out_shape=[jax.ShapeDtypeStruct((slab + 2 * HALF, part), BF16)] * 2,
            grid=(1,),
            in_specs=[plain((HALF, part))] + [plain((slab, part))] * 2 + [plain((slab + 2 * HALF, part))] * 2,
            out_specs=[plain((slab + 2 * HALF, part))] * 2,
            compiler_params=params(),
            cost_estimate=CHEAP,
            name="hop",
        )(head, *operands)

    direct = ends(direct)
    send_f, send_b = firsts[-1], firsts[0]
    for k in range(line - 2, 0, -1):
        got_f = up(send_f, 0, line - k)
        got_b = down(send_b, k, line)
        if k == 2:
            got_f, got_b, recv_far = lax.optimization_barrier((got_f, got_b, recv_far))
        if k > 1:
            send_f, send_b = hop(grads[k - 1], grads[line - k + 1], got_f, got_b)
    pieces = pl.pallas_call(
        final_kernel,
        out_shape=[jax.ShapeDtypeStruct((kr + HALF, part), F32)]
        + [jax.ShapeDtypeStruct((kr + 2 * HALF, part), BF16)] * (team - 1),
        grid_spec=pltpu.PrefetchScalarGridSpec(
            num_scalar_prefetch=1,
            grid=(1,),
            in_specs=[whole((slab, part)), whole((HALF, part))]
            + [whole((slab + 2 * HALF, part))] * 3,
            out_specs=[whole((kr + HALF, part))] + [whole((kr + 2 * HALF, part))] * (team - 1),
        ),
        compiler_params=params(),
        cost_estimate=CHEAP,
        name="final",
    )(where, grads[0], head, got_f, got_b, direct)
    pieces = [mate(piece, r) for r, piece in enumerate(pieces)]
    grad_weight, heads, std = pl.pallas_call(
        assemble_kernel,
        out_shape=(
            jax.ShapeDtypeStruct((kr, width), F32),
            jax.ShapeDtypeStruct((heads_n, width), F32),
            jax.ShapeDtypeStruct((1, LANES), F32),
        ),
        grid_spec=pltpu.PrefetchScalarGridSpec(
            num_scalar_prefetch=1,
            grid=(1,),
            in_specs=[whole(piece.shape) for piece in pieces],
            out_specs=[whole((kr, width)), whole((heads_n, width)), whole((1, LANES))],
        ),
        compiler_params=params(),
        cost_estimate=CHEAP,
        name="assemble",
    )(where, *pieces)
    grad_head = heads.T
    grad_std = std[0, :nact]

    recv_near = recv_near.reshape(line, team, some, per_peer, part)
    recv_far = recv_far.reshape(line, team, some, per_peer, part)

    def from_member(c, m):
        r = c ^ m
        return recv_near[:, c, r] if r < some else recv_far[:, c, r - some]

    hidden_out = jnp.concatenate(
        [jnp.stack([from_member(c, m) for m in range(team)], 1) for c in range(team)], -1
    ).reshape(rows, width)
    return (hidden_out, grad_weight, grad_head, grad_std)


def solution(mesh):
    return jax.shard_map(
        local,
        mesh=mesh,
        in_specs=(
            P(("groups", "fsdp"), None),
            P(("groups", "fsdp"), None),
            P(("groups", "fsdp"), None),
            P(("groups", "fsdp"), None),
            P(("groups", "fsdp")),
            P(("groups", "fsdp"), None),
            P(("groups", "fsdp"), None),
            P(),
            P("fsdp", None),
            P(),
            P(),
        ),
        out_specs=(
            P(("groups", "fsdp"), None),
            P(("groups", "fsdp"), None),
            P("groups", None),
            P("groups"),
        ),
        check_vma=False,
    )
```

time: 392 us -> 200 us (0.51)
  waiting for transfers between devices: 239 us -> 50.8 us
  blocking collectives: 90.8 us -> 0 us
  starting transfers between devices: 4.01 us -> 66 us
  Pallas kernels: 0 us -> 61.4 us
  matrix products: 26 us -> 0 us
  between operations: 16.5 us -> 0.94 us
  local copies, waits for them, and re-layouts: 3.81 us -> 16.9 us
  other arithmetic: 10.4 us -> 3.02 us
    reduce_scatter x1 -> x0, waiting for transfers between devices: 185 us -> none  [compute_rows(): lax.psum_scatter(lax.dot_general(columns, ghid_b, (((0,), (0,)), ((), ())...]
    psum x2 -> x0, blocking collectives: 90.8 us -> none  [the longest x1 54.6 us: compute_rows(): grad_head, grad_std = lax.psum((head_local, std_local), 'fsdp')]
    pallas_call x0 -> x13, Pallas kernels: none -> 61.4 us  [the longest x5 20.6 us: norm_piece(): pl.pallas_call(functools.partial(norm_kernel, len(xs)), out_shape=shapes,...]
    ppermute x0 -> x26, starting transfers between devices: none -> 53.1 us  [the longest x4 26.5 us: up(): lax.ppermute(x, 'fsdp', [(a * team + b, (a + 1) * team + b) for a in rang...]
    ppermute x0 -> x26, waiting for transfers between devices: none -> 50.8 us  [the longest x4 24 us: up(): lax.ppermute(x, 'fsdp', [(a * team + b, (a + 1) * team + b) for a in rang...]
    all_gather x1 -> x0, waiting for transfers between devices: 33.8 us -> none  [compute_rows(): lax.all_gather(out_weight, 'fsdp', axis=0, tiled=True)]
    dot_general x5 -> x0, matrix products: 26 us -> none  [the longest x1 12.9 us: compute_rows(): lax.dot_general(columns, ghid_b, (((0,), (0,)), ((), ())), preferred_elem...]
    psum x1 -> x0, waiting for transfers between devices: 19.9 us -> none  [compute_rows(): grad_head, grad_std = lax.psum((head_local, std_local), 'fsdp')]
  transfers between devices with their start and end apart: 4 -> 28, of which waited for: 3 -> 13; matrix products, arithmetic and copies ran while one was open for 6% -> 6% of each run, Pallas kernels for 0% -> 23%
where the time goes in v1:
time: 200 us; the launch traced here: 199 us
  starting transfers between devices  66 us (33%)
  Pallas kernels  61.4 us (31%)
  waiting for transfers between devices  50.8 us (25%)
  local copies, waits for them, and re-layouts  16.9 us (8%)
  other arithmetic  3.02 us (2%)
    ppermute x4, starting transfers between devices, up(): lax.ppermute(x, 'fsdp', [(a * team + b, (a + 1) * team + b) for a in rang...  26.5 us
    ppermute x4, waiting for transfers between devices, up(): lax.ppermute(x, 'fsdp', [(a * team + b, (a + 1) * team + b) for a in rang...  24 us
    ppermute x16, waiting for transfers between devices, mate(): return lax.ppermute(x, 'fsdp', [(i, i ^ r) for i in range(n)]) if r else x  21.7 us
    pallas_call x5, Pallas kernels, norm_piece(): pl.pallas_call(functools.partial(norm_kernel, len(xs)), out_shape=shapes,...  20.6 us
    pallas_call x2, Pallas kernels, hidden(): pl.pallas_call(functools.partial(hidden_kernel, line, nact, packed, given...  15.9 us
    all_to_all x2, starting transfers between devices, scatter(): return lax.all_to_all(send, 'fsdp', split_axis=0, concat_axis=0, tiled=True)  12.8 us
    ppermute x16, starting transfers between devices, mate(): return lax.ppermute(x, 'fsdp', [(i, i ^ r) for i in range(n)]) if r else x  11.7 us
    pallas_call x1, Pallas kernels, local(): pl.pallas_call(functools.partial(rest_kernel, line, team, nact, width, to...  11 us
  transfers between devices with their start and end apart: 28, of which 13 were waited for; matrix products, arithmetic and copies ran while one was open for 6% of the time, Pallas kernels for 23%

profile of v1, /device:TPU:0, one launch (start us, length us, event | category | flops | bytes accessed | tf_op | source)
XLA Modules:
  0.0 199.1 jit_solution(1402796800295262464)
XLA Ops:
  3.0 3.0 %collective-permute-start.2 = (bf16[128,512]{1,0:T(8,128)(2,1)S(1)}, bf16[128,512]{1,0:T(8,128)(2,1)S(1)}, u32[]{:S(2)}, u32[]{:S(2)}) collective-permute-start(bf16[128,512]{1,0:T(8,128)(2,1)S(1)} %get-tuple-element.187), channel_id=1, source_target_pairs={{0,2},{1,3},{2,0},{3,1},{4,6},{5,7},{6,4},{7,5},{8,10},{9,11},{10,... | collective-permute-start | bytes 393224 | tf_op jit(solution)/shard_map/ppermute | solution.py:422
  7.2 2.1 %small.1 = (bf16[32,384]{1,0:T(8,128)(2,1)}, bf16[16,512]{1,0:T(8,128)(2,1)}) custom-call(f32[16,24]{1,0:T(8,128)} %reward_ref.1, f32[16,25]{1,0:T(8,128)} %value_ref.1, s32[16,24]{1,0:T(8,128)} %done_ref.1, bf16[12,384]{1,0:T(8,128)(2,1)} %bitcast.85, bf16[12,384]{1,0:T(8,128)(2,1)} %bitcast.86, s32[1,384]{1,0:T(1,128)} %broadcast_in_dim.12.perm_ref), custom_call_target="tpu_custom_call" | custom-call | flops 1 | bytes 1 | tf_op jit(solution)/shard_map/small/pallas_call | solution.py:443
  11.9 2.9 %slice.57 = bf16[256,2048]{1,0:T(8,128)(2,1)} slice(bf16[384,2048]{1,0:T(8,128)(2,1)} %refs_1_), slice={[0:256], [0:2048]} | slice | bytes 2097152 | tf_op jit(solution)/shard_map/slice | solution.py:489
  16.9 2.6 %join.1.refs_0_ = bf16[528,512]{1,0:T(8,128)(2,1)} custom-call(s32[2]{0:T(128)} %pad_add_fusion.where_ref, bf16[128,512]{1,0:T(8,128)(2,1)} %get-tuple-element.88.refs_0_, bf16[128,512]{1,0:T(8,128)(2,1)} %copy-done.18, bf16[128,512]{1,0:T(8,128)(2,1)} %copy-done.19, bf16[128,512]{1,0:T(8,128)(2,1)} %copy-done.20, bf16[16,512]{1,0:T(8,128)(2,1)} %get-tuple-element.92.refs_4_), custom_call_target="tpu_custom_call" | custom-call | flops 1 | bytes 1 | tf_op jit(solution)/shard_map/join/pallas_call | solution.py:470
  19.5 5.5 %collective-permute-start.4 = (bf16[528,512]{1,0:T(8,128)(2,1)}, bf16[528,512]{1,0:T(8,128)(2,1)S(1)}, u32[]{:S(2)}, u32[]{:S(2)}) collective-permute-start(bf16[528,512]{1,0:T(8,128)(2,1)} %join.1.refs_0_), channel_id=1, source_target_pairs={{0,12},{1,13},{2,14},{3,15},{12,0},{13,1},{14,2},{15,3},{16,28},{1... | collective-permute-start | bytes 1622024 | tf_op jit(solution)/shard_map/ppermute | solution.py:437
  25.1 2.1 %collective-permute-start.5 = (bf16[528,512]{1,0:T(8,128)(2,1)}, bf16[528,512]{1,0:T(8,128)(2,1)}, u32[]{:S(2)}, u32[]{:S(2)}) collective-permute-start(bf16[528,512]{1,0:T(8,128)(2,1)} %join.1.refs_0_), channel_id=1, source_target_pairs={{0,4},{1,5},{2,6},{3,7},{4,8},{5,9},{6,10},{7,11},{8,12},{9,13},{1... | collective-permute-start | bytes 1622024 | tf_op jit(solution)/shard_map/ppermute | solution.py:425
  28.7 4.9 %norm.5 = (bf16[1536,2048]{1,0:T(8,128)(2,1)}, bf16[2048,1536]{1,0:T(8,128)(2,1)}, bf16[1536,512]{1,0:T(8,128)(2,1)}) custom-call(s32[2]{0:T(128)} %pad_add_fusion.where_ref, bf16[384,2048]{1,0:T(8,128)(2,1)} %refs_1_, bf16[384,2048]{1,0:T(8,128)(2,1)} %refs_1_, f32[1,2048]{1,0:T(1,128)} %bitcast.80), custom_call_target="tpu_custom_call" | custom-call | flops 1 | bytes 1 | tf_op jit(solution)/shard_map/norm/pallas_call | solution.py:158
  33.6 5.0 %norm.6 = (bf16[1536,2048]{1,0:T(8,128)(2,1)}, bf16[2048,1536]{1,0:T(8,128)(2,1)}, bf16[1536,512]{1,0:T(8,128)(2,1)}) custom-call(s32[2]{0:T(128)} %pad_add_fusion.where_ref, bf16[384,2048]{1,0:T(8,128)(2,1)} %copy-done.1, bf16[384,2048]{1,0:T(8,128)(2,1)} %copy-done.1, ...), custom_call_target="tpu_custom_call", output_to_operand_aliasing={{0}: (4, {}), {1}: (5, {}), {2}: (6, {})} | custom-call | flops 1 | bytes 1 | tf_op jit(solution)/shard_map/norm/pallas_call | solution.py:158
  38.6 10.5 %collective-permute-done.5.refs_1_ = bf16[528,512]{1,0:T(8,128)(2,1)} collective-permute-done((bf16[528,512]{1,0:T(8,128)(2,1)}, bf16[528,512]{1,0:T(8,128)(2,1)}, u32[]{:S(2)}, u32[]{:S(2)}) %collective-permute-start.5) | collective-permute-done | bytes 540704 | tf_op jit(solution)/shard_map/ppermute | solution.py:425
  52.7 1.9 slice.58
  57.5 3.5 %norm.7 = (bf16[1536,2048]{1,0:T(8,128)(2,1)}, bf16[2048,1536]{1,0:T(8,128)(2,1)}, bf16[1536,512]{1,0:T(8,128)(2,1)}) custom-call(s32[2]{0:T(128)} %pad_add_fusion.where_ref, bf16[256,2048]{1,0:T(8,128)(2,1)} %copy-done.2, bf16[256,2048]{1,0:T(8,128)(2,1)} %copy-done.2, ...), custom_call_target="tpu_custom_call", output_to_operand_aliasing={{0}: (4, {}), {1}: (5, {}), {2}: (6, {})} | custom-call | flops 1 | bytes 1 | tf_op jit(solution)/shard_map/norm/pallas_call | solution.py:158
  62.0 3.5 %norm.8 = (bf16[1536,2048]{1,0:T(8,128)(2,1)}, bf16[2048,1536]{1,0:T(8,128)(2,1)}, bf16[1536,512]{1,0:T(8,128)(2,1)}) custom-call(s32[2]{0:T(128)} %pad_add_fusion.where_ref, bf16[256,2048]{1,0:T(8,128)(2,1)} %copy-done.3, bf16[256,2048]{1,0:T(8,128)(2,1)} %copy-done.3, ...), custom_call_target="tpu_custom_call", output_to_operand_aliasing={{0}: (4, {}), {1}: (5, {}), {2}: (6, {})} | custom-call | flops 1 | bytes 1 | tf_op jit(solution)/shard_map/norm/pallas_call | solution.py:158
  65.5 4.8 %collective-permute-done.12.refs_3_ = bf16[32,768]{1,0:T(8,128)(2,1)} collective-permute-done((bf16[32,768]{1,0:T(8,128)(2,1)S(1)}, bf16[32,768]{1,0:T(8,128)(2,1)}, u32[]{:S(2)}, u32[]{:S(2)}) %collective-permute-start.12) | collective-permute-done | bytes 49184 | tf_op jit(solution)/shard_map/ppermute | solution.py:422
  70.3 8.4 %hidden.2 = (bf16[768,512]{1,0:T(8,128)(2,1)}, f32[16,768]{1,0:T(8,128)}, bf16[16,48,512]{2,1,0:T(8,128)(2,1)}, bf16[2048,512]{1,0:T(8,128)(2,1)}) custom-call(s32[2]{0:T(128)} %pad_add_fusion.where_ref, bf16[528,512]{1,0:T(8,128)(2,1)} %join.1.refs_0_, bf16[528,512]{1,0:T(8,128)(2,1)} %collective-permute-done.5.refs_1_, ...), custom_call_target="tpu_custom_call" | custom-call | flops 1 | bytes 1 | tf_op jit(solution)/shard_map/hidden/pallas_call | solution.py:525
  78.7 7.3 %all-to-all-start = ((bf16[16,48,512]{2,1,0:T(8,128)(2,1)}), bf16[16,48,512]{2,1,0:T(8,128)(2,1)S(1)}, u32[]{:S(2)}, u32[]{:S(2)}) async-start(bf16[16,48,512]{2,1,0:T(8,128)(2,1)} %get-tuple-element.138), calls=%async_computation | async-start | bytes 1572864 | tf_op jit(solution)/shard_map/all_to_all | solution.py:562
  88.9 3.7 %norm.9 = (bf16[1536,2048]{1,0:T(8,128)(2,1)}, bf16[2048,1536]{1,0:T(8,128)(2,1)}, bf16[1536,512]{1,0:T(8,128)(2,1)}) custom-call(s32[2]{0:T(128)} %pad_add_fusion.where_ref, bf16[128,2048]{1,0:T(8,128)(2,1)} %copy-done.4, bf16[128,2048]{1,0:T(8,128)(2,1)} %copy-done.5, ...), custom_call_target="tpu_custom_call", output_to_operand_aliasing={{0}: (6, {}), {1}: (7, {}), {2}: (8, {})} | custom-call | flops 1 | bytes 1 | tf_op jit(solution)/shard_map/norm/pallas_call | solution.py:158
  92.6 7.4 %hidden.3 = (bf16[768,512]{1,0:T(8,128)(2,1)}, f32[16,768]{1,0:T(8,128)}, bf16[16,48,512]{2,1,0:T(8,128)(2,1)}) custom-call(s32[2]{0:T(128)} %pad_add_fusion.where_ref, bf16[2048,512]{1,0:T(8,128)(2,1)} %get-tuple-element.125.refs_0_, bf16[1536,2048]{1,0:T(8,128)(2,1)} %get-tuple-element.134.refs_1_, bf16[1536,512]{1,0:T(8,128)(2,1)} %get-tuple-element.135.refs_2_, ...), custom_call_target="tpu_custom_call" | custom-call | flops 1 | bytes 1 | tf_op jit(solution)/shard_map/hidden/pallas_call | solution.py:525
  102.9 4.3 %collective-permute-done.16.refs_2_ = f32[16,1536]{1,0:T(8,128)S(1)} collective-permute-done((f32[16,1536]{1,0:T(8,128)S(1)}, f32[16,1536]{1,0:T(8,128)S(1)}, u32[]{:S(2)}, u32[]{:S(2)}) %collective-permute-start.16) | collective-permute-done | bytes 98336 | tf_op jit(solution)/shard_map/ppermute | solution.py:422
  107.2 1.8 collective-permute-done.17.refs_3_
  109.0 5.5 %all-to-all-start.1 = ((bf16[16,48,512]{2,1,0:T(8,128)(2,1)}), bf16[16,48,512]{2,1,0:T(8,128)(2,1)S(1)}, u32[]{:S(2)}, u32[]{:S(2)}) async-start(bf16[16,48,512]{2,1,0:T(8,128)(2,1)} %get-tuple-element.150), calls=%async_computation.1 | async-start | bytes 1572864 | tf_op jit(solution)/shard_map/all_to_all | solution.py:562
  117.4 11.0 %rest.1 = (f32[512,512]{1,0:T(8,128)}, f32[512,512]{1,0:T(8,128)}, f32[512,512]{1,0:T(8,128)}, f32[512,512]{1,0:T(8,128)}, bf16[544,512]{1,0:T(8,128)(2,1)}, /*i...) custom-call(s32[2]{0:T(128)} %pad_add_fusion.where_ref, f32[16,1536]{1,0:T(8,128)} %copy-done.14, f32[16,1536]{1,0:T(8,128)} %copy-done.21, ...), custom_call_target="tpu_custom_call" | custom-call | flops 1 | bytes 1 | tf_op jit(solution)/shard_map/rest/pallas_call | solution.py:580
  128.4 3.8 %collective-permute-start.18 = (bf16[544,512]{1,0:T(8,128)(2,1)}, bf16[544,512]{1,0:T(8,128)(2,1)S(1)}, u32[]{:S(2)}, u32[]{:S(2)}) collective-permute-start(bf16[544,512]{1,0:T(8,128)(2,1)} %get-tuple-element.149), channel_id=1, source_target_pairs={{0,4},{1,5},{2,6},{3,7},{4,8},{5,9},{6,10},{7,11},{16,20},{17,21},... | collective-permute-start | bytes 1671176 | tf_op jit(solution)/shard_map/ppermute | solution.py:425
  133.0 4.9 %collective-permute-start.22 = (bf16[544,512]{1,0:T(8,128)(2,1)}, bf16[544,512]{1,0:T(8,128)(2,1)S(1)}, u32[]{:S(2)}, u32[]{:S(2)}) collective-permute-start(bf16[544,512]{1,0:T(8,128)(2,1)} %get-tuple-element.160), channel_id=1, source_target_pairs={{0,12},{1,13},{2,14},{3,15},{12,0},{13,1},{14,2},{15,3},{16,28},{1... | collective-permute-start | bytes 1671176 | tf_op jit(solution)/shard_map/ppermute | solution.py:437
  137.9 7.7 %collective-permute-done.18.refs_2_ = bf16[544,512]{1,0:T(8,128)(2,1)S(1)} collective-permute-done((bf16[544,512]{1,0:T(8,128)(2,1)}, bf16[544,512]{1,0:T(8,128)(2,1)S(1)}, u32[]{:S(2)}, u32[]{:S(2)}) %collective-permute-start.18) | collective-permute-done | bytes 557088 | tf_op jit(solution)/shard_map/ppermute | solution.py:425
  146.5 3.0 %hop.1 = (bf16[544,512]{1,0:T(8,128)(2,1)}, bf16[544,512]{1,0:T(8,128)(2,1)}) custom-call(f32[16,512]{1,0:T(8,128)} %get-tuple-element.153.head_ref, f32[512,512]{1,0:T(8,128)} %get-tuple-element.154.refs_0_, f32[512,512]{1,0:T(8,128)} %get-tuple-element.155.refs_1_, bf16[544,512]{1,0:T(8,128)(2,1)} %copy-done.6, bf16[544,512]{1,0:T(8,128)(2,1)} %copy-done.7), custom_call_target="tpu_custom_call" | custom-call | flops 1 | bytes 1 | tf_op jit(solution)/shard_map/hop/pallas_call | solution.py:609
  149.5 19.1 %collective-permute-start.20 = (bf16[544,512]{1,0:T(8,128)(2,1)}, bf16[544,512]{1,0:T(8,128)(2,1)S(1)}, u32[]{:S(2)}, u32[]{:S(2)}) collective-permute-start(bf16[544,512]{1,0:T(8,128)(2,1)} %get-tuple-element.158), channel_id=1, source_target_pairs={{0,4},{1,5},{2,6},{3,7},{4,8},{5,9},{6,10},{7,11},{8,12},{9,13},{1... | collective-permute-start | bytes 1671176 | tf_op jit(solution)/shard_map/ppermute | solution.py:425
  170.1 5.8 %collective-permute-done.20.refs_0_ = bf16[544,512]{1,0:T(8,128)(2,1)S(1)} collective-permute-done((bf16[544,512]{1,0:T(8,128)(2,1)}, bf16[544,512]{1,0:T(8,128)(2,1)S(1)}, u32[]{:S(2)}, u32[]{:S(2)}) %collective-permute-start.20) | collective-permute-done | bytes 557088 | tf_op jit(solution)/shard_map/ppermute | solution.py:425
  175.9 4.3 %collective-permute-done.21.refs_1_ = bf16[544,512]{1,0:T(8,128)(2,1)S(1)} collective-permute-done((bf16[544,512]{1,0:T(8,128)(2,1)}, bf16[544,512]{1,0:T(8,128)(2,1)S(1)}, u32[]{:S(2)}, u32[]{:S(2)}) %collective-permute-start.21) | collective-permute-done | bytes 557088 | tf_op jit(solution)/shard_map/ppermute | solution.py:430
  181.1 3.4 %final.1 = (f32[144,512]{1,0:T(8,128)}, bf16[160,512]{1,0:T(8,128)(2,1)}, bf16[160,512]{1,0:T(8,128)(2,1)}, bf16[160,512]{1,0:T(8,128)(2,1)}) custom-call(s32[2]{0:T(128)} %pad_add_fusion.where_ref, f32[512,512]{1,0:T(8,128)} %get-tuple-element.152.mine_ref, f32[16,512]{1,0:T(8,128)} %get-tuple-element.153.head_ref, bf16[544,512]{1,0:T(8,128)(2,1)} %copy-done.9, ...), custom_call_target="tpu_custom_call" | custom-call | flops 1 | bytes 1 | tf_op jit(solution)/shard_map/final/pallas_call | solution.py:629
  187.8 3.9 %collective-permute-done.24.refs_2_ = bf16[160,512]{1,0:T(8,128)(2,1)S(1)} collective-permute-done((bf16[160,512]{1,0:T(8,128)(2,1)}, bf16[160,512]{1,0:T(8,128)(2,1)S(1)}, u32[]{:S(2)}, u32[]{:S(2)}) %collective-permute-start.24) | collective-permute-done | bytes 163872 | tf_op jit(solution)/shard_map/ppermute | solution.py:422
  191.6 2.7 %collective-permute-done.25.refs_3_ = bf16[160,512]{1,0:T(8,128)(2,1)S(1)} collective-permute-done((bf16[160,512]{1,0:T(8,128)(2,1)}, bf16[160,512]{1,0:T(8,128)(2,1)S(1)}, u32[]{:S(2)}, u32[]{:S(2)}) %collective-permute-start.25) | collective-permute-done | bytes 163872 | tf_op jit(solution)/shard_map/ppermute | solution.py:422
  195.0 2.9 %assemble.1 = (f32[128,2048]{1,0:T(8,128)}, f32[13,2048]{1,0:T(8,128)}, f32[1,128]{1,0:T(1,128)}) custom-call(s32[2]{0:T(128)} %pad_add_fusion.where_ref, f32[144,512]{1,0:T(8,128)} %get-tuple-element.161.refs_0_, bf16[160,512]{1,0:T(8,128)(2,1)} %copy-done.15, bf16[160,512]{1,0:T(8,128)(2,1)} %copy-done.16, bf16[160,512]{1,0:T(8,128)(2,1)} %copy-done.17), custom_call_target="tpu_custom_call" | custom-call | flops 1 | bytes 1 | tf_op jit(solution)/shard_map/assemble/pallas_call | solution.py:645
  (112 shorter events, 34.9 us)
Async XLA Ops:
  0.6 54.5 %copy-start = (bf16[2048,13]{0,1:T(8,128)(2,1)S(1)}, bf16[2048,13]{0,1:T(8,128)(2,1)}, u32[]{:S(2)}) copy-start(bf16[2048,13]{0,1:T(8,128)(2,1)} %param.20) | copy-start | bytes 159748
  0.6 11.3 %collective-permute-start = (bf16[384,2048]{1,0:T(8,128)(2,1)}, bf16[384,2048]{1,0:T(8,128)(2,1)S(1)}, u32[]{:S(2)}, u32[]{:S(2)}) collective-permute-start(bf16[384,2048]{1,0:T(8,128)(2,1)} %refs_1_), channel_id=1, source_target_pairs={{0,1},{1,0},{2,3},{3,2},{4,5},{5,4},{6,7},{7,6},{8,9},{9,8},{10,11... | collective-permute-start | bytes 4718600 | tf_op jit(solution)/shard_map/ppermute | solution.py:422
  3.0 6.4 %collective-permute-start.1 = (bf16[128,512]{1,0:T(8,128)(2,1)S(1)}, bf16[128,512]{1,0:T(8,128)(2,1)S(1)}, u32[]{:S(2)}, u32[]{:S(2)}) collective-permute-start(bf16[128,512]{1,0:T(8,128)(2,1)S(1)} %get-tuple-element.185), channel_id=1, source_target_pairs={{0,1},{1,0},{2,3},{3,2},{4,5},{5,4},{6,7},{7,6},{8,9},{9,8},{10,11... | collective-permute-start | bytes 393224 | tf_op jit(solution)/shard_map/ppermute | solution.py:422
  3.0 7.3 %collective-permute-start.2 = (bf16[128,512]{1,0:T(8,128)(2,1)S(1)}, bf16[128,512]{1,0:T(8,128)(2,1)S(1)}, u32[]{:S(2)}, u32[]{:S(2)}) collective-permute-start(bf16[128,512]{1,0:T(8,128)(2,1)S(1)} %get-tuple-element.187), channel_id=1, source_target_pairs={{0,2},{1,3},{2,0},{3,1},{4,6},{5,7},{6,4},{7,5},{8,10},{9,11},{10,... | collective-permute-start | bytes 393224 | tf_op jit(solution)/shard_map/ppermute | solution.py:422
  6.0 6.0 %collective-permute-start.3 = (bf16[128,512]{1,0:T(8,128)(2,1)S(1)}, bf16[128,512]{1,0:T(8,128)(2,1)S(1)}, u32[]{:S(2)}, u32[]{:S(2)}) collective-permute-start(bf16[128,512]{1,0:T(8,128)(2,1)S(1)} %get-tuple-element.184), channel_id=1, source_target_pairs={{0,3},{1,2},{2,1},{3,0},{4,7},{5,6},{6,5},{7,4},{8,11},{9,10},{10,... | collective-permute-start | bytes 393224 | tf_op jit(solution)/shard_map/ppermute | solution.py:422
  14.9 35.0 %collective-permute-start.7 = (bf16[256,2048]{1,0:T(8,128)(2,1)}, bf16[256,2048]{1,0:T(8,128)(2,1)S(1)}, u32[]{:S(2)}, u32[]{:S(2)}) collective-permute-start(bf16[256,2048]{1,0:T(8,128)(2,1)} %slice.57), channel_id=1, source_target_pairs={{0,2},{1,3},{2,0},{3,1},{4,6},{5,7},{6,4},{7,5},{8,10},{9,11},{10,... | collective-permute-start | bytes 3145736 | tf_op jit(solution)/shard_map/ppermute | solution.py:422
  19.5 19.1 %collective-permute-start.4 = (bf16[528,512]{1,0:T(8,128)(2,1)}, bf16[528,512]{1,0:T(8,128)(2,1)S(1)}, u32[]{:S(2)}, u32[]{:S(2)}) collective-permute-start(bf16[528,512]{1,0:T(8,128)(2,1)} %join.1.refs_0_), channel_id=1, source_target_pairs={{0,12},{1,13},{2,14},{3,15},{12,0},{13,1},{14,2},{15,3},{16,28},{1... | collective-permute-start | bytes 1622024 | tf_op jit(solution)/shard_map/ppermute | solution.py:437
  25.1 24.1 %collective-permute-start.5 = (bf16[528,512]{1,0:T(8,128)(2,1)}, bf16[528,512]{1,0:T(8,128)(2,1)}, u32[]{:S(2)}, u32[]{:S(2)}) collective-permute-start(bf16[528,512]{1,0:T(8,128)(2,1)} %join.1.refs_0_), channel_id=1, source_target_pairs={{0,4},{1,5},{2,6},{3,7},{4,8},{5,9},{6,10},{7,11},{8,12},{9,13},{1... | collective-permute-start | bytes 1622024 | tf_op jit(solution)/shard_map/ppermute | solution.py:425
  27.1 22.8 %collective-permute-start.6 = (bf16[528,512]{1,0:T(8,128)(2,1)}, bf16[528,512]{1,0:T(8,128)(2,1)}, u32[]{:S(2)}, u32[]{:S(2)}) collective-permute-start(bf16[528,512]{1,0:T(8,128)(2,1)} %join.1.refs_0_), channel_id=1, source_target_pairs={{4,0},{5,1},{6,2},{7,3},{8,4},{9,5},{10,6},{11,7},{12,8},{13,9},{1... | collective-permute-start | bytes 1622024 | tf_op jit(solution)/shard_map/ppermute | solution.py:430
  28.4 10.2 %collective-permute-start.8 = (bf16[32,384]{1,0:T(8,128)(2,1)S(1)}, bf16[32,384]{1,0:T(8,128)(2,1)S(1)}, u32[]{:S(2)}, u32[]{:S(2)}) collective-permute-start(bf16[32,384]{1,0:T(8,128)(2,1)S(1)} %copy-done.25), channel_id=1, source_target_pairs={{0,1},{1,0},{2,3},{3,2},{4,5},{5,4},{6,7},{7,6},{8,9},{9,8},{10,11... | collective-permute-start | bytes 73736 | tf_op jit(solution)/shard_map/ppermute | solution.py:422
  38.6 22.4 %copy-start.11 = (bf16[528,512]{1,0:T(8,128)(2,1)}, bf16[528,512]{1,0:T(8,128)(2,1)S(1)}, u32[]{:S(2)}) copy-start(bf16[528,512]{1,0:T(8,128)(2,1)S(1)} %collective-permute-done.4.refs_5_) | copy-start | bytes 1622020
  49.9 11.1 %collective-permute-start.13 = (bf16[256,2048]{1,0:T(8,128)(2,1)S(1)}, bf16[256,2048]{1,0:T(8,128)(2,1)S(1)}, u32[]{:S(2)}, u32[]{:S(2)}) collective-permute-start(bf16[256,2048]{1,0:T(8,128)(2,1)S(1)} %collective-permute-done.7.refs_0_.refs_1_), channel_id=1, source_target_pairs={{0,1},{1,0},{2,3},{3,2},{4,5},{5,4},{6,7},{7,6},{8,9},{9,8},{10,11... | collective-permute-start | bytes 3145736 | tf_op jit(solution)/shard_map/ppermute | solution.py:422
  50.0 20.3 %collective-permute-start.10 = (bf16[528,512]{1,0:T(8,128)(2,1)}, bf16[528,512]{1,0:T(8,128)(2,1)}, u32[]{:S(2)}, u32[]{:S(2)}) collective-permute-start(bf16[528,512]{1,0:T(8,128)(2,1)} %collective-permute-done.6.refs_3_), channel_id=1, source_target_pairs={{4,0},{5,1},{6,2},{7,3},{8,4},{9,5},{10,6},{11,7},{20,16},{21,17},... | collective-permute-start | bytes 1622024 | tf_op jit(solution)/shard_map/ppermute | solution.py:430
  51.2 19.0 %collective-permute-start.9 = (bf16[528,512]{1,0:T(8,128)(2,1)}, bf16[528,512]{1,0:T(8,128)(2,1)}, u32[]{:S(2)}, u32[]{:S(2)}) collective-permute-start(bf16[528,512]{1,0:T(8,128)(2,1)} %collective-permute-done.5.refs_1_), channel_id=1, source_target_pairs={{4,8},{5,9},{6,10},{7,11},{8,12},{9,13},{10,14},{11,15},{20,24},{2... | collective-permute-start | bytes 1622024 | tf_op jit(solution)/shard_map/ppermute | solution.py:425
  54.6 15.7 %collective-permute-start.11 = (bf16[128,2048]{1,0:T(8,128)(2,1)}, bf16[128,2048]{1,0:T(8,128)(2,1)S(1)}, u32[]{:S(2)}, u32[]{:S(2)}) collective-permute-start(bf16[128,2048]{1,0:T(8,128)(2,1)} %slice.58), channel_id=1, source_target_pairs={{0,2},{1,3},{2,0},{3,1},{4,6},{5,7},{6,4},{7,5},{8,10},{9,11},{10,... | collective-permute-start | bytes 1572872 | tf_op jit(solution)/shard_map/ppermute | solution.py:422
  55.1 15.1 %collective-permute-start.12 = (bf16[32,768]{1,0:T(8,128)(2,1)S(1)}, bf16[32,768]{1,0:T(8,128)(2,1)}, u32[]{:S(2)}, u32[]{:S(2)}) collective-permute-start(bf16[32,768]{1,0:T(8,128)(2,1)S(1)} %constant_dynamic-update-slice_fusion.refs_8_), channel_id=1, source_target_pairs={{0,2},{1,3},{2,0},{3,1},{4,6},{5,7},{6,4},{7,5},{8,10},{9,11},{10,... | collective-permute-start | bytes 147464 | tf_op jit(solution)/shard_map/ppermute | solution.py:422
  78.7 30.3 %all-to-all-start = ((bf16[16,48,512]{2,1,0:T(8,128)(2,1)}), bf16[16,48,512]{2,1,0:T(8,128)(2,1)S(1)}, u32[]{:S(2)}, u32[]{:S(2)}) async-start(bf16[16,48,512]{2,1,0:T(8,128)(2,1)} %get-tuple-element.138), calls=%async_computation | async-start | bytes 1572864 | tf_op jit(solution)/shard_map/all_to_all | solution.py:562
  86.1 2.0 %collective-permute-start.14 = (bf16[128,2048]{1,0:T(8,128)(2,1)S(1)}, bf16[128,2048]{1,0:T(8,128)(2,1)S(1)}, u32[]{:S(2)}, u32[]{:S(2)}) collective-permute-start(bf16[128,2048]{1,0:T(8,128)(2,1)S(1)} %collective-permute-done.11.refs_0_.refs_2_), channel_id=1, source_target_pairs={{0,1},{1,0},{2,3},{3,2},{4,5},{5,4},{6,7},{7,6},{8,9},{9,8},{10,11... | collective-permute-start | bytes 1572872 | tf_op jit(solution)/shard_map/ppermute | solution.py:422
  92.6 22.0 %copy-start.26 = (f32[12]{0:T(128)S(1)}, f32[12]{0:T(128)}, u32[]{:S(2)}) copy-start(f32[12]{0:T(128)} %param.21) | copy-start | bytes 148
  92.6 22.7 %copy-start.13 = (bf16[32,768]{1,0:T(8,128)(2,1)S(1)}, bf16[32,768]{1,0:T(8,128)(2,1)}, u32[]{:S(2)}) copy-start(bf16[32,768]{1,0:T(8,128)(2,1)} %copy-done.12) | copy-start | bytes 147460
  100.8 2.1 %collective-permute-start.15 = (f32[16,1536]{1,0:T(8,128)S(1)}, f32[16,1536]{1,0:T(8,128)S(1)}, u32[]{:S(2)}, u32[]{:S(2)}) collective-permute-start(f32[16,1536]{1,0:T(8,128)S(1)} %constant_dynamic-update-slice_fusion.2.refs_0_), channel_id=1, source_target_pairs={{0,1},{1,0},{2,3},{3,2},{4,5},{5,4},{6,7},{7,6},{8,9},{9,8},{10,11... | collective-permute-start | bytes 294920 | tf_op jit(solution)/shard_map/ppermute | solution.py:422
  101.2 6.0 %collective-permute-start.16 = (f32[16,1536]{1,0:T(8,128)S(1)}, f32[16,1536]{1,0:T(8,128)S(1)}, u32[]{:S(2)}, u32[]{:S(2)}) collective-permute-start(f32[16,1536]{1,0:T(8,128)S(1)} %constant_dynamic-update-slice_fusion.2.refs_0_), channel_id=1, source_target_pairs={{0,2},{1,3},{2,0},{3,1},{4,6},{5,7},{6,4},{7,5},{8,10},{9,11},{10,... | collective-permute-start | bytes 294920 | tf_op jit(solution)/shard_map/ppermute | solution.py:422
  102.9 6.1 %collective-permute-start.17 = (f32[16,1536]{1,0:T(8,128)S(1)}, f32[16,1536]{1,0:T(8,128)S(1)}, u32[]{:S(2)}, u32[]{:S(2)}) collective-permute-start(f32[16,1536]{1,0:T(8,128)S(1)} %constant_dynamic-update-slice_fusion.2.refs_0_), channel_id=1, source_target_pairs={{0,3},{1,2},{2,1},{3,0},{4,7},{5,6},{6,5},{7,4},{8,11},{9,10},{10,... | collective-permute-start | bytes 294920 | tf_op jit(solution)/shard_map/ppermute | solution.py:422
  109.0 36.5 %all-to-all-start.1 = ((bf16[16,48,512]{2,1,0:T(8,128)(2,1)}), bf16[16,48,512]{2,1,0:T(8,128)(2,1)S(1)}, u32[]{:S(2)}, u32[]{:S(2)}) async-start(bf16[16,48,512]{2,1,0:T(8,128)(2,1)} %get-tuple-element.150), calls=%async_computation.1 | async-start | bytes 1572864 | tf_op jit(solution)/shard_map/all_to_all | solution.py:562
  128.4 17.1 %collective-permute-start.18 = (bf16[544,512]{1,0:T(8,128)(2,1)}, bf16[544,512]{1,0:T(8,128)(2,1)S(1)}, u32[]{:S(2)}, u32[]{:S(2)}) collective-permute-start(bf16[544,512]{1,0:T(8,128)(2,1)} %get-tuple-element.149), channel_id=1, source_target_pairs={{0,4},{1,5},{2,6},{3,7},{4,8},{5,9},{6,10},{7,11},{16,20},{17,21},... | collective-permute-start | bytes 1671176 | tf_op jit(solution)/shard_map/ppermute | solution.py:425
  132.3 13.3 %collective-permute-start.19 = (bf16[544,512]{1,0:T(8,128)(2,1)}, bf16[544,512]{1,0:T(8,128)(2,1)S(1)}, u32[]{:S(2)}, u32[]{:S(2)}) collective-permute-start(bf16[544,512]{1,0:T(8,128)(2,1)} %get-tuple-element.149), channel_id=1, source_target_pairs={{8,4},{9,5},{10,6},{11,7},{12,8},{13,9},{14,10},{15,11},{24,20},{2... | collective-permute-start | bytes 1671176 | tf_op jit(solution)/shard_map/ppermute | solution.py:430
  133.0 37.1 %collective-permute-start.22 = (bf16[544,512]{1,0:T(8,128)(2,1)}, bf16[544,512]{1,0:T(8,128)(2,1)S(1)}, u32[]{:S(2)}, u32[]{:S(2)}) collective-permute-start(bf16[544,512]{1,0:T(8,128)(2,1)} %get-tuple-element.160), channel_id=1, source_target_pairs={{0,12},{1,13},{2,14},{3,15},{12,0},{13,1},{14,2},{15,3},{16,28},{1... | collective-permute-start | bytes 1671176 | tf_op jit(solution)/shard_map/ppermute | solution.py:437
  149.5 26.4 %collective-permute-start.20 = (bf16[544,512]{1,0:T(8,128)(2,1)}, bf16[544,512]{1,0:T(8,128)(2,1)S(1)}, u32[]{:S(2)}, u32[]{:S(2)}) collective-permute-start(bf16[544,512]{1,0:T(8,128)(2,1)} %get-tuple-element.158), channel_id=1, source_target_pairs={{0,4},{1,5},{2,6},{3,7},{4,8},{5,9},{6,10},{7,11},{8,12},{9,13},{1... | collective-permute-start | bytes 1671176 | tf_op jit(solution)/shard_map/ppermute | solution.py:425
  168.6 11.6 %collective-permute-start.21 = (bf16[544,512]{1,0:T(8,128)(2,1)}, bf16[544,512]{1,0:T(8,128)(2,1)S(1)}, u32[]{:S(2)}, u32[]{:S(2)}) collective-permute-start(bf16[544,512]{1,0:T(8,128)(2,1)} %get-tuple-element.159), channel_id=1, source_target_pairs={{4,0},{5,1},{6,2},{7,3},{8,4},{9,5},{10,6},{11,7},{12,8},{13,9},{1... | collective-permute-start | bytes 1671176 | tf_op jit(solution)/shard_map/ppermute | solution.py:430
  184.4 3.3 %collective-permute-start.23 = (bf16[160,512]{1,0:T(8,128)(2,1)}, bf16[160,512]{1,0:T(8,128)(2,1)S(1)}, u32[]{:S(2)}, u32[]{:S(2)}) collective-permute-start(bf16[160,512]{1,0:T(8,128)(2,1)} %get-tuple-element.162), channel_id=1, source_target_pairs={{0,1},{1,0},{2,3},{3,2},{4,5},{5,4},{6,7},{7,6},{8,9},{9,8},{10,11... | collective-permute-start | bytes 491528 | tf_op jit(solution)/shard_map/ppermute | solution.py:422
  184.4 7.2 %collective-permute-start.24 = (bf16[160,512]{1,0:T(8,128)(2,1)}, bf16[160,512]{1,0:T(8,128)(2,1)S(1)}, u32[]{:S(2)}, u32[]{:S(2)}) collective-permute-start(bf16[160,512]{1,0:T(8,128)(2,1)} %get-tuple-element.163), channel_id=1, source_target_pairs={{0,2},{1,3},{2,0},{3,1},{4,6},{5,7},{6,4},{7,5},{8,10},{9,11},{10,... | collective-permute-start | bytes 491528 | tf_op jit(solution)/shard_map/ppermute | solution.py:422
  185.9 8.5 %collective-permute-start.25 = (bf16[160,512]{1,0:T(8,128)(2,1)}, bf16[160,512]{1,0:T(8,128)(2,1)S(1)}, u32[]{:S(2)}, u32[]{:S(2)}) collective-permute-start(bf16[160,512]{1,0:T(8,128)(2,1)} %get-tuple-element.164), channel_id=1, source_target_pairs={{0,3},{1,2},{2,1},{3,0},{4,7},{5,6},{6,5},{7,4},{8,11},{9,10},{10,... | collective-permute-start | bytes 491528 | tf_op jit(solution)/shard_map/ppermute | solution.py:422
  (23 other events, 175.3 us)

commit v2 on v1

--- a/solution.py
+++ b/solution.py
@@ -15,14 +15,12 @@
 BF16 = jnp.bfloat16
 LANES = 128
 HALF = 16
-VMEM_BYTES = 56 * 1024 * 1024
+MIB = 1024 * 1024
 CHEAP = pl.CostEstimate(flops=1, bytes_accessed=1, transcendentals=0)
 
 
-def params():
-    return pltpu.CompilerParams(
-        vmem_limit_bytes=VMEM_BYTES, dimension_semantics=("arbitrary",)
-    )
+def params(mib=50):
+    return pltpu.CompilerParams(vmem_limit_bytes=mib * MIB, dimension_semantics=("arbitrary",))
 
 
 def split(x):
@@ -123,113 +121,107 @@
     block_ref[kr * len(pieces) :, :] = pair_ref[...]
 
 
-def norm_kernel(count, where_ref, *refs):
-    x_refs, xq_refs, gain_ref = refs[:count], refs[count : 2 * count], refs[2 * count]
-    normed_ref, turned_ref, xq_ref = refs[-3:]
-    if count == 1:
-        x, xq = x_refs[0][...], xq_refs[0][...]
+def norm_kernel(*refs):
+    x_refs, gain_ref, normed_ref, turned_ref = refs[:-3], refs[-3], refs[-2], refs[-1]
+
+    def one(x):
+        xf = x.astype(F32)
+        rms = lax.rsqrt(jnp.mean(xf * xf, -1, keepdims=True) + NORM_EPS)
+        normed = xf * rms * gain_ref[...]
+        normed_ref[...] = normed.astype(BF16)
+        turned_ref[...] = normed.T.astype(BF16)
+
+    if len(x_refs) == 1:
+        one(x_refs[0][...])
     else:
-        first = pl.program_id(0) == 0
-        x = jnp.where(first, x_refs[0][...], x_refs[1][...])
-        xq = jnp.where(first, xq_refs[0][...], xq_refs[1][...])
-    xf = x.astype(F32)
-    rms = lax.rsqrt(jnp.mean(xf * xf, -1, keepdims=True) + NORM_EPS)
-    normed = xf * rms * gain_ref[...]
-    normed_ref[...] = normed.astype(BF16)
-    turned_ref[...] = normed.T.astype(BF16)
-    xq_ref[...] = xq
-
-
-def norm_piece(where, xs, gain, start, apart, total, part, buffers):
+        for i, ref in enumerate(x_refs):
+            pl.when(pl.program_id(0) == i)(functools.partial(lambda ref: one(ref[...]), ref))
+
+
+def norm(xs, gain):
     rows, width = xs[0].shape
-    step = LANES
-    base = start // step
-    far = apart // step
-    if len(xs) == 1:
-        grid, source, target = rows // step, (lambda i: i), (lambda i: base + i)
-    else:
-        grid, source, target = len(xs), (lambda i: 0), (lambda i: base + i * far)
-    shapes = (
-        jax.ShapeDtypeStruct((total, width), BF16),
-        jax.ShapeDtypeStruct((width, total), BF16),
-        jax.ShapeDtypeStruct((total, part), BF16),
-    )
-    buffers = () if buffers is None else buffers
+    grid = rows // LANES if len(xs) == 1 else len(xs)
+    source = (lambda i: (i, 0)) if len(xs) == 1 else (lambda i: (0, 0))
     return pl.pallas_call(
-        functools.partial(norm_kernel, len(xs)),
-        out_shape=shapes,
-        grid_spec=pltpu.PrefetchScalarGridSpec(
-            num_scalar_prefetch=1,
-            grid=(grid,),
-            in_specs=[pl.BlockSpec((step, width), lambda i, w: (source(i), 0))] * len(xs)
-            + [pl.BlockSpec((step, part), lambda i, w: (source(i), w[0]))] * len(xs)
-            + [pl.BlockSpec((1, width), lambda i, w: (0, 0))]
-            + [pl.BlockSpec(memory_space=pl.ANY)] * len(buffers),
-            out_specs=[
-                pl.BlockSpec((step, width), lambda i, w: (target(i), 0)),
-                pl.BlockSpec((width, step), lambda i, w: (0, target(i))),
-                pl.BlockSpec((step, part), lambda i, w: (target(i), 0)),
-            ],
-        ),
-        input_output_aliases={2 * len(xs) + 2 + i: i for i in range(len(buffers))},
-        compiler_params=params(),
+        norm_kernel,
+        out_shape=(
+            jax.ShapeDtypeStruct((rows * len(xs), width), BF16),
+            jax.ShapeDtypeStruct((width, rows * len(xs)), BF16),
+        ),
+        grid=(grid,),
+        in_specs=[pl.BlockSpec((LANES, width), source)] * len(xs)
+        + [pl.BlockSpec((1, width), lambda i: (0, 0))],
+        out_specs=[
+            pl.BlockSpec((LANES, width), lambda i: (i, 0)),
+            pl.BlockSpec((width, LANES), lambda i: (0, i)),
+        ],
+        compiler_params=params(58),
         cost_estimate=CHEAP,
         name="norm",
-    )(where, *xs, *xs, gain, *buffers)
-
-
-def hidden_kernel(line, nact, packed, given, where_ref, *refs):
-    count = 1 if given else 2 * line - 2
+    )(*xs, gain)
+
+
+def hidden_kernel(line, nact, packed, given, layout, where_ref, *refs):
+    count = 1 if given else 2 * line - 3
     weights, refs = refs[:count], refs[count:]
-    normed_ref, xq_ref, row_ref, hw_ref, high_ref, sums_ref, send_ref = refs[:7]
-    w_ref = weights[0] if given else refs[7]
-    step = pl.program_id(0)
+    n_x = 1 + max(p[0] for pieces in layout for p in pieces)
+    n_normed = 1 + max(p[1] for pieces in layout for p in pieces)
+    xq_refs, refs = refs[:n_x], refs[n_x:]
+    normed_refs, refs = refs[:n_normed], refs[n_normed:]
+    row_ref, hw_ref, high_ref, sums_ref, send_ref = refs[:5]
+    w_ref = weights[0] if given else refs[5]
+    sorted_ref = refs[-1]
     z = where_ref[1]
-    rows = normed_ref.shape[0]
+    members = len(layout)
+    rows = high_ref.shape[0] // members
     slab = w_ref.shape[0] // line
 
-    def pick():
-        own, direct = weights[0], weights[-1]
-        fwd, bwd = weights[1 : line - 1] + (direct,), weights[line - 1 : -1] + (direct,)
+    if not given:
+        own, fwd, bwd = weights[0], weights[1 : line - 1], weights[line - 1 :]
         w_ref[pl.ds(pl.multiple_of(z * slab, slab), slab), :] = own[:slab, :]
         for j in range(1, line):
             place = pl.multiple_of(lax.rem(z - j + line, line) * slab, slab)
-            w_ref[pl.ds(place, slab), :] = jnp.where(
-                z >= j, fwd[j - 1][:slab, :], bwd[line - j - 1][:slab, :]
-            )
-
-    if not given:
-        pl.when(step == 0)(pick)
-
-    hidden = xq_ref[...].astype(F32) + dot(normed_ref[...], w_ref[...])
-    high, low = split(hidden)
-    high_ref[...] = high
-    heads = dot(high, hw_ref[...]) + dot(low, hw_ref[...])
-    lane = lax.broadcasted_iota(jnp.int32, heads.shape, 1)
-    square = jnp.sum(hidden * hidden, 1, keepdims=True)
-    sums = jnp.where(lane == nact + 1, square, heads).T[:HALF]
-    if not given:
-        pair = jnp.zeros((HALF, LANES), F32)
-        for ref in weights:
-            pair = pair + ref[slab:, :LANES].astype(F32)
-        pair = jnp.concatenate([pair[:1], jnp.zeros((1, rows - LANES), F32)], 1)
-        row = lax.broadcasted_iota(jnp.int32, sums.shape, 0)
-        sums = jnp.where(row == nact + 2, pair, sums)
-    sums_ref[...] = sums
-    slot = row_ref[HALF + nact : HALF + nact + 1, :].astype(F32) * 256.0
-    slot = (slot + row_ref[HALF + nact + 1 : HALF + nact + 2, :].astype(F32)).astype(jnp.int32)
-    order = jnp.where(lax.broadcasted_iota(jnp.int32, (rows, rows), 0) == slot, 1.0, 0.0).astype(BF16)
-    ranked = dot(order, high)
-    if not packed:
-        send_ref[...] = ranked.astype(BF16)
-        return
-    sorted_ref = refs[-1]
-    sorted_ref[pl.ds(pl.multiple_of(step * rows, rows), rows), :] = ranked
-
-    @pl.when(step == sorted_ref.shape[0] // rows - 1)
-    def _():
+            if j == 1:
+                block = fwd[0][:slab, :]
+            elif j == line - 1:
+                block = bwd[0][:slab, :]
+            else:
+                block = jnp.where(z >= j, fwd[j - 1][:slab, :], bwd[line - j - 1][:slab, :])
+            w_ref[pl.ds(place, slab), :] = block
+
+    for m, pieces in enumerate(layout):
+        at = m * rows
+        for x, normed, first, size in pieces:
+            piece = dot(normed_refs[normed][first : first + size, :], w_ref[...])
+            sorted_ref[at : at + size, :] = piece + xq_refs[x][...].astype(F32)
+            at += size
+        here = slice(m * rows, (m + 1) * rows)
+        hidden = sorted_ref[here, :]
+        high, low = split(hidden)
+        high_ref[here, :] = high
+        heads = dot(high, hw_ref[...]) + dot(low, hw_ref[...])
+        lane = lax.broadcasted_iota(jnp.int32, heads.shape, 1)
+        square = jnp.sum(hidden * hidden, 1, keepdims=True)
+        sums = jnp.where(lane == nact + 1, square, heads).T[:HALF]
+        if not given:
+            pair = jnp.zeros((HALF, LANES), F32)
+            for ref in weights:
+                pair = pair + ref[slab:, :LANES].astype(F32)
+            pair = jnp.concatenate([pair[:1], jnp.zeros((1, rows - LANES), F32)], 1)
+            row = lax.broadcasted_iota(jnp.int32, sums.shape, 0)
+            sums = jnp.where(row == nact + 2, pair, sums)
+        sums_ref[:, here] = sums
+        slot = row_ref[HALF + nact : HALF + nact + 1, here].astype(F32) * 256.0
+        slot = slot + row_ref[HALF + nact + 1 : HALF + nact + 2, here].astype(F32)
+        slot = slot.astype(jnp.int32)
+        order = lax.broadcasted_iota(jnp.int32, (rows, rows), 0) == slot
+        ranked = dot(jnp.where(order, 1.0, 0.0).astype(BF16), high)
+        if packed:
+            sorted_ref[here, :] = ranked
+        else:
+            send_ref[here, :] = ranked.astype(BF16)
+    if packed:
         n, size, _ = send_ref.shape
-        members = sorted_ref.shape[0] // rows
         peer = size // members
         for j in range(n):
             send_ref[j] = jnp.concatenate(
@@ -238,16 +230,15 @@
             ).astype(BF16)
 
 
-def rest_kernel(line, team, nact, width, total_rows, where_ref, *refs):
+def rest_kernel(line, team, nact, width, total_rows, places, where_ref, *refs):
     sums, refs = refs[:team], refs[team:]
     row_ref, isd_ref, *high_refs = refs[:4]
-    hw_ref, turned_ref = refs[4:6]
-    grads = refs[6 : 6 + line]
-    firsts, (direct_ref, head_ref, ghid_ref) = refs[6 + line : -3], refs[-3:]
-    z = where_ref[1]
+    hw_ref, *turned_refs = refs[4:10]
+    grad_ref = refs[10]
+    firsts, (head_ref, ghid_ref) = refs[11:-2], refs[-2:]
     step = pl.program_id(0)
     scale = total_rows**-0.5
-    slab, part = grads[0].shape
+    slab, part = grad_ref.shape
 
     @pl.when(step == 0)
     def _():
@@ -302,31 +293,25 @@
                 0,
             ).T
             ghn = dot(jnp.concatenate(split(turned), 1), hw_ref[...])
-            ghid_ref[here, :] = (
-                ghn - high.astype(F32) * turned[:, HALF : HALF + 1]
-            ).astype(BF16)
+            ghid = (ghn - high.astype(F32) * turned[:, HALF : HALF + 1]).astype(BF16)
+            for first, size, place in places[r]:
+                ghid_ref[place : place + size, :] = ghid[first : first + size]
         row = lax.broadcasted_iota(jnp.int32, (HALF, part), 0)
         lane = lax.broadcasted_iota(jnp.int32, (HALF, part), 1)
         std = jnp.where(row == lane, jnp.sum(std, 1, keepdims=True), 0.0)
         std = jnp.sum(std, 0, keepdims=True)
         head = jnp.where(row == nact + 1, std, head)
         head_ref[...] = head
-        for ref in (*firsts, direct_ref):
+        for ref in firsts:
             ref[slab:, :] = jnp.concatenate(split(head), 0)
 
-    grad = dot(turned_ref[...], ghid_ref[...])
-    for k in range(line):
-
-        @pl.when(step == k)
-        def _(k=k):
-            grads[k][...] = grad
-            for ref, index in zip(firsts, first_blocks(line)):
-                if k == index:
-                    ref[:slab, :] = grad.astype(BF16)
-
-    @pl.when(step == jnp.where(z == 0, line - 1, 1))
-    def _():
-        direct_ref[:slab, :] = grad.astype(BF16)
+    grad = dot(jnp.concatenate([ref[...] for ref in turned_refs], 1), ghid_ref[...])
+    grad_ref[...] = grad
+    for ref, index in zip(firsts, first_blocks(line)):
+
+        @pl.when(step == index)
+        def _(ref=ref):
+            ref[:slab, :] = grad.astype(BF16)
 
 
 def first_blocks(line):
@@ -346,7 +331,7 @@
 
 
 def final_kernel(where_ref, mine_ref, head_ref, *refs):
-    got, pieces = refs[:3], refs[3:]
+    got, pieces = refs[:2], refs[2:]
     q = where_ref[0]
     slab = mine_ref.shape[0]
     kr = slab // len(pieces)
@@ -421,20 +406,13 @@
     def mate(x, r):
         return lax.ppermute(x, "fsdp", [(i, i ^ r) for i in range(n)]) if r else x
 
-    def up(x, low, high):
-        return lax.ppermute(
-            x, "fsdp", [(a * team + b, (a + 1) * team + b) for a in range(low, high) for b in range(team)]
-        )
-
-    def down(x, low, high):
-        return lax.ppermute(
-            x, "fsdp", [(a * team + b, (a - 1) * team + b) for a in range(low, high) for b in range(team)]
-        )
-
-    def ends(x):
-        far = n - team
-        pairs = [(b, far + b) for b in range(team)] + [(far + b, b) for b in range(team)]
-        return lax.ppermute(x, "fsdp", pairs)
+    def up(x, low, high, wrap=False):
+        steps = [(a, a + 1) for a in range(low, high)] + ([(line - 1, 0)] if wrap else [])
+        return lax.ppermute(x, "fsdp", [(a * team + i, b * team + i) for a, b in steps for i in range(team)])
+
+    def down(x, low, high, wrap=False):
+        steps = [(a, a - 1) for a in range(low, high)] + ([(0, line - 1)] if wrap else [])
+        return lax.ppermute(x, "fsdp", [(a * team + i, b * team + i) for a, b in steps for i in range(team)])
 
     pieces = [
         mate(lax.dynamic_slice(out_weight, (0, (q ^ r) * part), (kr, part)), r) for r in range(team)
@@ -457,16 +435,27 @@
         ],
         out_specs=[plain((2 * HALF, rows)), plain((HALF, part))],
         scratch_shapes=[pltpu.VMEM((reward.shape[0], LANES), F32), pltpu.VMEM((HALF, rows), F32)],
-        compiler_params=params(),
+        compiler_params=params(60),
         cost_estimate=CHEAP,
         name="small",
     )(reward, value_old, done, old_mean.T, noise.T, minibatch_perm[None, :])
-    obs_late, x_core, small, pair, pieces = lax.optimization_barrier(
-        (obs_feat, x_core, small, pair, pieces)
+    cut = rows - LANES
+    obs_first = obs_feat[:cut]
+    x_core, small, pair, pieces, where, obs_first, obs_late, head_weight, log_std = (
+        lax.optimization_barrier(
+            (x_core, small, pair, pieces, where, obs_first, obs_feat, head_weight, log_std)
+        )
     )
+    obs_last = obs_late[cut:]
+
+    hw = lax.dynamic_slice(head_weight, (q * part, 0), (part, heads_n)).T
+    hw_twice = jnp.pad(hw, ((0, LANES - heads_n), (0, 0)))
+    hw_wide = hw_twice.T
+    hw_twice = jnp.concatenate([hw_twice, hw_twice], 0)
+    isd = jnp.pad(jnp.exp(-log_std), (0, HALF - nact))
+    isd = jnp.broadcast_to(isd[:, None], (HALF, LANES))
 
     gain = gain_in[None, :]
-    cut = rows // 3 * 2 if rows % 3 == 0 and rows // 3 % LANES == 0 else rows
     block = pl.pallas_call(
         join_kernel,
         out_shape=jax.ShapeDtypeStruct((slab + HALF, part), BF16),
@@ -481,18 +470,15 @@
         name="join",
     )(where, *pieces, pair)
 
-    def norm(xs, start, apart=0):
-        return norm_piece(where, xs, gain, start, apart, team_rows, part, buffers)
-
-    direct = ends(block)
-    fs, bs = [up(block, 0, line - 1)], [down(block, 1, line)]
-    far = mate(obs_late[:cut], 2)
+    fs, bs = [up(block, 0, line - 1, True)], [down(block, 1, line, True)]
+    far = mate(obs_first, 2)
     small_core = mate(small, 1)
-    buffers = None
-    buffers = norm([obs_late], 0)
-    buffers = norm([x_core], rows)
-    direct, fs, bs, far, small, small_core, buffers, obs_late = lax.optimization_barrier(
-        (direct, fs, bs, far, small, small_core, buffers, obs_late)
+    obs_late, small_core = lax.optimization_barrier((obs_late, small_core))
+    normed_own, normed_core = norm([obs_late], gain), norm([x_core], gain)
+    (fs, bs, far, small, small_core, normed_own, normed_core, obs_last, hw_wide, hw_twice, isd) = (
+        lax.optimization_barrier(
+            (fs, bs, far, small, small_core, normed_own, normed_core, obs_last, hw_wide, hw_twice, isd)
+        )
     )
     small = jnp.concatenate([small, small_core], 1)
     small_far = mate(small, 2)
@@ -500,30 +486,22 @@
         fs.append(up(fs[-1], j - 1, line - 1))
         bs.append(down(bs[-1], 1, line - j + 1))
     diag = mate(far, 1)
-    late = mate(obs_late[cut:], 2) if cut < rows else far
-    buffers = norm([far], 2 * rows)
-    buffers = norm([diag], 3 * rows)
-    fs, bs, late, small, small_far, buffers = lax.optimization_barrier(
-        (fs, bs, late, small, small_far, buffers)
+    late = mate(obs_last, 2)
+    normed_far, normed_diag = norm([far], gain), norm([diag], gain)
+    fs, bs, late, small, small_far, normed_far, normed_diag = lax.optimization_barrier(
+        (fs, bs, late, small, small_far, normed_far, normed_diag)
     )
-    weights = [block] + fs + bs + [direct]
-
-    hw = lax.dynamic_slice(head_weight, (q * part, 0), (part, heads_n)).T
-    hw_twice = jnp.pad(hw, ((0, LANES - heads_n), (0, 0)))
-    hw_wide = hw_twice.T
-    hw_twice = jnp.concatenate([hw_twice, hw_twice], 0)
-    isd = jnp.pad(jnp.exp(-log_std), (0, HALF - nact))
-    isd = jnp.broadcast_to(isd[:, None], (HALF, LANES))
+    weights = [block] + fs + bs
 
     packed = per_peer % 8 == 0 and team // 2 * per_peer % 16 == 0
     some = team // 2
     some_rows = some * rows
 
-    def hidden(weights, first, rowdata):
+    def hidden(weights, xs, normed, layout, rowdata):
         given = len(weights) == 1
         send_shape = (n, some * per_peer, part) if packed else (some_rows, part)
         out = pl.pallas_call(
-            functools.partial(hidden_kernel, line, nact, packed, given),
+            functools.partial(hidden_kernel, line, nact, packed, given, layout),
             out_shape=[
                 jax.ShapeDtypeStruct((some_rows, part), BF16),
                 jax.ShapeDtypeStruct((HALF, some_rows), F32),
@@ -532,26 +510,19 @@
             + ([] if given else [jax.ShapeDtypeStruct((width, part), BF16)]),
             grid_spec=pltpu.PrefetchScalarGridSpec(
                 num_scalar_prefetch=1,
-                grid=(some,),
+                grid=(1,),
                 in_specs=[whole(weight.shape) for weight in weights]
-                + [
-                    pl.BlockSpec((rows, width), lambda i, w: (first + i, 0)),
-                    pl.BlockSpec((rows, part), lambda i, w: (first + i, 0)),
-                    pl.BlockSpec((2 * HALF, rows), lambda i, w: (0, i)),
-                    whole((part, LANES)),
-                ],
-                out_specs=[
-                    pl.BlockSpec((rows, part), lambda i, w: (i, 0)),
-                    pl.BlockSpec((HALF, rows), lambda i, w: (0, i)),
-                    whole(send_shape) if packed else pl.BlockSpec((rows, part), lambda i, w: (i, 0)),
-                ]
+                + [pl.BlockSpec((x.shape[0], part), lambda i, w: (0, w[0])) for x in xs]
+                + [whole(x.shape) for x in normed]
+                + [whole((2 * HALF, some_rows)), whole((part, LANES))],
+                out_specs=[whole((some_rows, part)), whole((HALF, some_rows)), whole(send_shape)]
                 + ([] if given else [whole((width, part))]),
-                scratch_shapes=[pltpu.VMEM((some_rows, part), F32)] if packed else [],
+                scratch_shapes=[pltpu.VMEM((some_rows, part), F32)],
             ),
-            compiler_params=params(),
+            compiler_params=params(58),
             cost_estimate=CHEAP,
             name="hidden",
-        )(where, *weights, normed, xq, rowdata, hw_wide)
+        )(where, *weights, *xs, *normed, rowdata, hw_wide)
         if not packed:
             high, sums, send, *weight = out
             send = send.reshape(some, n, per_peer, part).transpose(1, 0, 2, 3)
@@ -561,26 +532,36 @@
     def scatter(send):
         return lax.all_to_all(send, "fsdp", split_axis=0, concat_axis=0, tiled=True)
 
-    normed, turned, xq = buffers
-    high_near, sums_near, send, weight = hidden(weights, 0, small)
+    small_all = jnp.concatenate([small, small_far], 1)
+    layout = [[(0, 0, 0, rows)], [(1, 1, 0, rows)]]
+    high_near, sums_near, send, weight = hidden(
+        weights, [obs_feat, x_core], [normed_own[0], normed_core[0]], layout, small
+    )
     recv_near = scatter(send)
-    if cut < rows:
-        last = mate(late, 1)
-        late, last, sums_near, buffers = lax.optimization_barrier((late, last, sums_near, buffers))
-        buffers = norm([late, last], 2 * rows + cut, rows)
-        normed, turned, xq = buffers
-    high_far, sums_far, send, *_ = hidden([weight], some, small_far)
+    last = mate(late, 1)
+    late, last, sums_near, small_all = lax.optimization_barrier((late, last, sums_near, small_all))
+    normed_last = norm([late, last], gain)
+    layout = [[(0, 0, 0, cut), (2, 2, 0, LANES)], [(1, 1, 0, cut), (3, 2, LANES, LANES)]]
+    high_far, sums_far, send, *_ = hidden(
+        [weight],
+        [far, diag, late, last],
+        [normed_far[0], normed_diag[0], normed_last[0]],
+        layout,
+        small_far,
+    )
     sums = jnp.concatenate([sums_near, sums_far], 1)
     sums = [mate(sums, r) for r in range(team)]
     send, recv_near, *sums = lax.optimization_barrier((send, recv_near, *sums))
     recv_far = scatter(send)
-    small = jnp.concatenate([small, small_far], 1)
-
     nfirst = len(first_blocks(line))
+    turned = [pair[1] for pair in (normed_own, normed_core, normed_far, normed_diag, normed_last)]
+    places = [[(0, rows, 0)], [(0, rows, rows)]] + [
+        [(0, cut, 2 * rows + i * cut), (cut, LANES, 2 * rows + 2 * cut + i * LANES)] for i in range(2)
+    ]
     outs = pl.pallas_call(
-        functools.partial(rest_kernel, line, team, nact, width, total_rows),
-        out_shape=[jax.ShapeDtypeStruct((slab, part), F32)] * line
-        + [jax.ShapeDtypeStruct((slab + 2 * HALF, part), BF16)] * (nfirst + 1)
+        functools.partial(rest_kernel, line, team, nact, width, total_rows, places),
+        out_shape=[jax.ShapeDtypeStruct((width, part), F32)]
+        + [jax.ShapeDtypeStruct((slab + 2 * HALF, part), BF16)] * nfirst
         + [jax.ShapeDtypeStruct((HALF, part), F32)],
         grid_spec=pltpu.PrefetchScalarGridSpec(
             num_scalar_prefetch=1,
@@ -592,40 +573,47 @@
                 whole((some_rows, part)),
                 whole((some_rows, part)),
                 whole((2 * LANES, part)),
-                pl.BlockSpec((slab, team_rows), lambda i, w: (lax.rem(w[1] + i, line), 0)),
+            ]
+            + [
+                pl.BlockSpec((slab, piece.shape[1]), lambda i, w: (lax.rem(w[1] + i, line), 0))
+                for piece in turned
             ],
-            out_specs=[whole((slab, part))] * line
-            + [whole((slab + 2 * HALF, part))] * (nfirst + 1)
+            out_specs=[pl.BlockSpec((slab, part), lambda i, w: (i, 0))]
+            + [whole((slab + 2 * HALF, part))] * nfirst
             + [whole((HALF, part))],
             scratch_shapes=[pltpu.VMEM((team_rows, part), BF16)],
         ),
-        compiler_params=params(),
+        compiler_params=params(58),
         cost_estimate=CHEAP,
         name="rest",
-    )(where, *sums, small, isd, high_near, high_far, hw_twice, turned)
-    grads, firsts, direct, head = outs[:line], outs[line:-2], outs[-2], outs[-1]
-
-    def hop(*operands):
+    )(where, *sums, small_all, isd, high_near, high_far, hw_twice, *turned)
+    grads, firsts, head = outs[0], outs[1:-1], outs[-1]
+
+    def hop(up_block, down_block, *got):
         return pl.pallas_call(
             hop_kernel,
             out_shape=[jax.ShapeDtypeStruct((slab + 2 * HALF, part), BF16)] * 2,
             grid=(1,),
-            in_specs=[plain((HALF, part))] + [plain((slab, part))] * 2 + [plain((slab + 2 * HALF, part))] * 2,
+            in_specs=[
+                plain((HALF, part)),
+                pl.BlockSpec((slab, part), lambda i: (up_block, 0)),
+                pl.BlockSpec((slab, part), lambda i: (down_block, 0)),
+            ]
+            + [plain((slab + 2 * HALF, part))] * 2,
             out_specs=[plain((slab + 2 * HALF, part))] * 2,
             compiler_params=params(),
             cost_estimate=CHEAP,
             name="hop",
-        )(head, *operands)
-
-    direct = ends(direct)
+        )(head, grads, grads, *got)
+
     send_f, send_b = firsts[-1], firsts[0]
     for k in range(line - 2, 0, -1):
-        got_f = up(send_f, 0, line - k)
-        got_b = down(send_b, k, line)
+        got_f = up(send_f, 0, line - k, k == 1)
+        got_b = down(send_b, k, line, k == 1)
         if k == 2:
             got_f, got_b, recv_far = lax.optimization_barrier((got_f, got_b, recv_far))
         if k > 1:
-            send_f, send_b = hop(grads[k - 1], grads[line - k + 1], got_f, got_b)
+            send_f, send_b = hop(k - 1, line - k + 1, got_f, got_b)
     pieces = pl.pallas_call(
         final_kernel,
         out_shape=[jax.ShapeDtypeStruct((kr + HALF, part), F32)]
@@ -634,13 +622,13 @@
             num_scalar_prefetch=1,
             grid=(1,),
             in_specs=[whole((slab, part)), whole((HALF, part))]
-            + [whole((slab + 2 * HALF, part))] * 3,
+            + [whole((slab + 2 * HALF, part))] * 2,
             out_specs=[whole((kr + HALF, part))] + [whole((kr + 2 * HALF, part))] * (team - 1),
         ),
         compiler_params=params(),
         cost_estimate=CHEAP,
         name="final",
-    )(where, grads[0], head, got_f, got_b, direct)
+    )(where, grads, head, got_f, got_b)
     pieces = [mate(piece, r) for r, piece in enumerate(pieces)]
     grad_weight, heads, std = pl.pallas_call(
         assemble_kernel,

time: 200 us -> 178 us (0.89)
  starting transfers between devices: 66 us -> 39.9 us
  waiting for transfers between devices: 50.8 us -> 69.4 us
  Pallas kernels: 61.4 us -> 49.6 us
  local copies, waits for them, and re-layouts: 16.9 us -> 14.5 us
    ppermute x10 -> x8, starting transfers between devices: 41.4 us -> 16.4 us  [the longest x4 10.8 us: up(): lax.ppermute(x, 'fsdp', [(a * team + i, b * team + i) for a, b in steps f...]
    ppermute x10 -> x8, waiting for transfers between devices: 29.1 us -> 49 us  [the longest x4 36.2 us: up(): lax.ppermute(x, 'fsdp', [(a * team + i, b * team + i) for a, b in steps f...]
    pallas_call x5, Pallas kernels: 20.6 us -> 16.6 us  [norm(): pl.pallas_call(norm_kernel, out_shape=(jax.ShapeDtypeStruct((rows * len(x...]
    pallas_call x1, Pallas kernels: 2.6 us -> 0.58 us  [local(): pl.pallas_call(join_kernel, out_shape=jax.ShapeDtypeStruct((slab + HALF,...]
    unnamed x56 -> x44, local copies, waits for them, and re-layouts: 4.29 us -> 3.71 us
  transfers between devices with their start and end apart: 28 -> 26, of which waited for: 13 -> 13; matrix products, arithmetic and copies ran while one was open for 6% -> 7% of each run, Pallas kernels for 23% -> 21%
where the time goes in v2:
time: 178 us; the launch traced here: 177 us
  waiting for transfers between devices  69.4 us (39%)
  Pallas kernels  49.6 us (28%)
  starting transfers between devices  39.9 us (22%)
  local copies, waits for them, and re-layouts  14.5 us (8%)
  other arithmetic  2.42 us (1%)
    ppermute x4, waiting for transfers between devices, up(): lax.ppermute(x, 'fsdp', [(a * team + i, b * team + i) for a, b in steps f...  36.2 us
    ppermute x16, waiting for transfers between devices, mate(): return lax.ppermute(x, 'fsdp', [(i, i ^ r) for i in range(n)]) if r else x  20.4 us
    pallas_call x5, Pallas kernels, norm(): pl.pallas_call(norm_kernel, out_shape=(jax.ShapeDtypeStruct((rows * len(x...  16.6 us
    pallas_call x2, Pallas kernels, hidden(): pl.pallas_call(functools.partial(hidden_kernel, line, nact, packed, given...  14.8 us
    ppermute x4, waiting for transfers between devices, down(): lax.ppermute(x, 'fsdp', [(a * team + i, b * team + i) for a, b in steps f...  12.8 us
    ppermute x16, starting transfers between devices, mate(): return lax.ppermute(x, 'fsdp', [(i, i ^ r) for i in range(n)]) if r else x  11.9 us
    all_to_all x2, starting transfers between devices, scatter(): return lax.all_to_all(send, 'fsdp', split_axis=0, concat_axis=0, tiled=True)  11.5 us
    ppermute x4, starting transfers between devices, up(): lax.ppermute(x, 'fsdp', [(a * team + i, b * team + i) for a, b in steps f...  10.8 us
  transfers between devices with their start and end apart: 26, of which 13 were waited for; matrix products, arithmetic and copies ran while one was open for 7% of the time, Pallas kernels for 21%

profile of v2, /device:TPU:0, one launch (start us, length us, event | category | flops | bytes accessed | tf_op | source)
XLA Modules:
  0.0 176.7 jit_solution(17761808388656464458)
XLA Ops:
  2.3 2.7 %collective-permute-start.3 = (bf16[128,512]{1,0:T(8,128)(2,1)S(1)}, bf16[128,512]{1,0:T(8,128)(2,1)S(1)}, u32[]{:S(2)}, u32[]{:S(2)}) collective-permute-start(bf16[128,512]{1,0:T(8,128)(2,1)S(1)} %get-tuple-element.184), channel_id=1, source_target_pairs={{0,3},{1,2},{2,1},{3,0},{4,7},{5,6},{6,5},{7,4},{8,11},{9,10},{10,... | collective-permute-start | bytes 393224 | tf_op jit(solution)/shard_map/ppermute | solution.py:407
  6.7 2.1 %small.1 = (bf16[32,384]{1,0:T(8,128)(2,1)}, bf16[16,512]{1,0:T(8,128)(2,1)}) custom-call(f32[16,24]{1,0:T(8,128)} %reward_ref.1, f32[16,25]{1,0:T(8,128)} %value_ref.1, s32[16,24]{1,0:T(8,128)} %done_ref.1, bf16[12,384]{1,0:T(8,128)(2,1)} %bitcast.85, bf16[12,384]{1,0:T(8,128)(2,1)} %bitcast.86, s32[1,384]{1,0:T(1,128)} %broadcast_in_dim.12.perm_ref), custom_call_target="tpu_custom_call" | custom-call | flops 1 | bytes 1 | tf_op jit(solution)/shard_map/small/pallas_call | solution.py:421
  8.8 2.3 %slice.57 = bf16[256,2048]{1,0:T(8,128)(2,1)} slice(bf16[384,2048]{1,0:T(8,128)(2,1)} %refs_5_.1), slice={[0:256], [0:2048]} | slice | bytes 2097152 | tf_op jit(solution)/shard_map/slice | solution.py:443
  11.9 1.7 collective-permute-start.6
  14.9 3.7 %collective-permute-start.5 = (bf16[528,512]{1,0:T(8,128)(2,1)S(1)}, bf16[528,512]{1,0:T(8,128)(2,1)}, u32[]{:S(2)}, u32[]{:S(2)}) collective-permute-start(bf16[528,512]{1,0:T(8,128)(2,1)S(1)} %join.1.refs_0_), channel_id=1, source_target_pairs={{4,0},{5,1},{6,2},{7,3},{8,4},{9,5},{10,6},{11,7},{12,8},{13,9},{1... | collective-permute-start | bytes 1622024 | tf_op jit(solution)/shard_map/ppermute | solution.py:415
  19.4 4.1 %norm.6 = (bf16[384,2048]{1,0:T(8,128)(2,1)}, bf16[2048,384]{1,0:T(8,128)(2,1)}) custom-call(bf16[384,2048]{1,0:T(8,128)(2,1)} %copy-done.7, f32[1,2048]{1,0:T(1,128)} %bitcast.80), custom_call_target="tpu_custom_call" | custom-call | flops 1 | bytes 1 | tf_op jit(solution)/shard_map/norm/pallas_call | solution.py:145
  23.4 1.9 %slice.58 = bf16[128,2048]{1,0:T(8,128)(2,1)} slice(bf16[384,2048]{1,0:T(8,128)(2,1)} %refs_5_.1), slice={[256:384], [0:2048]} | slice | bytes 1048576 | tf_op jit(solution)/shard_map/slice | solution.py:449
  25.3 4.1 %norm.5 = (bf16[384,2048]{1,0:T(8,128)(2,1)}, bf16[2048,384]{1,0:T(8,128)(2,1)}) custom-call(bf16[384,2048]{1,0:T(8,128)(2,1)} %refs_5_.1, f32[1,2048]{1,0:T(1,128)} %bitcast.81), custom_call_target="tpu_custom_call" | custom-call | flops 1 | bytes 1 | tf_op jit(solution)/shard_map/norm/pallas_call | solution.py:145
  29.5 1.8 %collective-permute-done.5.refs_3_ = bf16[528,512]{1,0:T(8,128)(2,1)} collective-permute-done((bf16[528,512]{1,0:T(8,128)(2,1)S(1)}, bf16[528,512]{1,0:T(8,128)(2,1)}, u32[]{:S(2)}, u32[]{:S(2)}) %collective-permute-start.5) | collective-permute-done | bytes 540704 | tf_op jit(solution)/shard_map/ppermute | solution.py:415
  31.3 10.8 %collective-permute-done.4.refs_1_ = bf16[528,512]{1,0:T(8,128)(2,1)} collective-permute-done((bf16[528,512]{1,0:T(8,128)(2,1)S(1)}, bf16[528,512]{1,0:T(8,128)(2,1)}, u32[]{:S(2)}, u32[]{:S(2)}) %collective-permute-start.4) | collective-permute-done | bytes 540704 | tf_op jit(solution)/shard_map/ppermute | solution.py:411
  46.9 2.7 %norm.7 = (bf16[256,2048]{1,0:T(8,128)(2,1)}, bf16[2048,256]{1,0:T(8,128)(2,1)}) custom-call(bf16[256,2048]{1,0:T(8,128)(2,1)} %collective-permute-done.6.refs_0_.refs_1_, f32[1,2048]{1,0:T(1,128)} %bitcast.82), custom_call_target="tpu_custom_call" | custom-call | flops 1 | bytes 1 | tf_op jit(solution)/shard_map/norm/pallas_call | solution.py:145
  51.4 2.7 %norm.8 = (bf16[256,2048]{1,0:T(8,128)(2,1)}, bf16[2048,256]{1,0:T(8,128)(2,1)}) custom-call(bf16[256,2048]{1,0:T(8,128)(2,1)} %copy-done.8, f32[1,2048]{1,0:T(1,128)} %bitcast.83), custom_call_target="tpu_custom_call" | custom-call | flops 1 | bytes 1 | tf_op jit(solution)/shard_map/norm/pallas_call | solution.py:145
  54.1 6.4 %collective-permute-done.11.refs_8_ = bf16[32,768]{1,0:T(8,128)(2,1)S(1)} collective-permute-done((bf16[32,768]{1,0:T(8,128)(2,1)S(1)}, bf16[32,768]{1,0:T(8,128)(2,1)S(1)}, u32[]{:S(2)}, u32[]{:S(2)}) %collective-permute-start.11) | collective-permute-done | bytes 49184 | tf_op jit(solution)/shard_map/ppermute | solution.py:407
  61.3 7.6 %hidden.2 = (bf16[768,512]{1,0:T(8,128)(2,1)}, f32[16,768]{1,0:T(8,128)}, bf16[16,48,512]{2,1,0:T(8,128)(2,1)}, bf16[2048,512]{1,0:T(8,128)(2,1)}) custom-call(s32[2]{0:T(128)} %copy-done.4, bf16[528,512]{1,0:T(8,128)(2,1)} %copy-done.1, bf16[528,512]{1,0:T(8,128)(2,1)} %collective-permute-done.4.refs_1_, bf16[528,512]{1,0:T(8,128)(2,1)} %copy-done.11, ...), custom_call_target="tpu_custom_call" | custom-call | flops 1 | bytes 1 | tf_op jit(solution)/shard_map/hidden/pallas_call | solution.py:503
  68.9 6.2 %all-to-all-start = ((bf16[16,48,512]{2,1,0:T(8,128)(2,1)}), bf16[16,48,512]{2,1,0:T(8,128)(2,1)S(1)}, u32[]{:S(2)}, u32[]{:S(2)}) async-start(bf16[16,48,512]{2,1,0:T(8,128)(2,1)} %get-tuple-element.134), calls=%async_computation | async-start | bytes 1572864 | tf_op jit(solution)/shard_map/all_to_all | solution.py:533
  77.9 3.0 %norm.9 = (bf16[256,2048]{1,0:T(8,128)(2,1)}, bf16[2048,256]{1,0:T(8,128)(2,1)}) custom-call(bf16[128,2048]{1,0:T(8,128)(2,1)} %copy-done.9, bf16[128,2048]{1,0:T(8,128)(2,1)} %copy-done.10, f32[1,2048]{1,0:T(1,128)} %bitcast.84), custom_call_target="tpu_custom_call" | custom-call | flops 1 | bytes 1 | tf_op jit(solution)/shard_map/norm/pallas_call | solution.py:145
  80.9 7.2 %hidden.3 = (bf16[768,512]{1,0:T(8,128)(2,1)}, f32[16,768]{1,0:T(8,128)}, bf16[16,48,512]{2,1,0:T(8,128)(2,1)}) custom-call(s32[2]{0:T(128)} %copy-done.4, bf16[2048,512]{1,0:T(8,128)(2,1)} %get-tuple-element.124.refs_0_, bf16[256,2048]{1,0:T(8,128)(2,1)} %collective-permute-done.6.refs_0_.refs_1_, bf16[256,2048]{1,0:T(8,128)(2,1)} %copy-done.8, ...), custom_call_target="tpu_custom_call" | custom-call | flops 1 | bytes 1 | tf_op jit(solution)/shard_map/hidden/pallas_call | solution.py:503
  89.0 1.6 collective-permute-start.16
  91.0 4.6 %collective-permute-done.16.refs_3_ = f32[16,1536]{1,0:T(8,128)S(1)} collective-permute-done((f32[16,1536]{1,0:T(8,128)S(1)}, f32[16,1536]{1,0:T(8,128)S(1)}, u32[]{:S(2)}, u32[]{:S(2)}) %collective-permute-start.16) | collective-permute-done | bytes 98336 | tf_op jit(solution)/shard_map/ppermute | solution.py:407
  95.6 2.3 %collective-permute-done.15.refs_2_ = f32[16,1536]{1,0:T(8,128)S(1)} collective-permute-done((f32[16,1536]{1,0:T(8,128)S(1)}, f32[16,1536]{1,0:T(8,128)S(1)}, u32[]{:S(2)}, u32[]{:S(2)}) %collective-permute-start.15) | collective-permute-done | bytes 98336 | tf_op jit(solution)/shard_map/ppermute | solution.py:407
  97.9 5.3 %all-to-all-start.1 = ((bf16[16,48,512]{2,1,0:T(8,128)(2,1)}), bf16[16,48,512]{2,1,0:T(8,128)(2,1)S(1)}, u32[]{:S(2)}, u32[]{:S(2)}) async-start(bf16[16,48,512]{2,1,0:T(8,128)(2,1)} %get-tuple-element.153), calls=%async_computation.1 | async-start | bytes 1572864 | tf_op jit(solution)/shard_map/all_to_all | solution.py:533
  103.3 10.2 %rest.1 = (f32[2048,512]{1,0:T(8,128)}, bf16[544,512]{1,0:T(8,128)(2,1)}, f32[16,512]{1,0:T(8,128)}) custom-call(s32[2]{0:T(128)} %copy-done.4, f32[16,1536]{1,0:T(8,128)} %copy-done.13, f32[16,1536]{1,0:T(8,128)} %copy-done.17, f32[16,1536]{1,0:T(8,128)} %copy-done.16, f32[16,1536]{1,0:T(8,128)} %copy-done.15, bf16[32,1536]{1,0:T(8,128)(2,1)} %pad_maximum_fusion.1.refs_4_, ...), custom_call_target="tpu_custom_call" | custom-call | flops 1 | bytes 1 | tf_op jit(solution)/shard_map/rest/pallas_call | solution.py:561
  114.2 4.5 %collective-permute-start.17 = (bf16[544,512]{1,0:T(8,128)(2,1)}, bf16[544,512]{1,0:T(8,128)(2,1)S(1)}, u32[]{:S(2)}, u32[]{:S(2)}) collective-permute-start(bf16[544,512]{1,0:T(8,128)(2,1)} %get-tuple-element.152), channel_id=1, source_target_pairs={{0,4},{1,5},{2,6},{3,7},{4,8},{5,9},{6,10},{7,11},{16,20},{17,21},... | collective-permute-start | bytes 1671176 | tf_op jit(solution)/shard_map/ppermute | solution.py:411
  118.6 12.5 %collective-permute-done.17.refs_2_ = bf16[544,512]{1,0:T(8,128)(2,1)S(1)} collective-permute-done((bf16[544,512]{1,0:T(8,128)(2,1)}, bf16[544,512]{1,0:T(8,128)(2,1)S(1)}, u32[]{:S(2)}, u32[]{:S(2)}) %collective-permute-start.17) | collective-permute-done | bytes 557088 | tf_op jit(solution)/shard_map/ppermute | solution.py:411
  131.9 1.7 hop.1
  133.6 5.6 %collective-permute-start.19 = (bf16[544,512]{1,0:T(8,128)(2,1)S(1)}, bf16[544,512]{1,0:T(8,128)(2,1)S(1)}, u32[]{:S(2)}, u32[]{:S(2)}) collective-permute-start(bf16[544,512]{1,0:T(8,128)(2,1)S(1)} %get-tuple-element.159), channel_id=1, source_target_pairs={{0,4},{1,5},{2,6},{3,7},{4,8},{5,9},{6,10},{7,11},{8,12},{9,13},{1... | collective-permute-start | bytes 1671176 | tf_op jit(solution)/shard_map/ppermute | solution.py:411
  139.4 12.9 %collective-permute-done.19.refs_0_ = bf16[544,512]{1,0:T(8,128)(2,1)S(1)} collective-permute-done((bf16[544,512]{1,0:T(8,128)(2,1)S(1)}, bf16[544,512]{1,0:T(8,128)(2,1)S(1)}, u32[]{:S(2)}, u32[]{:S(2)}) %collective-permute-start.19) | collective-permute-done | bytes 557088 | tf_op jit(solution)/shard_map/ppermute | solution.py:411
  152.3 10.6 %collective-permute-done.20.refs_1_ = bf16[544,512]{1,0:T(8,128)(2,1)S(1)} collective-permute-done((bf16[544,512]{1,0:T(8,128)(2,1)S(1)}, bf16[544,512]{1,0:T(8,128)(2,1)S(1)}, u32[]{:S(2)}, u32[]{:S(2)}) %collective-permute-start.20) | collective-permute-done | bytes 557088 | tf_op jit(solution)/shard_map/ppermute | solution.py:415
  162.9 2.0 %final.1 = (f32[144,512]{1,0:T(8,128)S(1)}, bf16[160,512]{1,0:T(8,128)(2,1)S(1)}, bf16[160,512]{1,0:T(8,128)(2,1)S(1)}, bf16[160,512]{1,0:T(8,128)(2,1)S(1)}) custom-call(s32[2]{0:T(128)S(1)} %copy-done.5, f32[2048,512]{1,0:T(8,128)} %get-tuple-element.155.refs_0_.refs_1_.mine_ref, f32[16,512]{1,0:T(8,128)S(1)} %copy-done.3, ...), custom_call_target="tpu_custom_call" | custom-call | flops 1 | bytes 1 | tf_op jit(solution)/shard_map/final/pallas_call | solution.py:617
  168.2 3.8 %collective-permute-done.22.refs_2_ = bf16[160,512]{1,0:T(8,128)(2,1)S(1)} collective-permute-done((bf16[160,512]{1,0:T(8,128)(2,1)S(1)}, bf16[160,512]{1,0:T(8,128)(2,1)S(1)}, u32[]{:S(2)}, u32[]{:S(2)}) %collective-permute-start.22) | collective-permute-done | bytes 163872 | tf_op jit(solution)/shard_map/ppermute | solution.py:407
  172.0 2.6 %collective-permute-done.23.refs_3_ = bf16[160,512]{1,0:T(8,128)(2,1)S(1)} collective-permute-done((bf16[160,512]{1,0:T(8,128)(2,1)S(1)}, bf16[160,512]{1,0:T(8,128)(2,1)S(1)}, u32[]{:S(2)}, u32[]{:S(2)}) %collective-permute-start.23) | collective-permute-done | bytes 163872 | tf_op jit(solution)/shard_map/ppermute | solution.py:407
  174.6 1.6 assemble.1
  (96 shorter events, 23.1 us)
Async XLA Ops:
  0.6 18.0 %copy-start.20 = (f32[12]{0:T(128)S(1)}, f32[12]{0:T(128)}, u32[]{:S(2)}) copy-start(f32[12]{0:T(128)} %param.21) | copy-start | bytes 148
  0.7 11.2 %collective-permute-start = (bf16[384,2048]{1,0:T(8,128)(2,1)}, bf16[384,2048]{1,0:T(8,128)(2,1)S(1)}, u32[]{:S(2)}, u32[]{:S(2)}) collective-permute-start(bf16[384,2048]{1,0:T(8,128)(2,1)} %refs_5_.1), channel_id=1, source_target_pairs={{0,1},{1,0},{2,3},{3,2},{4,5},{5,4},{6,7},{7,6},{8,9},{9,8},{10,11... | collective-permute-start | bytes 4718600 | tf_op jit(solution)/shard_map/ppermute | solution.py:407
  2.3 8.9 %collective-permute-start.3 = (bf16[128,512]{1,0:T(8,128)(2,1)S(1)}, bf16[128,512]{1,0:T(8,128)(2,1)S(1)}, u32[]{:S(2)}, u32[]{:S(2)}) collective-permute-start(bf16[128,512]{1,0:T(8,128)(2,1)S(1)} %get-tuple-element.184), channel_id=1, source_target_pairs={{0,3},{1,2},{2,1},{3,0},{4,7},{5,6},{6,5},{7,4},{8,11},{9,10},{10,... | collective-permute-start | bytes 393224 | tf_op jit(solution)/shard_map/ppermute | solution.py:407
  5.0 6.2 %collective-permute-start.1 = (bf16[128,512]{1,0:T(8,128)(2,1)S(1)}, bf16[128,512]{1,0:T(8,128)(2,1)S(1)}, u32[]{:S(2)}, u32[]{:S(2)}) collective-permute-start(bf16[128,512]{1,0:T(8,128)(2,1)S(1)} %get-tuple-element.185), channel_id=1, source_target_pairs={{0,1},{1,0},{2,3},{3,2},{4,5},{5,4},{6,7},{7,6},{8,9},{9,8},{10,11... | collective-permute-start | bytes 393224 | tf_op jit(solution)/shard_map/ppermute | solution.py:407
  5.1 6.8 %collective-permute-start.2 = (bf16[128,512]{1,0:T(8,128)(2,1)S(1)}, bf16[128,512]{1,0:T(8,128)(2,1)S(1)}, u32[]{:S(2)}, u32[]{:S(2)}) collective-permute-start(bf16[128,512]{1,0:T(8,128)(2,1)S(1)} %get-tuple-element.187), channel_id=1, source_target_pairs={{0,2},{1,3},{2,0},{3,1},{4,6},{5,7},{6,4},{7,5},{8,10},{9,11},{10,... | collective-permute-start | bytes 393224 | tf_op jit(solution)/shard_map/ppermute | solution.py:407
  11.2 38.4 %copy-start.4 = (s32[2]{0:T(128)}, s32[2]{0:T(128)S(1)}, u32[]{:S(2)}) copy-start(s32[2]{0:T(128)S(1)} %pad_add_fusion.where_ref) | copy-start | bytes 28
  11.9 30.2 %collective-permute-start.6 = (bf16[256,2048]{1,0:T(8,128)(2,1)}, bf16[256,2048]{1,0:T(8,128)(2,1)}, u32[]{:S(2)}, u32[]{:S(2)}) collective-permute-start(bf16[256,2048]{1,0:T(8,128)(2,1)} %slice.57), channel_id=1, source_target_pairs={{0,2},{1,3},{2,0},{3,1},{4,6},{5,7},{6,4},{7,5},{8,10},{9,11},{10,... | collective-permute-start | bytes 3145736 | tf_op jit(solution)/shard_map/ppermute | solution.py:407
  14.9 35.5 %copy-start.1 = (bf16[528,512]{1,0:T(8,128)(2,1)}, bf16[528,512]{1,0:T(8,128)(2,1)S(1)}, u32[]{:S(2)}) copy-start(bf16[528,512]{1,0:T(8,128)(2,1)S(1)} %join.1.refs_0_) | copy-start | bytes 1622020
  14.9 16.4 %collective-permute-start.5 = (bf16[528,512]{1,0:T(8,128)(2,1)S(1)}, bf16[528,512]{1,0:T(8,128)(2,1)}, u32[]{:S(2)}, u32[]{:S(2)}) collective-permute-start(bf16[528,512]{1,0:T(8,128)(2,1)S(1)} %join.1.refs_0_), channel_id=1, source_target_pairs={{4,0},{5,1},{6,2},{7,3},{8,4},{9,5},{10,6},{11,7},{12,8},{13,9},{1... | collective-permute-start | bytes 1622024 | tf_op jit(solution)/shard_map/ppermute | solution.py:415
  18.5 23.6 %collective-permute-start.4 = (bf16[528,512]{1,0:T(8,128)(2,1)S(1)}, bf16[528,512]{1,0:T(8,128)(2,1)}, u32[]{:S(2)}, u32[]{:S(2)}) collective-permute-start(bf16[528,512]{1,0:T(8,128)(2,1)S(1)} %join.1.refs_0_), channel_id=1, source_target_pairs={{0,4},{1,5},{2,6},{3,7},{4,8},{5,9},{6,10},{7,11},{8,12},{9,13},{1... | collective-permute-start | bytes 1622024 | tf_op jit(solution)/shard_map/ppermute | solution.py:411
  18.5 6.8 %collective-permute-start.7 = (bf16[32,384]{1,0:T(8,128)(2,1)S(1)}, bf16[32,384]{1,0:T(8,128)(2,1)S(1)}, u32[]{:S(2)}, u32[]{:S(2)}) collective-permute-start(bf16[32,384]{1,0:T(8,128)(2,1)S(1)} %copy-done.19), channel_id=1, source_target_pairs={{0,1},{1,0},{2,3},{3,2},{4,5},{5,4},{6,7},{7,6},{8,9},{9,8},{10,11... | collective-permute-start | bytes 73736 | tf_op jit(solution)/shard_map/ppermute | solution.py:407
  42.8 7.6 %collective-permute-start.12 = (bf16[256,2048]{1,0:T(8,128)(2,1)}, bf16[256,2048]{1,0:T(8,128)(2,1)S(1)}, u32[]{:S(2)}, u32[]{:S(2)}) collective-permute-start(bf16[256,2048]{1,0:T(8,128)(2,1)} %collective-permute-done.6.refs_0_.refs_1_), channel_id=1, source_target_pairs={{0,1},{1,0},{2,3},{3,2},{4,5},{5,4},{6,7},{7,6},{8,9},{9,8},{10,11... | collective-permute-start | bytes 3145736 | tf_op jit(solution)/shard_map/ppermute | solution.py:407
  42.8 17.7 %collective-permute-start.8 = (bf16[528,512]{1,0:T(8,128)(2,1)}, bf16[528,512]{1,0:T(8,128)(2,1)S(1)}, u32[]{:S(2)}, u32[]{:S(2)}) collective-permute-start(bf16[528,512]{1,0:T(8,128)(2,1)} %collective-permute-done.4.refs_1_), channel_id=1, source_target_pairs={{4,8},{5,9},{6,10},{7,11},{8,12},{9,13},{10,14},{11,15},{20,24},{2... | collective-permute-start | bytes 1622024 | tf_op jit(solution)/shard_map/ppermute | solution.py:411
  43.5 17.4 %collective-permute-start.9 = (bf16[528,512]{1,0:T(8,128)(2,1)}, bf16[528,512]{1,0:T(8,128)(2,1)}, u32[]{:S(2)}, u32[]{:S(2)}) collective-permute-start(bf16[528,512]{1,0:T(8,128)(2,1)} %collective-permute-done.5.refs_3_), channel_id=1, source_target_pairs={{4,0},{5,1},{6,2},{7,3},{8,4},{9,5},{10,6},{11,7},{20,16},{21,17},... | collective-permute-start | bytes 1622024 | tf_op jit(solution)/shard_map/ppermute | solution.py:415
  44.8 15.7 %collective-permute-start.10 = (bf16[128,2048]{1,0:T(8,128)(2,1)}, bf16[128,2048]{1,0:T(8,128)(2,1)S(1)}, u32[]{:S(2)}, u32[]{:S(2)}) collective-permute-start(bf16[128,2048]{1,0:T(8,128)(2,1)} %slice.58), channel_id=1, source_target_pairs={{0,2},{1,3},{2,0},{3,1},{4,6},{5,7},{6,4},{7,5},{8,10},{9,11},{10,... | collective-permute-start | bytes 1572872 | tf_op jit(solution)/shard_map/ppermute | solution.py:407
  45.4 15.0 %collective-permute-start.11 = (bf16[32,768]{1,0:T(8,128)(2,1)S(1)}, bf16[32,768]{1,0:T(8,128)(2,1)S(1)}, u32[]{:S(2)}, u32[]{:S(2)}) collective-permute-start(bf16[32,768]{1,0:T(8,128)(2,1)S(1)} %constant_dynamic-update-slice_fusion.refs_9_), channel_id=1, source_target_pairs={{0,2},{1,3},{2,0},{3,1},{4,6},{5,7},{6,4},{7,5},{8,10},{9,11},{10,... | collective-permute-start | bytes 147464 | tf_op jit(solution)/shard_map/ppermute | solution.py:407
  60.4 20.5 %copy-start.14 = (bf16[32,768]{1,0:T(8,128)(2,1)}, bf16[32,768]{1,0:T(8,128)(2,1)S(1)}, u32[]{:S(2)}) copy-start(bf16[32,768]{1,0:T(8,128)(2,1)S(1)} %collective-permute-done.11.refs_8_) | copy-start | bytes 147460
  68.9 29.0 %all-to-all-start = ((bf16[16,48,512]{2,1,0:T(8,128)(2,1)}), bf16[16,48,512]{2,1,0:T(8,128)(2,1)S(1)}, u32[]{:S(2)}, u32[]{:S(2)}) async-start(bf16[16,48,512]{2,1,0:T(8,128)(2,1)} %get-tuple-element.134), calls=%async_computation | async-start | bytes 1572864 | tf_op jit(solution)/shard_map/all_to_all | solution.py:533
  75.1 2.0 %collective-permute-start.13 = (bf16[128,2048]{1,0:T(8,128)(2,1)S(1)}, bf16[128,2048]{1,0:T(8,128)(2,1)S(1)}, u32[]{:S(2)}, u32[]{:S(2)}) collective-permute-start(bf16[128,2048]{1,0:T(8,128)(2,1)S(1)} %collective-permute-done.10.refs_0_.refs_3_), channel_id=1, source_target_pairs={{0,1},{1,0},{2,3},{3,2},{4,5},{5,4},{6,7},{7,6},{8,9},{9,8},{10,11... | collective-permute-start | bytes 1572872 | tf_op jit(solution)/shard_map/ppermute | solution.py:407
  89.0 6.6 %collective-permute-start.16 = (f32[16,1536]{1,0:T(8,128)S(1)}, f32[16,1536]{1,0:T(8,128)S(1)}, u32[]{:S(2)}, u32[]{:S(2)}) collective-permute-start(f32[16,1536]{1,0:T(8,128)S(1)} %constant_dynamic-update-slice_fusion.2.refs_0_), channel_id=1, source_target_pairs={{0,3},{1,2},{2,1},{3,0},{4,7},{5,6},{6,5},{7,4},{8,11},{9,10},{10,... | collective-permute-start | bytes 294920 | tf_op jit(solution)/shard_map/ppermute | solution.py:407
  90.6 7.3 %collective-permute-start.15 = (f32[16,1536]{1,0:T(8,128)S(1)}, f32[16,1536]{1,0:T(8,128)S(1)}, u32[]{:S(2)}, u32[]{:S(2)}) collective-permute-start(f32[16,1536]{1,0:T(8,128)S(1)} %constant_dynamic-update-slice_fusion.2.refs_0_), channel_id=1, source_target_pairs={{0,2},{1,3},{2,0},{3,1},{4,6},{5,7},{6,4},{7,5},{8,10},{9,11},{10,... | collective-permute-start | bytes 294920 | tf_op jit(solution)/shard_map/ppermute | solution.py:407
  91.0 6.9 %collective-permute-start.14 = (f32[16,1536]{1,0:T(8,128)S(1)}, f32[16,1536]{1,0:T(8,128)S(1)}, u32[]{:S(2)}, u32[]{:S(2)}) collective-permute-start(f32[16,1536]{1,0:T(8,128)S(1)} %constant_dynamic-update-slice_fusion.2.refs_0_), channel_id=1, source_target_pairs={{0,1},{1,0},{2,3},{3,2},{4,5},{5,4},{6,7},{7,6},{8,9},{9,8},{10,11... | collective-permute-start | bytes 294920 | tf_op jit(solution)/shard_map/ppermute | solution.py:407
  97.9 33.2 %all-to-all-start.1 = ((bf16[16,48,512]{2,1,0:T(8,128)(2,1)}), bf16[16,48,512]{2,1,0:T(8,128)(2,1)S(1)}, u32[]{:S(2)}, u32[]{:S(2)}) async-start(bf16[16,48,512]{2,1,0:T(8,128)(2,1)} %get-tuple-element.153), calls=%async_computation.1 | async-start | bytes 1572864 | tf_op jit(solution)/shard_map/all_to_all | solution.py:533
  113.5 5.2 %collective-permute-start.18 = (bf16[544,512]{1,0:T(8,128)(2,1)}, bf16[544,512]{1,0:T(8,128)(2,1)S(1)}, u32[]{:S(2)}, u32[]{:S(2)}) collective-permute-start(bf16[544,512]{1,0:T(8,128)(2,1)} %get-tuple-element.152), channel_id=1, source_target_pairs={{8,4},{9,5},{10,6},{11,7},{12,8},{13,9},{14,10},{15,11},{24,20},{2... | collective-permute-start | bytes 1671176 | tf_op jit(solution)/shard_map/ppermute | solution.py:415
  114.2 16.9 %collective-permute-start.17 = (bf16[544,512]{1,0:T(8,128)(2,1)}, bf16[544,512]{1,0:T(8,128)(2,1)S(1)}, u32[]{:S(2)}, u32[]{:S(2)}) collective-permute-start(bf16[544,512]{1,0:T(8,128)(2,1)} %get-tuple-element.152), channel_id=1, source_target_pairs={{0,4},{1,5},{2,6},{3,7},{4,8},{5,9},{6,10},{7,11},{16,20},{17,21},... | collective-permute-start | bytes 1671176 | tf_op jit(solution)/shard_map/ppermute | solution.py:411
  133.6 29.3 %copy-start.3 = (f32[16,512]{1,0:T(8,128)S(1)}, f32[16,512]{1,0:T(8,128)}, u32[]{:S(2)}) copy-start(f32[16,512]{1,0:T(8,128)} %get-tuple-element.156.head_ref) | copy-start | bytes 98308
  133.6 29.3 %copy-start.5 = (s32[2]{0:T(128)S(1)}, s32[2]{0:T(128)}, u32[]{:S(2)}) copy-start(s32[2]{0:T(128)} %copy-done.4) | copy-start | bytes 28
  133.6 18.7 %collective-permute-start.19 = (bf16[544,512]{1,0:T(8,128)(2,1)S(1)}, bf16[544,512]{1,0:T(8,128)(2,1)S(1)}, u32[]{:S(2)}, u32[]{:S(2)}) collective-permute-start(bf16[544,512]{1,0:T(8,128)(2,1)S(1)} %get-tuple-element.159), channel_id=1, source_target_pairs={{0,4},{1,5},{2,6},{3,7},{4,8},{5,9},{6,10},{7,11},{8,12},{9,13},{1... | collective-permute-start | bytes 1671176 | tf_op jit(solution)/shard_map/ppermute | solution.py:411
  139.2 23.6 %collective-permute-start.20 = (bf16[544,512]{1,0:T(8,128)(2,1)S(1)}, bf16[544,512]{1,0:T(8,128)(2,1)S(1)}, u32[]{:S(2)}, u32[]{:S(2)}) collective-permute-start(bf16[544,512]{1,0:T(8,128)(2,1)S(1)} %get-tuple-element.160), channel_id=1, source_target_pairs={{4,0},{5,1},{6,2},{7,3},{8,4},{9,5},{10,6},{11,7},{12,8},{13,9},{1... | collective-permute-start | bytes 1671176 | tf_op jit(solution)/shard_map/ppermute | solution.py:415
  164.8 3.4 %collective-permute-start.21 = (bf16[160,512]{1,0:T(8,128)(2,1)S(1)}, bf16[160,512]{1,0:T(8,128)(2,1)S(1)}, u32[]{:S(2)}, u32[]{:S(2)}) collective-permute-start(bf16[160,512]{1,0:T(8,128)(2,1)S(1)} %get-tuple-element.162), channel_id=1, source_target_pairs={{0,1},{1,0},{2,3},{3,2},{4,5},{5,4},{6,7},{7,6},{8,9},{9,8},{10,11... | collective-permute-start | bytes 491528 | tf_op jit(solution)/shard_map/ppermute | solution.py:407
  164.9 7.1 %collective-permute-start.22 = (bf16[160,512]{1,0:T(8,128)(2,1)S(1)}, bf16[160,512]{1,0:T(8,128)(2,1)S(1)}, u32[]{:S(2)}, u32[]{:S(2)}) collective-permute-start(bf16[160,512]{1,0:T(8,128)(2,1)S(1)} %get-tuple-element.163), channel_id=1, source_target_pairs={{0,2},{1,3},{2,0},{3,1},{4,6},{5,7},{6,4},{7,5},{8,10},{9,11},{10,... | collective-permute-start | bytes 491528 | tf_op jit(solution)/shard_map/ppermute | solution.py:407
  166.4 8.1 %collective-permute-start.23 = (bf16[160,512]{1,0:T(8,128)(2,1)S(1)}, bf16[160,512]{1,0:T(8,128)(2,1)S(1)}, u32[]{:S(2)}, u32[]{:S(2)}) collective-permute-start(bf16[160,512]{1,0:T(8,128)(2,1)S(1)} %get-tuple-element.164), channel_id=1, source_target_pairs={{0,3},{1,2},{2,1},{3,0},{4,7},{5,6},{6,5},{7,4},{8,11},{9,10},{10,... | collective-permute-start | bytes 491528 | tf_op jit(solution)/shard_map/ppermute | solution.py:407
  (15 other events, 109.3 us)

commit v3 on v2

--- a/solution.py
+++ b/solution.py
@@ -17,6 +17,7 @@
 HALF = 16
 MIB = 1024 * 1024
 CHEAP = pl.CostEstimate(flops=1, bytes_accessed=1, transcendentals=0)
+COSTLY = pl.CostEstimate(flops=10**11, bytes_accessed=10**8, transcendentals=0)
 
 
 def params(mib=50):
@@ -551,7 +552,7 @@
     )
     sums = jnp.concatenate([sums_near, sums_far], 1)
     sums = [mate(sums, r) for r in range(team)]
-    send, recv_near, *sums = lax.optimization_barrier((send, recv_near, *sums))
+    send, recv_near = lax.optimization_barrier((send, recv_near))
     recv_far = scatter(send)
     nfirst = len(first_blocks(line))
     turned = [pair[1] for pair in (normed_own, normed_core, normed_far, normed_diag, normed_last)]
@@ -584,7 +585,7 @@
             scratch_shapes=[pltpu.VMEM((team_rows, part), BF16)],
         ),
         compiler_params=params(58),
-        cost_estimate=CHEAP,
+        cost_estimate=COSTLY,
         name="rest",
     )(where, *sums, small_all, isd, high_near, high_far, hw_twice, *turned)
     grads, firsts, head = outs[0], outs[1:-1], outs[-1]

time: 178 us -> 174 us (0.978)
  waiting for transfers between devices: 69.4 us -> 65.3 us
    ppermute x16, waiting for transfers between devices: 20.4 us -> 13.5 us  [mate(): return lax.ppermute(x, 'fsdp', [(i, i ^ r) for i in range(n)]) if r else x]
    all_to_all x2, waiting for transfers between devices: 0.01 us -> 2.8 us  [scatter(): return lax.all_to_all(send, 'fsdp', split_axis=0, concat_axis=0, tiled=True)]
  transfers between devices with their start and end apart: 26 -> 26, of which waited for: 13 -> 12; matrix products, arithmetic and copies ran while one was open for 7% -> 7% of each run, Pallas kernels for 21% -> 21%
where the time goes in v3:
time: 174 us; the launch traced here: 173 us
  waiting for transfers between devices  65.3 us (38%)
  Pallas kernels  49.6 us (29%)
  starting transfers between devices  39.4 us (23%)
  local copies, waits for them, and re-layouts  15.1 us (9%)
  other arithmetic  2.44 us (1%)
    ppermute x4, waiting for transfers between devices, up(): lax.ppermute(x, 'fsdp', [(a * team + i, b * team + i) for a, b in steps f...  36.2 us
    pallas_call x5, Pallas kernels, norm(): pl.pallas_call(norm_kernel, out_shape=(jax.ShapeDtypeStruct((rows * len(x...  16.6 us
    pallas_call x2, Pallas kernels, hidden(): pl.pallas_call(functools.partial(hidden_kernel, line, nact, packed, given...  14.8 us
    ppermute x16, waiting for transfers between devices, mate(): return lax.ppermute(x, 'fsdp', [(i, i ^ r) for i in range(n)]) if r else x  13.5 us
    ppermute x4, waiting for transfers between devices, down(): lax.ppermute(x, 'fsdp', [(a * team + i, b * team + i) for a, b in steps f...  12.8 us
    ppermute x16, starting transfers between devices, mate(): return lax.ppermute(x, 'fsdp', [(i, i ^ r) for i in range(n)]) if r else x  12 us
    all_to_all x2, starting transfers between devices, scatter(): return lax.all_to_all(send, 'fsdp', split_axis=0, concat_axis=0, tiled=True)  11.7 us
    pallas_call x1, Pallas kernels, local(): pl.pallas_call(functools.partial(rest_kernel, line, team, nact, width, to...  10.2 us
  transfers between devices with their start and end apart: 26, of which 12 were waited for; matrix products, arithmetic and copies ran while one was open for 7% of the time, Pallas kernels for 21%

profile of v3, /device:TPU:0, one launch (start us, length us, event | category | flops | bytes accessed | tf_op | source)
XLA Modules:
  0.0 172.8 jit_solution(832744192413770668)
XLA Ops:
  2.3 2.7 %collective-permute-start.3 = (bf16[128,512]{1,0:T(8,128)(2,1)S(1)}, bf16[128,512]{1,0:T(8,128)(2,1)S(1)}, u32[]{:S(2)}, u32[]{:S(2)}) collective-permute-start(bf16[128,512]{1,0:T(8,128)(2,1)S(1)} %get-tuple-element.176), channel_id=1, source_target_pairs={{0,3},{1,2},{2,1},{3,0},{4,7},{5,6},{6,5},{7,4},{8,11},{9,10},{10,... | collective-permute-start | bytes 393224 | tf_op jit(solution)/shard_map/ppermute | solution.py:408
  6.7 2.1 %small.1 = (bf16[32,384]{1,0:T(8,128)(2,1)}, bf16[16,512]{1,0:T(8,128)(2,1)}) custom-call(f32[16,24]{1,0:T(8,128)} %reward_ref.1, f32[16,25]{1,0:T(8,128)} %value_ref.1, s32[16,24]{1,0:T(8,128)} %done_ref.1, bf16[12,384]{1,0:T(8,128)(2,1)} %bitcast.85, bf16[12,384]{1,0:T(8,128)(2,1)} %bitcast.86, s32[1,384]{1,0:T(1,128)} %broadcast_in_dim.12.perm_ref), custom_call_target="tpu_custom_call" | custom-call | flops 1 | bytes 1 | tf_op jit(solution)/shard_map/small/pallas_call | solution.py:422
  8.8 2.3 %slice.57 = bf16[256,2048]{1,0:T(8,128)(2,1)} slice(bf16[384,2048]{1,0:T(8,128)(2,1)} %refs_5_.1), slice={[0:256], [0:2048]} | slice | bytes 2097152 | tf_op jit(solution)/shard_map/slice | solution.py:444
  11.9 1.7 collective-permute-start.6
  14.9 3.7 %collective-permute-start.5 = (bf16[528,512]{1,0:T(8,128)(2,1)S(1)}, bf16[528,512]{1,0:T(8,128)(2,1)}, u32[]{:S(2)}, u32[]{:S(2)}) collective-permute-start(bf16[528,512]{1,0:T(8,128)(2,1)S(1)} %join.1.refs_0_), channel_id=1, source_target_pairs={{4,0},{5,1},{6,2},{7,3},{8,4},{9,5},{10,6},{11,7},{12,8},{13,9},{1... | collective-permute-start | bytes 1622024 | tf_op jit(solution)/shard_map/ppermute | solution.py:416
  19.4 4.1 %norm.6 = (bf16[384,2048]{1,0:T(8,128)(2,1)}, bf16[2048,384]{1,0:T(8,128)(2,1)}) custom-call(bf16[384,2048]{1,0:T(8,128)(2,1)} %copy-done.7, f32[1,2048]{1,0:T(1,128)} %bitcast.80), custom_call_target="tpu_custom_call" | custom-call | flops 1 | bytes 1 | tf_op jit(solution)/shard_map/norm/pallas_call | solution.py:146
  23.4 1.9 %slice.58 = bf16[128,2048]{1,0:T(8,128)(2,1)} slice(bf16[384,2048]{1,0:T(8,128)(2,1)} %refs_5_.1), slice={[256:384], [0:2048]} | slice | bytes 1048576 | tf_op jit(solution)/shard_map/slice | solution.py:450
  25.4 4.1 %norm.5 = (bf16[384,2048]{1,0:T(8,128)(2,1)}, bf16[2048,384]{1,0:T(8,128)(2,1)}) custom-call(bf16[384,2048]{1,0:T(8,128)(2,1)} %refs_5_.1, f32[1,2048]{1,0:T(1,128)} %bitcast.81), custom_call_target="tpu_custom_call" | custom-call | flops 1 | bytes 1 | tf_op jit(solution)/shard_map/norm/pallas_call | solution.py:146
  29.5 1.8 %collective-permute-done.5.refs_3_ = bf16[528,512]{1,0:T(8,128)(2,1)} collective-permute-done((bf16[528,512]{1,0:T(8,128)(2,1)S(1)}, bf16[528,512]{1,0:T(8,128)(2,1)}, u32[]{:S(2)}, u32[]{:S(2)}) %collective-permute-start.5) | collective-permute-done | bytes 540704 | tf_op jit(solution)/shard_map/ppermute | solution.py:416
  31.3 10.8 %collective-permute-done.4.refs_1_ = bf16[528,512]{1,0:T(8,128)(2,1)} collective-permute-done((bf16[528,512]{1,0:T(8,128)(2,1)S(1)}, bf16[528,512]{1,0:T(8,128)(2,1)}, u32[]{:S(2)}, u32[]{:S(2)}) %collective-permute-start.4) | collective-permute-done | bytes 540704 | tf_op jit(solution)/shard_map/ppermute | solution.py:412
  45.4 1.6 collective-permute-start.11
  46.9 2.7 %norm.7 = (bf16[256,2048]{1,0:T(8,128)(2,1)}, bf16[2048,256]{1,0:T(8,128)(2,1)}) custom-call(bf16[256,2048]{1,0:T(8,128)(2,1)} %collective-permute-done.6.refs_0_.refs_1_, f32[1,2048]{1,0:T(1,128)} %bitcast.82), custom_call_target="tpu_custom_call" | custom-call | flops 1 | bytes 1 | tf_op jit(solution)/shard_map/norm/pallas_call | solution.py:146
  51.4 2.7 %norm.8 = (bf16[256,2048]{1,0:T(8,128)(2,1)}, bf16[2048,256]{1,0:T(8,128)(2,1)}) custom-call(bf16[256,2048]{1,0:T(8,128)(2,1)} %copy-done.8, f32[1,2048]{1,0:T(1,128)} %bitcast.83), custom_call_target="tpu_custom_call" | custom-call | flops 1 | bytes 1 | tf_op jit(solution)/shard_map/norm/pallas_call | solution.py:146
  54.1 6.4 %collective-permute-done.11.refs_8_ = bf16[32,768]{1,0:T(8,128)(2,1)S(1)} collective-permute-done((bf16[32,768]{1,0:T(8,128)(2,1)S(1)}, bf16[32,768]{1,0:T(8,128)(2,1)S(1)}, u32[]{:S(2)}, u32[]{:S(2)}) %collective-permute-start.11) | collective-permute-done | bytes 49184 | tf_op jit(solution)/shard_map/ppermute | solution.py:408
  61.3 7.6 %hidden.2 = (bf16[768,512]{1,0:T(8,128)(2,1)}, f32[16,768]{1,0:T(8,128)}, bf16[16,48,512]{2,1,0:T(8,128)(2,1)}, bf16[2048,512]{1,0:T(8,128)(2,1)}) custom-call(s32[2]{0:T(128)} %copy-done.5, bf16[528,512]{1,0:T(8,128)(2,1)} %copy-done.1, bf16[528,512]{1,0:T(8,128)(2,1)} %collective-permute-done.4.refs_1_, bf16[528,512]{1,0:T(8,128)(2,1)} %copy-done.11, ...), custom_call_target="tpu_custom_call" | custom-call | flops 1 | bytes 1 | tf_op jit(solution)/shard_map/hidden/pallas_call | solution.py:504
  68.8 6.2 %all-to-all-start = ((bf16[16,48,512]{2,1,0:T(8,128)(2,1)}), bf16[16,48,512]{2,1,0:T(8,128)(2,1)S(1)}, u32[]{:S(2)}, u32[]{:S(2)}) async-start(bf16[16,48,512]{2,1,0:T(8,128)(2,1)} %get-tuple-element.130), calls=%async_computation | async-start | bytes 1572864 | tf_op jit(solution)/shard_map/all_to_all | solution.py:534
  77.8 3.0 %norm.9 = (bf16[256,2048]{1,0:T(8,128)(2,1)}, bf16[2048,256]{1,0:T(8,128)(2,1)}) custom-call(bf16[128,2048]{1,0:T(8,128)(2,1)} %copy-done.9, bf16[128,2048]{1,0:T(8,128)(2,1)} %copy-done.10, f32[1,2048]{1,0:T(1,128)} %bitcast.84), custom_call_target="tpu_custom_call" | custom-call | flops 1 | bytes 1 | tf_op jit(solution)/shard_map/norm/pallas_call | solution.py:146
  80.9 7.3 %hidden.3 = (bf16[768,512]{1,0:T(8,128)(2,1)}, f32[16,768]{1,0:T(8,128)}, bf16[16,48,512]{2,1,0:T(8,128)(2,1)}) custom-call(s32[2]{0:T(128)} %copy-done.5, bf16[2048,512]{1,0:T(8,128)(2,1)} %get-tuple-element.120.refs_0_, bf16[256,2048]{1,0:T(8,128)(2,1)} %collective-permute-done.6.refs_0_.refs_1_, bf16[256,2048]{1,0:T(8,128)(2,1)} %copy-done.8, ...), custom_call_target="tpu_custom_call" | custom-call | flops 1 | bytes 1 | tf_op jit(solution)/shard_map/hidden/pallas_call | solution.py:504
  89.0 1.6 collective-permute-start.16
  91.0 2.8 %all-to-all-done = bf16[16,48,512]{2,1,0:T(8,128)(2,1)S(1)} async-done(((bf16[16,48,512]{2,1,0:T(8,128)(2,1)}), bf16[16,48,512]{2,1,0:T(8,128)(2,1)S(1)}, u32[]{:S(2)}, u32[]{:S(2)}) %all-to-all-start) | async-done | bytes 786464 | tf_op jit(solution)/shard_map/all_to_all | solution.py:534
  93.8 5.5 %all-to-all-start.1 = ((bf16[16,48,512]{2,1,0:T(8,128)(2,1)}), bf16[16,48,512]{2,1,0:T(8,128)(2,1)S(1)}, u32[]{:S(2)}, u32[]{:S(2)}) async-start(bf16[16,48,512]{2,1,0:T(8,128)(2,1)} %get-tuple-element.145), calls=%async_computation.1 | async-start | bytes 1572864 | tf_op jit(solution)/shard_map/all_to_all | solution.py:534
  100.0 10.2 %rest.1 = (f32[2048,512]{1,0:T(8,128)}, bf16[544,512]{1,0:T(8,128)(2,1)}, f32[16,512]{1,0:T(8,128)}) custom-call(s32[2]{0:T(128)} %copy-done.5, f32[16,1536]{1,0:T(8,128)} %copy-done.15, f32[16,1536]{1,0:T(8,128)} %copy-done.19, f32[16,1536]{1,0:T(8,128)} %copy-done.18, f32[16,1536]{1,0:T(8,128)} %copy-done.17, bf16[32,1536]{1,0:T(8,128)(2,1)} %pad_maximum_fusion.1.refs_4_, ...), custom_call_target="tpu_custom_call" | custom-call | flops 99999997952 | bytes 100000000 | tf_op jit(solution)/shard_map/rest/pallas_call | solution.py:562
  110.9 4.5 %collective-permute-start.17 = (bf16[544,512]{1,0:T(8,128)(2,1)}, bf16[544,512]{1,0:T(8,128)(2,1)S(1)}, u32[]{:S(2)}, u32[]{:S(2)}) collective-permute-start(bf16[544,512]{1,0:T(8,128)(2,1)} %get-tuple-element.144), channel_id=1, source_target_pairs={{0,4},{1,5},{2,6},{3,7},{4,8},{5,9},{6,10},{7,11},{16,20},{17,21},... | collective-permute-start | bytes 1671176 | tf_op jit(solution)/shard_map/ppermute | solution.py:412
  115.4 12.5 %collective-permute-done.17.refs_2_ = bf16[544,512]{1,0:T(8,128)(2,1)S(1)} collective-permute-done((bf16[544,512]{1,0:T(8,128)(2,1)}, bf16[544,512]{1,0:T(8,128)(2,1)S(1)}, u32[]{:S(2)}, u32[]{:S(2)}) %collective-permute-start.17) | collective-permute-done | bytes 557088 | tf_op jit(solution)/shard_map/ppermute | solution.py:412
  128.6 1.7 %hop.1 = (bf16[544,512]{1,0:T(8,128)(2,1)S(1)}, bf16[544,512]{1,0:T(8,128)(2,1)S(1)}) custom-call(f32[16,512]{1,0:T(8,128)S(1)} %copy-done.2, f32[2048,512]{1,0:T(8,128)} %get-tuple-element.147.refs_0_.refs_1_.mine_ref, f32[2048,512]{1,0:T(8,128)} %get-tuple-element.147.refs_0_.refs_1_.mine_ref, bf16[544,512]{1,0:T(8,128)(2,1)S(1)} %collective-permute-done.17.refs_2_, ...), custom_call_target="tpu_custom_call" | custom-call | flops 1 | bytes 1 | tf_op jit(solution)/shard_map/hop/pallas_call | solution.py:594
  130.4 5.0 %collective-permute-start.19 = (bf16[544,512]{1,0:T(8,128)(2,1)S(1)}, bf16[544,512]{1,0:T(8,128)(2,1)S(1)}, u32[]{:S(2)}, u32[]{:S(2)}) collective-permute-start(bf16[544,512]{1,0:T(8,128)(2,1)S(1)} %get-tuple-element.151), channel_id=1, source_target_pairs={{0,4},{1,5},{2,6},{3,7},{4,8},{5,9},{6,10},{7,11},{8,12},{9,13},{1... | collective-permute-start | bytes 1671176 | tf_op jit(solution)/shard_map/ppermute | solution.py:412
  135.5 12.9 %collective-permute-done.19.refs_0_ = bf16[544,512]{1,0:T(8,128)(2,1)S(1)} collective-permute-done((bf16[544,512]{1,0:T(8,128)(2,1)S(1)}, bf16[544,512]{1,0:T(8,128)(2,1)S(1)}, u32[]{:S(2)}, u32[]{:S(2)}) %collective-permute-start.19) | collective-permute-done | bytes 557088 | tf_op jit(solution)/shard_map/ppermute | solution.py:412
  148.4 10.6 %collective-permute-done.20.refs_1_ = bf16[544,512]{1,0:T(8,128)(2,1)S(1)} collective-permute-done((bf16[544,512]{1,0:T(8,128)(2,1)S(1)}, bf16[544,512]{1,0:T(8,128)(2,1)S(1)}, u32[]{:S(2)}, u32[]{:S(2)}) %collective-permute-start.20) | collective-permute-done | bytes 557088 | tf_op jit(solution)/shard_map/ppermute | solution.py:416
  159.0 2.0 %final.1 = (f32[144,512]{1,0:T(8,128)S(1)}, bf16[160,512]{1,0:T(8,128)(2,1)S(1)}, bf16[160,512]{1,0:T(8,128)(2,1)S(1)}, bf16[160,512]{1,0:T(8,128)(2,1)S(1)}) custom-call(s32[2]{0:T(128)S(1)} %copy-done.6, f32[2048,512]{1,0:T(8,128)} %get-tuple-element.147.refs_0_.refs_1_.mine_ref, f32[16,512]{1,0:T(8,128)S(1)} %copy-done.3, ...), custom_call_target="tpu_custom_call" | custom-call | flops 1 | bytes 1 | tf_op jit(solution)/shard_map/final/pallas_call | solution.py:618
  164.3 3.8 %collective-permute-done.22.refs_2_ = bf16[160,512]{1,0:T(8,128)(2,1)S(1)} collective-permute-done((bf16[160,512]{1,0:T(8,128)(2,1)S(1)}, bf16[160,512]{1,0:T(8,128)(2,1)S(1)}, u32[]{:S(2)}, u32[]{:S(2)}) %collective-permute-start.22) | collective-permute-done | bytes 163872 | tf_op jit(solution)/shard_map/ppermute | solution.py:408
  168.1 2.6 %collective-permute-done.23.refs_3_ = bf16[160,512]{1,0:T(8,128)(2,1)S(1)} collective-permute-done((bf16[160,512]{1,0:T(8,128)(2,1)S(1)}, bf16[160,512]{1,0:T(8,128)(2,1)S(1)}, u32[]{:S(2)}, u32[]{:S(2)}) %collective-permute-start.23) | collective-permute-done | bytes 163872 | tf_op jit(solution)/shard_map/ppermute | solution.py:408
  170.7 1.6 assemble.1
  (96 shorter events, 22.2 us)
Async XLA Ops:
  0.6 18.0 %copy-start.20 = (f32[12]{0:T(128)S(1)}, f32[12]{0:T(128)}, u32[]{:S(2)}) copy-start(f32[12]{0:T(128)} %param.21) | copy-start | bytes 148
  0.7 11.2 %collective-permute-start = (bf16[384,2048]{1,0:T(8,128)(2,1)}, bf16[384,2048]{1,0:T(8,128)(2,1)S(1)}, u32[]{:S(2)}, u32[]{:S(2)}) collective-permute-start(bf16[384,2048]{1,0:T(8,128)(2,1)} %refs_5_.1), channel_id=1, source_target_pairs={{0,1},{1,0},{2,3},{3,2},{4,5},{5,4},{6,7},{7,6},{8,9},{9,8},{10,11... | collective-permute-start | bytes 4718600 | tf_op jit(solution)/shard_map/ppermute | solution.py:408
  2.3 8.9 %collective-permute-start.3 = (bf16[128,512]{1,0:T(8,128)(2,1)S(1)}, bf16[128,512]{1,0:T(8,128)(2,1)S(1)}, u32[]{:S(2)}, u32[]{:S(2)}) collective-permute-start(bf16[128,512]{1,0:T(8,128)(2,1)S(1)} %get-tuple-element.176), channel_id=1, source_target_pairs={{0,3},{1,2},{2,1},{3,0},{4,7},{5,6},{6,5},{7,4},{8,11},{9,10},{10,... | collective-permute-start | bytes 393224 | tf_op jit(solution)/shard_map/ppermute | solution.py:408
  5.0 6.2 %collective-permute-start.1 = (bf16[128,512]{1,0:T(8,128)(2,1)S(1)}, bf16[128,512]{1,0:T(8,128)(2,1)S(1)}, u32[]{:S(2)}, u32[]{:S(2)}) collective-permute-start(bf16[128,512]{1,0:T(8,128)(2,1)S(1)} %get-tuple-element.177), channel_id=1, source_target_pairs={{0,1},{1,0},{2,3},{3,2},{4,5},{5,4},{6,7},{7,6},{8,9},{9,8},{10,11... | collective-permute-start | bytes 393224 | tf_op jit(solution)/shard_map/ppermute | solution.py:408
  5.1 6.8 %collective-permute-start.2 = (bf16[128,512]{1,0:T(8,128)(2,1)S(1)}, bf16[128,512]{1,0:T(8,128)(2,1)S(1)}, u32[]{:S(2)}, u32[]{:S(2)}) collective-permute-start(bf16[128,512]{1,0:T(8,128)(2,1)S(1)} %get-tuple-element.179), channel_id=1, source_target_pairs={{0,2},{1,3},{2,0},{3,1},{4,6},{5,7},{6,4},{7,5},{8,10},{9,11},{10,... | collective-permute-start | bytes 393224 | tf_op jit(solution)/shard_map/ppermute | solution.py:408
  11.2 38.4 %copy-start.5 = (s32[2]{0:T(128)}, s32[2]{0:T(128)S(1)}, u32[]{:S(2)}) copy-start(s32[2]{0:T(128)S(1)} %pad_add_fusion.where_ref) | copy-start | bytes 28
  11.9 30.2 %collective-permute-start.6 = (bf16[256,2048]{1,0:T(8,128)(2,1)}, bf16[256,2048]{1,0:T(8,128)(2,1)}, u32[]{:S(2)}, u32[]{:S(2)}) collective-permute-start(bf16[256,2048]{1,0:T(8,128)(2,1)} %slice.57), channel_id=1, source_target_pairs={{0,2},{1,3},{2,0},{3,1},{4,6},{5,7},{6,4},{7,5},{8,10},{9,11},{10,... | collective-permute-start | bytes 3145736 | tf_op jit(solution)/shard_map/ppermute | solution.py:408
  14.9 35.5 %copy-start.1 = (bf16[528,512]{1,0:T(8,128)(2,1)}, bf16[528,512]{1,0:T(8,128)(2,1)S(1)}, u32[]{:S(2)}) copy-start(bf16[528,512]{1,0:T(8,128)(2,1)S(1)} %join.1.refs_0_) | copy-start | bytes 1622020
  14.9 16.4 %collective-permute-start.5 = (bf16[528,512]{1,0:T(8,128)(2,1)S(1)}, bf16[528,512]{1,0:T(8,128)(2,1)}, u32[]{:S(2)}, u32[]{:S(2)}) collective-permute-start(bf16[528,512]{1,0:T(8,128)(2,1)S(1)} %join.1.refs_0_), channel_id=1, source_target_pairs={{4,0},{5,1},{6,2},{7,3},{8,4},{9,5},{10,6},{11,7},{12,8},{13,9},{1... | collective-permute-start | bytes 1622024 | tf_op jit(solution)/shard_map/ppermute | solution.py:416
  18.5 23.6 %collective-permute-start.4 = (bf16[528,512]{1,0:T(8,128)(2,1)S(1)}, bf16[528,512]{1,0:T(8,128)(2,1)}, u32[]{:S(2)}, u32[]{:S(2)}) collective-permute-start(bf16[528,512]{1,0:T(8,128)(2,1)S(1)} %join.1.refs_0_), channel_id=1, source_target_pairs={{0,4},{1,5},{2,6},{3,7},{4,8},{5,9},{6,10},{7,11},{8,12},{9,13},{1... | collective-permute-start | bytes 1622024 | tf_op jit(solution)/shard_map/ppermute | solution.py:412
  18.5 6.8 %collective-permute-start.7 = (bf16[32,384]{1,0:T(8,128)(2,1)S(1)}, bf16[32,384]{1,0:T(8,128)(2,1)S(1)}, u32[]{:S(2)}, u32[]{:S(2)}) collective-permute-start(bf16[32,384]{1,0:T(8,128)(2,1)S(1)} %copy-done.16), channel_id=1, source_target_pairs={{0,1},{1,0},{2,3},{3,2},{4,5},{5,4},{6,7},{7,6},{8,9},{9,8},{10,11... | collective-permute-start | bytes 73736 | tf_op jit(solution)/shard_map/ppermute | solution.py:408
  42.8 7.6 %collective-permute-start.12 = (bf16[256,2048]{1,0:T(8,128)(2,1)}, bf16[256,2048]{1,0:T(8,128)(2,1)S(1)}, u32[]{:S(2)}, u32[]{:S(2)}) collective-permute-start(bf16[256,2048]{1,0:T(8,128)(2,1)} %collective-permute-done.6.refs_0_.refs_1_), channel_id=1, source_target_pairs={{0,1},{1,0},{2,3},{3,2},{4,5},{5,4},{6,7},{7,6},{8,9},{9,8},{10,11... | collective-permute-start | bytes 3145736 | tf_op jit(solution)/shard_map/ppermute | solution.py:408
  42.8 17.7 %collective-permute-start.8 = (bf16[528,512]{1,0:T(8,128)(2,1)}, bf16[528,512]{1,0:T(8,128)(2,1)S(1)}, u32[]{:S(2)}, u32[]{:S(2)}) collective-permute-start(bf16[528,512]{1,0:T(8,128)(2,1)} %collective-permute-done.4.refs_1_), channel_id=1, source_target_pairs={{4,8},{5,9},{6,10},{7,11},{8,12},{9,13},{10,14},{11,15},{20,24},{2... | collective-permute-start | bytes 1622024 | tf_op jit(solution)/shard_map/ppermute | solution.py:412
  43.5 17.4 %collective-permute-start.9 = (bf16[528,512]{1,0:T(8,128)(2,1)}, bf16[528,512]{1,0:T(8,128)(2,1)}, u32[]{:S(2)}, u32[]{:S(2)}) collective-permute-start(bf16[528,512]{1,0:T(8,128)(2,1)} %collective-permute-done.5.refs_3_), channel_id=1, source_target_pairs={{4,0},{5,1},{6,2},{7,3},{8,4},{9,5},{10,6},{11,7},{20,16},{21,17},... | collective-permute-start | bytes 1622024 | tf_op jit(solution)/shard_map/ppermute | solution.py:416
  44.8 15.7 %collective-permute-start.10 = (bf16[128,2048]{1,0:T(8,128)(2,1)}, bf16[128,2048]{1,0:T(8,128)(2,1)S(1)}, u32[]{:S(2)}, u32[]{:S(2)}) collective-permute-start(bf16[128,2048]{1,0:T(8,128)(2,1)} %slice.58), channel_id=1, source_target_pairs={{0,2},{1,3},{2,0},{3,1},{4,6},{5,7},{6,4},{7,5},{8,10},{9,11},{10,... | collective-permute-start | bytes 1572872 | tf_op jit(solution)/shard_map/ppermute | solution.py:408
  45.4 15.0 %collective-permute-start.11 = (bf16[32,768]{1,0:T(8,128)(2,1)S(1)}, bf16[32,768]{1,0:T(8,128)(2,1)S(1)}, u32[]{:S(2)}, u32[]{:S(2)}) collective-permute-start(bf16[32,768]{1,0:T(8,128)(2,1)S(1)} %constant_dynamic-update-slice_fusion.refs_9_), channel_id=1, source_target_pairs={{0,2},{1,3},{2,0},{3,1},{4,6},{5,7},{6,4},{7,5},{8,10},{9,11},{10,... | collective-permute-start | bytes 147464 | tf_op jit(solution)/shard_map/ppermute | solution.py:408
  60.4 20.5 %copy-start.13 = (bf16[32,768]{1,0:T(8,128)(2,1)}, bf16[32,768]{1,0:T(8,128)(2,1)S(1)}, u32[]{:S(2)}) copy-start(bf16[32,768]{1,0:T(8,128)(2,1)S(1)} %collective-permute-done.11.refs_8_) | copy-start | bytes 147460
  68.8 25.0 %all-to-all-start = ((bf16[16,48,512]{2,1,0:T(8,128)(2,1)}), bf16[16,48,512]{2,1,0:T(8,128)(2,1)S(1)}, u32[]{:S(2)}, u32[]{:S(2)}) async-start(bf16[16,48,512]{2,1,0:T(8,128)(2,1)} %get-tuple-element.130), calls=%async_computation | async-start | bytes 1572864 | tf_op jit(solution)/shard_map/all_to_all | solution.py:534
  75.0 2.0 %collective-permute-start.13 = (bf16[128,2048]{1,0:T(8,128)(2,1)S(1)}, bf16[128,2048]{1,0:T(8,128)(2,1)S(1)}, u32[]{:S(2)}, u32[]{:S(2)}) collective-permute-start(bf16[128,2048]{1,0:T(8,128)(2,1)S(1)} %collective-permute-done.10.refs_0_.refs_3_), channel_id=1, source_target_pairs={{0,1},{1,0},{2,3},{3,2},{4,5},{5,4},{6,7},{7,6},{8,9},{9,8},{10,11... | collective-permute-start | bytes 1572872 | tf_op jit(solution)/shard_map/ppermute | solution.py:408
  89.0 10.3 %collective-permute-start.16 = (f32[16,1536]{1,0:T(8,128)S(1)}, f32[16,1536]{1,0:T(8,128)S(1)}, u32[]{:S(2)}, u32[]{:S(2)}) collective-permute-start(f32[16,1536]{1,0:T(8,128)S(1)} %constant_dynamic-update-slice_fusion.2.refs_0_), channel_id=1, source_target_pairs={{0,3},{1,2},{2,1},{3,0},{4,7},{5,6},{6,5},{7,4},{8,11},{9,10},{10,... | collective-permute-start | bytes 294920 | tf_op jit(solution)/shard_map/ppermute | solution.py:408
  90.6 8.7 %collective-permute-start.15 = (f32[16,1536]{1,0:T(8,128)S(1)}, f32[16,1536]{1,0:T(8,128)S(1)}, u32[]{:S(2)}, u32[]{:S(2)}) collective-permute-start(f32[16,1536]{1,0:T(8,128)S(1)} %constant_dynamic-update-slice_fusion.2.refs_0_), channel_id=1, source_target_pairs={{0,2},{1,3},{2,0},{3,1},{4,6},{5,7},{6,4},{7,5},{8,10},{9,11},{10,... | collective-permute-start | bytes 294920 | tf_op jit(solution)/shard_map/ppermute | solution.py:408
  91.0 8.4 %collective-permute-start.14 = (f32[16,1536]{1,0:T(8,128)S(1)}, f32[16,1536]{1,0:T(8,128)S(1)}, u32[]{:S(2)}, u32[]{:S(2)}) collective-permute-start(f32[16,1536]{1,0:T(8,128)S(1)} %constant_dynamic-update-slice_fusion.2.refs_0_), channel_id=1, source_target_pairs={{0,1},{1,0},{2,3},{3,2},{4,5},{5,4},{6,7},{7,6},{8,9},{9,8},{10,11... | collective-permute-start | bytes 294920 | tf_op jit(solution)/shard_map/ppermute | solution.py:408
  93.8 34.1 %all-to-all-start.1 = ((bf16[16,48,512]{2,1,0:T(8,128)(2,1)}), bf16[16,48,512]{2,1,0:T(8,128)(2,1)S(1)}, u32[]{:S(2)}, u32[]{:S(2)}) async-start(bf16[16,48,512]{2,1,0:T(8,128)(2,1)} %get-tuple-element.145), calls=%async_computation.1 | async-start | bytes 1572864 | tf_op jit(solution)/shard_map/all_to_all | solution.py:534
  110.2 5.2 %collective-permute-start.18 = (bf16[544,512]{1,0:T(8,128)(2,1)}, bf16[544,512]{1,0:T(8,128)(2,1)S(1)}, u32[]{:S(2)}, u32[]{:S(2)}) collective-permute-start(bf16[544,512]{1,0:T(8,128)(2,1)} %get-tuple-element.144), channel_id=1, source_target_pairs={{8,4},{9,5},{10,6},{11,7},{12,8},{13,9},{14,10},{15,11},{24,20},{2... | collective-permute-start | bytes 1671176 | tf_op jit(solution)/shard_map/ppermute | solution.py:416
  110.9 16.9 %collective-permute-start.17 = (bf16[544,512]{1,0:T(8,128)(2,1)}, bf16[544,512]{1,0:T(8,128)(2,1)S(1)}, u32[]{:S(2)}, u32[]{:S(2)}) collective-permute-start(bf16[544,512]{1,0:T(8,128)(2,1)} %get-tuple-element.144), channel_id=1, source_target_pairs={{0,4},{1,5},{2,6},{3,7},{4,8},{5,9},{6,10},{7,11},{16,20},{17,21},... | collective-permute-start | bytes 1671176 | tf_op jit(solution)/shard_map/ppermute | solution.py:412
  130.3 28.6 %copy-start.3 = (f32[16,512]{1,0:T(8,128)S(1)}, f32[16,512]{1,0:T(8,128)}, u32[]{:S(2)}) copy-start(f32[16,512]{1,0:T(8,128)} %get-tuple-element.148.head_ref) | copy-start | bytes 98308
  130.4 28.6 %copy-start.6 = (s32[2]{0:T(128)S(1)}, s32[2]{0:T(128)}, u32[]{:S(2)}) copy-start(s32[2]{0:T(128)} %copy-done.5) | copy-start | bytes 28
  130.4 18.0 %collective-permute-start.19 = (bf16[544,512]{1,0:T(8,128)(2,1)S(1)}, bf16[544,512]{1,0:T(8,128)(2,1)S(1)}, u32[]{:S(2)}, u32[]{:S(2)}) collective-permute-start(bf16[544,512]{1,0:T(8,128)(2,1)S(1)} %get-tuple-element.151), channel_id=1, source_target_pairs={{0,4},{1,5},{2,6},{3,7},{4,8},{5,9},{6,10},{7,11},{8,12},{9,13},{1... | collective-permute-start | bytes 1671176 | tf_op jit(solution)/shard_map/ppermute | solution.py:412
  135.3 23.6 %collective-permute-start.20 = (bf16[544,512]{1,0:T(8,128)(2,1)S(1)}, bf16[544,512]{1,0:T(8,128)(2,1)S(1)}, u32[]{:S(2)}, u32[]{:S(2)}) collective-permute-start(bf16[544,512]{1,0:T(8,128)(2,1)S(1)} %get-tuple-element.152), channel_id=1, source_target_pairs={{4,0},{5,1},{6,2},{7,3},{8,4},{9,5},{10,6},{11,7},{12,8},{13,9},{1... | collective-permute-start | bytes 1671176 | tf_op jit(solution)/shard_map/ppermute | solution.py:416
  160.9 3.4 %collective-permute-start.21 = (bf16[160,512]{1,0:T(8,128)(2,1)S(1)}, bf16[160,512]{1,0:T(8,128)(2,1)S(1)}, u32[]{:S(2)}, u32[]{:S(2)}) collective-permute-start(bf16[160,512]{1,0:T(8,128)(2,1)S(1)} %get-tuple-element.154), channel_id=1, source_target_pairs={{0,1},{1,0},{2,3},{3,2},{4,5},{5,4},{6,7},{7,6},{8,9},{9,8},{10,11... | collective-permute-start | bytes 491528 | tf_op jit(solution)/shard_map/ppermute | solution.py:408
  161.0 7.1 %collective-permute-start.22 = (bf16[160,512]{1,0:T(8,128)(2,1)S(1)}, bf16[160,512]{1,0:T(8,128)(2,1)S(1)}, u32[]{:S(2)}, u32[]{:S(2)}) collective-permute-start(bf16[160,512]{1,0:T(8,128)(2,1)S(1)} %get-tuple-element.155), channel_id=1, source_target_pairs={{0,2},{1,3},{2,0},{3,1},{4,6},{5,7},{6,4},{7,5},{8,10},{9,11},{10,... | collective-permute-start | bytes 491528 | tf_op jit(solution)/shard_map/ppermute | solution.py:408
  162.5 8.1 %collective-permute-start.23 = (bf16[160,512]{1,0:T(8,128)(2,1)S(1)}, bf16[160,512]{1,0:T(8,128)(2,1)S(1)}, u32[]{:S(2)}, u32[]{:S(2)}) collective-permute-start(bf16[160,512]{1,0:T(8,128)(2,1)S(1)} %get-tuple-element.156), channel_id=1, source_target_pairs={{0,3},{1,2},{2,1},{3,0},{4,7},{5,6},{6,5},{7,4},{8,11},{9,10},{10,... | collective-permute-start | bytes 491528 | tf_op jit(solution)/shard_map/ppermute | solution.py:408
  (15 other events, 89.0 us)

commit v4 on v3

--- a/solution.py
+++ b/solution.py
@@ -14,6 +14,7 @@
 F32 = jnp.float32
 BF16 = jnp.bfloat16
 LANES = 128
+HALVES = 2
 HALF = 16
 MIB = 1024 * 1024
 CHEAP = pl.CostEstimate(flops=1, bytes_accessed=1, transcendentals=0)
@@ -162,56 +163,79 @@
     )(*xs, gain)
 
 
-def hidden_kernel(line, nact, packed, given, layout, where_ref, *refs):
-    count = 1 if given else 2 * line - 3
-    weights, refs = refs[:count], refs[count:]
-    n_x = 1 + max(p[0] for pieces in layout for p in pieces)
-    n_normed = 1 + max(p[1] for pieces in layout for p in pieces)
-    xq_refs, refs = refs[:n_x], refs[n_x:]
-    normed_refs, refs = refs[:n_normed], refs[n_normed:]
-    row_ref, hw_ref, high_ref, sums_ref, send_ref = refs[:5]
-    w_ref = weights[0] if given else refs[5]
-    sorted_ref = refs[-1]
+def early_kernel(line, pieces, where_ref, *refs):
+    blocks, refs = refs[:3], refs[3:]
+    xq_refs, normed_refs, (sum_ref, pair_ref) = refs[:pieces], refs[pieces:-2], refs[-2:]
+    z = where_ref[1]
+    slab = blocks[0].shape[0] - HALF
+    at = 0
+    for xq, normed in zip(xq_refs, normed_refs):
+        rows = xq.shape[0]
+        total = xq[...].astype(F32)
+        for block, step in zip(blocks, (0, line - 1, 1)):
+            place = pl.multiple_of(lax.rem(z + step, line) * slab, slab)
+            total = total + dot(normed[:, pl.ds(place, slab)], block[:slab, :])
+        sum_ref[at : at + rows, :] = total
+        at += rows
+    pair = jnp.zeros(pair_ref.shape, F32)
+    for block in blocks:
+        pair = pair + block[slab:, :LANES].astype(F32)
+    pair_ref[...] = pair
+
+
+def hidden_kernel(line, nact, packed, layout, where_ref, *refs):
+    late = len(layout[0][0]) == 4
+    n_x = 1 + max(index for pieces in layout for index, *_ in pieces)
+    js = line - 3
+    blocks, refs = refs[: 2 * js], refs[2 * js :]
+    if late:
+        near, refs = refs[:3], refs[3:]
+        w_ref, refs = refs[-1], refs[:-1]
+    else:
+        early_ref, pair_ref, refs = refs[0], refs[1], refs[2:]
+    n_columns = len(refs) - 6
+    columns, refs = refs[:n_columns], refs[n_columns:]
+    row_ref, hw_ref, high_ref, sums_ref, send_ref, sorted_ref = refs
     z = where_ref[1]
     members = len(layout)
     rows = high_ref.shape[0] // members
-    slab = w_ref.shape[0] // line
-
-    if not given:
-        own, fwd, bwd = weights[0], weights[1 : line - 1], weights[line - 1 :]
-        w_ref[pl.ds(pl.multiple_of(z * slab, slab), slab), :] = own[:slab, :]
-        for j in range(1, line):
+    slab = blocks[0].shape[0] - HALF
+
+    def far_block(j):
+        return jnp.where(z >= j, blocks[j - 2][:slab, :], blocks[js + line - j - 2][:slab, :])
+
+    if late:
+        for j in range(line):
             place = pl.multiple_of(lax.rem(z - j + line, line) * slab, slab)
-            if j == 1:
-                block = fwd[0][:slab, :]
-            elif j == line - 1:
-                block = bwd[0][:slab, :]
-            else:
-                block = jnp.where(z >= j, fwd[j - 1][:slab, :], bwd[line - j - 1][:slab, :])
-            w_ref[pl.ds(place, slab), :] = block
+            nearest = j in (0, 1, line - 1)
+            w_ref[pl.ds(place, slab), :] = near[min(j, 2)][:slab, :] if nearest else far_block(j)
 
     for m, pieces in enumerate(layout):
         at = m * rows
-        for x, normed, first, size in pieces:
-            piece = dot(normed_refs[normed][first : first + size, :], w_ref[...])
-            sorted_ref[at : at + size, :] = piece + xq_refs[x][...].astype(F32)
+        for index, size, *place in pieces:
+            if late:
+                normed = columns[n_x + place[0]][place[1] : place[1] + size, :]
+                total = columns[index][...].astype(F32) + dot(normed, w_ref[...])
+            else:
+                total = early_ref[at : at + size, :]
+                for j in range(2, line - 1):
+                    total = total + dot(columns[index * js + j - 2][...], far_block(j))
+            sorted_ref[at : at + size, :] = total
             at += size
         here = slice(m * rows, (m + 1) * rows)
         hidden = sorted_ref[here, :]
         high, low = split(hidden)
         high_ref[here, :] = high
-        heads = dot(high, hw_ref[...]) + dot(low, hw_ref[...])
+        heads = dot_t(high, hw_ref[...]) + dot_t(low, hw_ref[...])
         lane = lax.broadcasted_iota(jnp.int32, heads.shape, 1)
         square = jnp.sum(hidden * hidden, 1, keepdims=True)
         sums = jnp.where(lane == nact + 1, square, heads).T[:HALF]
-        if not given:
-            pair = jnp.zeros((HALF, LANES), F32)
-            for ref in weights:
-                pair = pair + ref[slab:, :LANES].astype(F32)
-            pair = jnp.concatenate([pair[:1], jnp.zeros((1, rows - LANES), F32)], 1)
-            row = lax.broadcasted_iota(jnp.int32, sums.shape, 0)
-            sums = jnp.where(row == nact + 2, pair, sums)
-        sums_ref[:, here] = sums
+        pair = jnp.zeros((HALF, LANES), F32) if late else pair_ref[...]
+        for ref in (*near, *blocks) if late else blocks:
+            pair = pair + ref[slab:, :LANES].astype(F32)
+        pair = jnp.concatenate([pair[:1], jnp.zeros((1, rows - LANES), F32)], 1)
+        row = lax.broadcasted_iota(jnp.int32, sums.shape, 0)
+        sums_ref[:, here] = jnp.where(row == nact + 2, pair, sums)
         slot = row_ref[HALF + nact : HALF + nact + 1, here].astype(F32) * 256.0
         slot = slot + row_ref[HALF + nact + 1 : HALF + nact + 2, here].astype(F32)
         slot = slot.astype(jnp.int32)
@@ -231,7 +255,7 @@
             ).astype(BF16)
 
 
-def rest_kernel(line, team, nact, width, total_rows, places, where_ref, *refs):
+def rest_kernel(line, team, nact, width, total_rows, places, halves, where_ref, *refs):
     sums, refs = refs[:team], refs[team:]
     row_ref, isd_ref, *high_refs = refs[:4]
     hw_ref, *turned_refs = refs[4:10]
@@ -303,16 +327,20 @@
         std = jnp.sum(std, 0, keepdims=True)
         head = jnp.where(row == nact + 1, std, head)
         head_ref[...] = head
-        for ref in firsts:
-            ref[slab:, :] = jnp.concatenate(split(head), 0)
+        for i, ref in enumerate(firsts):
+            cols = ref.shape[1]
+            h = i % halves
+            ref[slab:, :] = head[:, h * cols : (h + 1) * cols].astype(BF16)
 
     grad = dot(jnp.concatenate([ref[...] for ref in turned_refs], 1), ghid_ref[...])
     grad_ref[...] = grad
-    for ref, index in zip(firsts, first_blocks(line)):
+    for i, index in enumerate(first_blocks(line)):
 
         @pl.when(step == index)
-        def _(ref=ref):
-            ref[:slab, :] = grad.astype(BF16)
+        def _(i=i):
+            for h, ref in enumerate(firsts[i * halves : (i + 1) * halves]):
+                cols = ref.shape[1]
+                ref[:slab, :] = grad[:, h * cols : (h + 1) * cols].astype(BF16)
 
 
 def first_blocks(line):
@@ -324,11 +352,7 @@
     for mine, got, send in zip(refs[:2], refs[2:4], refs[4:]):
         slab = mine.shape[0]
         send[:slab, :] = (mine[...] + got[:slab, :].astype(F32)).astype(BF16)
-        send[slab:, :] = jnp.concatenate(split(head + joined(got, slab)), 0)
-
-
-def joined(ref, slab):
-    return ref[slab : slab + HALF, :].astype(F32) + ref[slab + HALF :, :].astype(F32)
+        send[slab:, :] = (head + got[slab:, :].astype(F32)).astype(BF16)
 
 
 def final_kernel(where_ref, mine_ref, head_ref, *refs):
@@ -338,31 +362,29 @@
     kr = slab // len(pieces)
     head = head_ref[...]
     for ref in got:
-        head = head + joined(ref, slab)
+        head = head + ref[slab:, :].astype(F32)
     for r, piece in enumerate(pieces):
         here = pl.ds(pl.multiple_of((q ^ r) * kr, kr), kr)
         total = mine_ref[here, :]
         for ref in got:
             total = total + ref[here, :].astype(F32)
-        if r == 0:
-            piece[:kr, :] = total
-            piece[kr:, :] = head
-        else:
-            piece[:kr, :] = total.astype(BF16)
-            piece[kr:, :] = jnp.concatenate(split(head), 0)
-
-
-def assemble_kernel(where_ref, *refs):
+        piece[:kr, :] = total.astype(piece.dtype)
+        piece[kr:, :] = head.astype(piece.dtype)
+
+
+def assemble_kernel(halves, where_ref, *refs):
     pieces, (grad_ref, head_ref, std_ref) = refs[:-3], refs[-3:]
     heads_n = head_ref.shape[0]
     q = where_ref[0]
-    kr, part = grad_ref.shape[0], pieces[0].shape[1]
-    for r, piece in enumerate(pieces):
-        here = pl.ds(pl.multiple_of((q ^ r) * part, part), part)
+    kr, cols = grad_ref.shape[0], pieces[0].shape[1]
+    team = len(pieces) // halves
+    for i, piece in enumerate(pieces):
+        h, r = i // team, i % team
+        here = pl.ds(pl.multiple_of(((q ^ r) * halves + h) * cols, cols), cols)
         grad_ref[:, here] = piece[:kr, :].astype(F32)
-        head = piece[kr:, :] if r == 0 else joined(piece, kr)
+        head = piece[kr:, :].astype(F32)
         head_ref[:, here] = head[:heads_n]
-        if r == 0:
+        if i == 0:
             std_ref[...] = head[heads_n : heads_n + 1, :LANES]
 
 
@@ -451,7 +473,6 @@
 
     hw = lax.dynamic_slice(head_weight, (q * part, 0), (part, heads_n)).T
     hw_twice = jnp.pad(hw, ((0, LANES - heads_n), (0, 0)))
-    hw_wide = hw_twice.T
     hw_twice = jnp.concatenate([hw_twice, hw_twice], 0)
     isd = jnp.pad(jnp.exp(-log_std), (0, HALF - nact))
     isd = jnp.broadcast_to(isd[:, None], (HALF, LANES))
@@ -476,9 +497,9 @@
     small_core = mate(small, 1)
     obs_late, small_core = lax.optimization_barrier((obs_late, small_core))
     normed_own, normed_core = norm([obs_late], gain), norm([x_core], gain)
-    (fs, bs, far, small, small_core, normed_own, normed_core, obs_last, hw_wide, hw_twice, isd) = (
+    (fs, bs, far, small, small_core, normed_own, normed_core, obs_last, hw_twice, isd) = (
         lax.optimization_barrier(
-            (fs, bs, far, small, small_core, normed_own, normed_core, obs_last, hw_wide, hw_twice, isd)
+            (fs, bs, far, small, small_core, normed_own, normed_core, obs_last, hw_twice, isd)
         )
     )
     small = jnp.concatenate([small, small_core], 1)
@@ -488,81 +509,129 @@
         bs.append(down(bs[-1], 1, line - j + 1))
     diag = mate(far, 1)
     late = mate(obs_last, 2)
-    normed_far, normed_diag = norm([far], gain), norm([diag], gain)
-    fs, bs, late, small, small_far, normed_far, normed_diag = lax.optimization_barrier(
-        (fs, bs, late, small, small_far, normed_far, normed_diag)
+    normed_far = norm([far], gain)
+    near_blocks = [block, fs[0], bs[0]]
+
+    def early(xs, normed):
+        size = sum(x.shape[0] for x in xs)
+        return pl.pallas_call(
+            functools.partial(early_kernel, line, len(xs)),
+            out_shape=(
+                jax.ShapeDtypeStruct((size, part), F32),
+                jax.ShapeDtypeStruct((HALF, LANES), F32),
+            ),
+            grid_spec=pltpu.PrefetchScalarGridSpec(
+                num_scalar_prefetch=1,
+                grid=(1,),
+                in_specs=[whole(block.shape)] * 3
+                + [pl.BlockSpec((x.shape[0], part), lambda i, w: (0, w[0])) for x in xs]
+                + [whole(x.shape) for x in normed],
+                out_specs=[whole((size, part)), whole((HALF, LANES))],
+            ),
+            compiler_params=params(58),
+            cost_estimate=CHEAP,
+            name="early",
+        )(where, *near_blocks, *xs, *normed)
+
+    in_columns = slab % LANES == 0
+    early_near = early([obs_late, x_core], [normed_own[0], normed_core[0]]) if in_columns else ()
+    fs, bs, late, small, small_far, normed_far, diag, early_near = lax.optimization_barrier(
+        (fs, bs, late, small, small_far, normed_far, diag, early_near)
     )
-    weights = [block] + fs + bs
+    far_blocks = fs[1:] + bs[1:]
 
     packed = per_peer % 8 == 0 and team // 2 * per_peer % 16 == 0
     some = team // 2
     some_rows = some * rows
 
-    def hidden(weights, xs, normed, layout, rowdata):
-        given = len(weights) == 1
+    def hidden(layout, rowdata, operands, specs, scratch=()):
         send_shape = (n, some * per_peer, part) if packed else (some_rows, part)
         out = pl.pallas_call(
-            functools.partial(hidden_kernel, line, nact, packed, given, layout),
+            functools.partial(hidden_kernel, line, nact, packed, layout),
             out_shape=[
                 jax.ShapeDtypeStruct((some_rows, part), BF16),
                 jax.ShapeDtypeStruct((HALF, some_rows), F32),
                 jax.ShapeDtypeStruct(send_shape, BF16),
-            ]
-            + ([] if given else [jax.ShapeDtypeStruct((width, part), BF16)]),
+            ],
             grid_spec=pltpu.PrefetchScalarGridSpec(
                 num_scalar_prefetch=1,
                 grid=(1,),
-                in_specs=[whole(weight.shape) for weight in weights]
-                + [pl.BlockSpec((x.shape[0], part), lambda i, w: (0, w[0])) for x in xs]
-                + [whole(x.shape) for x in normed]
-                + [whole((2 * HALF, some_rows)), whole((part, LANES))],
-                out_specs=[whole((some_rows, part)), whole((HALF, some_rows)), whole(send_shape)]
-                + ([] if given else [whole((width, part))]),
-                scratch_shapes=[pltpu.VMEM((some_rows, part), F32)],
+                in_specs=[whole(block.shape)] * len(far_blocks)
+                + specs
+                + [whole((2 * HALF, some_rows)), whole((LANES, part))],
+                out_specs=[whole((some_rows, part)), whole((HALF, some_rows)), whole(send_shape)],
+                scratch_shapes=[pltpu.VMEM((some_rows, part), F32), *scratch],
             ),
             compiler_params=params(58),
             cost_estimate=CHEAP,
             name="hidden",
-        )(where, *weights, *xs, *normed, rowdata, hw_wide)
+        )(where, *far_blocks, *operands, rowdata, hw_twice)
         if not packed:
-            high, sums, send, *weight = out
+            high, sums, send = out
             send = send.reshape(some, n, per_peer, part).transpose(1, 0, 2, 3)
-            return high, sums, send.reshape(n, some * per_peer, part), *weight
+            return high, sums, send.reshape(n, some * per_peer, part)
         return out
 
     def scatter(send):
         return lax.all_to_all(send, "fsdp", split_axis=0, concat_axis=0, tiled=True)
 
     small_all = jnp.concatenate([small, small_far], 1)
-    layout = [[(0, 0, 0, rows)], [(1, 1, 0, rows)]]
-    high_near, sums_near, send, weight = hidden(
-        weights, [obs_feat, x_core], [normed_own[0], normed_core[0]], layout, small
-    )
+    def at_once(layout, rowdata, xs, normed):
+        return hidden(
+            layout,
+            rowdata,
+            [*near_blocks, *xs, *normed],
+            [whole(block.shape) for block in near_blocks]
+            + [pl.BlockSpec((x.shape[0], part), lambda i, w: (0, w[0])) for x in xs]
+            + [whole(x.shape) for x in normed],
+            [pltpu.VMEM((width, part), BF16)],
+        )
+
+    normed = [normed_own[0], normed_core[0]]
+    if in_columns:
+        columns = [(x, j) for x in normed for j in range(2, line - 1)]
+        high_near, sums_near, send = hidden(
+            [[(0, rows)], [(1, rows)]],
+            small,
+            [*early_near] + [x for x, _ in columns],
+            [whole(x.shape) for x in early_near]
+            + [
+                pl.BlockSpec((rows, slab), lambda i, w, j=j: (0, lax.rem(w[1] - j + line, line)))
+                for _, j in columns
+            ],
+        )
+    else:
+        layout = [[(0, rows, 0, 0)], [(1, rows, 1, 0)]]
+        high_near, sums_near, send = at_once(layout, small, [obs_late, x_core], normed)
     recv_near = scatter(send)
     last = mate(late, 1)
-    late, last, sums_near, small_all = lax.optimization_barrier((late, last, sums_near, small_all))
+    late, last, diag, sums_near, small_all = lax.optimization_barrier(
+        (late, last, diag, sums_near, small_all)
+    )
+    normed_diag = norm([diag], gain)
     normed_last = norm([late, last], gain)
-    layout = [[(0, 0, 0, cut), (2, 2, 0, LANES)], [(1, 1, 0, cut), (3, 2, LANES, LANES)]]
-    high_far, sums_far, send, *_ = hidden(
-        [weight],
+    high_far, sums_far, send = at_once(
+        [[(0, cut, 0, 0), (2, LANES, 2, 0)], [(1, cut, 1, 0), (3, LANES, 2, LANES)]],
+        small_far,
         [far, diag, late, last],
         [normed_far[0], normed_diag[0], normed_last[0]],
-        layout,
-        small_far,
     )
     sums = jnp.concatenate([sums_near, sums_far], 1)
     sums = [mate(sums, r) for r in range(team)]
     send, recv_near = lax.optimization_barrier((send, recv_near))
     recv_far = scatter(send)
     nfirst = len(first_blocks(line))
+    halves = HALVES
+    cols = part // halves
+    message = (slab + HALF, cols)
     turned = [pair[1] for pair in (normed_own, normed_core, normed_far, normed_diag, normed_last)]
     places = [[(0, rows, 0)], [(0, rows, rows)]] + [
         [(0, cut, 2 * rows + i * cut), (cut, LANES, 2 * rows + 2 * cut + i * LANES)] for i in range(2)
     ]
     outs = pl.pallas_call(
-        functools.partial(rest_kernel, line, team, nact, width, total_rows, places),
+        functools.partial(rest_kernel, line, team, nact, width, total_rows, places, halves),
         out_shape=[jax.ShapeDtypeStruct((width, part), F32)]
-        + [jax.ShapeDtypeStruct((slab + 2 * HALF, part), BF16)] * nfirst
+        + [jax.ShapeDtypeStruct(message, BF16)] * (nfirst * halves)
         + [jax.ShapeDtypeStruct((HALF, part), F32)],
         grid_spec=pltpu.PrefetchScalarGridSpec(
             num_scalar_prefetch=1,
@@ -580,7 +649,7 @@
                 for piece in turned
             ],
             out_specs=[pl.BlockSpec((slab, part), lambda i, w: (i, 0))]
-            + [whole((slab + 2 * HALF, part))] * nfirst
+            + [whole(message)] * (nfirst * halves)
             + [whole((HALF, part))],
             scratch_shapes=[pltpu.VMEM((team_rows, part), BF16)],
         ),
@@ -590,49 +659,55 @@
     )(where, *sums, small_all, isd, high_near, high_far, hw_twice, *turned)
     grads, firsts, head = outs[0], outs[1:-1], outs[-1]
 
-    def hop(up_block, down_block, *got):
+    def hop(h, up_block, down_block, *got):
         return pl.pallas_call(
             hop_kernel,
-            out_shape=[jax.ShapeDtypeStruct((slab + 2 * HALF, part), BF16)] * 2,
+            out_shape=[jax.ShapeDtypeStruct(message, BF16)] * 2,
             grid=(1,),
             in_specs=[
-                plain((HALF, part)),
-                pl.BlockSpec((slab, part), lambda i: (up_block, 0)),
-                pl.BlockSpec((slab, part), lambda i: (down_block, 0)),
+                pl.BlockSpec((HALF, cols), lambda i: (0, h)),
+                pl.BlockSpec((slab, cols), lambda i: (up_block, h)),
+                pl.BlockSpec((slab, cols), lambda i: (down_block, h)),
             ]
-            + [plain((slab + 2 * HALF, part))] * 2,
-            out_specs=[plain((slab + 2 * HALF, part))] * 2,
+            + [plain(message)] * 2,
+            out_specs=[plain(message)] * 2,
             compiler_params=params(),
             cost_estimate=CHEAP,
             name="hop",
         )(head, grads, grads, *got)
 
-    send_f, send_b = firsts[-1], firsts[0]
+    def final(h, *got):
+        return pl.pallas_call(
+            final_kernel,
+            out_shape=[jax.ShapeDtypeStruct((kr + HALF, cols), F32)]
+            + [jax.ShapeDtypeStruct((kr + HALF, cols), BF16)] * (team - 1),
+            grid_spec=pltpu.PrefetchScalarGridSpec(
+                num_scalar_prefetch=1,
+                grid=(1,),
+                in_specs=[
+                    pl.BlockSpec((slab, cols), lambda i, w: (0, h)),
+                    pl.BlockSpec((HALF, cols), lambda i, w: (0, h)),
+                ]
+                + [whole(message)] * 2,
+                out_specs=[whole((kr + HALF, cols))] * team,
+            ),
+            compiler_params=params(),
+            cost_estimate=CHEAP,
+            name="final",
+        )(where, grads, head, *got)
+
+    got = [(firsts[h - halves], firsts[h]) for h in range(halves)]
     for k in range(line - 2, 0, -1):
-        got_f = up(send_f, 0, line - k, k == 1)
-        got_b = down(send_b, k, line, k == 1)
+        if k < line - 2:
+            got = [hop(h, k, line - k, *got[h]) for h in range(halves)]
+        got = [(up(f, 0, line - k, k == 1), down(b, k, line, k == 1)) for f, b in got]
         if k == 2:
-            got_f, got_b, recv_far = lax.optimization_barrier((got_f, got_b, recv_far))
-        if k > 1:
-            send_f, send_b = hop(k - 1, line - k + 1, got_f, got_b)
-    pieces = pl.pallas_call(
-        final_kernel,
-        out_shape=[jax.ShapeDtypeStruct((kr + HALF, part), F32)]
-        + [jax.ShapeDtypeStruct((kr + 2 * HALF, part), BF16)] * (team - 1),
-        grid_spec=pltpu.PrefetchScalarGridSpec(
-            num_scalar_prefetch=1,
-            grid=(1,),
-            in_specs=[whole((slab, part)), whole((HALF, part))]
-            + [whole((slab + 2 * HALF, part))] * 2,
-            out_specs=[whole((kr + HALF, part))] + [whole((kr + 2 * HALF, part))] * (team - 1),
-        ),
-        compiler_params=params(),
-        cost_estimate=CHEAP,
-        name="final",
-    )(where, grads, head, got_f, got_b)
-    pieces = [mate(piece, r) for r, piece in enumerate(pieces)]
+            got, recv_far = lax.optimization_barrier((got, recv_far)) if halves == 1 else (got, recv_far)
+    pieces = []
+    for h in range(halves):
+        pieces += [mate(piece, r) for r, piece in enumerate(final(h, *got[h]))]
     grad_weight, heads, std = pl.pallas_call(
-        assemble_kernel,
+        functools.partial(assemble_kernel, halves),
         out_shape=(
             jax.ShapeDtypeStruct((kr, width), F32),
             jax.ShapeDtypeStruct((heads_n, width), F32),

time: 174 us -> 164 us (0.943)
  waiting for transfers between devices: 65.3 us -> 35.3 us
  starting transfers between devices: 39.4 us -> 55.1 us
  Pallas kernels: 49.6 us -> 56 us
  local copies, waits for them, and re-layouts: 15.1 us -> 13.1 us
    ppermute x4 -> x6, waiting for transfers between devices: 36.2 us -> 6.13 us  [up(): lax.ppermute(x, 'fsdp', [(a * team + i, b * team + i) for a, b in steps f...]
    ppermute x4 -> x6, starting transfers between devices: 10.1 us -> 25.6 us  [up(): lax.ppermute(x, 'fsdp', [(a * team + i, b * team + i) for a, b in steps f...]
    pallas_call x5 -> x8, Pallas kernels: 20.2 us -> 26.4 us  [the longest x2 13 us: hidden(): pl.pallas_call(functools.partial(hidden_kernel, line, nact, packed, layou...]
    ppermute x4 -> x6, waiting for transfers between devices: 12.8 us -> 18.6 us  [down(): lax.ppermute(x, 'fsdp', [(a * team + i, b * team + i) for a, b in steps f...]
    ppermute x16 -> x19, waiting for transfers between devices: 13.5 us -> 10.4 us  [mate(): return lax.ppermute(x, 'fsdp', [(i, i ^ r) for i in range(n)]) if r else x]
    all_to_all x2, waiting for transfers between devices: 2.8 us -> 0.29 us  [scatter(): return lax.all_to_all(send, 'fsdp', split_axis=0, concat_axis=0, tiled=True)]
    ppermute x16 -> x19, starting transfers between devices: 12 us -> 13.5 us  [mate(): return lax.ppermute(x, 'fsdp', [(i, i ^ r) for i in range(n)]) if r else x]
    unnamed x44 -> x54, local copies, waits for them, and re-layouts: 4.35 us -> 2.99 us
  transfers between devices with their start and end apart: 26 -> 33, of which waited for: 12 -> 13; matrix products, arithmetic and copies ran while one was open for 7% -> 6% of each run, Pallas kernels for 21% -> 31%
where the time goes in v4:
time: 164 us; the launch traced here: 162 us
  Pallas kernels  56 us (34%)
  starting transfers between devices  55.1 us (34%)
  waiting for transfers between devices  35.3 us (22%)
  local copies, waits for them, and re-layouts  13.1 us (8%)
  other arithmetic  1.68 us (1%)
    ppermute x6, starting transfers between devices, up(): lax.ppermute(x, 'fsdp', [(a * team + i, b * team + i) for a, b in steps f...  25.6 us
    ppermute x6, waiting for transfers between devices, down(): lax.ppermute(x, 'fsdp', [(a * team + i, b * team + i) for a, b in steps f...  18.6 us
    pallas_call x5, Pallas kernels, norm(): pl.pallas_call(norm_kernel, out_shape=(jax.ShapeDtypeStruct((rows * len(x...  16.8 us
    ppermute x19, starting transfers between devices, mate(): return lax.ppermute(x, 'fsdp', [(i, i ^ r) for i in range(n)]) if r else x  13.5 us
    pallas_call x2, Pallas kernels, hidden(): pl.pallas_call(functools.partial(hidden_kernel, line, nact, packed, layou...  13 us
    all_to_all x2, starting transfers between devices, scatter(): return lax.all_to_all(send, 'fsdp', split_axis=0, concat_axis=0, tiled=True)  11.1 us
    ppermute x19, waiting for transfers between devices, mate(): return lax.ppermute(x, 'fsdp', [(i, i ^ r) for i in range(n)]) if r else x  10.4 us
    pallas_call x1, Pallas kernels, local(): pl.pallas_call(functools.partial(rest_kernel, line, team, nact, width, to...  10.2 us
  transfers between devices with their start and end apart: 33, of which 13 were waited for; matrix products, arithmetic and copies ran while one was open for 6% of the time, Pallas kernels for 31%

profile of v4, /device:TPU:0, one launch (start us, length us, event | category | flops | bytes accessed | tf_op | source)
XLA Modules:
  0.0 162.2 jit_solution(5370429417148846776)
XLA Ops:
  2.4 3.0 %collective-permute-start.2 = (bf16[128,512]{1,0:T(8,128)(2,1)S(1)}, bf16[128,512]{1,0:T(8,128)(2,1)S(1)}, u32[]{:S(2)}, u32[]{:S(2)}) collective-permute-start(bf16[128,512]{1,0:T(8,128)(2,1)S(1)} %get-tuple-element.187), channel_id=1, source_target_pairs={{0,2},{1,3},{2,0},{3,1},{4,6},{5,7},{6,4},{7,5},{8,10},{9,11},{10,... | collective-permute-start | bytes 393224 | tf_op jit(solution)/shard_map/ppermute | solution.py:430
  6.6 2.1 %small.1 = (bf16[32,384]{1,0:T(8,128)(2,1)}, bf16[16,512]{1,0:T(8,128)(2,1)}) custom-call(f32[16,24]{1,0:T(8,128)} %reward_ref.1, f32[16,25]{1,0:T(8,128)} %value_ref.1, s32[16,24]{1,0:T(8,128)} %done_ref.1, bf16[12,384]{1,0:T(8,128)(2,1)} %bitcast.83, bf16[12,384]{1,0:T(8,128)(2,1)} %bitcast.84, s32[1,384]{1,0:T(1,128)} %broadcast_in_dim.12.perm_ref), custom_call_target="tpu_custom_call" | custom-call | flops 1 | bytes 1 | tf_op jit(solution)/shard_map/small/pallas_call | solution.py:444
  8.7 2.3 %slice.57 = bf16[256,2048]{1,0:T(8,128)(2,1)} slice(bf16[384,2048]{1,0:T(8,128)(2,1)} %refs_3_), slice={[0:256], [0:2048]} | slice | bytes 2097152 | tf_op jit(solution)/shard_map/slice | solution.py:466
  14.1 1.6 %collective-permute-start.4 = (bf16[528,512]{1,0:T(8,128)(2,1)S(1)}, bf16[528,512]{1,0:T(8,128)(2,1)S(1)}, u32[]{:S(2)}, u32[]{:S(2)}) collective-permute-start(bf16[528,512]{1,0:T(8,128)(2,1)S(1)} %join.1.refs_0_.refs_2_), channel_id=1, source_target_pairs={{0,4},{1,5},{2,6},{3,7},{4,8},{5,9},{6,10},{7,11},{8,12},{9,13},{1... | collective-permute-start | bytes 1622024 | tf_op jit(solution)/shard_map/ppermute | solution.py:434
  15.8 2.2 %collective-permute-start.5 = (bf16[528,512]{1,0:T(8,128)(2,1)S(1)}, bf16[528,512]{1,0:T(8,128)(2,1)S(1)}, u32[]{:S(2)}, u32[]{:S(2)}) collective-permute-start(bf16[528,512]{1,0:T(8,128)(2,1)S(1)} %join.1.refs_0_.refs_2_), channel_id=1, source_target_pairs={{4,0},{5,1},{6,2},{7,3},{8,4},{9,5},{10,6},{11,7},{12,8},{13,9},{1... | collective-permute-start | bytes 1622024 | tf_op jit(solution)/shard_map/ppermute | solution.py:438
  18.8 4.1 %norm.6 = (bf16[384,2048]{1,0:T(8,128)(2,1)}, bf16[2048,384]{1,0:T(8,128)(2,1)}) custom-call(bf16[384,2048]{1,0:T(8,128)(2,1)} %copy-done.7, f32[1,2048]{1,0:T(1,128)} %bitcast.78), custom_call_target="tpu_custom_call" | custom-call | flops 1 | bytes 1 | tf_op jit(solution)/shard_map/norm/pallas_call | solution.py:147
  22.9 1.9 %slice.58 = bf16[128,2048]{1,0:T(8,128)(2,1)} slice(bf16[384,2048]{1,0:T(8,128)(2,1)} %refs_3_), slice={[256:384], [0:2048]} | slice | bytes 1048576 | tf_op jit(solution)/shard_map/slice | solution.py:472
  24.8 4.1 %norm.5 = (bf16[384,2048]{1,0:T(8,128)(2,1)}, bf16[2048,384]{1,0:T(8,128)(2,1)}) custom-call(bf16[384,2048]{1,0:T(8,128)(2,1)} %refs_3_, f32[1,2048]{1,0:T(1,128)} %bitcast.79), custom_call_target="tpu_custom_call" | custom-call | flops 1 | bytes 1 | tf_op jit(solution)/shard_map/norm/pallas_call | solution.py:147
  28.9 2.2 %collective-permute-done.4.refs_1_.refs_3_ = bf16[528,512]{1,0:T(8,128)(2,1)S(1)} collective-permute-done((bf16[528,512]{1,0:T(8,128)(2,1)S(1)}, bf16[528,512]{1,0:T(8,128)(2,1)S(1)}, u32[]{:S(2)}, u32[]{:S(2)}) %collective-permute-start.4) | collective-permute-done | bytes 540704 | tf_op jit(solution)/shard_map/ppermute | solution.py:434
  31.1 10.6 %collective-permute-done.5.refs_2_.refs_4_ = bf16[528,512]{1,0:T(8,128)(2,1)S(1)} collective-permute-done((bf16[528,512]{1,0:T(8,128)(2,1)S(1)}, bf16[528,512]{1,0:T(8,128)(2,1)S(1)}, u32[]{:S(2)}, u32[]{:S(2)}) %collective-permute-start.5) | collective-permute-done | bytes 540704 | tf_op jit(solution)/shard_map/ppermute | solution.py:438
  46.6 2.7 %norm.7 = (bf16[256,2048]{1,0:T(8,128)(2,1)}, bf16[2048,256]{1,0:T(8,128)(2,1)}) custom-call(bf16[256,2048]{1,0:T(8,128)(2,1)} %copy-done.8, f32[1,2048]{1,0:T(1,128)} %bitcast.80), custom_call_target="tpu_custom_call" | custom-call | flops 1 | bytes 1 | tf_op jit(solution)/shard_map/norm/pallas_call | solution.py:147
  49.3 5.9 %early.1 = (f32[768,512]{1,0:T(8,128)}, f32[16,128]{1,0:T(8,128)}) custom-call(s32[2]{0:T(128)} %copy-done.4, bf16[528,512]{1,0:T(8,128)(2,1)} %copy-done.1, bf16[528,512]{1,0:T(8,128)(2,1)} %copy-done.10, bf16[528,512]{1,0:T(8,128)(2,1)} %copy-done.11, bf16[384,2048]{1,0:T(8,128)(2,1)} %refs_3_, bf16[384,2048]{1,0:T(8,128)(2,1)} %copy-done.7, ...), custom_call_target="tpu_custom_call" | custom-call | flops 1 | bytes 1 | tf_op jit(solution)/shard_map/early/pallas_call | solution.py:517
  55.2 4.9 %collective-permute-done.11.refs_12_ = bf16[32,768]{1,0:T(8,128)(2,1)S(1)} collective-permute-done((bf16[32,768]{1,0:T(8,128)(2,1)S(1)}, bf16[32,768]{1,0:T(8,128)(2,1)S(1)}, u32[]{:S(2)}, u32[]{:S(2)}) %collective-permute-start.11) | collective-permute-done | bytes 49184 | tf_op jit(solution)/shard_map/ppermute | solution.py:430
  61.7 5.3 %hidden.2 = (bf16[768,512]{1,0:T(8,128)(2,1)}, f32[16,768]{1,0:T(8,128)}, bf16[16,48,512]{2,1,0:T(8,128)(2,1)}) custom-call(s32[2]{0:T(128)} %copy-done.4, bf16[528,512]{1,0:T(8,128)(2,1)} %copy-done.12, bf16[528,512]{1,0:T(8,128)(2,1)} %copy-done.13, f32[768,512]{1,0:T(8,128)} %get-tuple-element.122.refs_2_, f32[16,128]{1,0:T(8,128)} %get-tuple-element.123.refs_3_, ...), custom_call_target="tpu_custom_call" | custom-call | flops 1 | bytes 1 | tf_op jit(solution)/shard_map/hidden/pallas_call | solution.py:549
  67.0 5.6 %all-to-all-start = ((bf16[16,48,512]{2,1,0:T(8,128)(2,1)}), bf16[16,48,512]{2,1,0:T(8,128)(2,1)S(1)}, u32[]{:S(2)}, u32[]{:S(2)}) async-start(bf16[16,48,512]{2,1,0:T(8,128)(2,1)} %get-tuple-element.135), calls=%async_computation | async-start | bytes 1572864 | tf_op jit(solution)/shard_map/all_to_all | solution.py:576
  74.5 2.9 %norm.8 = (bf16[256,2048]{1,0:T(8,128)(2,1)}, bf16[2048,256]{1,0:T(8,128)(2,1)}) custom-call(bf16[256,2048]{1,0:T(8,128)(2,1)} %copy-done.9, f32[1,2048]{1,0:T(1,128)} %bitcast.81), custom_call_target="tpu_custom_call" | custom-call | flops 1 | bytes 1 | tf_op jit(solution)/shard_map/norm/pallas_call | solution.py:147
  77.4 3.0 %norm.9 = (bf16[256,2048]{1,0:T(8,128)(2,1)}, bf16[2048,256]{1,0:T(8,128)(2,1)}) custom-call(bf16[128,2048]{1,0:T(8,128)(2,1)} %copy-done.14, bf16[128,2048]{1,0:T(8,128)(2,1)} %copy-done.15, f32[1,2048]{1,0:T(1,128)} %bitcast.82), custom_call_target="tpu_custom_call" | custom-call | flops 1 | bytes 1 | tf_op jit(solution)/shard_map/norm/pallas_call | solution.py:147
  80.4 7.7 %hidden.3 = (bf16[768,512]{1,0:T(8,128)(2,1)}, f32[16,768]{1,0:T(8,128)}, bf16[16,48,512]{2,1,0:T(8,128)(2,1)}) custom-call(s32[2]{0:T(128)} %copy-done.4, bf16[528,512]{1,0:T(8,128)(2,1)} %copy-done.12, bf16[528,512]{1,0:T(8,128)(2,1)} %copy-done.13, bf16[528,512]{1,0:T(8,128)(2,1)} %copy-done.1, bf16[528,512]{1,0:T(8,128)(2,1)} %copy-done.10, ...), custom_call_target="tpu_custom_call" | custom-call | flops 1 | bytes 1 | tf_op jit(solution)/shard_map/hidden/pallas_call | solution.py:549
  89.3 1.7 %collective-permute-start.15 = (f32[16,1536]{1,0:T(8,128)S(1)}, f32[16,1536]{1,0:T(8,128)S(1)}, u32[]{:S(2)}, u32[]{:S(2)}) collective-permute-start(f32[16,1536]{1,0:T(8,128)S(1)} %constant_dynamic-update-slice_fusion.2.refs_0_), channel_id=1, source_target_pairs={{0,2},{1,3},{2,0},{3,1},{4,6},{5,7},{6,4},{7,5},{8,10},{9,11},{10,... | collective-permute-start | bytes 294920 | tf_op jit(solution)/shard_map/ppermute | solution.py:430
  91.2 5.5 %all-to-all-start.1 = ((bf16[16,48,512]{2,1,0:T(8,128)(2,1)}), bf16[16,48,512]{2,1,0:T(8,128)(2,1)S(1)}, u32[]{:S(2)}, u32[]{:S(2)}) async-start(bf16[16,48,512]{2,1,0:T(8,128)(2,1)} %get-tuple-element.137), calls=%async_computation.1 | async-start | bytes 1572864 | tf_op jit(solution)/shard_map/all_to_all | solution.py:576
  97.5 10.2 %rest.1 = (f32[2048,512]{1,0:T(8,128)}, bf16[528,256]{1,0:T(8,128)(2,1)}, bf16[528,256]{1,0:T(8,128)(2,1)}, f32[16,512]{1,0:T(8,128)}) custom-call(s32[2]{0:T(128)} %copy-done.4, f32[16,1536]{1,0:T(8,128)} %copy-done.20, f32[16,1536]{1,0:T(8,128)} %copy-done.22, f32[16,1536]{1,0:T(8,128)} %copy-done.23, f32[16,1536]{1,0:T(8,128)} %copy-done.24, ...), custom_call_target="tpu_custom_call" | custom-call | flops 99999997952 | bytes 100000000 | tf_op jit(solution)/shard_map/rest/pallas_call | solution.py:631
  107.7 3.8 %collective-permute-start.24 = (bf16[528,256]{1,0:T(8,128)(2,1)}, bf16[528,256]{1,0:T(8,128)(2,1)S(1)}, u32[]{:S(2)}, u32[]{:S(2)}) collective-permute-start(bf16[528,256]{1,0:T(8,128)(2,1)} %get-tuple-element.158), channel_id=1, source_target_pairs={{0,4},{1,5},{2,6},{3,7},{4,8},{5,9},{6,10},{7,11},{16,20},{17,21},... | collective-permute-start | bytes 811016 | tf_op jit(solution)/shard_map/ppermute | solution.py:434
  112.2 4.0 %collective-permute-start.17 = (bf16[528,256]{1,0:T(8,128)(2,1)}, bf16[528,256]{1,0:T(8,128)(2,1)S(1)}, u32[]{:S(2)}, u32[]{:S(2)}) collective-permute-start(bf16[528,256]{1,0:T(8,128)(2,1)} %get-tuple-element.151), channel_id=1, source_target_pairs={{0,4},{1,5},{2,6},{3,7},{4,8},{5,9},{6,10},{7,11},{16,20},{17,21},... | collective-permute-start | bytes 811016 | tf_op jit(solution)/shard_map/ppermute | solution.py:434
  116.9 1.8 %collective-permute-done.24.refs_2_ = bf16[528,256]{1,0:T(8,128)(2,1)S(1)} collective-permute-done((bf16[528,256]{1,0:T(8,128)(2,1)}, bf16[528,256]{1,0:T(8,128)(2,1)S(1)}, u32[]{:S(2)}, u32[]{:S(2)}) %collective-permute-start.24) | collective-permute-done | bytes 270368 | tf_op jit(solution)/shard_map/ppermute | solution.py:434
  120.7 6.0 %collective-permute-start.26 = (bf16[528,256]{1,0:T(8,128)(2,1)S(1)}, bf16[528,256]{1,0:T(8,128)(2,1)S(1)}, u32[]{:S(2)}, u32[]{:S(2)}) collective-permute-start(bf16[528,256]{1,0:T(8,128)(2,1)S(1)} %get-tuple-element.159), channel_id=1, source_target_pairs={{0,4},{1,5},{2,6},{3,7},{4,8},{5,9},{6,10},{7,11},{8,12},{9,13},{1... | collective-permute-start | bytes 811016 | tf_op jit(solution)/shard_map/ppermute | solution.py:434
  128.0 9.5 %collective-permute-start.19 = (bf16[528,256]{1,0:T(8,128)(2,1)S(1)}, bf16[528,256]{1,0:T(8,128)(2,1)S(1)}, u32[]{:S(2)}, u32[]{:S(2)}) collective-permute-start(bf16[528,256]{1,0:T(8,128)(2,1)S(1)} %get-tuple-element.152), channel_id=1, source_target_pairs={{0,4},{1,5},{2,6},{3,7},{4,8},{5,9},{6,10},{7,11},{8,12},{9,13},{1... | collective-permute-start | bytes 811016 | tf_op jit(solution)/shard_map/ppermute | solution.py:434
  137.5 2.7 %collective-permute-done.27.refs_1_ = bf16[528,256]{1,0:T(8,128)(2,1)S(1)} collective-permute-done((bf16[528,256]{1,0:T(8,128)(2,1)S(1)}, bf16[528,256]{1,0:T(8,128)(2,1)S(1)}, u32[]{:S(2)}, u32[]{:S(2)}) %collective-permute-start.27) | collective-permute-done | bytes 270368 | tf_op jit(solution)/shard_map/ppermute | solution.py:438
  140.3 1.7 %final.3 = (f32[144,256]{1,0:T(8,128)S(1)}, bf16[144,256]{1,0:T(8,128)(2,1)S(1)}, bf16[144,256]{1,0:T(8,128)(2,1)S(1)}, bf16[144,256]{1,0:T(8,128)(2,1)S(1)}) custom-call(s32[2]{0:T(128)S(1)} %copy-done.5, f32[2048,512]{1,0:T(8,128)} %get-tuple-element.149.refs_0_.refs_1_.mine_ref, f32[16,512]{1,0:T(8,128)S(1)} %copy-done.3, ...), custom_call_target="tpu_custom_call" | custom-call | flops 1 | bytes 1 | tf_op jit(solution)/shard_map/final/pallas_call | solution.py:680
  143.9 2.2 %collective-permute-done.19.refs_0_ = bf16[528,256]{1,0:T(8,128)(2,1)S(1)} collective-permute-done((bf16[528,256]{1,0:T(8,128)(2,1)S(1)}, bf16[528,256]{1,0:T(8,128)(2,1)S(1)}, u32[]{:S(2)}, u32[]{:S(2)}) %collective-permute-start.19) | collective-permute-done | bytes 270368 | tf_op jit(solution)/shard_map/ppermute | solution.py:434
  146.1 4.5 %collective-permute-done.20.refs_1_ = bf16[528,256]{1,0:T(8,128)(2,1)S(1)} collective-permute-done((bf16[528,256]{1,0:T(8,128)(2,1)S(1)}, bf16[528,256]{1,0:T(8,128)(2,1)S(1)}, u32[]{:S(2)}, u32[]{:S(2)}) %collective-permute-start.20) | collective-permute-done | bytes 270368 | tf_op jit(solution)/shard_map/ppermute | solution.py:438
  150.6 1.7 %final.2 = (f32[144,256]{1,0:T(8,128)S(1)}, bf16[144,256]{1,0:T(8,128)(2,1)S(1)}, bf16[144,256]{1,0:T(8,128)(2,1)S(1)}, bf16[144,256]{1,0:T(8,128)(2,1)S(1)}) custom-call(s32[2]{0:T(128)S(1)} %copy-done.5, f32[2048,512]{1,0:T(8,128)} %get-tuple-element.149.refs_0_.refs_1_.mine_ref, f32[16,512]{1,0:T(8,128)S(1)} %copy-done.3, ...), custom_call_target="tpu_custom_call" | custom-call | flops 1 | bytes 1 | tf_op jit(solution)/shard_map/final/pallas_call | solution.py:680
  154.3 3.0 %collective-permute-done.22.refs_2_ = bf16[144,256]{1,0:T(8,128)(2,1)S(1)} collective-permute-done((bf16[144,256]{1,0:T(8,128)(2,1)S(1)}, bf16[144,256]{1,0:T(8,128)(2,1)S(1)}, u32[]{:S(2)}, u32[]{:S(2)}) %collective-permute-start.22) | collective-permute-done | bytes 73760 | tf_op jit(solution)/shard_map/ppermute | solution.py:430
  (123 shorter events, 31.0 us)
Async XLA Ops:
  0.7 10.7 %collective-permute-start = (bf16[384,2048]{1,0:T(8,128)(2,1)}, bf16[384,2048]{1,0:T(8,128)(2,1)S(1)}, u32[]{:S(2)}, u32[]{:S(2)}) collective-permute-start(bf16[384,2048]{1,0:T(8,128)(2,1)} %refs_3_), channel_id=1, source_target_pairs={{0,1},{1,0},{2,3},{3,2},{4,5},{5,4},{6,7},{7,6},{8,9},{9,8},{10,11... | collective-permute-start | bytes 4718600 | tf_op jit(solution)/shard_map/ppermute | solution.py:430
  2.3 8.8 %collective-permute-start.1 = (bf16[128,512]{1,0:T(8,128)(2,1)S(1)}, bf16[128,512]{1,0:T(8,128)(2,1)S(1)}, u32[]{:S(2)}, u32[]{:S(2)}) collective-permute-start(bf16[128,512]{1,0:T(8,128)(2,1)S(1)} %get-tuple-element.185), channel_id=1, source_target_pairs={{0,1},{1,0},{2,3},{3,2},{4,5},{5,4},{6,7},{7,6},{8,9},{9,8},{10,11... | collective-permute-start | bytes 393224 | tf_op jit(solution)/shard_map/ppermute | solution.py:430
  2.4 8.7 %collective-permute-start.2 = (bf16[128,512]{1,0:T(8,128)(2,1)S(1)}, bf16[128,512]{1,0:T(8,128)(2,1)S(1)}, u32[]{:S(2)}, u32[]{:S(2)}) collective-permute-start(bf16[128,512]{1,0:T(8,128)(2,1)S(1)} %get-tuple-element.187), channel_id=1, source_target_pairs={{0,2},{1,3},{2,0},{3,1},{4,6},{5,7},{6,4},{7,5},{8,10},{9,11},{10,... | collective-permute-start | bytes 393224 | tf_op jit(solution)/shard_map/ppermute | solution.py:430
  5.4 6.0 %collective-permute-start.3 = (bf16[128,512]{1,0:T(8,128)(2,1)S(1)}, bf16[128,512]{1,0:T(8,128)(2,1)S(1)}, u32[]{:S(2)}, u32[]{:S(2)}) collective-permute-start(bf16[128,512]{1,0:T(8,128)(2,1)S(1)} %get-tuple-element.184), channel_id=1, source_target_pairs={{0,3},{1,2},{2,1},{3,0},{4,7},{5,6},{6,5},{7,4},{8,11},{9,10},{10,... | collective-permute-start | bytes 393224 | tf_op jit(solution)/shard_map/ppermute | solution.py:430
  11.4 30.3 %collective-permute-start.6 = (bf16[256,2048]{1,0:T(8,128)(2,1)}, bf16[256,2048]{1,0:T(8,128)(2,1)S(1)}, u32[]{:S(2)}, u32[]{:S(2)}) collective-permute-start(bf16[256,2048]{1,0:T(8,128)(2,1)} %slice.57), channel_id=1, source_target_pairs={{0,2},{1,3},{2,0},{3,1},{4,6},{5,7},{6,4},{7,5},{8,10},{9,11},{10,... | collective-permute-start | bytes 3145736 | tf_op jit(solution)/shard_map/ppermute | solution.py:430
  14.1 17.0 %collective-permute-start.4 = (bf16[528,512]{1,0:T(8,128)(2,1)S(1)}, bf16[528,512]{1,0:T(8,128)(2,1)S(1)}, u32[]{:S(2)}, u32[]{:S(2)}) collective-permute-start(bf16[528,512]{1,0:T(8,128)(2,1)S(1)} %join.1.refs_0_.refs_2_), channel_id=1, source_target_pairs={{0,4},{1,5},{2,6},{3,7},{4,8},{5,9},{6,10},{7,11},{8,12},{9,13},{1... | collective-permute-start | bytes 1622024 | tf_op jit(solution)/shard_map/ppermute | solution.py:434
  15.8 25.9 %collective-permute-start.5 = (bf16[528,512]{1,0:T(8,128)(2,1)S(1)}, bf16[528,512]{1,0:T(8,128)(2,1)S(1)}, u32[]{:S(2)}, u32[]{:S(2)}) collective-permute-start(bf16[528,512]{1,0:T(8,128)(2,1)S(1)} %join.1.refs_0_.refs_2_), channel_id=1, source_target_pairs={{4,0},{5,1},{6,2},{7,3},{8,4},{9,5},{10,6},{11,7},{12,8},{13,9},{1... | collective-permute-start | bytes 1622024 | tf_op jit(solution)/shard_map/ppermute | solution.py:438
  18.0 6.8 %collective-permute-start.7 = (bf16[32,384]{1,0:T(8,128)(2,1)S(1)}, bf16[32,384]{1,0:T(8,128)(2,1)S(1)}, u32[]{:S(2)}, u32[]{:S(2)}) collective-permute-start(bf16[32,384]{1,0:T(8,128)(2,1)S(1)} %copy-done.21), channel_id=1, source_target_pairs={{0,1},{1,0},{2,3},{3,2},{4,5},{5,4},{6,7},{7,6},{8,9},{9,8},{10,11... | collective-permute-start | bytes 73736 | tf_op jit(solution)/shard_map/ppermute | solution.py:430
  42.5 18.4 %collective-permute-start.12 = (bf16[256,2048]{1,0:T(8,128)(2,1)S(1)}, bf16[256,2048]{1,0:T(8,128)(2,1)S(1)}, u32[]{:S(2)}, u32[]{:S(2)}) collective-permute-start(bf16[256,2048]{1,0:T(8,128)(2,1)S(1)} %collective-permute-done.6.refs_0_.refs_5_), channel_id=1, source_target_pairs={{0,1},{1,0},{2,3},{3,2},{4,5},{5,4},{6,7},{7,6},{8,9},{9,8},{10,11... | collective-permute-start | bytes 3145736 | tf_op jit(solution)/shard_map/ppermute | solution.py:430
  42.5 17.7 %collective-permute-start.8 = (bf16[528,512]{1,0:T(8,128)(2,1)S(1)}, bf16[528,512]{1,0:T(8,128)(2,1)S(1)}, u32[]{:S(2)}, u32[]{:S(2)}) collective-permute-start(bf16[528,512]{1,0:T(8,128)(2,1)S(1)} %collective-permute-done.4.refs_1_.refs_3_), channel_id=1, source_target_pairs={{4,8},{5,9},{6,10},{7,11},{8,12},{9,13},{10,14},{11,15},{20,24},{2... | collective-permute-start | bytes 1622024 | tf_op jit(solution)/shard_map/ppermute | solution.py:434
  43.2 17.7 %collective-permute-start.9 = (bf16[528,512]{1,0:T(8,128)(2,1)S(1)}, bf16[528,512]{1,0:T(8,128)(2,1)S(1)}, u32[]{:S(2)}, u32[]{:S(2)}) collective-permute-start(bf16[528,512]{1,0:T(8,128)(2,1)S(1)} %collective-permute-done.5.refs_2_.refs_4_), channel_id=1, source_target_pairs={{4,0},{5,1},{6,2},{7,3},{8,4},{9,5},{10,6},{11,7},{20,16},{21,17},... | collective-permute-start | bytes 1622024 | tf_op jit(solution)/shard_map/ppermute | solution.py:438
  44.5 15.7 %collective-permute-start.10 = (bf16[128,2048]{1,0:T(8,128)(2,1)}, bf16[128,2048]{1,0:T(8,128)(2,1)S(1)}, u32[]{:S(2)}, u32[]{:S(2)}) collective-permute-start(bf16[128,2048]{1,0:T(8,128)(2,1)} %slice.58), channel_id=1, source_target_pairs={{0,2},{1,3},{2,0},{3,1},{4,6},{5,7},{6,4},{7,5},{8,10},{9,11},{10,... | collective-permute-start | bytes 1572872 | tf_op jit(solution)/shard_map/ppermute | solution.py:430
  45.1 15.0 %collective-permute-start.11 = (bf16[32,768]{1,0:T(8,128)(2,1)S(1)}, bf16[32,768]{1,0:T(8,128)(2,1)S(1)}, u32[]{:S(2)}, u32[]{:S(2)}) collective-permute-start(bf16[32,768]{1,0:T(8,128)(2,1)S(1)} %constant_dynamic-update-slice_fusion.refs_6_), channel_id=1, source_target_pairs={{0,2},{1,3},{2,0},{3,1},{4,6},{5,7},{6,4},{7,5},{8,10},{9,11},{10,... | collective-permute-start | bytes 147464 | tf_op jit(solution)/shard_map/ppermute | solution.py:430
  67.0 24.3 %all-to-all-start = ((bf16[16,48,512]{2,1,0:T(8,128)(2,1)}), bf16[16,48,512]{2,1,0:T(8,128)(2,1)S(1)}, u32[]{:S(2)}, u32[]{:S(2)}) async-start(bf16[16,48,512]{2,1,0:T(8,128)(2,1)} %get-tuple-element.135), calls=%async_computation | async-start | bytes 1572864 | tf_op jit(solution)/shard_map/all_to_all | solution.py:576
  72.5 2.0 %collective-permute-start.13 = (bf16[128,2048]{1,0:T(8,128)(2,1)S(1)}, bf16[128,2048]{1,0:T(8,128)(2,1)S(1)}, u32[]{:S(2)}, u32[]{:S(2)}) collective-permute-start(bf16[128,2048]{1,0:T(8,128)(2,1)S(1)} %collective-permute-done.10.refs_0_.refs_7_), channel_id=1, source_target_pairs={{0,1},{1,0},{2,3},{3,2},{4,5},{5,4},{6,7},{7,6},{8,9},{9,8},{10,11... | collective-permute-start | bytes 1572872 | tf_op jit(solution)/shard_map/ppermute | solution.py:430
  88.9 7.9 %collective-permute-start.14 = (f32[16,1536]{1,0:T(8,128)S(1)}, f32[16,1536]{1,0:T(8,128)S(1)}, u32[]{:S(2)}, u32[]{:S(2)}) collective-permute-start(f32[16,1536]{1,0:T(8,128)S(1)} %constant_dynamic-update-slice_fusion.2.refs_0_), channel_id=1, source_target_pairs={{0,1},{1,0},{2,3},{3,2},{4,5},{5,4},{6,7},{7,6},{8,9},{9,8},{10,11... | collective-permute-start | bytes 294920 | tf_op jit(solution)/shard_map/ppermute | solution.py:430
  89.3 7.5 %collective-permute-start.15 = (f32[16,1536]{1,0:T(8,128)S(1)}, f32[16,1536]{1,0:T(8,128)S(1)}, u32[]{:S(2)}, u32[]{:S(2)}) collective-permute-start(f32[16,1536]{1,0:T(8,128)S(1)} %constant_dynamic-update-slice_fusion.2.refs_0_), channel_id=1, source_target_pairs={{0,2},{1,3},{2,0},{3,1},{4,6},{5,7},{6,4},{7,5},{8,10},{9,11},{10,... | collective-permute-start | bytes 294920 | tf_op jit(solution)/shard_map/ppermute | solution.py:430
  91.0 5.9 %collective-permute-start.16 = (f32[16,1536]{1,0:T(8,128)S(1)}, f32[16,1536]{1,0:T(8,128)S(1)}, u32[]{:S(2)}, u32[]{:S(2)}) collective-permute-start(f32[16,1536]{1,0:T(8,128)S(1)} %constant_dynamic-update-slice_fusion.2.refs_0_), channel_id=1, source_target_pairs={{0,3},{1,2},{2,1},{3,0},{4,7},{5,6},{6,5},{7,4},{8,11},{9,10},{10,... | collective-permute-start | bytes 294920 | tf_op jit(solution)/shard_map/ppermute | solution.py:430
  91.2 69.4 %all-to-all-start.1 = ((bf16[16,48,512]{2,1,0:T(8,128)(2,1)}), bf16[16,48,512]{2,1,0:T(8,128)(2,1)S(1)}, u32[]{:S(2)}, u32[]{:S(2)}) async-start(bf16[16,48,512]{2,1,0:T(8,128)(2,1)} %get-tuple-element.137), calls=%async_computation.1 | async-start | bytes 1572864 | tf_op jit(solution)/shard_map/all_to_all | solution.py:576
  107.7 11.0 %collective-permute-start.24 = (bf16[528,256]{1,0:T(8,128)(2,1)}, bf16[528,256]{1,0:T(8,128)(2,1)S(1)}, u32[]{:S(2)}, u32[]{:S(2)}) collective-permute-start(bf16[528,256]{1,0:T(8,128)(2,1)} %get-tuple-element.158), channel_id=1, source_target_pairs={{0,4},{1,5},{2,6},{3,7},{4,8},{5,9},{6,10},{7,11},{16,20},{17,21},... | collective-permute-start | bytes 811016 | tf_op jit(solution)/shard_map/ppermute | solution.py:434
  111.5 7.1 %collective-permute-start.25 = (bf16[528,256]{1,0:T(8,128)(2,1)}, bf16[528,256]{1,0:T(8,128)(2,1)S(1)}, u32[]{:S(2)}, u32[]{:S(2)}) collective-permute-start(bf16[528,256]{1,0:T(8,128)(2,1)} %get-tuple-element.158), channel_id=1, source_target_pairs={{8,4},{9,5},{10,6},{11,7},{12,8},{13,9},{14,10},{15,11},{24,20},{2... | collective-permute-start | bytes 811016 | tf_op jit(solution)/shard_map/ppermute | solution.py:438
  112.2 14.5 %collective-permute-start.17 = (bf16[528,256]{1,0:T(8,128)(2,1)}, bf16[528,256]{1,0:T(8,128)(2,1)S(1)}, u32[]{:S(2)}, u32[]{:S(2)}) collective-permute-start(bf16[528,256]{1,0:T(8,128)(2,1)} %get-tuple-element.151), channel_id=1, source_target_pairs={{0,4},{1,5},{2,6},{3,7},{4,8},{5,9},{6,10},{7,11},{16,20},{17,21},... | collective-permute-start | bytes 811016 | tf_op jit(solution)/shard_map/ppermute | solution.py:434
  116.2 10.5 %collective-permute-start.18 = (bf16[528,256]{1,0:T(8,128)(2,1)}, bf16[528,256]{1,0:T(8,128)(2,1)S(1)}, u32[]{:S(2)}, u32[]{:S(2)}) collective-permute-start(bf16[528,256]{1,0:T(8,128)(2,1)} %get-tuple-element.151), channel_id=1, source_target_pairs={{8,4},{9,5},{10,6},{11,7},{12,8},{13,9},{14,10},{15,11},{24,20},{2... | collective-permute-start | bytes 811016 | tf_op jit(solution)/shard_map/ppermute | solution.py:438
  120.7 16.8 %collective-permute-start.26 = (bf16[528,256]{1,0:T(8,128)(2,1)S(1)}, bf16[528,256]{1,0:T(8,128)(2,1)S(1)}, u32[]{:S(2)}, u32[]{:S(2)}) collective-permute-start(bf16[528,256]{1,0:T(8,128)(2,1)S(1)} %get-tuple-element.159), channel_id=1, source_target_pairs={{0,4},{1,5},{2,6},{3,7},{4,8},{5,9},{6,10},{7,11},{8,12},{9,13},{1... | collective-permute-start | bytes 811016 | tf_op jit(solution)/shard_map/ppermute | solution.py:434
  126.7 13.6 %collective-permute-start.27 = (bf16[528,256]{1,0:T(8,128)(2,1)S(1)}, bf16[528,256]{1,0:T(8,128)(2,1)S(1)}, u32[]{:S(2)}, u32[]{:S(2)}) collective-permute-start(bf16[528,256]{1,0:T(8,128)(2,1)S(1)} %get-tuple-element.160), channel_id=1, source_target_pairs={{4,0},{5,1},{6,2},{7,3},{8,4},{9,5},{10,6},{11,7},{12,8},{13,9},{1... | collective-permute-start | bytes 811016 | tf_op jit(solution)/shard_map/ppermute | solution.py:438
  128.0 18.0 %collective-permute-start.19 = (bf16[528,256]{1,0:T(8,128)(2,1)S(1)}, bf16[528,256]{1,0:T(8,128)(2,1)S(1)}, u32[]{:S(2)}, u32[]{:S(2)}) collective-permute-start(bf16[528,256]{1,0:T(8,128)(2,1)S(1)} %get-tuple-element.152), channel_id=1, source_target_pairs={{0,4},{1,5},{2,6},{3,7},{4,8},{5,9},{6,10},{7,11},{8,12},{9,13},{1... | collective-permute-start | bytes 811016 | tf_op jit(solution)/shard_map/ppermute | solution.py:434
  137.5 13.1 %collective-permute-start.20 = (bf16[528,256]{1,0:T(8,128)(2,1)S(1)}, bf16[528,256]{1,0:T(8,128)(2,1)S(1)}, u32[]{:S(2)}, u32[]{:S(2)}) collective-permute-start(bf16[528,256]{1,0:T(8,128)(2,1)S(1)} %get-tuple-element.153), channel_id=1, source_target_pairs={{4,0},{5,1},{6,2},{7,3},{8,4},{9,5},{10,6},{11,7},{12,8},{13,9},{1... | collective-permute-start | bytes 811016 | tf_op jit(solution)/shard_map/ppermute | solution.py:438
  141.9 12.0 %collective-permute-start.28 = (bf16[144,256]{1,0:T(8,128)(2,1)S(1)}, bf16[144,256]{1,0:T(8,128)(2,1)S(1)}, u32[]{:S(2)}, u32[]{:S(2)}) collective-permute-start(bf16[144,256]{1,0:T(8,128)(2,1)S(1)} %get-tuple-element.162), channel_id=1, source_target_pairs={{0,1},{1,0},{2,3},{3,2},{4,5},{5,4},{6,7},{7,6},{8,9},{9,8},{10,11... | collective-permute-start | bytes 221192 | tf_op jit(solution)/shard_map/ppermute | solution.py:430
  142.0 12.2 %collective-permute-start.29 = (bf16[144,256]{1,0:T(8,128)(2,1)S(1)}, bf16[144,256]{1,0:T(8,128)(2,1)S(1)}, u32[]{:S(2)}, u32[]{:S(2)}) collective-permute-start(bf16[144,256]{1,0:T(8,128)(2,1)S(1)} %get-tuple-element.163), channel_id=1, source_target_pairs={{0,2},{1,3},{2,0},{3,1},{4,6},{5,7},{6,4},{7,5},{8,10},{9,11},{10,... | collective-permute-start | bytes 221192 | tf_op jit(solution)/shard_map/ppermute | solution.py:430
  143.6 10.7 %collective-permute-start.30 = (bf16[144,256]{1,0:T(8,128)(2,1)S(1)}, bf16[144,256]{1,0:T(8,128)(2,1)S(1)}, u32[]{:S(2)}, u32[]{:S(2)}) collective-permute-start(bf16[144,256]{1,0:T(8,128)(2,1)S(1)} %get-tuple-element.164), channel_id=1, source_target_pairs={{0,3},{1,2},{2,1},{3,0},{4,7},{5,6},{6,5},{7,4},{8,11},{9,10},{10,... | collective-permute-start | bytes 221192 | tf_op jit(solution)/shard_map/ppermute | solution.py:430
  152.4 4.9 %collective-permute-start.22 = (bf16[144,256]{1,0:T(8,128)(2,1)S(1)}, bf16[144,256]{1,0:T(8,128)(2,1)S(1)}, u32[]{:S(2)}, u32[]{:S(2)}) collective-permute-start(bf16[144,256]{1,0:T(8,128)(2,1)S(1)} %get-tuple-element.156), channel_id=1, source_target_pairs={{0,2},{1,3},{2,0},{3,1},{4,6},{5,7},{6,4},{7,5},{8,10},{9,11},{10,... | collective-permute-start | bytes 221192 | tf_op jit(solution)/shard_map/ppermute | solution.py:430
  153.9 4.6 %collective-permute-start.23 = (bf16[144,256]{1,0:T(8,128)(2,1)S(1)}, bf16[144,256]{1,0:T(8,128)(2,1)S(1)}, u32[]{:S(2)}, u32[]{:S(2)}) collective-permute-start(bf16[144,256]{1,0:T(8,128)(2,1)S(1)} %get-tuple-element.157), channel_id=1, source_target_pairs={{0,3},{1,2},{2,1},{3,0},{4,7},{5,6},{6,5},{7,4},{8,11},{9,10},{10,... | collective-permute-start | bytes 221192 | tf_op jit(solution)/shard_map/ppermute | solution.py:430
  (27 other events, 273.4 us)

commit v5 on v4

--- a/solution.py
+++ b/solution.py
@@ -15,6 +15,7 @@
 BF16 = jnp.bfloat16
 LANES = 128
 HALVES = 2
+SMALL = 8
 HALF = 16
 MIB = 1024 * 1024
 CHEAP = pl.CostEstimate(flops=1, bytes_accessed=1, transcendentals=0)
@@ -193,12 +194,12 @@
         w_ref, refs = refs[-1], refs[:-1]
     else:
         early_ref, pair_ref, refs = refs[0], refs[1], refs[2:]
-    n_columns = len(refs) - 6
+    n_columns = len(refs) - 5
     columns, refs = refs[:n_columns], refs[n_columns:]
-    row_ref, hw_ref, high_ref, sums_ref, send_ref, sorted_ref = refs
+    row_ref, hidden_ref, sums_ref, send_ref, sorted_ref = refs
     z = where_ref[1]
     members = len(layout)
-    rows = high_ref.shape[0] // members
+    rows = hidden_ref.shape[0] // members
     slab = blocks[0].shape[0] - HALF
 
     def far_block(j):
@@ -224,18 +225,16 @@
             at += size
         here = slice(m * rows, (m + 1) * rows)
         hidden = sorted_ref[here, :]
-        high, low = split(hidden)
-        high_ref[here, :] = high
-        heads = dot_t(high, hw_ref[...]) + dot_t(low, hw_ref[...])
-        lane = lax.broadcasted_iota(jnp.int32, heads.shape, 1)
+        hidden_ref[here, :] = hidden
+        high = hidden.astype(BF16)
         square = jnp.sum(hidden * hidden, 1, keepdims=True)
-        sums = jnp.where(lane == nact + 1, square, heads).T[:HALF]
+        square = jnp.broadcast_to(square, (rows, LANES)).T[:SMALL]
         pair = jnp.zeros((HALF, LANES), F32) if late else pair_ref[...]
         for ref in (*near, *blocks) if late else blocks:
             pair = pair + ref[slab:, :LANES].astype(F32)
         pair = jnp.concatenate([pair[:1], jnp.zeros((1, rows - LANES), F32)], 1)
-        row = lax.broadcasted_iota(jnp.int32, sums.shape, 0)
-        sums_ref[:, here] = jnp.where(row == nact + 2, pair, sums)
+        row = lax.broadcasted_iota(jnp.int32, square.shape, 0)
+        sums_ref[:, here] = jnp.where(row == 1, pair, square)
         slot = row_ref[HALF + nact : HALF + nact + 1, here].astype(F32) * 256.0
         slot = slot + row_ref[HALF + nact + 1 : HALF + nact + 2, here].astype(F32)
         slot = slot.astype(jnp.int32)
@@ -255,9 +254,26 @@
             ).astype(BF16)
 
 
+def heads_kernel(team, width, *refs):
+    squares, (near_ref, far_ref, hw_ref, normed_ref, heads_ref, rinv_ref) = refs[:team], refs[team:]
+    step = pl.program_id(0)
+    rows = near_ref.shape[0]
+    total = jnp.zeros((1, rows), F32)
+    for s, ref in enumerate(squares):
+        place = pl.multiple_of((step ^ s) * rows, LANES)
+        total = total + ref[:1, pl.ds(place, rows)]
+    rinv = lax.rsqrt(total / width + NORM_EPS)
+    rinv_ref[...] = jnp.broadcast_to(rinv, rinv_ref.shape)
+    column = jnp.broadcast_to(rinv, (LANES, rows)).T[:, :1]
+    hidden = jnp.where(step < team // 2, near_ref[...], far_ref[...])
+    normed = (hidden * column).astype(BF16)
+    normed_ref[...] = normed
+    heads_ref[...] = dot_t(normed, hw_ref[...]).T[:HALF]
+
+
 def rest_kernel(line, team, nact, width, total_rows, places, halves, where_ref, *refs):
-    sums, refs = refs[:team], refs[team:]
-    row_ref, isd_ref, *high_refs = refs[:4]
+    sums, pairs, refs = refs[:team], refs[team : 2 * team], refs[2 * team :]
+    row_ref, log_std_ref, rinv_ref, high_ref = refs[:4]
     hw_ref, *turned_refs = refs[4:10]
     grad_ref = refs[10]
     firsts, (head_ref, ghid_ref) = refs[11:-2], refs[-2:]
@@ -267,13 +283,16 @@
 
     @pl.when(step == 0)
     def _():
-        half = team // 2
-        rows = high_refs[0].shape[0] // half
+        rows = high_ref.shape[0] // team
         row = lax.broadcasted_iota(jnp.int32, (HALF, rows), 0)
-        isd = isd_ref[:, :1]
-        pair = sums[0][nact + 2 : nact + 3, :LANES]
-        for other in sums[1:]:
-            pair = pair + other[nact + 2 : nact + 3, :LANES]
+        diagonal = lax.broadcasted_iota(jnp.int32, (HALF, nact), 0) == lax.broadcasted_iota(
+            jnp.int32, (HALF, nact), 1
+        )
+        std_log = jnp.sum(jnp.where(diagonal, log_std_ref[...], 0.0), 1, keepdims=True)
+        isd = jnp.where(lax.broadcasted_iota(jnp.int32, (HALF, 1), 0) < nact, jnp.exp(-std_log), 0.0)
+        pair = pairs[0][1:2, :]
+        for other in pairs[1:]:
+            pair = pair + other[1:2, :]
         lane = lax.broadcasted_iota(jnp.int32, (1, LANES), 1)
         mean = jnp.sum(jnp.where(lane < 3, pair, 0.0), 1, keepdims=True) / total_rows
         square = jnp.sum(jnp.where((lane >= 3) & (lane < 6), pair, 0.0), 1, keepdims=True) / total_rows
@@ -285,8 +304,8 @@
             total = sums[0][:, here]
             for s in range(1, team):
                 total = total + sums[s][:, (r ^ s) * rows : ((r ^ s) + 1) * rows]
-            rinv = lax.rsqrt(total[nact + 1 : nact + 2] / width + NORM_EPS)
-            heads = total * rinv
+            heads = total
+            rinv = rinv_ref[:1, here]
             top = row_ref[:HALF, here].astype(F32)
             offset = jnp.where(row < nact, top - heads, 0.0)
             sample = row_ref[HALF:, here].astype(F32)
@@ -306,13 +325,13 @@
             std = std + jnp.where(row < nact, glogr * slope * offset, 0.0)
             mean_gh = jnp.sum(ghead * heads, 0, keepdims=True) / width
             scaled = ghead * rinv
-            high = high_refs[r // half][(r % half) * rows : (r % half + 1) * rows, :]
-            both = dot(jnp.concatenate(split(scaled), 0), high)
+            high = high_ref[here, :]
+            both = dot(jnp.concatenate(split(ghead), 0), high)
             head = head + both[:HALF] + both[HALF:]
             turned = jnp.concatenate(
                 [
                     scaled,
-                    jnp.broadcast_to(rinv * rinv * mean_gh, (HALF, rows)),
+                    jnp.broadcast_to(rinv * mean_gh, (HALF, rows)),
                     jnp.zeros((LANES - 2 * HALF, rows), F32),
                 ],
                 0,
@@ -373,7 +392,7 @@
 
 
 def assemble_kernel(halves, where_ref, *refs):
-    pieces, (grad_ref, head_ref, std_ref) = refs[:-3], refs[-3:]
+    pieces, (grad_ref, head_ref) = refs[:-2], refs[-2:]
     heads_n = head_ref.shape[0]
     q = where_ref[0]
     kr, cols = grad_ref.shape[0], pieces[0].shape[1]
@@ -384,8 +403,6 @@
         grad_ref[:, here] = piece[:kr, :].astype(F32)
         head = piece[kr:, :].astype(F32)
         head_ref[:, here] = head[:heads_n]
-        if i == 0:
-            std_ref[...] = head[heads_n : heads_n + 1, :LANES]
 
 
 def plain(shape):
@@ -474,8 +491,6 @@
     hw = lax.dynamic_slice(head_weight, (q * part, 0), (part, heads_n)).T
     hw_twice = jnp.pad(hw, ((0, LANES - heads_n), (0, 0)))
     hw_twice = jnp.concatenate([hw_twice, hw_twice], 0)
-    isd = jnp.pad(jnp.exp(-log_std), (0, HALF - nact))
-    isd = jnp.broadcast_to(isd[:, None], (HALF, LANES))
 
     gain = gain_in[None, :]
     block = pl.pallas_call(
@@ -497,19 +512,19 @@
     small_core = mate(small, 1)
     obs_late, small_core = lax.optimization_barrier((obs_late, small_core))
     normed_own, normed_core = norm([obs_late], gain), norm([x_core], gain)
-    (fs, bs, far, small, small_core, normed_own, normed_core, obs_last, hw_twice, isd) = (
+    small = jnp.concatenate([small, small_core], 1)
+    small_far = mate(small, 2)
+    (fs, bs, far, small, small_far, normed_own, normed_core, obs_last, hw_twice) = (
         lax.optimization_barrier(
-            (fs, bs, far, small, small_core, normed_own, normed_core, obs_last, hw_twice, isd)
+            (fs, bs, far, small, small_far, normed_own, normed_core, obs_last, hw_twice)
         )
     )
-    small = jnp.concatenate([small, small_core], 1)
-    small_far = mate(small, 2)
     for j in range(2, line - 1):
         fs.append(up(fs[-1], j - 1, line - 1))
         bs.append(down(bs[-1], 1, line - j + 1))
     diag = mate(far, 1)
     late = mate(obs_last, 2)
-    normed_far = norm([far], gain)
+    normed_far, normed_diag = norm([far], gain), norm([diag], gain)
     near_blocks = [block, fs[0], bs[0]]
 
     def early(xs, normed):
@@ -535,8 +550,8 @@
 
     in_columns = slab % LANES == 0
     early_near = early([obs_late, x_core], [normed_own[0], normed_core[0]]) if in_columns else ()
-    fs, bs, late, small, small_far, normed_far, diag, early_near = lax.optimization_barrier(
-        (fs, bs, late, small, small_far, normed_far, diag, early_near)
+    fs, bs, late, small, small_far, normed_far, normed_diag, early_near = lax.optimization_barrier(
+        (fs, bs, late, small, small_far, normed_far, normed_diag, early_near)
     )
     far_blocks = fs[1:] + bs[1:]
 
@@ -549,8 +564,8 @@
         out = pl.pallas_call(
             functools.partial(hidden_kernel, line, nact, packed, layout),
             out_shape=[
-                jax.ShapeDtypeStruct((some_rows, part), BF16),
-                jax.ShapeDtypeStruct((HALF, some_rows), F32),
+                jax.ShapeDtypeStruct((some_rows, part), F32),
+                jax.ShapeDtypeStruct((SMALL, some_rows), F32),
                 jax.ShapeDtypeStruct(send_shape, BF16),
             ],
             grid_spec=pltpu.PrefetchScalarGridSpec(
@@ -558,14 +573,14 @@
                 grid=(1,),
                 in_specs=[whole(block.shape)] * len(far_blocks)
                 + specs
-                + [whole((2 * HALF, some_rows)), whole((LANES, part))],
-                out_specs=[whole((some_rows, part)), whole((HALF, some_rows)), whole(send_shape)],
+                + [whole((2 * HALF, some_rows))],
+                out_specs=[whole((some_rows, part)), whole((SMALL, some_rows)), whole(send_shape)],
                 scratch_shapes=[pltpu.VMEM((some_rows, part), F32), *scratch],
             ),
             compiler_params=params(58),
             cost_estimate=CHEAP,
             name="hidden",
-        )(where, *far_blocks, *operands, rowdata, hw_twice)
+        )(where, *far_blocks, *operands, rowdata)
         if not packed:
             high, sums, send = out
             send = send.reshape(some, n, per_peer, part).transpose(1, 0, 2, 3)
@@ -590,7 +605,7 @@
     normed = [normed_own[0], normed_core[0]]
     if in_columns:
         columns = [(x, j) for x in normed for j in range(2, line - 1)]
-        high_near, sums_near, send = hidden(
+        hidden_near, sums_near, send = hidden(
             [[(0, rows)], [(1, rows)]],
             small,
             [*early_near] + [x for x, _ in columns],
@@ -602,22 +617,43 @@
         )
     else:
         layout = [[(0, rows, 0, 0)], [(1, rows, 1, 0)]]
-        high_near, sums_near, send = at_once(layout, small, [obs_late, x_core], normed)
+        hidden_near, sums_near, send = at_once(layout, small, [obs_late, x_core], normed)
     recv_near = scatter(send)
     last = mate(late, 1)
-    late, last, diag, sums_near, small_all = lax.optimization_barrier(
-        (late, last, diag, sums_near, small_all)
-    )
-    normed_diag = norm([diag], gain)
+    late, last, sums_near, small_all = lax.optimization_barrier((late, last, sums_near, small_all))
     normed_last = norm([late, last], gain)
-    high_far, sums_far, send = at_once(
+    hidden_far, sums_far, send = at_once(
         [[(0, cut, 0, 0), (2, LANES, 2, 0)], [(1, cut, 1, 0), (3, LANES, 2, LANES)]],
         small_far,
         [far, diag, late, last],
         [normed_far[0], normed_diag[0], normed_last[0]],
     )
     sums = jnp.concatenate([sums_near, sums_far], 1)
-    sums = [mate(sums, r) for r in range(team)]
+    squares = [mate(sums, r) for r in range(team)]
+    normed_hidden, heads, rinv = pl.pallas_call(
+        functools.partial(heads_kernel, team, width),
+        out_shape=(
+            jax.ShapeDtypeStruct((team_rows, part), BF16),
+            jax.ShapeDtypeStruct((HALF, team_rows), F32),
+            jax.ShapeDtypeStruct((SMALL, team_rows), F32),
+        ),
+        grid=(team,),
+        in_specs=[plain((SMALL, team_rows))] * team
+        + [
+            pl.BlockSpec((rows, part), lambda i: (jnp.minimum(i, some - 1), 0)),
+            pl.BlockSpec((rows, part), lambda i: (jnp.maximum(i - some, 0), 0)),
+            plain((LANES, part)),
+        ],
+        out_specs=[
+            pl.BlockSpec((rows, part), lambda i: (i, 0)),
+            pl.BlockSpec((HALF, rows), lambda i: (0, i)),
+            pl.BlockSpec((SMALL, rows), lambda i: (0, i)),
+        ],
+        compiler_params=params(58),
+        cost_estimate=CHEAP,
+        name="heads",
+    )(*squares, hidden_near, hidden_far, hw_twice)
+    sums = [mate(heads, r) for r in range(team)]
     send, recv_near = lax.optimization_barrier((send, recv_near))
     recv_far = scatter(send)
     nfirst = len(first_blocks(line))
@@ -637,11 +673,12 @@
             num_scalar_prefetch=1,
             grid=(line,),
             in_specs=[whole((HALF, team_rows))] * team
+            + [pl.BlockSpec((SMALL, LANES), lambda i, w: (0, 0))] * team
             + [
                 whole((2 * HALF, team_rows)),
-                whole((HALF, LANES)),
-                whole((some_rows, part)),
-                whole((some_rows, part)),
+                whole((1, nact)),
+                whole((SMALL, team_rows)),
+                whole((team_rows, part)),
                 whole((2 * LANES, part)),
             ]
             + [
@@ -656,7 +693,7 @@
         compiler_params=params(58),
         cost_estimate=COSTLY,
         name="rest",
-    )(where, *sums, small_all, isd, high_near, high_far, hw_twice, *turned)
+    )(where, *sums, *squares, small_all, log_std[None, :], rinv, normed_hidden, hw_twice, *turned)
     grads, firsts, head = outs[0], outs[1:-1], outs[-1]
 
     def hop(h, up_block, down_block, *got):
@@ -696,46 +733,45 @@
             name="final",
         )(where, grads, head, *got)
 
+    recv_near = recv_near.reshape(line, team, some, per_peer, part)
+    recv_far = recv_far.reshape(line, team, some, per_peer, part)
+
+    def from_member(c, m):
+        r = c ^ m
+        return recv_near[:, c, r] if r < some else recv_far[:, c, r - some]
+
+    hidden_out = jnp.concatenate(
+        [jnp.stack([from_member(c, m) for m in range(team)], 1) for c in range(team)], -1
+    ).reshape(rows, width)
     got = [(firsts[h - halves], firsts[h]) for h in range(halves)]
     for k in range(line - 2, 0, -1):
         if k < line - 2:
             got = [hop(h, k, line - k, *got[h]) for h in range(halves)]
         got = [(up(f, 0, line - k, k == 1), down(b, k, line, k == 1)) for f, b in got]
         if k == 2:
-            got, recv_far = lax.optimization_barrier((got, recv_far)) if halves == 1 else (got, recv_far)
+            got[0], hidden_out = lax.optimization_barrier((got[0], hidden_out))
     pieces = []
     for h in range(halves):
         pieces += [mate(piece, r) for r, piece in enumerate(final(h, *got[h]))]
-    grad_weight, heads, std = pl.pallas_call(
+    grad_weight, heads = pl.pallas_call(
         functools.partial(assemble_kernel, halves),
         out_shape=(
             jax.ShapeDtypeStruct((kr, width), F32),
             jax.ShapeDtypeStruct((heads_n, width), F32),
-            jax.ShapeDtypeStruct((1, LANES), F32),
         ),
         grid_spec=pltpu.PrefetchScalarGridSpec(
             num_scalar_prefetch=1,
             grid=(1,),
             in_specs=[whole(piece.shape) for piece in pieces],
-            out_specs=[whole((kr, width)), whole((heads_n, width)), whole((1, LANES))],
+            out_specs=[whole((kr, width)), whole((heads_n, width))],
         ),
         compiler_params=params(),
         cost_estimate=CHEAP,
         name="assemble",
     )(where, *pieces)
     grad_head = heads.T
-    grad_std = std[0, :nact]
-
-    recv_near = recv_near.reshape(line, team, some, per_peer, part)
-    recv_far = recv_far.reshape(line, team, some, per_peer, part)
-
-    def from_member(c, m):
-        r = c ^ m
-        return recv_near[:, c, r] if r < some else recv_far[:, c, r - some]
-
-    hidden_out = jnp.concatenate(
-        [jnp.stack([from_member(c, m) for m in range(team)], 1) for c in range(team)], -1
-    ).reshape(rows, width)
+    grad_std = pieces[0][kr + heads_n, :nact]
+
     return (hidden_out, grad_weight, grad_head, grad_std)
 
 

time: 164 us -> 169 us (1.030)
  Pallas kernels: 56 us -> 60.4 us
  starting transfers between devices: 55.1 us -> 52.2 us
  local copies, waits for them, and re-layouts: 13.1 us -> 14.8 us
    ppermute x19 -> x22, waiting for transfers between devices: 10.4 us -> 20.4 us  [mate(): return lax.ppermute(x, 'fsdp', [(i, i ^ r) for i in range(n)]) if r else x]
    ppermute x6, waiting for transfers between devices: 18.6 us -> 11 us  [down(): lax.ppermute(x, 'fsdp', [(a * team + i, b * team + i) for a, b in steps f...]
    pallas_call x0 -> x1, Pallas kernels: none -> 5.06 us  [local(): pl.pallas_call(functools.partial(heads_kernel, team, width), out_shape=(j...]
    ppermute x6, starting transfers between devices: 25.6 us -> 21.7 us  [up(): lax.ppermute(x, 'fsdp', [(a * team + i, b * team + i) for a, b in steps f...]
    unnamed x54 -> x60, local copies, waits for them, and re-layouts: 2.99 us -> 5.67 us
    ppermute x6, waiting for transfers between devices: 6.13 us -> 3.97 us  [up(): lax.ppermute(x, 'fsdp', [(a * team + i, b * team + i) for a, b in steps f...]
    ppermute x19 -> x22, starting transfers between devices: 13.5 us -> 14.6 us  [mate(): return lax.ppermute(x, 'fsdp', [(i, i ^ r) for i in range(n)]) if r else x]
  transfers between devices with their start and end apart: 33 -> 36, of which waited for: 13 -> 15; matrix products, arithmetic and copies ran while one was open for 6% -> 7% of each run, Pallas kernels for 31% -> 32%
where the time goes in v5:
time: 169 us; the launch traced here: 167 us
  Pallas kernels  60.4 us (36%)
  starting transfers between devices  52.2 us (31%)
  waiting for transfers between devices  35.4 us (21%)
  local copies, waits for them, and re-layouts  14.8 us (9%)
  other arithmetic  3.24 us (2%)
    ppermute x6, starting transfers between devices, up(): lax.ppermute(x, 'fsdp', [(a * team + i, b * team + i) for a, b in steps f...  21.7 us
    ppermute x22, waiting for transfers between devices, mate(): return lax.ppermute(x, 'fsdp', [(i, i ^ r) for i in range(n)]) if r else x  20.4 us
    pallas_call x5, Pallas kernels, norm(): pl.pallas_call(norm_kernel, out_shape=(jax.ShapeDtypeStruct((rows * len(x...  16.5 us
    ppermute x22, starting transfers between devices, mate(): return lax.ppermute(x, 'fsdp', [(i, i ^ r) for i in range(n)]) if r else x  14.6 us
    pallas_call x2, Pallas kernels, hidden(): pl.pallas_call(functools.partial(hidden_kernel, line, nact, packed, layou...  12.5 us
    all_to_all x2, starting transfers between devices, scatter(): return lax.all_to_all(send, 'fsdp', split_axis=0, concat_axis=0, tiled=True)  11 us
    ppermute x6, waiting for transfers between devices, down(): lax.ppermute(x, 'fsdp', [(a * team + i, b * team + i) for a, b in steps f...  11 us
    pallas_call x1, Pallas kernels, local(): pl.pallas_call(functools.partial(rest_kernel, line, team, nact, width, to...  10.2 us
  transfers between devices with their start and end apart: 36, of which 15 were waited for; matrix products, arithmetic and copies ran while one was open for 7% of the time, Pallas kernels for 32%

profile of v5, /device:TPU:0, one launch (start us, length us, event | category | flops | bytes accessed | tf_op | source)
XLA Modules:
  0.0 167.0 jit_solution(5896639438649886242)
XLA Ops:
  2.4 3.0 %collective-permute-start.2 = (bf16[128,512]{1,0:T(8,128)(2,1)S(1)}, bf16[128,512]{1,0:T(8,128)(2,1)S(1)}, u32[]{:S(2)}, u32[]{:S(2)}) collective-permute-start(bf16[128,512]{1,0:T(8,128)(2,1)S(1)} %get-tuple-element.195), channel_id=1, source_target_pairs={{0,2},{1,3},{2,0},{3,1},{4,6},{5,7},{6,4},{7,5},{8,10},{9,11},{10,... | collective-permute-start | bytes 393224 | tf_op jit(solution)/shard_map/ppermute | solution.py:447
  6.6 2.1 %small.1 = (bf16[32,384]{1,0:T(8,128)(2,1)}, bf16[16,512]{1,0:T(8,128)(2,1)}) custom-call(f32[16,24]{1,0:T(8,128)} %reward_ref.1, f32[16,25]{1,0:T(8,128)} %value_ref.1, s32[16,24]{1,0:T(8,128)} %done_ref.1, bf16[12,384]{1,0:T(8,128)(2,1)} %bitcast.84, bf16[12,384]{1,0:T(8,128)(2,1)} %bitcast.85, s32[1,384]{1,0:T(1,128)} %broadcast_in_dim.9.perm_ref), custom_call_target="tpu_custom_call" | custom-call | flops 1 | bytes 1 | tf_op jit(solution)/shard_map/small/pallas_call | solution.py:461
  8.7 2.3 %slice.57 = bf16[256,2048]{1,0:T(8,128)(2,1)} slice(bf16[384,2048]{1,0:T(8,128)(2,1)} %refs_3_), slice={[0:256], [0:2048]} | slice | bytes 2097152 | tf_op jit(solution)/shard_map/slice | solution.py:483
  15.8 2.2 %collective-permute-start.5 = (bf16[528,512]{1,0:T(8,128)(2,1)S(1)}, bf16[528,512]{1,0:T(8,128)(2,1)S(1)}, u32[]{:S(2)}, u32[]{:S(2)}) collective-permute-start(bf16[528,512]{1,0:T(8,128)(2,1)S(1)} %join.1.refs_0_.refs_2_), channel_id=1, source_target_pairs={{4,0},{5,1},{6,2},{7,3},{8,4},{9,5},{10,6},{11,7},{12,8},{13,9},{1... | collective-permute-start | bytes 1622024 | tf_op jit(solution)/shard_map/ppermute | solution.py:455
  20.6 4.1 %norm.6 = (bf16[384,2048]{1,0:T(8,128)(2,1)}, bf16[2048,384]{1,0:T(8,128)(2,1)}) custom-call(bf16[384,2048]{1,0:T(8,128)(2,1)} %copy-done.7, f32[1,2048]{1,0:T(1,128)} %bitcast.79), custom_call_target="tpu_custom_call" | custom-call | flops 1 | bytes 1 | tf_op jit(solution)/shard_map/norm/pallas_call | solution.py:148
  25.8 4.1 %norm.5 = (bf16[384,2048]{1,0:T(8,128)(2,1)}, bf16[2048,384]{1,0:T(8,128)(2,1)}) custom-call(bf16[384,2048]{1,0:T(8,128)(2,1)} %refs_3_, f32[1,2048]{1,0:T(1,128)} %bitcast.80), custom_call_target="tpu_custom_call" | custom-call | flops 1 | bytes 1 | tf_op jit(solution)/shard_map/norm/pallas_call | solution.py:148
  29.9 8.2 %collective-permute-done.8.refs_12_ = bf16[32,768]{1,0:T(8,128)(2,1)S(1)} collective-permute-done((bf16[32,768]{1,0:T(8,128)(2,1)S(1)}, bf16[32,768]{1,0:T(8,128)(2,1)S(1)}, u32[]{:S(2)}, u32[]{:S(2)}) %collective-permute-start.8) | collective-permute-done | bytes 49184 | tf_op jit(solution)/shard_map/ppermute | solution.py:447
  38.1 3.6 %collective-permute-done.5.refs_2_.refs_4_ = bf16[528,512]{1,0:T(8,128)(2,1)S(1)} collective-permute-done((bf16[528,512]{1,0:T(8,128)(2,1)S(1)}, bf16[528,512]{1,0:T(8,128)(2,1)S(1)}, u32[]{:S(2)}, u32[]{:S(2)}) %collective-permute-start.5) | collective-permute-done | bytes 540704 | tf_op jit(solution)/shard_map/ppermute | solution.py:455
  44.4 2.7 %norm.7 = (bf16[256,2048]{1,0:T(8,128)(2,1)}, bf16[2048,256]{1,0:T(8,128)(2,1)}) custom-call(bf16[256,2048]{1,0:T(8,128)(2,1)} %copy-done.8, f32[1,2048]{1,0:T(1,128)} %bitcast.81), custom_call_target="tpu_custom_call" | custom-call | flops 1 | bytes 1 | tf_op jit(solution)/shard_map/norm/pallas_call | solution.py:148
  47.1 5.8 %early.1 = (f32[768,512]{1,0:T(8,128)}, f32[16,128]{1,0:T(8,128)}) custom-call(s32[2]{0:T(128)} %copy-done.4, bf16[528,512]{1,0:T(8,128)(2,1)} %copy-done.1, bf16[528,512]{1,0:T(8,128)(2,1)} %copy-done.10, bf16[528,512]{1,0:T(8,128)(2,1)} %copy-done.11, bf16[384,2048]{1,0:T(8,128)(2,1)} %refs_3_, bf16[384,2048]{1,0:T(8,128)(2,1)} %copy-done.7, ...), custom_call_target="tpu_custom_call" | custom-call | flops 1 | bytes 1 | tf_op jit(solution)/shard_map/early/pallas_call | solution.py:532
  54.0 2.6 %norm.8 = (bf16[256,2048]{1,0:T(8,128)(2,1)}, bf16[2048,256]{1,0:T(8,128)(2,1)}) custom-call(bf16[256,2048]{1,0:T(8,128)(2,1)} %copy-done.9, f32[1,2048]{1,0:T(1,128)} %bitcast.82), custom_call_target="tpu_custom_call" | custom-call | flops 1 | bytes 1 | tf_op jit(solution)/shard_map/norm/pallas_call | solution.py:148
  59.3 5.2 %hidden.2 = (f32[768,512]{1,0:T(8,128)}, f32[8,768]{1,0:T(8,128)}, bf16[16,48,512]{2,1,0:T(8,128)(2,1)}) custom-call(s32[2]{0:T(128)} %copy-done.4, bf16[528,512]{1,0:T(8,128)(2,1)} %copy-done.13, bf16[528,512]{1,0:T(8,128)(2,1)} %copy-done.12, f32[768,512]{1,0:T(8,128)} %get-tuple-element.126.refs_2_, f32[16,128]{1,0:T(8,128)} %get-tuple-element.127.refs_3_, ...), custom_call_target="tpu_custom_call" | custom-call | flops 1 | bytes 1 | tf_op jit(solution)/shard_map/hidden/pallas_call | solution.py:564
  64.5 5.7 %all-to-all-start = ((bf16[16,48,512]{2,1,0:T(8,128)(2,1)}), bf16[16,48,512]{2,1,0:T(8,128)(2,1)S(1)}, u32[]{:S(2)}, u32[]{:S(2)}) async-start(bf16[16,48,512]{2,1,0:T(8,128)(2,1)} %get-tuple-element.153), calls=%async_computation | async-start | bytes 1572864 | tf_op jit(solution)/shard_map/all_to_all | solution.py:591
  73.0 3.0 %norm.9 = (bf16[256,2048]{1,0:T(8,128)(2,1)}, bf16[2048,256]{1,0:T(8,128)(2,1)}) custom-call(bf16[128,2048]{1,0:T(8,128)(2,1)} %copy-done.14, bf16[128,2048]{1,0:T(8,128)(2,1)} %copy-done.15, f32[1,2048]{1,0:T(1,128)} %bitcast.83), custom_call_target="tpu_custom_call" | custom-call | flops 1 | bytes 1 | tf_op jit(solution)/shard_map/norm/pallas_call | solution.py:148
  76.0 7.4 %hidden.3 = (f32[768,512]{1,0:T(8,128)}, f32[8,768]{1,0:T(8,128)}, bf16[16,48,512]{2,1,0:T(8,128)(2,1)}) custom-call(s32[2]{0:T(128)} %copy-done.4, bf16[528,512]{1,0:T(8,128)(2,1)} %copy-done.13, bf16[528,512]{1,0:T(8,128)(2,1)} %copy-done.12, bf16[528,512]{1,0:T(8,128)(2,1)} %copy-done.1, bf16[528,512]{1,0:T(8,128)(2,1)} %copy-done.10, ...), custom_call_target="tpu_custom_call" | custom-call | flops 1 | bytes 1 | tf_op jit(solution)/shard_map/hidden/pallas_call | solution.py:564
  84.5 1.7 %collective-permute-start.15 = (f32[8,1536]{1,0:T(8,128)S(1)}, f32[8,1536]{1,0:T(8,128)S(1)}, u32[]{:S(2)}, u32[]{:S(2)}) collective-permute-start(f32[8,1536]{1,0:T(8,128)S(1)} %constant_dynamic-update-slice_fusion.2.refs_0_.refs_4_), channel_id=1, source_target_pairs={{0,2},{1,3},{2,0},{3,1},{4,6},{5,7},{6,4},{7,5},{8,10},{9,11},{10,... | collective-permute-start | bytes 147464 | tf_op jit(solution)/shard_map/ppermute | solution.py:447
  86.2 3.9 %collective-permute-done.15.refs_2_.refs_6_ = f32[8,1536]{1,0:T(8,128)S(1)} collective-permute-done((f32[8,1536]{1,0:T(8,128)S(1)}, f32[8,1536]{1,0:T(8,128)S(1)}, u32[]{:S(2)}, u32[]{:S(2)}) %collective-permute-start.15) | collective-permute-done | bytes 49184 | tf_op jit(solution)/shard_map/ppermute | solution.py:447
  91.4 5.1 %heads.1 = (bf16[1536,512]{1,0:T(8,128)(2,1)}, f32[16,1536]{1,0:T(8,128)}, f32[8,1536]{1,0:T(8,128)}) custom-call(f32[8,1536]{1,0:T(8,128)} %copy-done.20, f32[8,1536]{1,0:T(8,128)} %copy-done.21, f32[8,1536]{1,0:T(8,128)} %copy-done.22, f32[8,1536]{1,0:T(8,128)} %copy-done.23, f32[768,512]{1,0:T(8,128)} %get-tuple-element.138.refs_4_, ...), custom_call_target="tpu_custom_call" | custom-call | flops 1 | bytes 1 | tf_op jit(solution)/shard_map/heads/pallas_call | solution.py:633
  98.4 5.3 %all-to-all-start.1 = ((bf16[16,48,512]{2,1,0:T(8,128)(2,1)}), bf16[16,48,512]{2,1,0:T(8,128)(2,1)S(1)}, u32[]{:S(2)}, u32[]{:S(2)}) async-start(bf16[16,48,512]{2,1,0:T(8,128)(2,1)} %get-tuple-element.155), calls=%async_computation.1 | async-start | bytes 1572864 | tf_op jit(solution)/shard_map/all_to_all | solution.py:591
  104.4 10.2 %rest.1 = (f32[2048,512]{1,0:T(8,128)}, bf16[528,256]{1,0:T(8,128)(2,1)}, bf16[528,256]{1,0:T(8,128)(2,1)}, f32[16,512]{1,0:T(8,128)}) custom-call(s32[2]{0:T(128)} %copy-done.4, f32[16,1536]{1,0:T(8,128)} %get-tuple-element.141.refs_0_, f32[16,1536]{1,0:T(8,128)} %copy-done.26, f32[16,1536]{1,0:T(8,128)} %copy-done.27, f32[16,1536]{1,0:T(8,128)} %copy-done.28, ...), custom_call_target="tpu_custom_call" | custom-call | flops 99999997952 | bytes 100000000 | tf_op jit(solution)/shard_map/rest/pallas_call | solution.py:667
  114.6 3.8 %collective-permute-start.27 = (bf16[528,256]{1,0:T(8,128)(2,1)}, bf16[528,256]{1,0:T(8,128)(2,1)S(1)}, u32[]{:S(2)}, u32[]{:S(2)}) collective-permute-start(bf16[528,256]{1,0:T(8,128)(2,1)} %get-tuple-element.167), channel_id=1, source_target_pairs={{0,4},{1,5},{2,6},{3,7},{4,8},{5,9},{6,10},{7,11},{16,20},{17,21},... | collective-permute-start | bytes 811016 | tf_op jit(solution)/shard_map/ppermute | solution.py:451
  119.2 4.0 %collective-permute-start.20 = (bf16[528,256]{1,0:T(8,128)(2,1)}, bf16[528,256]{1,0:T(8,128)(2,1)S(1)}, u32[]{:S(2)}, u32[]{:S(2)}) collective-permute-start(bf16[528,256]{1,0:T(8,128)(2,1)} %get-tuple-element.151), channel_id=1, source_target_pairs={{0,4},{1,5},{2,6},{3,7},{4,8},{5,9},{6,10},{7,11},{16,20},{17,21},... | collective-permute-start | bytes 811016 | tf_op jit(solution)/shard_map/ppermute | solution.py:451
  123.8 1.8 %collective-permute-done.27.refs_2_ = bf16[528,256]{1,0:T(8,128)(2,1)S(1)} collective-permute-done((bf16[528,256]{1,0:T(8,128)(2,1)}, bf16[528,256]{1,0:T(8,128)(2,1)S(1)}, u32[]{:S(2)}, u32[]{:S(2)}) %collective-permute-start.27) | collective-permute-done | bytes 270368 | tf_op jit(solution)/shard_map/ppermute | solution.py:451
  127.7 5.9 %collective-permute-start.29 = (bf16[528,256]{1,0:T(8,128)(2,1)S(1)}, bf16[528,256]{1,0:T(8,128)(2,1)S(1)}, u32[]{:S(2)}, u32[]{:S(2)}) collective-permute-start(bf16[528,256]{1,0:T(8,128)(2,1)S(1)} %get-tuple-element.168), channel_id=1, source_target_pairs={{0,4},{1,5},{2,6},{3,7},{4,8},{5,9},{6,10},{7,11},{8,12},{9,13},{1... | collective-permute-start | bytes 811016 | tf_op jit(solution)/shard_map/ppermute | solution.py:451
  134.4 1.8 %maximum_maximum_fusion = bf16[4,4,24,2048]{3,2,0,1:T(8,128)(2,1)S(1)} fusion(bf16[4,1,24,512]{3,2,0,1:T(8,128)(2,1)} %get-tuple-element.183, bf16[4,1,24,512]{3,2,0,1:T(8,128)(2,1)S(1)} %get-tuple-element.177, bf16[4,1,24,512]{3,2,0,1:T(8,128)(2,1)S(1)} %get-tuple-element.190, bf16[4,1,24,512]{3,2,0,1:T(8,128)(2,1)S(1)} %get-tuple-element.191, ...), kind=kLoop, calls=%fused_computation | loop fusion | flops 25165824 | bytes 3145728 | tf_op jit(solution)/shard_map/concatenate | solution.py:743
  138.8 5.7 %collective-permute-start.22 = (bf16[528,256]{1,0:T(8,128)(2,1)S(1)}, bf16[528,256]{1,0:T(8,128)(2,1)S(1)}, u32[]{:S(2)}, u32[]{:S(2)}) collective-permute-start(bf16[528,256]{1,0:T(8,128)(2,1)S(1)} %get-tuple-element.161), channel_id=1, source_target_pairs={{0,4},{1,5},{2,6},{3,7},{4,8},{5,9},{6,10},{7,11},{8,12},{9,13},{1... | collective-permute-start | bytes 811016 | tf_op jit(solution)/shard_map/ppermute | solution.py:451
  144.5 2.7 %collective-permute-done.30.refs_1_ = bf16[528,256]{1,0:T(8,128)(2,1)S(1)} collective-permute-done((bf16[528,256]{1,0:T(8,128)(2,1)S(1)}, bf16[528,256]{1,0:T(8,128)(2,1)S(1)}, u32[]{:S(2)}, u32[]{:S(2)}) %collective-permute-start.30) | collective-permute-done | bytes 270368 | tf_op jit(solution)/shard_map/ppermute | solution.py:455
  147.2 1.7 final.3
  150.8 2.2 %collective-permute-done.22.refs_0_ = bf16[528,256]{1,0:T(8,128)(2,1)S(1)} collective-permute-done((bf16[528,256]{1,0:T(8,128)(2,1)S(1)}, bf16[528,256]{1,0:T(8,128)(2,1)S(1)}, u32[]{:S(2)}, u32[]{:S(2)}) %collective-permute-start.22) | collective-permute-done | bytes 270368 | tf_op jit(solution)/shard_map/ppermute | solution.py:451
  153.0 4.5 %collective-permute-done.23.refs_1_ = bf16[528,256]{1,0:T(8,128)(2,1)S(1)} collective-permute-done((bf16[528,256]{1,0:T(8,128)(2,1)S(1)}, bf16[528,256]{1,0:T(8,128)(2,1)S(1)}, u32[]{:S(2)}, u32[]{:S(2)}) %collective-permute-start.23) | collective-permute-done | bytes 270368 | tf_op jit(solution)/shard_map/ppermute | solution.py:455
  157.5 1.7 %final.2 = (f32[144,256]{1,0:T(8,128)S(1)}, bf16[144,256]{1,0:T(8,128)(2,1)S(1)}, bf16[144,256]{1,0:T(8,128)(2,1)S(1)}, bf16[144,256]{1,0:T(8,128)(2,1)S(1)}) custom-call(s32[2]{0:T(128)S(1)} %copy-done.5, f32[2048,512]{1,0:T(8,128)} %get-tuple-element.157.refs_0_.refs_1_.mine_ref, f32[16,512]{1,0:T(8,128)S(1)} %copy-done.3, ...), custom_call_target="tpu_custom_call" | custom-call | flops 1 | bytes 1 | tf_op jit(solution)/shard_map/final/pallas_call | solution.py:717
  161.7 2.5 %collective-permute-done.25.refs_2_ = bf16[144,256]{1,0:T(8,128)(2,1)S(1)} collective-permute-done((bf16[144,256]{1,0:T(8,128)(2,1)S(1)}, bf16[144,256]{1,0:T(8,128)(2,1)S(1)}, u32[]{:S(2)}, u32[]{:S(2)}) %collective-permute-start.25) | collective-permute-done | bytes 73760 | tf_op jit(solution)/shard_map/ppermute | solution.py:447
  (133 shorter events, 39.7 us)
Async XLA Ops:
  0.6 10.7 %collective-permute-start = (bf16[384,2048]{1,0:T(8,128)(2,1)}, bf16[384,2048]{1,0:T(8,128)(2,1)S(1)}, u32[]{:S(2)}, u32[]{:S(2)}) collective-permute-start(bf16[384,2048]{1,0:T(8,128)(2,1)} %refs_3_), channel_id=1, source_target_pairs={{0,1},{1,0},{2,3},{3,2},{4,5},{5,4},{6,7},{7,6},{8,9},{9,8},{10,11... | collective-permute-start | bytes 4718600 | tf_op jit(solution)/shard_map/ppermute | solution.py:447
  2.3 8.8 %collective-permute-start.1 = (bf16[128,512]{1,0:T(8,128)(2,1)S(1)}, bf16[128,512]{1,0:T(8,128)(2,1)S(1)}, u32[]{:S(2)}, u32[]{:S(2)}) collective-permute-start(bf16[128,512]{1,0:T(8,128)(2,1)S(1)} %get-tuple-element.193), channel_id=1, source_target_pairs={{0,1},{1,0},{2,3},{3,2},{4,5},{5,4},{6,7},{7,6},{8,9},{9,8},{10,11... | collective-permute-start | bytes 393224 | tf_op jit(solution)/shard_map/ppermute | solution.py:447
  2.4 8.7 %collective-permute-start.2 = (bf16[128,512]{1,0:T(8,128)(2,1)S(1)}, bf16[128,512]{1,0:T(8,128)(2,1)S(1)}, u32[]{:S(2)}, u32[]{:S(2)}) collective-permute-start(bf16[128,512]{1,0:T(8,128)(2,1)S(1)} %get-tuple-element.195), channel_id=1, source_target_pairs={{0,2},{1,3},{2,0},{3,1},{4,6},{5,7},{6,4},{7,5},{8,10},{9,11},{10,... | collective-permute-start | bytes 393224 | tf_op jit(solution)/shard_map/ppermute | solution.py:447
  5.4 6.0 %collective-permute-start.3 = (bf16[128,512]{1,0:T(8,128)(2,1)S(1)}, bf16[128,512]{1,0:T(8,128)(2,1)S(1)}, u32[]{:S(2)}, u32[]{:S(2)}) collective-permute-start(bf16[128,512]{1,0:T(8,128)(2,1)S(1)} %get-tuple-element.192), channel_id=1, source_target_pairs={{0,3},{1,2},{2,1},{3,0},{4,7},{5,6},{6,5},{7,4},{8,11},{9,10},{10,... | collective-permute-start | bytes 393224 | tf_op jit(solution)/shard_map/ppermute | solution.py:447
  11.4 30.3 %collective-permute-start.6 = (bf16[256,2048]{1,0:T(8,128)(2,1)}, bf16[256,2048]{1,0:T(8,128)(2,1)S(1)}, u32[]{:S(2)}, u32[]{:S(2)}) collective-permute-start(bf16[256,2048]{1,0:T(8,128)(2,1)} %slice.57), channel_id=1, source_target_pairs={{0,2},{1,3},{2,0},{3,1},{4,6},{5,7},{6,4},{7,5},{8,10},{9,11},{10,... | collective-permute-start | bytes 3145736 | tf_op jit(solution)/shard_map/ppermute | solution.py:447
  14.1 24.0 %collective-permute-start.4 = (bf16[528,512]{1,0:T(8,128)(2,1)S(1)}, bf16[528,512]{1,0:T(8,128)(2,1)S(1)}, u32[]{:S(2)}, u32[]{:S(2)}) collective-permute-start(bf16[528,512]{1,0:T(8,128)(2,1)S(1)} %join.1.refs_0_.refs_2_), channel_id=1, source_target_pairs={{0,4},{1,5},{2,6},{3,7},{4,8},{5,9},{6,10},{7,11},{8,12},{9,13},{1... | collective-permute-start | bytes 1622024 | tf_op jit(solution)/shard_map/ppermute | solution.py:451
  15.8 25.9 %collective-permute-start.5 = (bf16[528,512]{1,0:T(8,128)(2,1)S(1)}, bf16[528,512]{1,0:T(8,128)(2,1)S(1)}, u32[]{:S(2)}, u32[]{:S(2)}) collective-permute-start(bf16[528,512]{1,0:T(8,128)(2,1)S(1)} %join.1.refs_0_.refs_2_), channel_id=1, source_target_pairs={{4,0},{5,1},{6,2},{7,3},{8,4},{9,5},{10,6},{11,7},{12,8},{13,9},{1... | collective-permute-start | bytes 1622024 | tf_op jit(solution)/shard_map/ppermute | solution.py:455
  19.2 18.9 %collective-permute-start.8 = (bf16[32,768]{1,0:T(8,128)(2,1)S(1)}, bf16[32,768]{1,0:T(8,128)(2,1)S(1)}, u32[]{:S(2)}, u32[]{:S(2)}) collective-permute-start(bf16[32,768]{1,0:T(8,128)(2,1)S(1)} %constant_dynamic-update-slice_fusion.refs_6_), channel_id=1, source_target_pairs={{0,2},{1,3},{2,0},{3,1},{4,6},{5,7},{6,4},{7,5},{8,10},{9,11},{10,... | collective-permute-start | bytes 147464 | tf_op jit(solution)/shard_map/ppermute | solution.py:447
  41.7 11.2 %collective-permute-start.12 = (bf16[256,2048]{1,0:T(8,128)(2,1)S(1)}, bf16[256,2048]{1,0:T(8,128)(2,1)S(1)}, u32[]{:S(2)}, u32[]{:S(2)}) collective-permute-start(bf16[256,2048]{1,0:T(8,128)(2,1)S(1)} %collective-permute-done.6.refs_0_.refs_5_), channel_id=1, source_target_pairs={{0,1},{1,0},{2,3},{3,2},{4,5},{5,4},{6,7},{7,6},{8,9},{9,8},{10,11... | collective-permute-start | bytes 3145736 | tf_op jit(solution)/shard_map/ppermute | solution.py:447
  41.8 16.6 %collective-permute-start.10 = (bf16[528,512]{1,0:T(8,128)(2,1)S(1)}, bf16[528,512]{1,0:T(8,128)(2,1)S(1)}, u32[]{:S(2)}, u32[]{:S(2)}) collective-permute-start(bf16[528,512]{1,0:T(8,128)(2,1)S(1)} %collective-permute-done.5.refs_2_.refs_4_), channel_id=1, source_target_pairs={{4,0},{5,1},{6,2},{7,3},{8,4},{9,5},{10,6},{11,7},{20,16},{21,17},... | collective-permute-start | bytes 1622024 | tf_op jit(solution)/shard_map/ppermute | solution.py:455
  43.1 15.3 %collective-permute-start.9 = (bf16[528,512]{1,0:T(8,128)(2,1)S(1)}, bf16[528,512]{1,0:T(8,128)(2,1)S(1)}, u32[]{:S(2)}, u32[]{:S(2)}) collective-permute-start(bf16[528,512]{1,0:T(8,128)(2,1)S(1)} %collective-permute-done.4.refs_1_.refs_3_), channel_id=1, source_target_pairs={{4,8},{5,9},{6,10},{7,11},{8,12},{9,13},{10,14},{11,15},{20,24},{2... | collective-permute-start | bytes 1622024 | tf_op jit(solution)/shard_map/ppermute | solution.py:451
  43.8 14.4 %collective-permute-start.11 = (bf16[128,2048]{1,0:T(8,128)(2,1)S(1)}, bf16[128,2048]{1,0:T(8,128)(2,1)S(1)}, u32[]{:S(2)}, u32[]{:S(2)}) collective-permute-start(bf16[128,2048]{1,0:T(8,128)(2,1)S(1)} %slice.58), channel_id=1, source_target_pairs={{0,2},{1,3},{2,0},{3,1},{4,6},{5,7},{6,4},{7,5},{8,10},{9,11},{10,... | collective-permute-start | bytes 1572872 | tf_op jit(solution)/shard_map/ppermute | solution.py:447
  64.5 33.9 %all-to-all-start = ((bf16[16,48,512]{2,1,0:T(8,128)(2,1)}), bf16[16,48,512]{2,1,0:T(8,128)(2,1)S(1)}, u32[]{:S(2)}, u32[]{:S(2)}) async-start(bf16[16,48,512]{2,1,0:T(8,128)(2,1)} %get-tuple-element.153), calls=%async_computation | async-start | bytes 1572864 | tf_op jit(solution)/shard_map/all_to_all | solution.py:591
  84.5 5.6 %collective-permute-start.15 = (f32[8,1536]{1,0:T(8,128)S(1)}, f32[8,1536]{1,0:T(8,128)S(1)}, u32[]{:S(2)}, u32[]{:S(2)}) collective-permute-start(f32[8,1536]{1,0:T(8,128)S(1)} %constant_dynamic-update-slice_fusion.2.refs_0_.refs_4_), channel_id=1, source_target_pairs={{0,2},{1,3},{2,0},{3,1},{4,6},{5,7},{6,4},{7,5},{8,10},{9,11},{10,... | collective-permute-start | bytes 147464 | tf_op jit(solution)/shard_map/ppermute | solution.py:447
  86.2 4.6 %collective-permute-start.16 = (f32[8,1536]{1,0:T(8,128)S(1)}, f32[8,1536]{1,0:T(8,128)S(1)}, u32[]{:S(2)}, u32[]{:S(2)}) collective-permute-start(f32[8,1536]{1,0:T(8,128)S(1)} %constant_dynamic-update-slice_fusion.2.refs_0_.refs_4_), channel_id=1, source_target_pairs={{0,3},{1,2},{2,1},{3,0},{4,7},{5,6},{6,5},{7,4},{8,11},{9,10},{10,... | collective-permute-start | bytes 147464 | tf_op jit(solution)/shard_map/ppermute | solution.py:447
  96.5 7.2 %collective-permute-start.17 = (f32[16,1536]{1,0:T(8,128)}, f32[16,1536]{1,0:T(8,128)S(1)}, u32[]{:S(2)}, u32[]{:S(2)}) collective-permute-start(f32[16,1536]{1,0:T(8,128)} %get-tuple-element.141.refs_0_), channel_id=1, source_target_pairs={{0,1},{1,0},{2,3},{3,2},{4,5},{5,4},{6,7},{7,6},{8,9},{9,8},{10,11... | collective-permute-start | bytes 294920 | tf_op jit(solution)/shard_map/ppermute | solution.py:447
  96.6 7.1 %collective-permute-start.18 = (f32[16,1536]{1,0:T(8,128)}, f32[16,1536]{1,0:T(8,128)S(1)}, u32[]{:S(2)}, u32[]{:S(2)}) collective-permute-start(f32[16,1536]{1,0:T(8,128)} %get-tuple-element.141.refs_0_), channel_id=1, source_target_pairs={{0,2},{1,3},{2,0},{3,1},{4,6},{5,7},{6,4},{7,5},{8,10},{9,11},{10,... | collective-permute-start | bytes 294920 | tf_op jit(solution)/shard_map/ppermute | solution.py:447
  97.7 6.0 %collective-permute-start.19 = (f32[16,1536]{1,0:T(8,128)}, f32[16,1536]{1,0:T(8,128)S(1)}, u32[]{:S(2)}, u32[]{:S(2)}) collective-permute-start(f32[16,1536]{1,0:T(8,128)} %get-tuple-element.141.refs_0_), channel_id=1, source_target_pairs={{0,3},{1,2},{2,1},{3,0},{4,7},{5,6},{6,5},{7,4},{8,11},{9,10},{10,... | collective-permute-start | bytes 294920 | tf_op jit(solution)/shard_map/ppermute | solution.py:447
  98.4 35.9 %all-to-all-start.1 = ((bf16[16,48,512]{2,1,0:T(8,128)(2,1)}), bf16[16,48,512]{2,1,0:T(8,128)(2,1)S(1)}, u32[]{:S(2)}, u32[]{:S(2)}) async-start(bf16[16,48,512]{2,1,0:T(8,128)(2,1)} %get-tuple-element.155), calls=%async_computation.1 | async-start | bytes 1572864 | tf_op jit(solution)/shard_map/all_to_all | solution.py:591
  114.6 11.0 %collective-permute-start.27 = (bf16[528,256]{1,0:T(8,128)(2,1)}, bf16[528,256]{1,0:T(8,128)(2,1)S(1)}, u32[]{:S(2)}, u32[]{:S(2)}) collective-permute-start(bf16[528,256]{1,0:T(8,128)(2,1)} %get-tuple-element.167), channel_id=1, source_target_pairs={{0,4},{1,5},{2,6},{3,7},{4,8},{5,9},{6,10},{7,11},{16,20},{17,21},... | collective-permute-start | bytes 811016 | tf_op jit(solution)/shard_map/ppermute | solution.py:451
  118.5 7.1 %collective-permute-start.28 = (bf16[528,256]{1,0:T(8,128)(2,1)}, bf16[528,256]{1,0:T(8,128)(2,1)S(1)}, u32[]{:S(2)}, u32[]{:S(2)}) collective-permute-start(bf16[528,256]{1,0:T(8,128)(2,1)} %get-tuple-element.167), channel_id=1, source_target_pairs={{8,4},{9,5},{10,6},{11,7},{12,8},{13,9},{14,10},{15,11},{24,20},{2... | collective-permute-start | bytes 811016 | tf_op jit(solution)/shard_map/ppermute | solution.py:455
  119.2 18.3 %collective-permute-start.20 = (bf16[528,256]{1,0:T(8,128)(2,1)}, bf16[528,256]{1,0:T(8,128)(2,1)S(1)}, u32[]{:S(2)}, u32[]{:S(2)}) collective-permute-start(bf16[528,256]{1,0:T(8,128)(2,1)} %get-tuple-element.151), channel_id=1, source_target_pairs={{0,4},{1,5},{2,6},{3,7},{4,8},{5,9},{6,10},{7,11},{16,20},{17,21},... | collective-permute-start | bytes 811016 | tf_op jit(solution)/shard_map/ppermute | solution.py:451
  123.1 14.3 %collective-permute-start.21 = (bf16[528,256]{1,0:T(8,128)(2,1)}, bf16[528,256]{1,0:T(8,128)(2,1)S(1)}, u32[]{:S(2)}, u32[]{:S(2)}) collective-permute-start(bf16[528,256]{1,0:T(8,128)(2,1)} %get-tuple-element.151), channel_id=1, source_target_pairs={{8,4},{9,5},{10,6},{11,7},{12,8},{13,9},{14,10},{15,11},{24,20},{2... | collective-permute-start | bytes 811016 | tf_op jit(solution)/shard_map/ppermute | solution.py:455
  127.7 16.8 %collective-permute-start.29 = (bf16[528,256]{1,0:T(8,128)(2,1)S(1)}, bf16[528,256]{1,0:T(8,128)(2,1)S(1)}, u32[]{:S(2)}, u32[]{:S(2)}) collective-permute-start(bf16[528,256]{1,0:T(8,128)(2,1)S(1)} %get-tuple-element.168), channel_id=1, source_target_pairs={{0,4},{1,5},{2,6},{3,7},{4,8},{5,9},{6,10},{7,11},{8,12},{9,13},{1... | collective-permute-start | bytes 811016 | tf_op jit(solution)/shard_map/ppermute | solution.py:451
  133.5 13.7 %collective-permute-start.30 = (bf16[528,256]{1,0:T(8,128)(2,1)S(1)}, bf16[528,256]{1,0:T(8,128)(2,1)S(1)}, u32[]{:S(2)}, u32[]{:S(2)}) collective-permute-start(bf16[528,256]{1,0:T(8,128)(2,1)S(1)} %get-tuple-element.169), channel_id=1, source_target_pairs={{4,0},{5,1},{6,2},{7,3},{8,4},{9,5},{10,6},{11,7},{12,8},{13,9},{1... | collective-permute-start | bytes 811016 | tf_op jit(solution)/shard_map/ppermute | solution.py:455
  138.8 14.2 %collective-permute-start.22 = (bf16[528,256]{1,0:T(8,128)(2,1)S(1)}, bf16[528,256]{1,0:T(8,128)(2,1)S(1)}, u32[]{:S(2)}, u32[]{:S(2)}) collective-permute-start(bf16[528,256]{1,0:T(8,128)(2,1)S(1)} %get-tuple-element.161), channel_id=1, source_target_pairs={{0,4},{1,5},{2,6},{3,7},{4,8},{5,9},{6,10},{7,11},{8,12},{9,13},{1... | collective-permute-start | bytes 811016 | tf_op jit(solution)/shard_map/ppermute | solution.py:451
  144.5 13.0 %collective-permute-start.23 = (bf16[528,256]{1,0:T(8,128)(2,1)S(1)}, bf16[528,256]{1,0:T(8,128)(2,1)S(1)}, u32[]{:S(2)}, u32[]{:S(2)}) collective-permute-start(bf16[528,256]{1,0:T(8,128)(2,1)S(1)} %get-tuple-element.162), channel_id=1, source_target_pairs={{4,0},{5,1},{6,2},{7,3},{8,4},{9,5},{10,6},{11,7},{12,8},{13,9},{1... | collective-permute-start | bytes 811016 | tf_op jit(solution)/shard_map/ppermute | solution.py:455
  148.9 11.9 %collective-permute-start.31 = (bf16[144,256]{1,0:T(8,128)(2,1)S(1)}, bf16[144,256]{1,0:T(8,128)(2,1)S(1)}, u32[]{:S(2)}, u32[]{:S(2)}) collective-permute-start(bf16[144,256]{1,0:T(8,128)(2,1)S(1)} %get-tuple-element.171), channel_id=1, source_target_pairs={{0,1},{1,0},{2,3},{3,2},{4,5},{5,4},{6,7},{7,6},{8,9},{9,8},{10,11... | collective-permute-start | bytes 221192 | tf_op jit(solution)/shard_map/ppermute | solution.py:447
  148.9 12.7 %collective-permute-start.32 = (bf16[144,256]{1,0:T(8,128)(2,1)S(1)}, bf16[144,256]{1,0:T(8,128)(2,1)S(1)}, u32[]{:S(2)}, u32[]{:S(2)}) collective-permute-start(bf16[144,256]{1,0:T(8,128)(2,1)S(1)} %get-tuple-element.172), channel_id=1, source_target_pairs={{0,2},{1,3},{2,0},{3,1},{4,6},{5,7},{6,4},{7,5},{8,10},{9,11},{10,... | collective-permute-start | bytes 221192 | tf_op jit(solution)/shard_map/ppermute | solution.py:447
  150.5 11.2 %collective-permute-start.33 = (bf16[144,256]{1,0:T(8,128)(2,1)S(1)}, bf16[144,256]{1,0:T(8,128)(2,1)S(1)}, u32[]{:S(2)}, u32[]{:S(2)}) collective-permute-start(bf16[144,256]{1,0:T(8,128)(2,1)S(1)} %get-tuple-element.173), channel_id=1, source_target_pairs={{0,3},{1,2},{2,1},{3,0},{4,7},{5,6},{6,5},{7,4},{8,11},{9,10},{10,... | collective-permute-start | bytes 221192 | tf_op jit(solution)/shard_map/ppermute | solution.py:447
  159.3 4.9 %collective-permute-start.25 = (bf16[144,256]{1,0:T(8,128)(2,1)S(1)}, bf16[144,256]{1,0:T(8,128)(2,1)S(1)}, u32[]{:S(2)}, u32[]{:S(2)}) collective-permute-start(bf16[144,256]{1,0:T(8,128)(2,1)S(1)} %get-tuple-element.165), channel_id=1, source_target_pairs={{0,2},{1,3},{2,0},{3,1},{4,6},{5,7},{6,4},{7,5},{8,10},{9,11},{10,... | collective-permute-start | bytes 221192 | tf_op jit(solution)/shard_map/ppermute | solution.py:447
  160.8 4.5 %collective-permute-start.26 = (bf16[144,256]{1,0:T(8,128)(2,1)S(1)}, bf16[144,256]{1,0:T(8,128)(2,1)S(1)}, u32[]{:S(2)}, u32[]{:S(2)}) collective-permute-start(bf16[144,256]{1,0:T(8,128)(2,1)S(1)} %get-tuple-element.166), channel_id=1, source_target_pairs={{0,3},{1,2},{2,1},{3,0},{4,7},{5,6},{6,5},{7,4},{8,11},{9,10},{10,... | collective-permute-start | bytes 221192 | tf_op jit(solution)/shard_map/ppermute | solution.py:447
  (33 other events, 243.3 us)

commit v6 on v5

--- a/solution.py
+++ b/solution.py
@@ -184,7 +184,7 @@
     pair_ref[...] = pair
 
 
-def hidden_kernel(line, nact, packed, layout, where_ref, *refs):
+def hidden_kernel(line, nact, packed, layout, raw, joined, where_ref, *refs):
     late = len(layout[0][0]) == 4
     n_x = 1 + max(index for pieces in layout for index, *_ in pieces)
     js = line - 3
@@ -192,6 +192,7 @@
     if late:
         near, refs = refs[:3], refs[3:]
         w_ref, refs = refs[-1], refs[:-1]
+        gain_ref = refs[-7 if joined else -6]
     else:
         early_ref, pair_ref, refs = refs[0], refs[1], refs[2:]
     n_columns = len(refs) - 5
@@ -211,11 +212,18 @@
             nearest = j in (0, 1, line - 1)
             w_ref[pl.ds(place, slab), :] = near[min(j, 2)][:slab, :] if nearest else far_block(j)
 
+    ahead = columns[-1].shape[1] if joined else 0
+    if joined:
+        sums_ref[:, :ahead] = columns[-1][...]
     for m, pieces in enumerate(layout):
         at = m * rows
         for index, size, *place in pieces:
             if late:
                 normed = columns[n_x + place[0]][place[1] : place[1] + size, :]
+                if place[0] in raw:
+                    xf = normed.astype(F32)
+                    rms = lax.rsqrt(jnp.mean(xf * xf, -1, keepdims=True) + NORM_EPS)
+                    normed = (xf * rms * gain_ref[...]).astype(BF16)
                 total = columns[index][...].astype(F32) + dot(normed, w_ref[...])
             else:
                 total = early_ref[at : at + size, :]
@@ -234,7 +242,7 @@
             pair = pair + ref[slab:, :LANES].astype(F32)
         pair = jnp.concatenate([pair[:1], jnp.zeros((1, rows - LANES), F32)], 1)
         row = lax.broadcasted_iota(jnp.int32, square.shape, 0)
-        sums_ref[:, here] = jnp.where(row == 1, pair, square)
+        sums_ref[:, ahead + m * rows : ahead + (m + 1) * rows] = jnp.where(row == 1, pair, square)
         slot = row_ref[HALF + nact : HALF + nact + 1, here].astype(F32) * 256.0
         slot = slot + row_ref[HALF + nact + 1 : HALF + nact + 2, here].astype(F32)
         slot = slot.astype(jnp.int32)
@@ -559,13 +567,14 @@
     some = team // 2
     some_rows = some * rows
 
-    def hidden(layout, rowdata, operands, specs, scratch=()):
+    def hidden(layout, rowdata, operands, specs, scratch=(), raw=(), joined=False):
+        sum_rows = team_rows if joined else some_rows
         send_shape = (n, some * per_peer, part) if packed else (some_rows, part)
         out = pl.pallas_call(
-            functools.partial(hidden_kernel, line, nact, packed, layout),
+            functools.partial(hidden_kernel, line, nact, packed, layout, raw, joined),
             out_shape=[
                 jax.ShapeDtypeStruct((some_rows, part), F32),
-                jax.ShapeDtypeStruct((SMALL, some_rows), F32),
+                jax.ShapeDtypeStruct((SMALL, sum_rows), F32),
                 jax.ShapeDtypeStruct(send_shape, BF16),
             ],
             grid_spec=pltpu.PrefetchScalarGridSpec(
@@ -574,7 +583,7 @@
                 in_specs=[whole(block.shape)] * len(far_blocks)
                 + specs
                 + [whole((2 * HALF, some_rows))],
-                out_specs=[whole((some_rows, part)), whole((SMALL, some_rows)), whole(send_shape)],
+                out_specs=[whole((some_rows, part)), whole((SMALL, sum_rows)), whole(send_shape)],
                 scratch_shapes=[pltpu.VMEM((some_rows, part), F32), *scratch],
             ),
             compiler_params=params(58),
@@ -590,16 +599,17 @@
     def scatter(send):
         return lax.all_to_all(send, "fsdp", split_axis=0, concat_axis=0, tiled=True)
 
-    small_all = jnp.concatenate([small, small_far], 1)
-    def at_once(layout, rowdata, xs, normed):
+    def at_once(layout, rowdata, xs, normed, raw=(), others=()):
         return hidden(
             layout,
             rowdata,
-            [*near_blocks, *xs, *normed],
+            [*near_blocks, *xs, *normed, gain, *others],
             [whole(block.shape) for block in near_blocks]
             + [pl.BlockSpec((x.shape[0], part), lambda i, w: (0, w[0])) for x in xs]
-            + [whole(x.shape) for x in normed],
+            + [whole(x.shape) for x in (*normed, gain, *others)],
             [pltpu.VMEM((width, part), BF16)],
+            raw,
+            len(others) > 0,
         )
 
     normed = [normed_own[0], normed_core[0]]
@@ -620,16 +630,20 @@
         hidden_near, sums_near, send = at_once(layout, small, [obs_late, x_core], normed)
     recv_near = scatter(send)
     last = mate(late, 1)
-    late, last, sums_near, small_all = lax.optimization_barrier((late, last, sums_near, small_all))
-    normed_last = norm([late, last], gain)
-    hidden_far, sums_far, send = at_once(
-        [[(0, cut, 0, 0), (2, LANES, 2, 0)], [(1, cut, 1, 0), (3, LANES, 2, LANES)]],
+    late, last, sums_near = lax.optimization_barrier((late, last, sums_near))
+    hidden_far, sums, send = at_once(
+        [[(0, cut, 0, 0), (2, LANES, 2, 0)], [(1, cut, 1, 0), (3, LANES, 3, 0)]],
         small_far,
         [far, diag, late, last],
-        [normed_far[0], normed_diag[0], normed_last[0]],
+        [normed_far[0], normed_diag[0], late, last],
+        (2, 3),
+        (sums_near,),
     )
-    sums = jnp.concatenate([sums_near, sums_far], 1)
     squares = [mate(sums, r) for r in range(team)]
+    late, last, small, small_far, sums = lax.optimization_barrier((late, last, small, small_far, sums))
+    normed_last = norm([late, last], gain)
+    small_all = jnp.concatenate([small, small_far], 1)
+    squares, normed_last, small_all = lax.optimization_barrier((squares, normed_last, small_all))
     normed_hidden, heads, rinv = pl.pallas_call(
         functools.partial(heads_kernel, team, width),
         out_shape=(

time: 169 us -> 165 us (0.976)
  waiting for transfers between devices: 35.4 us -> 31.2 us
    ppermute x22, waiting for transfers between devices: 20.4 us -> 16.6 us  [mate(): return lax.ppermute(x, 'fsdp', [(i, i ^ r) for i in range(n)]) if r else x]
    ppermute x6, waiting for transfers between devices: 11 us -> 7.82 us  [down(): lax.ppermute(x, 'fsdp', [(a * team + i, b * team + i) for a, b in steps f...]
    ppermute x6, waiting for transfers between devices: 3.97 us -> 6.85 us  [up(): lax.ppermute(x, 'fsdp', [(a * team + i, b * team + i) for a, b in steps f...]
    unnamed x60 -> x55, local copies, waits for them, and re-layouts: 5.67 us -> 5.48 us
  transfers between devices with their start and end apart: 36 -> 36, of which waited for: 15 -> 14; matrix products, arithmetic and copies ran while one was open for 7% -> 7% of each run, Pallas kernels for 32% -> 33%
where the time goes in v6:
time: 165 us; the launch traced here: 163 us
  Pallas kernels  60.4 us (37%)
  starting transfers between devices  53 us (32%)
  waiting for transfers between devices  31.2 us (19%)
  local copies, waits for them, and re-layouts  13.9 us (8%)
  other arithmetic  3.23 us (2%)
    ppermute x6, starting transfers between devices, up(): lax.ppermute(x, 'fsdp', [(a * team + i, b * team + i) for a, b in steps f...  20.9 us
    ppermute x22, waiting for transfers between devices, mate(): return lax.ppermute(x, 'fsdp', [(i, i ^ r) for i in range(n)]) if r else x  16.6 us
    pallas_call x5, Pallas kernels, norm(): pl.pallas_call(norm_kernel, out_shape=(jax.ShapeDtypeStruct((rows * len(x...  16.5 us
    ppermute x22, starting transfers between devices, mate(): return lax.ppermute(x, 'fsdp', [(i, i ^ r) for i in range(n)]) if r else x  15.1 us
    pallas_call x2, Pallas kernels, hidden(): pl.pallas_call(functools.partial(hidden_kernel, line, nact, packed, layou...  12.4 us
    all_to_all x2, starting transfers between devices, scatter(): return lax.all_to_all(send, 'fsdp', split_axis=0, concat_axis=0, tiled=True)  10.7 us
    pallas_call x1, Pallas kernels, local(): pl.pallas_call(functools.partial(rest_kernel, line, team, nact, width, to...  10.2 us
    ppermute x6, waiting for transfers between devices, down(): lax.ppermute(x, 'fsdp', [(a * team + i, b * team + i) for a, b in steps f...  7.82 us
  transfers between devices with their start and end apart: 36, of which 14 were waited for; matrix products, arithmetic and copies ran while one was open for 7% of the time, Pallas kernels for 33%

profile of v6, /device:TPU:0, one launch (start us, length us, event | category | flops | bytes accessed | tf_op | source)
XLA Modules:
  0.0 162.7 jit_solution(8966021411349574295)
XLA Ops:
  2.3 2.7 %collective-permute-start.3 = (bf16[128,512]{1,0:T(8,128)(2,1)S(1)}, bf16[128,512]{1,0:T(8,128)(2,1)S(1)}, u32[]{:S(2)}, u32[]{:S(2)}) collective-permute-start(bf16[128,512]{1,0:T(8,128)(2,1)S(1)} %get-tuple-element.208), channel_id=1, source_target_pairs={{0,3},{1,2},{2,1},{3,0},{4,7},{5,6},{6,5},{7,4},{8,11},{9,10},{10,... | collective-permute-start | bytes 393224 | tf_op jit(solution)/shard_map/ppermute | solution.py:455
  6.7 2.1 %small.1 = (bf16[32,384]{1,0:T(8,128)(2,1)}, bf16[16,512]{1,0:T(8,128)(2,1)}) custom-call(f32[16,24]{1,0:T(8,128)} %reward_ref.1, f32[16,25]{1,0:T(8,128)} %value_ref.1, s32[16,24]{1,0:T(8,128)} %done_ref.1, bf16[12,384]{1,0:T(8,128)(2,1)} %bitcast.85, bf16[12,384]{1,0:T(8,128)(2,1)} %bitcast.86, s32[1,384]{1,0:T(1,128)} %broadcast_in_dim.9.perm_ref), custom_call_target="tpu_custom_call" | custom-call | flops 1 | bytes 1 | tf_op jit(solution)/shard_map/small/pallas_call | solution.py:469
  8.8 2.3 %slice.57 = bf16[256,2048]{1,0:T(8,128)(2,1)} slice(bf16[384,2048]{1,0:T(8,128)(2,1)} %refs_3_), slice={[0:256], [0:2048]} | slice | bytes 2097152 | tf_op jit(solution)/shard_map/slice | solution.py:491
  11.9 1.7 %collective-permute-start.6 = (bf16[256,2048]{1,0:T(8,128)(2,1)}, bf16[256,2048]{1,0:T(8,128)(2,1)S(1)}, u32[]{:S(2)}, u32[]{:S(2)}) collective-permute-start(bf16[256,2048]{1,0:T(8,128)(2,1)} %slice.57), channel_id=1, source_target_pairs={{0,2},{1,3},{2,0},{3,1},{4,6},{5,7},{6,4},{7,5},{8,10},{9,11},{10,... | collective-permute-start | bytes 3145736 | tf_op jit(solution)/shard_map/ppermute | solution.py:455
  14.9 3.7 %collective-permute-start.5 = (bf16[528,512]{1,0:T(8,128)(2,1)S(1)}, bf16[528,512]{1,0:T(8,128)(2,1)S(1)}, u32[]{:S(2)}, u32[]{:S(2)}) collective-permute-start(bf16[528,512]{1,0:T(8,128)(2,1)S(1)} %join.1.refs_0_.refs_2_), channel_id=1, source_target_pairs={{4,0},{5,1},{6,2},{7,3},{8,4},{9,5},{10,6},{11,7},{12,8},{13,9},{1... | collective-permute-start | bytes 1622024 | tf_op jit(solution)/shard_map/ppermute | solution.py:463
  21.1 4.1 %norm.6 = (bf16[384,2048]{1,0:T(8,128)(2,1)}, bf16[2048,384]{1,0:T(8,128)(2,1)}) custom-call(bf16[384,2048]{1,0:T(8,128)(2,1)} %copy-done.7, f32[1,2048]{1,0:T(1,128)} %bitcast.79), custom_call_target="tpu_custom_call" | custom-call | flops 1 | bytes 1 | tf_op jit(solution)/shard_map/norm/pallas_call | solution.py:148
  26.2 4.1 %norm.5 = (bf16[384,2048]{1,0:T(8,128)(2,1)}, bf16[2048,384]{1,0:T(8,128)(2,1)}) custom-call(bf16[384,2048]{1,0:T(8,128)(2,1)} %refs_3_, f32[1,2048]{1,0:T(1,128)} %bitcast.80), custom_call_target="tpu_custom_call" | custom-call | flops 1 | bytes 1 | tf_op jit(solution)/shard_map/norm/pallas_call | solution.py:148
  30.4 7.7 %collective-permute-done.8.refs_15_ = bf16[32,768]{1,0:T(8,128)(2,1)S(1)} collective-permute-done((bf16[32,768]{1,0:T(8,128)(2,1)S(1)}, bf16[32,768]{1,0:T(8,128)(2,1)S(1)}, u32[]{:S(2)}, u32[]{:S(2)}) %collective-permute-start.8) | collective-permute-done | bytes 49184 | tf_op jit(solution)/shard_map/ppermute | solution.py:455
  38.1 3.9 %collective-permute-done.4.refs_1_.refs_3_ = bf16[528,512]{1,0:T(8,128)(2,1)S(1)} collective-permute-done((bf16[528,512]{1,0:T(8,128)(2,1)S(1)}, bf16[528,512]{1,0:T(8,128)(2,1)S(1)}, u32[]{:S(2)}, u32[]{:S(2)}) %collective-permute-start.4) | collective-permute-done | bytes 540704 | tf_op jit(solution)/shard_map/ppermute | solution.py:459
  44.7 2.7 %norm.7 = (bf16[256,2048]{1,0:T(8,128)(2,1)}, bf16[2048,256]{1,0:T(8,128)(2,1)}) custom-call(bf16[256,2048]{1,0:T(8,128)(2,1)} %copy-done.10, f32[1,2048]{1,0:T(1,128)} %bitcast.81), custom_call_target="tpu_custom_call" | custom-call | flops 1 | bytes 1 | tf_op jit(solution)/shard_map/norm/pallas_call | solution.py:148
  47.4 5.9 %early.1 = (f32[768,512]{1,0:T(8,128)}, f32[16,128]{1,0:T(8,128)}) custom-call(s32[2]{0:T(128)} %copy-done.4, bf16[528,512]{1,0:T(8,128)(2,1)} %copy-done.1, bf16[528,512]{1,0:T(8,128)(2,1)} %copy-done.13, bf16[528,512]{1,0:T(8,128)(2,1)} %copy-done.12, bf16[384,2048]{1,0:T(8,128)(2,1)} %refs_3_, bf16[384,2048]{1,0:T(8,128)(2,1)} %copy-done.7, ...), custom_call_target="tpu_custom_call" | custom-call | flops 1 | bytes 1 | tf_op jit(solution)/shard_map/early/pallas_call | solution.py:540
  54.3 2.7 %norm.8 = (bf16[256,2048]{1,0:T(8,128)(2,1)}, bf16[2048,256]{1,0:T(8,128)(2,1)}) custom-call(bf16[256,2048]{1,0:T(8,128)(2,1)} %copy-done.11, f32[1,2048]{1,0:T(1,128)} %bitcast.82), custom_call_target="tpu_custom_call" | custom-call | flops 1 | bytes 1 | tf_op jit(solution)/shard_map/norm/pallas_call | solution.py:148
  60.7 4.9 %hidden.2 = (f32[768,512]{1,0:T(8,128)}, f32[8,768]{1,0:T(8,128)}, bf16[16,48,512]{2,1,0:T(8,128)(2,1)}) custom-call(s32[2]{0:T(128)} %copy-done.4, bf16[528,512]{1,0:T(8,128)(2,1)} %copy-done.14, bf16[528,512]{1,0:T(8,128)(2,1)} %copy-done.15, f32[768,512]{1,0:T(8,128)} %get-tuple-element.134.refs_2_, f32[16,128]{1,0:T(8,128)} %get-tuple-element.135.refs_3_, ...), custom_call_target="tpu_custom_call" | custom-call | flops 1 | bytes 1 | tf_op jit(solution)/shard_map/hidden/pallas_call | solution.py:573
  65.6 4.3 %all-to-all-start = ((bf16[16,48,512]{2,1,0:T(8,128)(2,1)}), bf16[16,48,512]{2,1,0:T(8,128)(2,1)S(1)}, u32[]{:S(2)}, u32[]{:S(2)}) async-start(bf16[16,48,512]{2,1,0:T(8,128)(2,1)} %get-tuple-element.169), calls=%async_computation | async-start | bytes 1572864 | tf_op jit(solution)/shard_map/all_to_all | solution.py:600
  72.8 7.5 %hidden.3 = (f32[768,512]{1,0:T(8,128)}, f32[8,1536]{1,0:T(8,128)}, bf16[16,48,512]{2,1,0:T(8,128)(2,1)}) custom-call(s32[2]{0:T(128)} %copy-done.4, bf16[528,512]{1,0:T(8,128)(2,1)} %copy-done.14, bf16[528,512]{1,0:T(8,128)(2,1)} %copy-done.15, bf16[528,512]{1,0:T(8,128)(2,1)} %copy-done.1, bf16[528,512]{1,0:T(8,128)(2,1)} %copy-done.13, ...), custom_call_target="tpu_custom_call" | custom-call | flops 1 | bytes 1 | tf_op jit(solution)/shard_map/hidden/pallas_call | solution.py:573
  80.3 1.6 %collective-permute-start.16 = (f32[8,1536]{1,0:T(8,128)}, f32[8,1536]{1,0:T(8,128)S(1)}, u32[]{:S(2)}, u32[]{:S(2)}) collective-permute-start(f32[8,1536]{1,0:T(8,128)} %get-tuple-element.150.refs_0_.refs_4_), channel_id=1, source_target_pairs={{0,3},{1,2},{2,1},{3,0},{4,7},{5,6},{6,5},{7,4},{8,11},{9,10},{10,... | collective-permute-start | bytes 147464 | tf_op jit(solution)/shard_map/ppermute | solution.py:455
  82.9 3.0 %norm.9 = (bf16[256,2048]{1,0:T(8,128)(2,1)}, bf16[2048,256]{1,0:T(8,128)(2,1)}) custom-call(bf16[128,2048]{1,0:T(8,128)(2,1)} %copy-done.8, bf16[128,2048]{1,0:T(8,128)(2,1)} %copy-done.9, f32[1,2048]{1,0:T(1,128)} %bitcast.84), custom_call_target="tpu_custom_call" | custom-call | flops 1 | bytes 1 | tf_op jit(solution)/shard_map/norm/pallas_call | solution.py:148
  87.0 5.1 %heads.1 = (bf16[1536,512]{1,0:T(8,128)(2,1)}, f32[16,1536]{1,0:T(8,128)}, f32[8,1536]{1,0:T(8,128)}) custom-call(f32[8,1536]{1,0:T(8,128)} %get-tuple-element.150.refs_0_.refs_4_, f32[8,1536]{1,0:T(8,128)} %copy-done.22, f32[8,1536]{1,0:T(8,128)} %copy-done.21, f32[8,1536]{1,0:T(8,128)} %copy-done.20, f32[768,512]{1,0:T(8,128)} %get-tuple-element.154.refs_4_, ...), custom_call_target="tpu_custom_call" | custom-call | flops 1 | bytes 1 | tf_op jit(solution)/shard_map/heads/pallas_call | solution.py:647
  94.0 6.4 %all-to-all-start.1 = ((bf16[16,48,512]{2,1,0:T(8,128)(2,1)}), bf16[16,48,512]{2,1,0:T(8,128)(2,1)S(1)}, u32[]{:S(2)}, u32[]{:S(2)}) async-start(bf16[16,48,512]{2,1,0:T(8,128)(2,1)} %get-tuple-element.171), calls=%async_computation.1 | async-start | bytes 1572864 | tf_op jit(solution)/shard_map/all_to_all | solution.py:600
  101.1 10.2 %rest.1 = (f32[2048,512]{1,0:T(8,128)}, bf16[528,256]{1,0:T(8,128)(2,1)}, bf16[528,256]{1,0:T(8,128)(2,1)}, f32[16,512]{1,0:T(8,128)}) custom-call(s32[2]{0:T(128)} %copy-done.4, f32[16,1536]{1,0:T(8,128)} %get-tuple-element.157.refs_0_, f32[16,1536]{1,0:T(8,128)} %copy-done.26, f32[16,1536]{1,0:T(8,128)} %copy-done.25, f32[16,1536]{1,0:T(8,128)} %copy-done.24, ...), custom_call_target="tpu_custom_call" | custom-call | flops 99999997952 | bytes 100000000 | tf_op jit(solution)/shard_map/rest/pallas_call | solution.py:681
  112.0 4.5 %collective-permute-start.27 = (bf16[528,256]{1,0:T(8,128)(2,1)}, bf16[528,256]{1,0:T(8,128)(2,1)S(1)}, u32[]{:S(2)}, u32[]{:S(2)}) collective-permute-start(bf16[528,256]{1,0:T(8,128)(2,1)} %get-tuple-element.183), channel_id=1, source_target_pairs={{0,4},{1,5},{2,6},{3,7},{4,8},{5,9},{6,10},{7,11},{16,20},{17,21},... | collective-permute-start | bytes 811016 | tf_op jit(solution)/shard_map/ppermute | solution.py:459
  117.1 5.2 %collective-permute-start.20 = (bf16[528,256]{1,0:T(8,128)(2,1)}, bf16[528,256]{1,0:T(8,128)(2,1)S(1)}, u32[]{:S(2)}, u32[]{:S(2)}) collective-permute-start(bf16[528,256]{1,0:T(8,128)(2,1)} %get-tuple-element.167), channel_id=1, source_target_pairs={{0,4},{1,5},{2,6},{3,7},{4,8},{5,9},{6,10},{7,11},{16,20},{17,21},... | collective-permute-start | bytes 811016 | tf_op jit(solution)/shard_map/ppermute | solution.py:459
  125.3 5.0 %collective-permute-start.29 = (bf16[528,256]{1,0:T(8,128)(2,1)S(1)}, bf16[528,256]{1,0:T(8,128)(2,1)S(1)}, u32[]{:S(2)}, u32[]{:S(2)}) collective-permute-start(bf16[528,256]{1,0:T(8,128)(2,1)S(1)} %get-tuple-element.184), channel_id=1, source_target_pairs={{0,4},{1,5},{2,6},{3,7},{4,8},{5,9},{6,10},{7,11},{8,12},{9,13},{1... | collective-permute-start | bytes 811016 | tf_op jit(solution)/shard_map/ppermute | solution.py:459
  131.1 1.8 %maximum_maximum_fusion = bf16[4,4,24,2048]{3,2,0,1:T(8,128)(2,1)S(1)} fusion(bf16[4,1,24,512]{3,2,0,1:T(8,128)(2,1)} %get-tuple-element.199, bf16[4,1,24,512]{3,2,0,1:T(8,128)(2,1)S(1)} %get-tuple-element.193, bf16[4,1,24,512]{3,2,0,1:T(8,128)(2,1)S(1)} %get-tuple-element.206, bf16[4,1,24,512]{3,2,0,1:T(8,128)(2,1)S(1)} %get-tuple-element.207, ...), kind=kLoop, calls=%fused_computation | loop fusion | flops 25165824 | bytes 3145728 | tf_op jit(solution)/shard_map/concatenate | solution.py:757
  135.5 5.6 %collective-permute-start.22 = (bf16[528,256]{1,0:T(8,128)(2,1)S(1)}, bf16[528,256]{1,0:T(8,128)(2,1)S(1)}, u32[]{:S(2)}, u32[]{:S(2)}) collective-permute-start(bf16[528,256]{1,0:T(8,128)(2,1)S(1)} %get-tuple-element.177), channel_id=1, source_target_pairs={{0,4},{1,5},{2,6},{3,7},{4,8},{5,9},{6,10},{7,11},{8,12},{9,13},{1... | collective-permute-start | bytes 811016 | tf_op jit(solution)/shard_map/ppermute | solution.py:459
  142.5 1.7 %final.3 = (f32[144,256]{1,0:T(8,128)S(1)}, bf16[144,256]{1,0:T(8,128)(2,1)S(1)}, bf16[144,256]{1,0:T(8,128)(2,1)S(1)}, bf16[144,256]{1,0:T(8,128)(2,1)S(1)}) custom-call(s32[2]{0:T(128)S(1)} %copy-done.5, f32[2048,512]{1,0:T(8,128)} %get-tuple-element.173.refs_0_.refs_1_.mine_ref, f32[16,512]{1,0:T(8,128)S(1)} %copy-done.3, ...), custom_call_target="tpu_custom_call" | custom-call | flops 1 | bytes 1 | tf_op jit(solution)/shard_map/final/pallas_call | solution.py:731
  144.2 2.0 %collective-permute-start.32 = (bf16[144,256]{1,0:T(8,128)(2,1)S(1)}, bf16[144,256]{1,0:T(8,128)(2,1)S(1)}, u32[]{:S(2)}, u32[]{:S(2)}) collective-permute-start(bf16[144,256]{1,0:T(8,128)(2,1)S(1)} %get-tuple-element.188), channel_id=1, source_target_pairs={{0,2},{1,3},{2,0},{3,1},{4,6},{5,7},{6,4},{7,5},{8,10},{9,11},{10,... | collective-permute-start | bytes 221192 | tf_op jit(solution)/shard_map/ppermute | solution.py:455
  146.3 2.0 %collective-permute-done.22.refs_0_ = bf16[528,256]{1,0:T(8,128)(2,1)S(1)} collective-permute-done((bf16[528,256]{1,0:T(8,128)(2,1)S(1)}, bf16[528,256]{1,0:T(8,128)(2,1)S(1)}, u32[]{:S(2)}, u32[]{:S(2)}) %collective-permute-start.22) | collective-permute-done | bytes 270368 | tf_op jit(solution)/shard_map/ppermute | solution.py:459
  148.3 5.0 %collective-permute-done.23.refs_1_ = bf16[528,256]{1,0:T(8,128)(2,1)S(1)} collective-permute-done((bf16[528,256]{1,0:T(8,128)(2,1)S(1)}, bf16[528,256]{1,0:T(8,128)(2,1)S(1)}, u32[]{:S(2)}, u32[]{:S(2)}) %collective-permute-start.23) | collective-permute-done | bytes 270368 | tf_op jit(solution)/shard_map/ppermute | solution.py:463
  153.3 1.7 %final.2 = (f32[144,256]{1,0:T(8,128)S(1)}, bf16[144,256]{1,0:T(8,128)(2,1)S(1)}, bf16[144,256]{1,0:T(8,128)(2,1)S(1)}, bf16[144,256]{1,0:T(8,128)(2,1)S(1)}) custom-call(s32[2]{0:T(128)S(1)} %copy-done.5, f32[2048,512]{1,0:T(8,128)} %get-tuple-element.173.refs_0_.refs_1_.mine_ref, f32[16,512]{1,0:T(8,128)S(1)} %copy-done.3, ...), custom_call_target="tpu_custom_call" | custom-call | flops 1 | bytes 1 | tf_op jit(solution)/shard_map/final/pallas_call | solution.py:731
  155.1 1.7 %collective-permute-start.25 = (bf16[144,256]{1,0:T(8,128)(2,1)S(1)}, bf16[144,256]{1,0:T(8,128)(2,1)S(1)}, u32[]{:S(2)}, u32[]{:S(2)}) collective-permute-start(bf16[144,256]{1,0:T(8,128)(2,1)S(1)} %get-tuple-element.181), channel_id=1, source_target_pairs={{0,2},{1,3},{2,0},{3,1},{4,6},{5,7},{6,4},{7,5},{8,10},{9,11},{10,... | collective-permute-start | bytes 221192 | tf_op jit(solution)/shard_map/ppermute | solution.py:455
  157.5 2.3 %collective-permute-done.25.refs_2_ = bf16[144,256]{1,0:T(8,128)(2,1)S(1)} collective-permute-done((bf16[144,256]{1,0:T(8,128)(2,1)S(1)}, bf16[144,256]{1,0:T(8,128)(2,1)S(1)}, u32[]{:S(2)}, u32[]{:S(2)}) %collective-permute-start.25) | collective-permute-done | bytes 73760 | tf_op jit(solution)/shard_map/ppermute | solution.py:455
  (127 shorter events, 36.8 us)
Async XLA Ops:
  0.6 11.2 %collective-permute-start = (bf16[384,2048]{1,0:T(8,128)(2,1)}, bf16[384,2048]{1,0:T(8,128)(2,1)S(1)}, u32[]{:S(2)}, u32[]{:S(2)}) collective-permute-start(bf16[384,2048]{1,0:T(8,128)(2,1)} %refs_3_), channel_id=1, source_target_pairs={{0,1},{1,0},{2,3},{3,2},{4,5},{5,4},{6,7},{7,6},{8,9},{9,8},{10,11... | collective-permute-start | bytes 4718600 | tf_op jit(solution)/shard_map/ppermute | solution.py:455
  2.3 8.9 %collective-permute-start.3 = (bf16[128,512]{1,0:T(8,128)(2,1)S(1)}, bf16[128,512]{1,0:T(8,128)(2,1)S(1)}, u32[]{:S(2)}, u32[]{:S(2)}) collective-permute-start(bf16[128,512]{1,0:T(8,128)(2,1)S(1)} %get-tuple-element.208), channel_id=1, source_target_pairs={{0,3},{1,2},{2,1},{3,0},{4,7},{5,6},{6,5},{7,4},{8,11},{9,10},{10,... | collective-permute-start | bytes 393224 | tf_op jit(solution)/shard_map/ppermute | solution.py:455
  5.0 6.2 %collective-permute-start.1 = (bf16[128,512]{1,0:T(8,128)(2,1)S(1)}, bf16[128,512]{1,0:T(8,128)(2,1)S(1)}, u32[]{:S(2)}, u32[]{:S(2)}) collective-permute-start(bf16[128,512]{1,0:T(8,128)(2,1)S(1)} %get-tuple-element.209), channel_id=1, source_target_pairs={{0,1},{1,0},{2,3},{3,2},{4,5},{5,4},{6,7},{7,6},{8,9},{9,8},{10,11... | collective-permute-start | bytes 393224 | tf_op jit(solution)/shard_map/ppermute | solution.py:455
  5.1 6.8 %collective-permute-start.2 = (bf16[128,512]{1,0:T(8,128)(2,1)S(1)}, bf16[128,512]{1,0:T(8,128)(2,1)S(1)}, u32[]{:S(2)}, u32[]{:S(2)}) collective-permute-start(bf16[128,512]{1,0:T(8,128)(2,1)S(1)} %get-tuple-element.211), channel_id=1, source_target_pairs={{0,2},{1,3},{2,0},{3,1},{4,6},{5,7},{6,4},{7,5},{8,10},{9,11},{10,... | collective-permute-start | bytes 393224 | tf_op jit(solution)/shard_map/ppermute | solution.py:455
  11.9 30.1 %collective-permute-start.6 = (bf16[256,2048]{1,0:T(8,128)(2,1)}, bf16[256,2048]{1,0:T(8,128)(2,1)S(1)}, u32[]{:S(2)}, u32[]{:S(2)}) collective-permute-start(bf16[256,2048]{1,0:T(8,128)(2,1)} %slice.57), channel_id=1, source_target_pairs={{0,2},{1,3},{2,0},{3,1},{4,6},{5,7},{6,4},{7,5},{8,10},{9,11},{10,... | collective-permute-start | bytes 3145736 | tf_op jit(solution)/shard_map/ppermute | solution.py:455
  14.9 23.2 %collective-permute-start.5 = (bf16[528,512]{1,0:T(8,128)(2,1)S(1)}, bf16[528,512]{1,0:T(8,128)(2,1)S(1)}, u32[]{:S(2)}, u32[]{:S(2)}) collective-permute-start(bf16[528,512]{1,0:T(8,128)(2,1)S(1)} %join.1.refs_0_.refs_2_), channel_id=1, source_target_pairs={{4,0},{5,1},{6,2},{7,3},{8,4},{9,5},{10,6},{11,7},{12,8},{13,9},{1... | collective-permute-start | bytes 1622024 | tf_op jit(solution)/shard_map/ppermute | solution.py:463
  18.5 23.4 %collective-permute-start.4 = (bf16[528,512]{1,0:T(8,128)(2,1)S(1)}, bf16[528,512]{1,0:T(8,128)(2,1)S(1)}, u32[]{:S(2)}, u32[]{:S(2)}) collective-permute-start(bf16[528,512]{1,0:T(8,128)(2,1)S(1)} %join.1.refs_0_.refs_2_), channel_id=1, source_target_pairs={{0,4},{1,5},{2,6},{3,7},{4,8},{5,9},{6,10},{7,11},{8,12},{9,13},{1... | collective-permute-start | bytes 1622024 | tf_op jit(solution)/shard_map/ppermute | solution.py:459
  19.7 18.3 %collective-permute-start.8 = (bf16[32,768]{1,0:T(8,128)(2,1)S(1)}, bf16[32,768]{1,0:T(8,128)(2,1)S(1)}, u32[]{:S(2)}, u32[]{:S(2)}) collective-permute-start(bf16[32,768]{1,0:T(8,128)(2,1)S(1)} %constant_dynamic-update-slice_fusion.refs_6_), channel_id=1, source_target_pairs={{0,2},{1,3},{2,0},{3,1},{4,6},{5,7},{6,4},{7,5},{8,10},{9,11},{10,... | collective-permute-start | bytes 147464 | tf_op jit(solution)/shard_map/ppermute | solution.py:455
  42.0 11.3 %collective-permute-start.12 = (bf16[256,2048]{1,0:T(8,128)(2,1)S(1)}, bf16[256,2048]{1,0:T(8,128)(2,1)S(1)}, u32[]{:S(2)}, u32[]{:S(2)}) collective-permute-start(bf16[256,2048]{1,0:T(8,128)(2,1)S(1)} %collective-permute-done.6.refs_0_.refs_5_), channel_id=1, source_target_pairs={{0,1},{1,0},{2,3},{3,2},{4,5},{5,4},{6,7},{7,6},{8,9},{9,8},{10,11... | collective-permute-start | bytes 3145736 | tf_op jit(solution)/shard_map/ppermute | solution.py:455
  42.1 16.4 %collective-permute-start.9 = (bf16[528,512]{1,0:T(8,128)(2,1)S(1)}, bf16[528,512]{1,0:T(8,128)(2,1)S(1)}, u32[]{:S(2)}, u32[]{:S(2)}) collective-permute-start(bf16[528,512]{1,0:T(8,128)(2,1)S(1)} %collective-permute-done.4.refs_1_.refs_3_), channel_id=1, source_target_pairs={{4,8},{5,9},{6,10},{7,11},{8,12},{9,13},{10,14},{11,15},{20,24},{2... | collective-permute-start | bytes 1622024 | tf_op jit(solution)/shard_map/ppermute | solution.py:459
  42.8 17.1 %collective-permute-start.10 = (bf16[528,512]{1,0:T(8,128)(2,1)S(1)}, bf16[528,512]{1,0:T(8,128)(2,1)S(1)}, u32[]{:S(2)}, u32[]{:S(2)}) collective-permute-start(bf16[528,512]{1,0:T(8,128)(2,1)S(1)} %collective-permute-done.5.refs_2_.refs_4_), channel_id=1, source_target_pairs={{4,0},{5,1},{6,2},{7,3},{8,4},{9,5},{10,6},{11,7},{20,16},{21,17},... | collective-permute-start | bytes 1622024 | tf_op jit(solution)/shard_map/ppermute | solution.py:463
  44.1 14.4 %collective-permute-start.11 = (bf16[128,2048]{1,0:T(8,128)(2,1)S(1)}, bf16[128,2048]{1,0:T(8,128)(2,1)S(1)}, u32[]{:S(2)}, u32[]{:S(2)}) collective-permute-start(bf16[128,2048]{1,0:T(8,128)(2,1)S(1)} %slice.58), channel_id=1, source_target_pairs={{0,2},{1,3},{2,0},{3,1},{4,6},{5,7},{6,4},{7,5},{8,10},{9,11},{10,... | collective-permute-start | bytes 1572872 | tf_op jit(solution)/shard_map/ppermute | solution.py:455
  65.6 28.4 %all-to-all-start = ((bf16[16,48,512]{2,1,0:T(8,128)(2,1)}), bf16[16,48,512]{2,1,0:T(8,128)(2,1)S(1)}, u32[]{:S(2)}, u32[]{:S(2)}) async-start(bf16[16,48,512]{2,1,0:T(8,128)(2,1)} %get-tuple-element.169), calls=%async_computation | async-start | bytes 1572864 | tf_op jit(solution)/shard_map/all_to_all | solution.py:600
  80.3 5.7 %collective-permute-start.16 = (f32[8,1536]{1,0:T(8,128)}, f32[8,1536]{1,0:T(8,128)S(1)}, u32[]{:S(2)}, u32[]{:S(2)}) collective-permute-start(f32[8,1536]{1,0:T(8,128)} %get-tuple-element.150.refs_0_.refs_4_), channel_id=1, source_target_pairs={{0,3},{1,2},{2,1},{3,0},{4,7},{5,6},{6,5},{7,4},{8,11},{9,10},{10,... | collective-permute-start | bytes 147464 | tf_op jit(solution)/shard_map/ppermute | solution.py:455
  81.9 4.5 %collective-permute-start.15 = (f32[8,1536]{1,0:T(8,128)}, f32[8,1536]{1,0:T(8,128)S(1)}, u32[]{:S(2)}, u32[]{:S(2)}) collective-permute-start(f32[8,1536]{1,0:T(8,128)} %get-tuple-element.150.refs_0_.refs_4_), channel_id=1, source_target_pairs={{0,2},{1,3},{2,0},{3,1},{4,6},{5,7},{6,4},{7,5},{8,10},{9,11},{10,... | collective-permute-start | bytes 147464 | tf_op jit(solution)/shard_map/ppermute | solution.py:455
  92.1 8.3 %collective-permute-start.19 = (f32[16,1536]{1,0:T(8,128)}, f32[16,1536]{1,0:T(8,128)S(1)}, u32[]{:S(2)}, u32[]{:S(2)}) collective-permute-start(f32[16,1536]{1,0:T(8,128)} %get-tuple-element.157.refs_0_), channel_id=1, source_target_pairs={{0,3},{1,2},{2,1},{3,0},{4,7},{5,6},{6,5},{7,4},{8,11},{9,10},{10,... | collective-permute-start | bytes 294920 | tf_op jit(solution)/shard_map/ppermute | solution.py:455
  93.4 6.9 %collective-permute-start.18 = (f32[16,1536]{1,0:T(8,128)}, f32[16,1536]{1,0:T(8,128)S(1)}, u32[]{:S(2)}, u32[]{:S(2)}) collective-permute-start(f32[16,1536]{1,0:T(8,128)} %get-tuple-element.157.refs_0_), channel_id=1, source_target_pairs={{0,2},{1,3},{2,0},{3,1},{4,6},{5,7},{6,4},{7,5},{8,10},{9,11},{10,... | collective-permute-start | bytes 294920 | tf_op jit(solution)/shard_map/ppermute | solution.py:455
  93.8 6.6 %collective-permute-start.17 = (f32[16,1536]{1,0:T(8,128)}, f32[16,1536]{1,0:T(8,128)S(1)}, u32[]{:S(2)}, u32[]{:S(2)}) collective-permute-start(f32[16,1536]{1,0:T(8,128)} %get-tuple-element.157.refs_0_), channel_id=1, source_target_pairs={{0,1},{1,0},{2,3},{3,2},{4,5},{5,4},{6,7},{7,6},{8,9},{9,8},{10,11... | collective-permute-start | bytes 294920 | tf_op jit(solution)/shard_map/ppermute | solution.py:455
  94.0 37.0 %all-to-all-start.1 = ((bf16[16,48,512]{2,1,0:T(8,128)(2,1)}), bf16[16,48,512]{2,1,0:T(8,128)(2,1)S(1)}, u32[]{:S(2)}, u32[]{:S(2)}) async-start(bf16[16,48,512]{2,1,0:T(8,128)(2,1)} %get-tuple-element.171), calls=%async_computation.1 | async-start | bytes 1572864 | tf_op jit(solution)/shard_map/all_to_all | solution.py:600
  111.3 11.0 %collective-permute-start.28 = (bf16[528,256]{1,0:T(8,128)(2,1)}, bf16[528,256]{1,0:T(8,128)(2,1)S(1)}, u32[]{:S(2)}, u32[]{:S(2)}) collective-permute-start(bf16[528,256]{1,0:T(8,128)(2,1)} %get-tuple-element.183), channel_id=1, source_target_pairs={{8,4},{9,5},{10,6},{11,7},{12,8},{13,9},{14,10},{15,11},{24,20},{2... | collective-permute-start | bytes 811016 | tf_op jit(solution)/shard_map/ppermute | solution.py:463
  112.0 11.2 %collective-permute-start.27 = (bf16[528,256]{1,0:T(8,128)(2,1)}, bf16[528,256]{1,0:T(8,128)(2,1)S(1)}, u32[]{:S(2)}, u32[]{:S(2)}) collective-permute-start(bf16[528,256]{1,0:T(8,128)(2,1)} %get-tuple-element.183), channel_id=1, source_target_pairs={{0,4},{1,5},{2,6},{3,7},{4,8},{5,9},{6,10},{7,11},{16,20},{17,21},... | collective-permute-start | bytes 811016 | tf_op jit(solution)/shard_map/ppermute | solution.py:459
  116.4 17.7 %collective-permute-start.21 = (bf16[528,256]{1,0:T(8,128)(2,1)}, bf16[528,256]{1,0:T(8,128)(2,1)S(1)}, u32[]{:S(2)}, u32[]{:S(2)}) collective-permute-start(bf16[528,256]{1,0:T(8,128)(2,1)} %get-tuple-element.167), channel_id=1, source_target_pairs={{8,4},{9,5},{10,6},{11,7},{12,8},{13,9},{14,10},{15,11},{24,20},{2... | collective-permute-start | bytes 811016 | tf_op jit(solution)/shard_map/ppermute | solution.py:463
  117.1 17.0 %collective-permute-start.20 = (bf16[528,256]{1,0:T(8,128)(2,1)}, bf16[528,256]{1,0:T(8,128)(2,1)S(1)}, u32[]{:S(2)}, u32[]{:S(2)}) collective-permute-start(bf16[528,256]{1,0:T(8,128)(2,1)} %get-tuple-element.167), channel_id=1, source_target_pairs={{0,4},{1,5},{2,6},{3,7},{4,8},{5,9},{6,10},{7,11},{16,20},{17,21},... | collective-permute-start | bytes 811016 | tf_op jit(solution)/shard_map/ppermute | solution.py:459
  125.3 15.8 %collective-permute-start.29 = (bf16[528,256]{1,0:T(8,128)(2,1)S(1)}, bf16[528,256]{1,0:T(8,128)(2,1)S(1)}, u32[]{:S(2)}, u32[]{:S(2)}) collective-permute-start(bf16[528,256]{1,0:T(8,128)(2,1)S(1)} %get-tuple-element.184), channel_id=1, source_target_pairs={{0,4},{1,5},{2,6},{3,7},{4,8},{5,9},{6,10},{7,11},{8,12},{9,13},{1... | collective-permute-start | bytes 811016 | tf_op jit(solution)/shard_map/ppermute | solution.py:459
  130.2 12.2 %collective-permute-start.30 = (bf16[528,256]{1,0:T(8,128)(2,1)S(1)}, bf16[528,256]{1,0:T(8,128)(2,1)S(1)}, u32[]{:S(2)}, u32[]{:S(2)}) collective-permute-start(bf16[528,256]{1,0:T(8,128)(2,1)S(1)} %get-tuple-element.185), channel_id=1, source_target_pairs={{4,0},{5,1},{6,2},{7,3},{8,4},{9,5},{10,6},{11,7},{12,8},{13,9},{1... | collective-permute-start | bytes 811016 | tf_op jit(solution)/shard_map/ppermute | solution.py:463
  135.5 12.8 %collective-permute-start.22 = (bf16[528,256]{1,0:T(8,128)(2,1)S(1)}, bf16[528,256]{1,0:T(8,128)(2,1)S(1)}, u32[]{:S(2)}, u32[]{:S(2)}) collective-permute-start(bf16[528,256]{1,0:T(8,128)(2,1)S(1)} %get-tuple-element.177), channel_id=1, source_target_pairs={{0,4},{1,5},{2,6},{3,7},{4,8},{5,9},{6,10},{7,11},{8,12},{9,13},{1... | collective-permute-start | bytes 811016 | tf_op jit(solution)/shard_map/ppermute | solution.py:459
  141.1 12.3 %collective-permute-start.23 = (bf16[528,256]{1,0:T(8,128)(2,1)S(1)}, bf16[528,256]{1,0:T(8,128)(2,1)S(1)}, u32[]{:S(2)}, u32[]{:S(2)}) collective-permute-start(bf16[528,256]{1,0:T(8,128)(2,1)S(1)} %get-tuple-element.178), channel_id=1, source_target_pairs={{4,0},{5,1},{6,2},{7,3},{8,4},{9,5},{10,6},{11,7},{12,8},{13,9},{1... | collective-permute-start | bytes 811016 | tf_op jit(solution)/shard_map/ppermute | solution.py:463
  144.1 12.7 %collective-permute-start.31 = (bf16[144,256]{1,0:T(8,128)(2,1)S(1)}, bf16[144,256]{1,0:T(8,128)(2,1)S(1)}, u32[]{:S(2)}, u32[]{:S(2)}) collective-permute-start(bf16[144,256]{1,0:T(8,128)(2,1)S(1)} %get-tuple-element.187), channel_id=1, source_target_pairs={{0,1},{1,0},{2,3},{3,2},{4,5},{5,4},{6,7},{7,6},{8,9},{9,8},{10,11... | collective-permute-start | bytes 221192 | tf_op jit(solution)/shard_map/ppermute | solution.py:455
  144.2 13.3 %collective-permute-start.32 = (bf16[144,256]{1,0:T(8,128)(2,1)S(1)}, bf16[144,256]{1,0:T(8,128)(2,1)S(1)}, u32[]{:S(2)}, u32[]{:S(2)}) collective-permute-start(bf16[144,256]{1,0:T(8,128)(2,1)S(1)} %get-tuple-element.188), channel_id=1, source_target_pairs={{0,2},{1,3},{2,0},{3,1},{4,6},{5,7},{6,4},{7,5},{8,10},{9,11},{10,... | collective-permute-start | bytes 221192 | tf_op jit(solution)/shard_map/ppermute | solution.py:455
  146.2 11.3 %collective-permute-start.33 = (bf16[144,256]{1,0:T(8,128)(2,1)S(1)}, bf16[144,256]{1,0:T(8,128)(2,1)S(1)}, u32[]{:S(2)}, u32[]{:S(2)}) collective-permute-start(bf16[144,256]{1,0:T(8,128)(2,1)S(1)} %get-tuple-element.189), channel_id=1, source_target_pairs={{0,3},{1,2},{2,1},{3,0},{4,7},{5,6},{6,5},{7,4},{8,11},{9,10},{10,... | collective-permute-start | bytes 221192 | tf_op jit(solution)/shard_map/ppermute | solution.py:455
  155.1 4.7 %collective-permute-start.25 = (bf16[144,256]{1,0:T(8,128)(2,1)S(1)}, bf16[144,256]{1,0:T(8,128)(2,1)S(1)}, u32[]{:S(2)}, u32[]{:S(2)}) collective-permute-start(bf16[144,256]{1,0:T(8,128)(2,1)S(1)} %get-tuple-element.181), channel_id=1, source_target_pairs={{0,2},{1,3},{2,0},{3,1},{4,6},{5,7},{6,4},{7,5},{8,10},{9,11},{10,... | collective-permute-start | bytes 221192 | tf_op jit(solution)/shard_map/ppermute | solution.py:455
  156.8 4.2 %collective-permute-start.26 = (bf16[144,256]{1,0:T(8,128)(2,1)S(1)}, bf16[144,256]{1,0:T(8,128)(2,1)S(1)}, u32[]{:S(2)}, u32[]{:S(2)}) collective-permute-start(bf16[144,256]{1,0:T(8,128)(2,1)S(1)} %get-tuple-element.182), channel_id=1, source_target_pairs={{0,3},{1,2},{2,1},{3,0},{4,7},{5,6},{6,5},{7,4},{8,11},{9,10},{10,... | collective-permute-start | bytes 221192 | tf_op jit(solution)/shard_map/ppermute | solution.py:455
  (31 other events, 221.5 us)

commit v7 on v6

--- a/solution.py
+++ b/solution.py
@@ -243,9 +243,8 @@
         pair = jnp.concatenate([pair[:1], jnp.zeros((1, rows - LANES), F32)], 1)
         row = lax.broadcasted_iota(jnp.int32, square.shape, 0)
         sums_ref[:, ahead + m * rows : ahead + (m + 1) * rows] = jnp.where(row == 1, pair, square)
-        slot = row_ref[HALF + nact : HALF + nact + 1, here].astype(F32) * 256.0
-        slot = slot + row_ref[HALF + nact + 1 : HALF + nact + 2, here].astype(F32)
-        slot = slot.astype(jnp.int32)
+        bottom = row_ref[HALF:, here].astype(F32)
+        slot = (bottom[nact : nact + 1] * 256.0 + bottom[nact + 1 : nact + 2]).astype(jnp.int32)
         order = lax.broadcasted_iota(jnp.int32, (rows, rows), 0) == slot
         ranked = dot(jnp.where(order, 1.0, 0.0).astype(BF16), high)
         if packed:
@@ -264,19 +263,25 @@
 
 def heads_kernel(team, width, *refs):
     squares, (near_ref, far_ref, hw_ref, normed_ref, heads_ref, rinv_ref) = refs[:team], refs[team:]
-    step = pl.program_id(0)
-    rows = near_ref.shape[0]
-    total = jnp.zeros((1, rows), F32)
-    for s, ref in enumerate(squares):
-        place = pl.multiple_of((step ^ s) * rows, LANES)
-        total = total + ref[:1, pl.ds(place, rows)]
-    rinv = lax.rsqrt(total / width + NORM_EPS)
-    rinv_ref[...] = jnp.broadcast_to(rinv, rinv_ref.shape)
-    column = jnp.broadcast_to(rinv, (LANES, rows)).T[:, :1]
-    hidden = jnp.where(step < team // 2, near_ref[...], far_ref[...])
-    normed = (hidden * column).astype(BF16)
-    normed_ref[...] = normed
-    heads_ref[...] = dot_t(normed, hw_ref[...]).T[:HALF]
+    some = team // 2
+    rows = near_ref.shape[0] // some
+
+    def run(first, hidden_ref):
+        for m in range(some):
+            here = slice(m * rows, (m + 1) * rows)
+            total = jnp.zeros((1, rows), F32)
+            for s, ref in enumerate(squares):
+                place = ((first + m) ^ s) * rows
+                total = total + ref[:1, place : place + rows]
+            rinv = lax.rsqrt(total / width + NORM_EPS)
+            rinv_ref[:, here] = jnp.broadcast_to(rinv, (SMALL, rows))
+            column = jnp.broadcast_to(rinv, (LANES, rows)).T[:, :1]
+            normed = (hidden_ref[here, :] * column).astype(BF16)
+            normed_ref[here, :] = normed
+            heads_ref[:, here] = dot_t(normed, hw_ref[...]).T[:HALF]
+
+    pl.when(pl.program_id(0) == 0)(lambda: run(0, near_ref))
+    pl.when(pl.program_id(0) == 1)(lambda: run(some, far_ref))
 
 
 def rest_kernel(line, team, nact, width, total_rows, places, halves, where_ref, *refs):
@@ -651,17 +656,13 @@
             jax.ShapeDtypeStruct((HALF, team_rows), F32),
             jax.ShapeDtypeStruct((SMALL, team_rows), F32),
         ),
-        grid=(team,),
+        grid=(2,),
         in_specs=[plain((SMALL, team_rows))] * team
-        + [
-            pl.BlockSpec((rows, part), lambda i: (jnp.minimum(i, some - 1), 0)),
-            pl.BlockSpec((rows, part), lambda i: (jnp.maximum(i - some, 0), 0)),
-            plain((LANES, part)),
-        ],
+        + [plain((some_rows, part)), plain((some_rows, part)), plain((LANES, part))],
         out_specs=[
-            pl.BlockSpec((rows, part), lambda i: (i, 0)),
-            pl.BlockSpec((HALF, rows), lambda i: (0, i)),
-            pl.BlockSpec((SMALL, rows), lambda i: (0, i)),
+            pl.BlockSpec((some_rows, part), lambda i: (i, 0)),
+            pl.BlockSpec((HALF, some_rows), lambda i: (0, i)),
+            pl.BlockSpec((SMALL, some_rows), lambda i: (0, i)),
         ],
         compiler_params=params(58),
         cost_estimate=CHEAP,

time: 165 us -> 164 us (level)
  no operation moved by 1% of the time
where the time goes in v7:
time: 164 us; the launch traced here: 162 us
  Pallas kernels  59.8 us (36%)
  starting transfers between devices  52.9 us (32%)
  waiting for transfers between devices  31.3 us (19%)
  local copies, waits for them, and re-layouts  13.9 us (8%)
  other arithmetic  3.23 us (2%)
    ppermute x6, starting transfers between devices, up(): lax.ppermute(x, 'fsdp', [(a * team + i, b * team + i) for a, b in steps f...  20.9 us
    ppermute x22, waiting for transfers between devices, mate(): return lax.ppermute(x, 'fsdp', [(i, i ^ r) for i in range(n)]) if r else x  16.6 us
    pallas_call x5, Pallas kernels, norm(): pl.pallas_call(norm_kernel, out_shape=(jax.ShapeDtypeStruct((rows * len(x...  16.5 us
    ppermute x22, starting transfers between devices, mate(): return lax.ppermute(x, 'fsdp', [(i, i ^ r) for i in range(n)]) if r else x  15.1 us
    pallas_call x2, Pallas kernels, hidden(): pl.pallas_call(functools.partial(hidden_kernel, line, nact, packed, layou...  12.4 us
    all_to_all x2, starting transfers between devices, scatter(): return lax.all_to_all(send, 'fsdp', split_axis=0, concat_axis=0, tiled=True)  10.7 us
    pallas_call x1, Pallas kernels, local(): pl.pallas_call(functools.partial(rest_kernel, line, team, nact, width, to...  10.2 us
    ppermute x6, waiting for transfers between devices, down(): lax.ppermute(x, 'fsdp', [(a * team + i, b * team + i) for a, b in steps f...  7.82 us
  transfers between devices with their start and end apart: 36, of which 14 were waited for; matrix products, arithmetic and copies ran while one was open for 7% of the time, Pallas kernels for 33%

profile of v7, /device:TPU:0, one launch (start us, length us, event | category | flops | bytes accessed | tf_op | source)
XLA Modules:
  0.0 162.0 jit_solution(3809470865876263091)
XLA Ops:
  2.3 2.7 %collective-permute-start.3 = (bf16[128,512]{1,0:T(8,128)(2,1)S(1)}, bf16[128,512]{1,0:T(8,128)(2,1)S(1)}, u32[]{:S(2)}, u32[]{:S(2)}) collective-permute-start(bf16[128,512]{1,0:T(8,128)(2,1)S(1)} %get-tuple-element.208), channel_id=1, source_target_pairs={{0,3},{1,2},{2,1},{3,0},{4,7},{5,6},{6,5},{7,4},{8,11},{9,10},{10,... | collective-permute-start | bytes 393224 | tf_op jit(solution)/shard_map/ppermute | solution.py:460
  6.7 2.1 %small.1 = (bf16[32,384]{1,0:T(8,128)(2,1)}, bf16[16,512]{1,0:T(8,128)(2,1)}) custom-call(f32[16,24]{1,0:T(8,128)} %reward_ref.1, f32[16,25]{1,0:T(8,128)} %value_ref.1, s32[16,24]{1,0:T(8,128)} %done_ref.1, bf16[12,384]{1,0:T(8,128)(2,1)} %bitcast.85, bf16[12,384]{1,0:T(8,128)(2,1)} %bitcast.86, s32[1,384]{1,0:T(1,128)} %broadcast_in_dim.9.perm_ref), custom_call_target="tpu_custom_call" | custom-call | flops 1 | bytes 1 | tf_op jit(solution)/shard_map/small/pallas_call | solution.py:474
  8.8 2.3 %slice.57 = bf16[256,2048]{1,0:T(8,128)(2,1)} slice(bf16[384,2048]{1,0:T(8,128)(2,1)} %refs_3_), slice={[0:256], [0:2048]} | slice | bytes 2097152 | tf_op jit(solution)/shard_map/slice | solution.py:496
  11.9 1.7 %collective-permute-start.6 = (bf16[256,2048]{1,0:T(8,128)(2,1)}, bf16[256,2048]{1,0:T(8,128)(2,1)S(1)}, u32[]{:S(2)}, u32[]{:S(2)}) collective-permute-start(bf16[256,2048]{1,0:T(8,128)(2,1)} %slice.57), channel_id=1, source_target_pairs={{0,2},{1,3},{2,0},{3,1},{4,6},{5,7},{6,4},{7,5},{8,10},{9,11},{10,... | collective-permute-start | bytes 3145736 | tf_op jit(solution)/shard_map/ppermute | solution.py:460
  14.9 3.7 %collective-permute-start.5 = (bf16[528,512]{1,0:T(8,128)(2,1)S(1)}, bf16[528,512]{1,0:T(8,128)(2,1)S(1)}, u32[]{:S(2)}, u32[]{:S(2)}) collective-permute-start(bf16[528,512]{1,0:T(8,128)(2,1)S(1)} %join.1.refs_0_.refs_2_), channel_id=1, source_target_pairs={{4,0},{5,1},{6,2},{7,3},{8,4},{9,5},{10,6},{11,7},{12,8},{13,9},{1... | collective-permute-start | bytes 1622024 | tf_op jit(solution)/shard_map/ppermute | solution.py:468
  21.1 4.1 %norm.6 = (bf16[384,2048]{1,0:T(8,128)(2,1)}, bf16[2048,384]{1,0:T(8,128)(2,1)}) custom-call(bf16[384,2048]{1,0:T(8,128)(2,1)} %copy-done.7, f32[1,2048]{1,0:T(1,128)} %bitcast.79), custom_call_target="tpu_custom_call" | custom-call | flops 1 | bytes 1 | tf_op jit(solution)/shard_map/norm/pallas_call | solution.py:148
  26.2 4.1 %norm.5 = (bf16[384,2048]{1,0:T(8,128)(2,1)}, bf16[2048,384]{1,0:T(8,128)(2,1)}) custom-call(bf16[384,2048]{1,0:T(8,128)(2,1)} %refs_3_, f32[1,2048]{1,0:T(1,128)} %bitcast.80), custom_call_target="tpu_custom_call" | custom-call | flops 1 | bytes 1 | tf_op jit(solution)/shard_map/norm/pallas_call | solution.py:148
  30.4 7.7 %collective-permute-done.8.refs_15_ = bf16[32,768]{1,0:T(8,128)(2,1)S(1)} collective-permute-done((bf16[32,768]{1,0:T(8,128)(2,1)S(1)}, bf16[32,768]{1,0:T(8,128)(2,1)S(1)}, u32[]{:S(2)}, u32[]{:S(2)}) %collective-permute-start.8) | collective-permute-done | bytes 49184 | tf_op jit(solution)/shard_map/ppermute | solution.py:460
  38.1 3.9 %collective-permute-done.4.refs_1_.refs_3_ = bf16[528,512]{1,0:T(8,128)(2,1)S(1)} collective-permute-done((bf16[528,512]{1,0:T(8,128)(2,1)S(1)}, bf16[528,512]{1,0:T(8,128)(2,1)S(1)}, u32[]{:S(2)}, u32[]{:S(2)}) %collective-permute-start.4) | collective-permute-done | bytes 540704 | tf_op jit(solution)/shard_map/ppermute | solution.py:464
  44.7 2.7 %norm.7 = (bf16[256,2048]{1,0:T(8,128)(2,1)}, bf16[2048,256]{1,0:T(8,128)(2,1)}) custom-call(bf16[256,2048]{1,0:T(8,128)(2,1)} %copy-done.10, f32[1,2048]{1,0:T(1,128)} %bitcast.81), custom_call_target="tpu_custom_call" | custom-call | flops 1 | bytes 1 | tf_op jit(solution)/shard_map/norm/pallas_call | solution.py:148
  47.4 5.9 %early.1 = (f32[768,512]{1,0:T(8,128)}, f32[16,128]{1,0:T(8,128)}) custom-call(s32[2]{0:T(128)} %copy-done.4, bf16[528,512]{1,0:T(8,128)(2,1)} %copy-done.1, bf16[528,512]{1,0:T(8,128)(2,1)} %copy-done.13, bf16[528,512]{1,0:T(8,128)(2,1)} %copy-done.12, bf16[384,2048]{1,0:T(8,128)(2,1)} %refs_3_, bf16[384,2048]{1,0:T(8,128)(2,1)} %copy-done.7, ...), custom_call_target="tpu_custom_call" | custom-call | flops 1 | bytes 1 | tf_op jit(solution)/shard_map/early/pallas_call | solution.py:545
  54.3 2.7 %norm.8 = (bf16[256,2048]{1,0:T(8,128)(2,1)}, bf16[2048,256]{1,0:T(8,128)(2,1)}) custom-call(bf16[256,2048]{1,0:T(8,128)(2,1)} %copy-done.11, f32[1,2048]{1,0:T(1,128)} %bitcast.82), custom_call_target="tpu_custom_call" | custom-call | flops 1 | bytes 1 | tf_op jit(solution)/shard_map/norm/pallas_call | solution.py:148
  60.7 4.9 %hidden.2 = (f32[768,512]{1,0:T(8,128)}, f32[8,768]{1,0:T(8,128)}, bf16[16,48,512]{2,1,0:T(8,128)(2,1)}) custom-call(s32[2]{0:T(128)} %copy-done.4, bf16[528,512]{1,0:T(8,128)(2,1)} %copy-done.14, bf16[528,512]{1,0:T(8,128)(2,1)} %copy-done.15, f32[768,512]{1,0:T(8,128)} %get-tuple-element.134.refs_2_, f32[16,128]{1,0:T(8,128)} %get-tuple-element.135.refs_3_, ...), custom_call_target="tpu_custom_call" | custom-call | flops 1 | bytes 1 | tf_op jit(solution)/shard_map/hidden/pallas_call | solution.py:578
  65.6 4.3 %all-to-all-start = ((bf16[16,48,512]{2,1,0:T(8,128)(2,1)}), bf16[16,48,512]{2,1,0:T(8,128)(2,1)S(1)}, u32[]{:S(2)}, u32[]{:S(2)}) async-start(bf16[16,48,512]{2,1,0:T(8,128)(2,1)} %get-tuple-element.169), calls=%async_computation | async-start | bytes 1572864 | tf_op jit(solution)/shard_map/all_to_all | solution.py:605
  72.8 7.5 %hidden.3 = (f32[768,512]{1,0:T(8,128)}, f32[8,1536]{1,0:T(8,128)}, bf16[16,48,512]{2,1,0:T(8,128)(2,1)}) custom-call(s32[2]{0:T(128)} %copy-done.4, bf16[528,512]{1,0:T(8,128)(2,1)} %copy-done.14, bf16[528,512]{1,0:T(8,128)(2,1)} %copy-done.15, bf16[528,512]{1,0:T(8,128)(2,1)} %copy-done.1, bf16[528,512]{1,0:T(8,128)(2,1)} %copy-done.13, ...), custom_call_target="tpu_custom_call" | custom-call | flops 1 | bytes 1 | tf_op jit(solution)/shard_map/hidden/pallas_call | solution.py:578
  80.3 1.6 %collective-permute-start.16 = (f32[8,1536]{1,0:T(8,128)}, f32[8,1536]{1,0:T(8,128)S(1)}, u32[]{:S(2)}, u32[]{:S(2)}) collective-permute-start(f32[8,1536]{1,0:T(8,128)} %get-tuple-element.150.refs_0_.refs_4_), channel_id=1, source_target_pairs={{0,3},{1,2},{2,1},{3,0},{4,7},{5,6},{6,5},{7,4},{8,11},{9,10},{10,... | collective-permute-start | bytes 147464 | tf_op jit(solution)/shard_map/ppermute | solution.py:460
  82.9 3.0 %norm.9 = (bf16[256,2048]{1,0:T(8,128)(2,1)}, bf16[2048,256]{1,0:T(8,128)(2,1)}) custom-call(bf16[128,2048]{1,0:T(8,128)(2,1)} %copy-done.8, bf16[128,2048]{1,0:T(8,128)(2,1)} %copy-done.9, f32[1,2048]{1,0:T(1,128)} %bitcast.84), custom_call_target="tpu_custom_call" | custom-call | flops 1 | bytes 1 | tf_op jit(solution)/shard_map/norm/pallas_call | solution.py:148
  87.0 4.4 %heads.1 = (bf16[1536,512]{1,0:T(8,128)(2,1)}, f32[16,1536]{1,0:T(8,128)}, f32[8,1536]{1,0:T(8,128)}) custom-call(f32[8,1536]{1,0:T(8,128)} %get-tuple-element.150.refs_0_.refs_4_, f32[8,1536]{1,0:T(8,128)} %copy-done.22, f32[8,1536]{1,0:T(8,128)} %copy-done.21, f32[8,1536]{1,0:T(8,128)} %copy-done.20, f32[768,512]{1,0:T(8,128)} %get-tuple-element.154.refs_4_, ...), custom_call_target="tpu_custom_call" | custom-call | flops 1 | bytes 1 | tf_op jit(solution)/shard_map/heads/pallas_call | solution.py:652
  93.3 6.4 %all-to-all-start.1 = ((bf16[16,48,512]{2,1,0:T(8,128)(2,1)}), bf16[16,48,512]{2,1,0:T(8,128)(2,1)S(1)}, u32[]{:S(2)}, u32[]{:S(2)}) async-start(bf16[16,48,512]{2,1,0:T(8,128)(2,1)} %get-tuple-element.171), calls=%async_computation.1 | async-start | bytes 1572864 | tf_op jit(solution)/shard_map/all_to_all | solution.py:605
  100.4 10.2 %rest.1 = (f32[2048,512]{1,0:T(8,128)}, bf16[528,256]{1,0:T(8,128)(2,1)}, bf16[528,256]{1,0:T(8,128)(2,1)}, f32[16,512]{1,0:T(8,128)}) custom-call(s32[2]{0:T(128)} %copy-done.4, f32[16,1536]{1,0:T(8,128)} %get-tuple-element.157.refs_0_, f32[16,1536]{1,0:T(8,128)} %copy-done.26, f32[16,1536]{1,0:T(8,128)} %copy-done.25, f32[16,1536]{1,0:T(8,128)} %copy-done.24, ...), custom_call_target="tpu_custom_call" | custom-call | flops 99999997952 | bytes 100000000 | tf_op jit(solution)/shard_map/rest/pallas_call | solution.py:682
  111.4 4.5 %collective-permute-start.27 = (bf16[528,256]{1,0:T(8,128)(2,1)}, bf16[528,256]{1,0:T(8,128)(2,1)S(1)}, u32[]{:S(2)}, u32[]{:S(2)}) collective-permute-start(bf16[528,256]{1,0:T(8,128)(2,1)} %get-tuple-element.183), channel_id=1, source_target_pairs={{0,4},{1,5},{2,6},{3,7},{4,8},{5,9},{6,10},{7,11},{16,20},{17,21},... | collective-permute-start | bytes 811016 | tf_op jit(solution)/shard_map/ppermute | solution.py:464
  116.5 5.2 %collective-permute-start.20 = (bf16[528,256]{1,0:T(8,128)(2,1)}, bf16[528,256]{1,0:T(8,128)(2,1)S(1)}, u32[]{:S(2)}, u32[]{:S(2)}) collective-permute-start(bf16[528,256]{1,0:T(8,128)(2,1)} %get-tuple-element.167), channel_id=1, source_target_pairs={{0,4},{1,5},{2,6},{3,7},{4,8},{5,9},{6,10},{7,11},{16,20},{17,21},... | collective-permute-start | bytes 811016 | tf_op jit(solution)/shard_map/ppermute | solution.py:464
  124.6 5.0 %collective-permute-start.29 = (bf16[528,256]{1,0:T(8,128)(2,1)S(1)}, bf16[528,256]{1,0:T(8,128)(2,1)S(1)}, u32[]{:S(2)}, u32[]{:S(2)}) collective-permute-start(bf16[528,256]{1,0:T(8,128)(2,1)S(1)} %get-tuple-element.184), channel_id=1, source_target_pairs={{0,4},{1,5},{2,6},{3,7},{4,8},{5,9},{6,10},{7,11},{8,12},{9,13},{1... | collective-permute-start | bytes 811016 | tf_op jit(solution)/shard_map/ppermute | solution.py:464
  130.5 1.8 %maximum_maximum_fusion = bf16[4,4,24,2048]{3,2,0,1:T(8,128)(2,1)S(1)} fusion(bf16[4,1,24,512]{3,2,0,1:T(8,128)(2,1)} %get-tuple-element.199, bf16[4,1,24,512]{3,2,0,1:T(8,128)(2,1)S(1)} %get-tuple-element.193, bf16[4,1,24,512]{3,2,0,1:T(8,128)(2,1)S(1)} %get-tuple-element.206, bf16[4,1,24,512]{3,2,0,1:T(8,128)(2,1)S(1)} %get-tuple-element.207, ...), kind=kLoop, calls=%fused_computation | loop fusion | flops 25165824 | bytes 3145728 | tf_op jit(solution)/shard_map/concatenate | solution.py:758
  134.9 5.6 %collective-permute-start.22 = (bf16[528,256]{1,0:T(8,128)(2,1)S(1)}, bf16[528,256]{1,0:T(8,128)(2,1)S(1)}, u32[]{:S(2)}, u32[]{:S(2)}) collective-permute-start(bf16[528,256]{1,0:T(8,128)(2,1)S(1)} %get-tuple-element.177), channel_id=1, source_target_pairs={{0,4},{1,5},{2,6},{3,7},{4,8},{5,9},{6,10},{7,11},{8,12},{9,13},{1... | collective-permute-start | bytes 811016 | tf_op jit(solution)/shard_map/ppermute | solution.py:464
  141.8 1.7 %final.3 = (f32[144,256]{1,0:T(8,128)S(1)}, bf16[144,256]{1,0:T(8,128)(2,1)S(1)}, bf16[144,256]{1,0:T(8,128)(2,1)S(1)}, bf16[144,256]{1,0:T(8,128)(2,1)S(1)}) custom-call(s32[2]{0:T(128)S(1)} %copy-done.5, f32[2048,512]{1,0:T(8,128)} %get-tuple-element.173.refs_0_.refs_1_.mine_ref, f32[16,512]{1,0:T(8,128)S(1)} %copy-done.3, ...), custom_call_target="tpu_custom_call" | custom-call | flops 1 | bytes 1 | tf_op jit(solution)/shard_map/final/pallas_call | solution.py:732
  143.6 2.0 %collective-permute-start.32 = (bf16[144,256]{1,0:T(8,128)(2,1)S(1)}, bf16[144,256]{1,0:T(8,128)(2,1)S(1)}, u32[]{:S(2)}, u32[]{:S(2)}) collective-permute-start(bf16[144,256]{1,0:T(8,128)(2,1)S(1)} %get-tuple-element.188), channel_id=1, source_target_pairs={{0,2},{1,3},{2,0},{3,1},{4,6},{5,7},{6,4},{7,5},{8,10},{9,11},{10,... | collective-permute-start | bytes 221192 | tf_op jit(solution)/shard_map/ppermute | solution.py:460
  145.6 2.0 %collective-permute-done.22.refs_0_ = bf16[528,256]{1,0:T(8,128)(2,1)S(1)} collective-permute-done((bf16[528,256]{1,0:T(8,128)(2,1)S(1)}, bf16[528,256]{1,0:T(8,128)(2,1)S(1)}, u32[]{:S(2)}, u32[]{:S(2)}) %collective-permute-start.22) | collective-permute-done | bytes 270368 | tf_op jit(solution)/shard_map/ppermute | solution.py:464
  147.7 5.0 %collective-permute-done.23.refs_1_ = bf16[528,256]{1,0:T(8,128)(2,1)S(1)} collective-permute-done((bf16[528,256]{1,0:T(8,128)(2,1)S(1)}, bf16[528,256]{1,0:T(8,128)(2,1)S(1)}, u32[]{:S(2)}, u32[]{:S(2)}) %collective-permute-start.23) | collective-permute-done | bytes 270368 | tf_op jit(solution)/shard_map/ppermute | solution.py:468
  152.7 1.7 %final.2 = (f32[144,256]{1,0:T(8,128)S(1)}, bf16[144,256]{1,0:T(8,128)(2,1)S(1)}, bf16[144,256]{1,0:T(8,128)(2,1)S(1)}, bf16[144,256]{1,0:T(8,128)(2,1)S(1)}) custom-call(s32[2]{0:T(128)S(1)} %copy-done.5, f32[2048,512]{1,0:T(8,128)} %get-tuple-element.173.refs_0_.refs_1_.mine_ref, f32[16,512]{1,0:T(8,128)S(1)} %copy-done.3, ...), custom_call_target="tpu_custom_call" | custom-call | flops 1 | bytes 1 | tf_op jit(solution)/shard_map/final/pallas_call | solution.py:732
  154.5 1.7 %collective-permute-start.25 = (bf16[144,256]{1,0:T(8,128)(2,1)S(1)}, bf16[144,256]{1,0:T(8,128)(2,1)S(1)}, u32[]{:S(2)}, u32[]{:S(2)}) collective-permute-start(bf16[144,256]{1,0:T(8,128)(2,1)S(1)} %get-tuple-element.181), channel_id=1, source_target_pairs={{0,2},{1,3},{2,0},{3,1},{4,6},{5,7},{6,4},{7,5},{8,10},{9,11},{10,... | collective-permute-start | bytes 221192 | tf_op jit(solution)/shard_map/ppermute | solution.py:460
  156.9 2.3 %collective-permute-done.25.refs_2_ = bf16[144,256]{1,0:T(8,128)(2,1)S(1)} collective-permute-done((bf16[144,256]{1,0:T(8,128)(2,1)S(1)}, bf16[144,256]{1,0:T(8,128)(2,1)S(1)}, u32[]{:S(2)}, u32[]{:S(2)}) %collective-permute-start.25) | collective-permute-done | bytes 73760 | tf_op jit(solution)/shard_map/ppermute | solution.py:460
  (127 shorter events, 36.8 us)
Async XLA Ops:
  0.6 11.2 %collective-permute-start = (bf16[384,2048]{1,0:T(8,128)(2,1)}, bf16[384,2048]{1,0:T(8,128)(2,1)S(1)}, u32[]{:S(2)}, u32[]{:S(2)}) collective-permute-start(bf16[384,2048]{1,0:T(8,128)(2,1)} %refs_3_), channel_id=1, source_target_pairs={{0,1},{1,0},{2,3},{3,2},{4,5},{5,4},{6,7},{7,6},{8,9},{9,8},{10,11... | collective-permute-start | bytes 4718600 | tf_op jit(solution)/shard_map/ppermute | solution.py:460
  2.3 8.9 %collective-permute-start.3 = (bf16[128,512]{1,0:T(8,128)(2,1)S(1)}, bf16[128,512]{1,0:T(8,128)(2,1)S(1)}, u32[]{:S(2)}, u32[]{:S(2)}) collective-permute-start(bf16[128,512]{1,0:T(8,128)(2,1)S(1)} %get-tuple-element.208), channel_id=1, source_target_pairs={{0,3},{1,2},{2,1},{3,0},{4,7},{5,6},{6,5},{7,4},{8,11},{9,10},{10,... | collective-permute-start | bytes 393224 | tf_op jit(solution)/shard_map/ppermute | solution.py:460
  5.0 6.2 %collective-permute-start.1 = (bf16[128,512]{1,0:T(8,128)(2,1)S(1)}, bf16[128,512]{1,0:T(8,128)(2,1)S(1)}, u32[]{:S(2)}, u32[]{:S(2)}) collective-permute-start(bf16[128,512]{1,0:T(8,128)(2,1)S(1)} %get-tuple-element.209), channel_id=1, source_target_pairs={{0,1},{1,0},{2,3},{3,2},{4,5},{5,4},{6,7},{7,6},{8,9},{9,8},{10,11... | collective-permute-start | bytes 393224 | tf_op jit(solution)/shard_map/ppermute | solution.py:460
  5.1 6.8 %collective-permute-start.2 = (bf16[128,512]{1,0:T(8,128)(2,1)S(1)}, bf16[128,512]{1,0:T(8,128)(2,1)S(1)}, u32[]{:S(2)}, u32[]{:S(2)}) collective-permute-start(bf16[128,512]{1,0:T(8,128)(2,1)S(1)} %get-tuple-element.211), channel_id=1, source_target_pairs={{0,2},{1,3},{2,0},{3,1},{4,6},{5,7},{6,4},{7,5},{8,10},{9,11},{10,... | collective-permute-start | bytes 393224 | tf_op jit(solution)/shard_map/ppermute | solution.py:460
  11.9 30.1 %collective-permute-start.6 = (bf16[256,2048]{1,0:T(8,128)(2,1)}, bf16[256,2048]{1,0:T(8,128)(2,1)S(1)}, u32[]{:S(2)}, u32[]{:S(2)}) collective-permute-start(bf16[256,2048]{1,0:T(8,128)(2,1)} %slice.57), channel_id=1, source_target_pairs={{0,2},{1,3},{2,0},{3,1},{4,6},{5,7},{6,4},{7,5},{8,10},{9,11},{10,... | collective-permute-start | bytes 3145736 | tf_op jit(solution)/shard_map/ppermute | solution.py:460
  14.9 23.2 %collective-permute-start.5 = (bf16[528,512]{1,0:T(8,128)(2,1)S(1)}, bf16[528,512]{1,0:T(8,128)(2,1)S(1)}, u32[]{:S(2)}, u32[]{:S(2)}) collective-permute-start(bf16[528,512]{1,0:T(8,128)(2,1)S(1)} %join.1.refs_0_.refs_2_), channel_id=1, source_target_pairs={{4,0},{5,1},{6,2},{7,3},{8,4},{9,5},{10,6},{11,7},{12,8},{13,9},{1... | collective-permute-start | bytes 1622024 | tf_op jit(solution)/shard_map/ppermute | solution.py:468
  18.5 23.4 %collective-permute-start.4 = (bf16[528,512]{1,0:T(8,128)(2,1)S(1)}, bf16[528,512]{1,0:T(8,128)(2,1)S(1)}, u32[]{:S(2)}, u32[]{:S(2)}) collective-permute-start(bf16[528,512]{1,0:T(8,128)(2,1)S(1)} %join.1.refs_0_.refs_2_), channel_id=1, source_target_pairs={{0,4},{1,5},{2,6},{3,7},{4,8},{5,9},{6,10},{7,11},{8,12},{9,13},{1... | collective-permute-start | bytes 1622024 | tf_op jit(solution)/shard_map/ppermute | solution.py:464
  19.7 18.3 %collective-permute-start.8 = (bf16[32,768]{1,0:T(8,128)(2,1)S(1)}, bf16[32,768]{1,0:T(8,128)(2,1)S(1)}, u32[]{:S(2)}, u32[]{:S(2)}) collective-permute-start(bf16[32,768]{1,0:T(8,128)(2,1)S(1)} %constant_dynamic-update-slice_fusion.refs_6_), channel_id=1, source_target_pairs={{0,2},{1,3},{2,0},{3,1},{4,6},{5,7},{6,4},{7,5},{8,10},{9,11},{10,... | collective-permute-start | bytes 147464 | tf_op jit(solution)/shard_map/ppermute | solution.py:460
  42.0 11.3 %collective-permute-start.12 = (bf16[256,2048]{1,0:T(8,128)(2,1)S(1)}, bf16[256,2048]{1,0:T(8,128)(2,1)S(1)}, u32[]{:S(2)}, u32[]{:S(2)}) collective-permute-start(bf16[256,2048]{1,0:T(8,128)(2,1)S(1)} %collective-permute-done.6.refs_0_.refs_5_), channel_id=1, source_target_pairs={{0,1},{1,0},{2,3},{3,2},{4,5},{5,4},{6,7},{7,6},{8,9},{9,8},{10,11... | collective-permute-start | bytes 3145736 | tf_op jit(solution)/shard_map/ppermute | solution.py:460
  42.1 16.4 %collective-permute-start.9 = (bf16[528,512]{1,0:T(8,128)(2,1)S(1)}, bf16[528,512]{1,0:T(8,128)(2,1)S(1)}, u32[]{:S(2)}, u32[]{:S(2)}) collective-permute-start(bf16[528,512]{1,0:T(8,128)(2,1)S(1)} %collective-permute-done.4.refs_1_.refs_3_), channel_id=1, source_target_pairs={{4,8},{5,9},{6,10},{7,11},{8,12},{9,13},{10,14},{11,15},{20,24},{2... | collective-permute-start | bytes 1622024 | tf_op jit(solution)/shard_map/ppermute | solution.py:464
  42.8 17.1 %collective-permute-start.10 = (bf16[528,512]{1,0:T(8,128)(2,1)S(1)}, bf16[528,512]{1,0:T(8,128)(2,1)S(1)}, u32[]{:S(2)}, u32[]{:S(2)}) collective-permute-start(bf16[528,512]{1,0:T(8,128)(2,1)S(1)} %collective-permute-done.5.refs_2_.refs_4_), channel_id=1, source_target_pairs={{4,0},{5,1},{6,2},{7,3},{8,4},{9,5},{10,6},{11,7},{20,16},{21,17},... | collective-permute-start | bytes 1622024 | tf_op jit(solution)/shard_map/ppermute | solution.py:468
  44.1 14.4 %collective-permute-start.11 = (bf16[128,2048]{1,0:T(8,128)(2,1)S(1)}, bf16[128,2048]{1,0:T(8,128)(2,1)S(1)}, u32[]{:S(2)}, u32[]{:S(2)}) collective-permute-start(bf16[128,2048]{1,0:T(8,128)(2,1)S(1)} %slice.58), channel_id=1, source_target_pairs={{0,2},{1,3},{2,0},{3,1},{4,6},{5,7},{6,4},{7,5},{8,10},{9,11},{10,... | collective-permute-start | bytes 1572872 | tf_op jit(solution)/shard_map/ppermute | solution.py:460
  65.6 27.7 %all-to-all-start = ((bf16[16,48,512]{2,1,0:T(8,128)(2,1)}), bf16[16,48,512]{2,1,0:T(8,128)(2,1)S(1)}, u32[]{:S(2)}, u32[]{:S(2)}) async-start(bf16[16,48,512]{2,1,0:T(8,128)(2,1)} %get-tuple-element.169), calls=%async_computation | async-start | bytes 1572864 | tf_op jit(solution)/shard_map/all_to_all | solution.py:605
  80.3 5.7 %collective-permute-start.16 = (f32[8,1536]{1,0:T(8,128)}, f32[8,1536]{1,0:T(8,128)S(1)}, u32[]{:S(2)}, u32[]{:S(2)}) collective-permute-start(f32[8,1536]{1,0:T(8,128)} %get-tuple-element.150.refs_0_.refs_4_), channel_id=1, source_target_pairs={{0,3},{1,2},{2,1},{3,0},{4,7},{5,6},{6,5},{7,4},{8,11},{9,10},{10,... | collective-permute-start | bytes 147464 | tf_op jit(solution)/shard_map/ppermute | solution.py:460
  81.9 4.5 %collective-permute-start.15 = (f32[8,1536]{1,0:T(8,128)}, f32[8,1536]{1,0:T(8,128)S(1)}, u32[]{:S(2)}, u32[]{:S(2)}) collective-permute-start(f32[8,1536]{1,0:T(8,128)} %get-tuple-element.150.refs_0_.refs_4_), channel_id=1, source_target_pairs={{0,2},{1,3},{2,0},{3,1},{4,6},{5,7},{6,4},{7,5},{8,10},{9,11},{10,... | collective-permute-start | bytes 147464 | tf_op jit(solution)/shard_map/ppermute | solution.py:460
  91.5 8.3 %collective-permute-start.19 = (f32[16,1536]{1,0:T(8,128)}, f32[16,1536]{1,0:T(8,128)S(1)}, u32[]{:S(2)}, u32[]{:S(2)}) collective-permute-start(f32[16,1536]{1,0:T(8,128)} %get-tuple-element.157.refs_0_), channel_id=1, source_target_pairs={{0,3},{1,2},{2,1},{3,0},{4,7},{5,6},{6,5},{7,4},{8,11},{9,10},{10,... | collective-permute-start | bytes 294920 | tf_op jit(solution)/shard_map/ppermute | solution.py:460
  92.8 6.9 %collective-permute-start.18 = (f32[16,1536]{1,0:T(8,128)}, f32[16,1536]{1,0:T(8,128)S(1)}, u32[]{:S(2)}, u32[]{:S(2)}) collective-permute-start(f32[16,1536]{1,0:T(8,128)} %get-tuple-element.157.refs_0_), channel_id=1, source_target_pairs={{0,2},{1,3},{2,0},{3,1},{4,6},{5,7},{6,4},{7,5},{8,10},{9,11},{10,... | collective-permute-start | bytes 294920 | tf_op jit(solution)/shard_map/ppermute | solution.py:460
  93.1 6.6 %collective-permute-start.17 = (f32[16,1536]{1,0:T(8,128)}, f32[16,1536]{1,0:T(8,128)S(1)}, u32[]{:S(2)}, u32[]{:S(2)}) collective-permute-start(f32[16,1536]{1,0:T(8,128)} %get-tuple-element.157.refs_0_), channel_id=1, source_target_pairs={{0,1},{1,0},{2,3},{3,2},{4,5},{5,4},{6,7},{7,6},{8,9},{9,8},{10,11... | collective-permute-start | bytes 294920 | tf_op jit(solution)/shard_map/ppermute | solution.py:460
  93.3 37.0 %all-to-all-start.1 = ((bf16[16,48,512]{2,1,0:T(8,128)(2,1)}), bf16[16,48,512]{2,1,0:T(8,128)(2,1)S(1)}, u32[]{:S(2)}, u32[]{:S(2)}) async-start(bf16[16,48,512]{2,1,0:T(8,128)(2,1)} %get-tuple-element.171), calls=%async_computation.1 | async-start | bytes 1572864 | tf_op jit(solution)/shard_map/all_to_all | solution.py:605
  110.7 11.0 %collective-permute-start.28 = (bf16[528,256]{1,0:T(8,128)(2,1)}, bf16[528,256]{1,0:T(8,128)(2,1)S(1)}, u32[]{:S(2)}, u32[]{:S(2)}) collective-permute-start(bf16[528,256]{1,0:T(8,128)(2,1)} %get-tuple-element.183), channel_id=1, source_target_pairs={{8,4},{9,5},{10,6},{11,7},{12,8},{13,9},{14,10},{15,11},{24,20},{2... | collective-permute-start | bytes 811016 | tf_op jit(solution)/shard_map/ppermute | solution.py:468
  111.4 11.2 %collective-permute-start.27 = (bf16[528,256]{1,0:T(8,128)(2,1)}, bf16[528,256]{1,0:T(8,128)(2,1)S(1)}, u32[]{:S(2)}, u32[]{:S(2)}) collective-permute-start(bf16[528,256]{1,0:T(8,128)(2,1)} %get-tuple-element.183), channel_id=1, source_target_pairs={{0,4},{1,5},{2,6},{3,7},{4,8},{5,9},{6,10},{7,11},{16,20},{17,21},... | collective-permute-start | bytes 811016 | tf_op jit(solution)/shard_map/ppermute | solution.py:464
  115.8 17.7 %collective-permute-start.21 = (bf16[528,256]{1,0:T(8,128)(2,1)}, bf16[528,256]{1,0:T(8,128)(2,1)S(1)}, u32[]{:S(2)}, u32[]{:S(2)}) collective-permute-start(bf16[528,256]{1,0:T(8,128)(2,1)} %get-tuple-element.167), channel_id=1, source_target_pairs={{8,4},{9,5},{10,6},{11,7},{12,8},{13,9},{14,10},{15,11},{24,20},{2... | collective-permute-start | bytes 811016 | tf_op jit(solution)/shard_map/ppermute | solution.py:468
  116.5 17.0 %collective-permute-start.20 = (bf16[528,256]{1,0:T(8,128)(2,1)}, bf16[528,256]{1,0:T(8,128)(2,1)S(1)}, u32[]{:S(2)}, u32[]{:S(2)}) collective-permute-start(bf16[528,256]{1,0:T(8,128)(2,1)} %get-tuple-element.167), channel_id=1, source_target_pairs={{0,4},{1,5},{2,6},{3,7},{4,8},{5,9},{6,10},{7,11},{16,20},{17,21},... | collective-permute-start | bytes 811016 | tf_op jit(solution)/shard_map/ppermute | solution.py:464
  124.6 15.8 %collective-permute-start.29 = (bf16[528,256]{1,0:T(8,128)(2,1)S(1)}, bf16[528,256]{1,0:T(8,128)(2,1)S(1)}, u32[]{:S(2)}, u32[]{:S(2)}) collective-permute-start(bf16[528,256]{1,0:T(8,128)(2,1)S(1)} %get-tuple-element.184), channel_id=1, source_target_pairs={{0,4},{1,5},{2,6},{3,7},{4,8},{5,9},{6,10},{7,11},{8,12},{9,13},{1... | collective-permute-start | bytes 811016 | tf_op jit(solution)/shard_map/ppermute | solution.py:464
  129.6 12.2 %collective-permute-start.30 = (bf16[528,256]{1,0:T(8,128)(2,1)S(1)}, bf16[528,256]{1,0:T(8,128)(2,1)S(1)}, u32[]{:S(2)}, u32[]{:S(2)}) collective-permute-start(bf16[528,256]{1,0:T(8,128)(2,1)S(1)} %get-tuple-element.185), channel_id=1, source_target_pairs={{4,0},{5,1},{6,2},{7,3},{8,4},{9,5},{10,6},{11,7},{12,8},{13,9},{1... | collective-permute-start | bytes 811016 | tf_op jit(solution)/shard_map/ppermute | solution.py:468
  134.9 12.8 %collective-permute-start.22 = (bf16[528,256]{1,0:T(8,128)(2,1)S(1)}, bf16[528,256]{1,0:T(8,128)(2,1)S(1)}, u32[]{:S(2)}, u32[]{:S(2)}) collective-permute-start(bf16[528,256]{1,0:T(8,128)(2,1)S(1)} %get-tuple-element.177), channel_id=1, source_target_pairs={{0,4},{1,5},{2,6},{3,7},{4,8},{5,9},{6,10},{7,11},{8,12},{9,13},{1... | collective-permute-start | bytes 811016 | tf_op jit(solution)/shard_map/ppermute | solution.py:464
  140.4 12.3 %collective-permute-start.23 = (bf16[528,256]{1,0:T(8,128)(2,1)S(1)}, bf16[528,256]{1,0:T(8,128)(2,1)S(1)}, u32[]{:S(2)}, u32[]{:S(2)}) collective-permute-start(bf16[528,256]{1,0:T(8,128)(2,1)S(1)} %get-tuple-element.178), channel_id=1, source_target_pairs={{4,0},{5,1},{6,2},{7,3},{8,4},{9,5},{10,6},{11,7},{12,8},{13,9},{1... | collective-permute-start | bytes 811016 | tf_op jit(solution)/shard_map/ppermute | solution.py:468
  143.5 12.7 %collective-permute-start.31 = (bf16[144,256]{1,0:T(8,128)(2,1)S(1)}, bf16[144,256]{1,0:T(8,128)(2,1)S(1)}, u32[]{:S(2)}, u32[]{:S(2)}) collective-permute-start(bf16[144,256]{1,0:T(8,128)(2,1)S(1)} %get-tuple-element.187), channel_id=1, source_target_pairs={{0,1},{1,0},{2,3},{3,2},{4,5},{5,4},{6,7},{7,6},{8,9},{9,8},{10,11... | collective-permute-start | bytes 221192 | tf_op jit(solution)/shard_map/ppermute | solution.py:460
  143.6 13.3 %collective-permute-start.32 = (bf16[144,256]{1,0:T(8,128)(2,1)S(1)}, bf16[144,256]{1,0:T(8,128)(2,1)S(1)}, u32[]{:S(2)}, u32[]{:S(2)}) collective-permute-start(bf16[144,256]{1,0:T(8,128)(2,1)S(1)} %get-tuple-element.188), channel_id=1, source_target_pairs={{0,2},{1,3},{2,0},{3,1},{4,6},{5,7},{6,4},{7,5},{8,10},{9,11},{10,... | collective-permute-start | bytes 221192 | tf_op jit(solution)/shard_map/ppermute | solution.py:460
  145.6 11.3 %collective-permute-start.33 = (bf16[144,256]{1,0:T(8,128)(2,1)S(1)}, bf16[144,256]{1,0:T(8,128)(2,1)S(1)}, u32[]{:S(2)}, u32[]{:S(2)}) collective-permute-start(bf16[144,256]{1,0:T(8,128)(2,1)S(1)} %get-tuple-element.189), channel_id=1, source_target_pairs={{0,3},{1,2},{2,1},{3,0},{4,7},{5,6},{6,5},{7,4},{8,11},{9,10},{10,... | collective-permute-start | bytes 221192 | tf_op jit(solution)/shard_map/ppermute | solution.py:460
  154.5 4.7 %collective-permute-start.25 = (bf16[144,256]{1,0:T(8,128)(2,1)S(1)}, bf16[144,256]{1,0:T(8,128)(2,1)S(1)}, u32[]{:S(2)}, u32[]{:S(2)}) collective-permute-start(bf16[144,256]{1,0:T(8,128)(2,1)S(1)} %get-tuple-element.181), channel_id=1, source_target_pairs={{0,2},{1,3},{2,0},{3,1},{4,6},{5,7},{6,4},{7,5},{8,10},{9,11},{10,... | collective-permute-start | bytes 221192 | tf_op jit(solution)/shard_map/ppermute | solution.py:460
  156.2 4.2 %collective-permute-start.26 = (bf16[144,256]{1,0:T(8,128)(2,1)S(1)}, bf16[144,256]{1,0:T(8,128)(2,1)S(1)}, u32[]{:S(2)}, u32[]{:S(2)}) collective-permute-start(bf16[144,256]{1,0:T(8,128)(2,1)S(1)} %get-tuple-element.182), channel_id=1, source_target_pairs={{0,3},{1,2},{2,1},{3,0},{4,7},{5,6},{6,5},{7,4},{8,11},{9,10},{10,... | collective-permute-start | bytes 221192 | tf_op jit(solution)/shard_map/ppermute | solution.py:460
  (31 other events, 221.5 us)
